TPU v7x, 512 devices: a whole 4x4x16 slice. The times are simulated.
512 devices in a mesh: dp: 32 (over y, x, core), tensor: 16 (over z).
Axes of the slice: x: 4, y: 4, z: 16, core: 2. Of those that a mesh axis runs over, the one named last changes fastest.
Arguments:
- activations: bfloat16 [32768, 5120], P('dp', 'tensor'), may hold values from -36 to 36, as said below
- out_grads: bfloat16 [32768, 4096], P('dp', 'tensor'), may hold values from -0.04375 to 0.04375, as said below
Outputs:
- combined: float32 [5120, 4096], P('dp', 'tensor')
Inputs may be any that keep to these rules, and one draw needn't show every extreme that they name: Replicas' activations share a common part and features have different scales. `out_grads`: Replicas' output gradients share a common part and columns have different scales.
All inputs are finite; a program needn't handle non-finite values.
Results may differ from a plain program's by a relative error of at most 0.0003.
Values may be sent and summed in bfloat16 or wider, within the bound.
No kernel may reach another device: no remote copies, remote signals or barrier semaphores. Data moves between devices by JAX's collectives and lax.ppermute only.
A program may use at most 64 MiB of HBM per device.

v0:
```python
import jax
import jax.numpy as jnp
from jax import lax
from jax.sharding import PartitionSpec as P

epsilon = 1e-06


def swapped(x, axis, apart):
    return lax.ppermute(x, axis, [(i, i ^ 1 << apart) for i in range(lax.axis_size(axis))])


def group_totals(partials, section):
    for bit_number in range(section + 1):
        partials = partials + swapped(partials, "dp", bit_number)
    return lax.psum(partials, "tensor")


def adasum_pair(mine, other, section, replica):
    upper_side = jnp.right_shift(replica, section) % 2 == 1
    mine_norm = jnp.sum(mine * mine)
    other_norm = jnp.sum(other * other)
    lower_norm = jnp.where(upper_side, other_norm, mine_norm)
    upper_norm = jnp.where(upper_side, mine_norm, other_norm)
    partials = jnp.stack([jnp.sum(mine * other), lower_norm, upper_norm])
    totals = group_totals(partials, section)
    lower_coef = 1.0 - totals[0] / (2.0 * (totals[1] + epsilon))
    upper_coef = 1.0 - totals[0] / (2.0 * (totals[2] + epsilon))
    mine_coef = jnp.where(upper_side, upper_coef, lower_coef)
    other_coef = jnp.where(upper_side, lower_coef, upper_coef)
    return mine_coef * mine + other_coef * other


def on_device(activations, out_grads):
    replicas = lax.axis_size("dp")
    section_count = replicas.bit_length() - 1
    replica = lax.axis_index("dp")
    columns = out_grads.shape[1]
    slab_rows = activations.shape[1]
    block_rows = slab_rows * lax.axis_size("tensor") // replicas
    full_grad = jnp.einsum(
        "tk,tf->kf",
        lax.all_gather(activations, "tensor", axis=1, tiled=True),
        out_grads,
        preferred_element_type=jnp.float32,
    )
    holding = full_grad.reshape(replicas, block_rows, columns)
    start_section = 0
    for section in range(start_section, section_count):
        section_bit = jnp.right_shift(replica, section) % 2
        paired = holding.reshape(-1, 2, block_rows, columns)
        keeping = lax.dynamic_index_in_dim(paired, section_bit, axis=1, keepdims=False)
        sending = lax.dynamic_index_in_dim(paired, 1 - section_bit, axis=1, keepdims=False)
        received = swapped(sending, "dp", section)
        holding = adasum_pair(keeping, received, section, replica)
    return holding.reshape(block_rows, columns)


def solution(mesh):
    return jax.shard_map(
        on_device,
        mesh=mesh,
        in_specs=(P("dp", "tensor"), P("dp", "tensor")),
        out_specs=P("dp", "tensor"),
        check_vma=False,
    )
```

profile of v0, /device:TPU:2, one launch (start us, length us, event | category | flops | bytes accessed | tf_op | source)
XLA Modules:
  0.0 496.2 jit_solution(4302938187155961320)
XLA Ops:
  7.3 133.7 %all-gather.2.cloned.1.call-done = bf16[1024,5120]{0,1:T(8,128)(2,1)} async-done(((bf16[1024,320]{0,1:T(8,128)(2,1)}), bf16[1024,5120]{0,1:T(8,128)(2,1)}) %all-gather.2.cloned.1.call-update) | async-done | bytes 10485776 | tf_op jit(solution)/shard_map/all_gather | solution.py:43
  140.9 5.6 %fusion.17 = f32[5120,256]{1,0:T(8,128)S(1)} fusion(bf16[1024,5120]{0,1:T(8,128)(2,1)} %all-gather.2.cloned.1.call-done, bf16[1024,256]{1,0:T(8,128)(2,1)S(1)} %copy-done), kind=kOutput, calls=%fused_computation.47 | convolution fusion | flops 2684354560 | bytes 16252928 | tf_op jit(solution)/shard_map/tk,tf->kf/dot_general | solution.py:41
  151.6 5.1 %collective-permute-done = f32[16,160,256]{2,1,0:T(8,128)S(1)} collective-permute-done((f32[16,160,256]{2,1,0:T(8,128)}, f32[16,160,256]{2,1,0:T(8,128)S(1)}, u32[]{:S(2)}, u32[]{:S(2)}) %collective-permute-start) | collective-permute-done | bytes 2621472 | tf_op jit(solution)/shard_map/ppermute | solution.py:10
  156.6 4.0 fusion
  167.6 28.6 %psum.35 = f32[3]{0:T(128)S(1)} all-reduce(f32[3]{0:T(128)S(1)} %fusion.24), channel_id=1, replica_groups=mesh['dp'=32,'tensor'=16] {'tensor'}, use_global_device_ids=true, to_apply=%region_3.4 | all-reduce | flops 3 | bytes 24 | tf_op jit(solution)/shard_map/psum | solution.py:16
  199.4 3.0 fusion.2
  206.1 23.4 %collective-permute-done.2 = f32[8,160,256]{2,1,0:T(8,128)} collective-permute-done((f32[8,160,256]{2,1,0:T(8,128)}, f32[8,160,256]{2,1,0:T(8,128)}, u32[]{:S(2)}, u32[]{:S(2)}) %collective-permute-start.2) | collective-permute-done | bytes 1310752 | tf_op jit(solution)/shard_map/ppermute | solution.py:10
  241.2 3.0 collective-permute-done.4
  244.9 29.4 %psum.36 = f32[3]{0:T(128)S(1)} all-reduce(f32[3]{0:T(128)S(1)} %fusion.28), channel_id=1, replica_groups=mesh['dp'=32,'tensor'=16] {'tensor'}, use_global_device_ids=true, to_apply=%region_7.8 | all-reduce | flops 3 | bytes 24 | tf_op jit(solution)/shard_map/psum | solution.py:16
  280.1 4.0 collective-permute-start.5
  284.1 10.0 %collective-permute-done.5 = f32[4,160,256]{2,1,0:T(8,128)S(1)} collective-permute-done((f32[4,160,256]{2,1,0:T(8,128)S(1)}, f32[4,160,256]{2,1,0:T(8,128)S(1)}, u32[]{:S(2)}, u32[]{:S(2)}) %collective-permute-start.5) | collective-permute-done | bytes 655392 | tf_op jit(solution)/shard_map/ppermute | solution.py:10
  309.1 4.0 collective-permute-start.8
  316.0 27.9 %psum.37 = f32[3]{0:T(128)S(1)} all-reduce(f32[3]{0:T(128)S(1)} %add.193), channel_id=1, replica_groups=mesh['dp'=32,'tensor'=16] {'tensor'}, use_global_device_ids=true, to_apply=%region_11.12 | all-reduce | flops 3 | bytes 24 | tf_op jit(solution)/shard_map/psum | solution.py:16
  348.3 3.4 collective-permute-start.9
  351.7 5.5 %collective-permute-done.9 = f32[2,160,256]{2,1,0:T(8,128)S(1)} collective-permute-done((f32[2,160,256]{2,1,0:T(8,128)S(1)}, f32[2,160,256]{2,1,0:T(8,128)S(1)}, u32[]{:S(2)}, u32[]{:S(2)}) %collective-permute-start.9) | collective-permute-done | bytes 327712 | tf_op jit(solution)/shard_map/ppermute | solution.py:10
  371.1 4.0 collective-permute-start.12
  378.0 3.4 collective-permute-start.13
  383.5 28.1 %psum.38 = f32[3]{0:T(128)S(1)} all-reduce(f32[3]{0:T(128)S(1)} %add.202), channel_id=1, replica_groups=mesh['dp'=32,'tensor'=16] {'tensor'}, use_global_device_ids=true, to_apply=%region_15.16 | all-reduce | flops 3 | bytes 24 | tf_op jit(solution)/shard_map/psum | solution.py:16
  415.0 4.9 collective-permute-start.14
  419.9 3.8 collective-permute-done.14
  437.5 4.0 collective-permute-start.17
  444.5 3.4 collective-permute-start.18
  449.9 4.9 collective-permute-start.19
  456.8 28.5 %psum.39 = f32[3]{0:T(128)S(1)} all-reduce(f32[3]{0:T(128)S(1)} %add.212), channel_id=1, replica_groups=mesh['dp'=32,'tensor'=16] {'tensor'}, use_global_device_ids=true, to_apply=%region_19.20 | all-reduce | flops 3 | bytes 24 | tf_op jit(solution)/shard_map/psum | solution.py:16
  (73 shorter events, 81.6 us)
Async XLA Ops:
  6.5 134.4 %copy-start = (bf16[1024,256]{1,0:T(8,128)(2,1)S(1)}, bf16[1024,256]{1,0:T(8,128)(2,1)}, u32[]{:S(2)}) copy-start(bf16[1024,256]{1,0:T(8,128)(2,1)} %param.3) | copy-start | bytes 1572868
  6.5 134.4 %all-gather.2.cloned.1.call-start = ((), (), s32[]{:S(2)}) async-start(), calls=%async_computation | async-start | bytes 11141120 | tf_op jit(solution)/shard_map/all_gather | solution.py:43
  146.5 3.1 copy-start.1
  149.6 7.0 %collective-permute-start = (f32[16,160,256]{2,1,0:T(8,128)}, f32[16,160,256]{2,1,0:T(8,128)S(1)}, u32[]{:S(2)}, u32[]{:S(2)}) collective-permute-start(f32[16,160,256]{2,1,0:T(8,128)} %dynamic-slice_bitcast_fusion), channel_id=1, source_target_pairs={{0,16},{16,0},{32,48},{48,32},{64,80},{80,64},{96,112},{112,96},{1... | collective-permute-start | bytes 7864328 | tf_op jit(solution)/shard_map/ppermute | solution.py:10
  156.6 4.0 copy-start.2
  163.9 3.0 collective-permute-start.1
  203.6 25.9 %collective-permute-start.2 = (f32[8,160,256]{2,1,0:T(8,128)}, f32[8,160,256]{2,1,0:T(8,128)}, u32[]{:S(2)}, u32[]{:S(2)}) collective-permute-start(f32[8,160,256]{2,1,0:T(8,128)} %dynamic-slice_bitcast_fusion.1), channel_id=1, source_target_pairs={{0,32},{16,48},{32,0},{48,16},{64,96},{80,112},{96,64},{112,80},{1... | collective-permute-start | bytes 3932168 | tf_op jit(solution)/shard_map/ppermute | solution.py:10
  235.0 3.0 collective-permute-start.3
  238.8 5.4 %collective-permute-start.4 = (f32[3]{0:T(128)S(1)}, f32[3]{0:T(128)S(1)}, u32[]{:S(2)}, u32[]{:S(2)}) collective-permute-start(f32[3]{0:T(128)S(1)} %fusion.23), channel_id=1, source_target_pairs={{0,32},{16,48},{32,0},{48,16},{64,96},{80,112},{96,64},{112,80},{1... | collective-permute-start | bytes 44 | tf_op jit(solution)/shard_map/ppermute | solution.py:10
  280.1 14.0 %collective-permute-start.5 = (f32[4,160,256]{2,1,0:T(8,128)S(1)}, f32[4,160,256]{2,1,0:T(8,128)S(1)}, u32[]{:S(2)}, u32[]{:S(2)}) collective-permute-start(f32[4,160,256]{2,1,0:T(8,128)S(1)} %dynamic-slice_bitcast_fusion.2), channel_id=1, source_target_pairs={{0,64},{16,80},{32,96},{48,112},{64,0},{80,16},{96,32},{112,48},{1... | collective-permute-start | bytes 1966088 | tf_op jit(solution)/shard_map/ppermute | solution.py:10
  299.2 3.0 collective-permute-start.6
  302.9 5.4 %collective-permute-start.7 = (f32[3]{0:T(128)S(1)}, f32[3]{0:T(128)S(1)}, u32[]{:S(2)}, u32[]{:S(2)}) collective-permute-start(f32[3]{0:T(128)S(1)} %fusion.22), channel_id=1, source_target_pairs={{0,32},{16,48},{32,0},{48,16},{64,96},{80,112},{96,64},{112,80},{1... | collective-permute-start | bytes 44 | tf_op jit(solution)/shard_map/ppermute | solution.py:10
  309.1 6.9 %collective-permute-start.8 = (f32[3]{0:T(128)S(1)}, f32[3]{0:T(128)S(1)}, u32[]{:S(2)}, u32[]{:S(2)}) collective-permute-start(f32[3]{0:T(128)S(1)} %fusion.27), channel_id=1, source_target_pairs={{0,64},{16,80},{32,96},{48,112},{64,0},{80,16},{96,32},{112,48},{1... | collective-permute-start | bytes 44 | tf_op jit(solution)/shard_map/ppermute | solution.py:10
  348.3 9.0 %collective-permute-start.9 = (f32[2,160,256]{2,1,0:T(8,128)S(1)}, f32[2,160,256]{2,1,0:T(8,128)S(1)}, u32[]{:S(2)}, u32[]{:S(2)}) collective-permute-start(f32[2,160,256]{2,1,0:T(8,128)S(1)} %dynamic-slice_bitcast_fusion.3), channel_id=1, source_target_pairs={{0,128},{16,144},{32,160},{48,176},{64,192},{80,208},{96,224},{112... | collective-permute-start | bytes 983048 | tf_op jit(solution)/shard_map/ppermute | solution.py:10
  361.2 3.0 collective-permute-start.10
  365.0 5.4 %collective-permute-start.11 = (f32[3]{0:T(128)S(1)}, f32[3]{0:T(128)S(1)}, u32[]{:S(2)}, u32[]{:S(2)}) collective-permute-start(f32[3]{0:T(128)S(1)} %fusion.21), channel_id=1, source_target_pairs={{0,32},{16,48},{32,0},{48,16},{64,96},{80,112},{96,64},{112,80},{1... | collective-permute-start | bytes 44 | tf_op jit(solution)/shard_map/ppermute | solution.py:10
  371.1 6.9 %collective-permute-start.12 = (f32[3]{0:T(128)S(1)}, f32[3]{0:T(128)S(1)}, u32[]{:S(2)}, u32[]{:S(2)}) collective-permute-start(f32[3]{0:T(128)S(1)} %fusion.26), channel_id=1, source_target_pairs={{0,64},{16,80},{32,96},{48,112},{64,0},{80,16},{96,32},{112,48},{1... | collective-permute-start | bytes 44 | tf_op jit(solution)/shard_map/ppermute | solution.py:10
  378.0 5.4 %collective-permute-start.13 = (f32[3]{0:T(128)S(1)}, f32[3]{0:T(128)S(1)}, u32[]{:S(2)}, u32[]{:S(2)}) collective-permute-start(f32[3]{0:T(128)S(1)} %add.201), channel_id=1, source_target_pairs={{0,128},{16,144},{32,160},{48,176},{64,192},{80,208},{96,224},{112... | collective-permute-start | bytes 44 | tf_op jit(solution)/shard_map/ppermute | solution.py:10
  415.0 8.7 %collective-permute-start.14 = (f32[1,160,256]{2,1,0:T(8,128)S(1)}, f32[1,160,256]{2,1,0:T(8,128)S(1)}, u32[]{:S(2)}, u32[]{:S(2)}) collective-permute-start(f32[1,160,256]{2,1,0:T(8,128)S(1)} %constant_dynamic-slice_fusion), channel_id=1, source_target_pairs={{0,256},{16,272},{32,288},{48,304},{64,320},{80,336},{96,352},{112... | collective-permute-start | bytes 491528 | tf_op jit(solution)/shard_map/ppermute | solution.py:10
  427.7 3.0 collective-permute-start.15
  431.4 5.4 %collective-permute-start.16 = (f32[3]{0:T(128)S(1)}, f32[3]{0:T(128)S(1)}, u32[]{:S(2)}, u32[]{:S(2)}) collective-permute-start(f32[3]{0:T(128)S(1)} %fusion.20), channel_id=1, source_target_pairs={{0,32},{16,48},{32,0},{48,16},{64,96},{80,112},{96,64},{112,80},{1... | collective-permute-start | bytes 44 | tf_op jit(solution)/shard_map/ppermute | solution.py:10
  437.5 6.9 %collective-permute-start.17 = (f32[3]{0:T(128)S(1)}, f32[3]{0:T(128)S(1)}, u32[]{:S(2)}, u32[]{:S(2)}) collective-permute-start(f32[3]{0:T(128)S(1)} %fusion.25), channel_id=1, source_target_pairs={{0,64},{16,80},{32,96},{48,112},{64,0},{80,16},{96,32},{112,48},{1... | collective-permute-start | bytes 44 | tf_op jit(solution)/shard_map/ppermute | solution.py:10
  444.5 5.4 %collective-permute-start.18 = (f32[3]{0:T(128)S(1)}, f32[3]{0:T(128)S(1)}, u32[]{:S(2)}, u32[]{:S(2)}) collective-permute-start(f32[3]{0:T(128)S(1)} %add.210), channel_id=1, source_target_pairs={{0,128},{16,144},{32,160},{48,176},{64,192},{80,208},{96,224},{112... | collective-permute-start | bytes 44 | tf_op jit(solution)/shard_map/ppermute | solution.py:10
  449.9 6.9 %collective-permute-start.19 = (f32[3]{0:T(128)S(1)}, f32[3]{0:T(128)S(1)}, u32[]{:S(2)}, u32[]{:S(2)}) collective-permute-start(f32[3]{0:T(128)S(1)} %add.211), channel_id=1, source_target_pairs={{0,256},{16,272},{32,288},{48,304},{64,320},{80,336},{96,352},{112... | collective-permute-start | bytes 44 | tf_op jit(solution)/shard_map/ppermute | solution.py:10
  (1 other events, 1.1 us)
Sparse Core Ops, SparseCore 0:
  9.4 131.4 all-gather.1
where the time goes:
time: 498 us; the launch traced here: 496 us
  waiting for transfers between devices  214 us (43%)
  blocking collectives  143 us (29%)
  starting transfers between devices  59.8 us (12%)
  between operations  39.2 us (8%)
  other arithmetic  26.2 us (5%)
  local copies, waits for them, and re-layouts  8.7 us (2%)
  matrix products  5.6 us (1%)
    psum x5, blocking collectives, group_totals(): return lax.psum(partials, 'tensor')  143 us
    all_gather x1, waiting for transfers between devices, on_device(): lax.all_gather(activations, 'tensor', axis=1, tiled=True)  134 us
    ppermute x20, waiting for transfers between devices, swapped(): lax.ppermute(x, axis, [(i, i ^ 1 << apart) for i in range(lax.axis_size(a...  79.8 us
    ppermute x20, starting transfers between devices, swapped(): lax.ppermute(x, axis, [(i, i ^ 1 << apart) for i in range(lax.axis_size(a...  59.8 us
  transfers between devices with their start and end apart: 21, of which 21 were waited for; matrix products, arithmetic and copies ran while one was open for 0% of the time, Pallas kernels for 0%

commit v1 on v0

v1 whole, which is shorter than its diff:
```python
import jax
import jax.numpy as jnp
from jax import lax
from jax.sharding import PartitionSpec as P

epsilon = 1e-06
CHUNKS = 1


def gram_total(gram):
    n = gram.shape[0]
    flat = gram.reshape(-1, 128)
    flat = jnp.sum(lax.all_gather(flat, "dp"), axis=0)
    peers = jnp.broadcast_to(flat, (lax.axis_size("tensor"), *flat.shape))
    flat = jnp.sum(lax.all_to_all(peers, "tensor", 0, 0), axis=0)
    return flat.reshape(n, n)


def tree_weights(gram):
    n = gram.shape[0]
    index = jnp.arange(n)
    weights = jnp.ones((n,), jnp.float32)
    width = 1
    while width < n:
        scaled = gram * weights[:, None] * weights[None, :]
        item = index // width
        same = (item[:, None] == item[None, :])
        partner = (item[:, None] == (item ^ 1)[None, :])
        own = jnp.sum(jnp.where(same, scaled, 0.0), axis=1)
        cross = jnp.sum(jnp.where(partner, scaled, 0.0), axis=1)
        own = jnp.sum(jnp.where(same, own[None, :], 0.0), axis=1)
        cross = jnp.sum(jnp.where(same, cross[None, :], 0.0), axis=1)
        own = jnp.maximum(own, 0.0)
        weights = weights * (1.0 - cross / (2.0 * (own + epsilon)))
        width *= 2
    return weights


def on_device(activations, out_grads):
    replicas = lax.axis_size("dp")
    slabs = lax.axis_size("tensor")
    tokens, slab_rows = activations.shape
    columns = out_grads.shape[1]
    block_rows = slab_rows * slabs // replicas
    per_slab = slab_rows // block_rows
    rows = block_rows // CHUNKS
    x = activations.T.reshape(per_slab, CHUNKS, rows, tokens)
    blocks = []
    gram = jnp.zeros((replicas, replicas), jnp.float32)
    for chunk in range(CHUNKS):
        part = lax.all_gather(x[:, chunk], "tensor", axis=0)
        part = part.reshape(replicas * rows, tokens)
        grad = jnp.dot(part, out_grads, preferred_element_type=jnp.float32)
        grad = grad.reshape(replicas, rows, columns)
        block = lax.all_to_all(grad, "dp", 0, 0)
        blocks.append(block)
        gram = gram + lax.dot_general(
            block, block, (((1, 2), (1, 2)), ((), ())),
            precision=lax.Precision.HIGHEST, preferred_element_type=jnp.float32,
        )
    weights = tree_weights(gram_total(gram))
    out = [jnp.sum(b * weights[:, None, None], axis=0) for b in blocks]
    return jnp.concatenate(out, axis=0)


def solution(mesh):
    return jax.shard_map(
        on_device,
        mesh=mesh,
        in_specs=(P("dp", "tensor"), P("dp", "tensor")),
        out_specs=P("dp", "tensor"),
        check_vma=False,
    )
```

time: 498 us -> 295 us (0.59)
  the two profiles are of different devices: /device:TPU:2 before, /device:TPU:1 now
where the time goes in v1:
time: 295 us; the launch traced here: 293 us
  waiting for transfers between devices  208 us (71%)
  blocking collectives  25.5 us (9%)
  matrix products  23.2 us (8%)
  starting transfers between devices  16.2 us (5%)
  between operations  13.5 us (5%)
  other arithmetic  5.47 us (2%)
    all_gather x1, waiting for transfers between devices, on_device(): part = lax.all_gather(x[:, chunk], 'tensor', axis=0)  135 us
    all_to_all x1, waiting for transfers between devices, on_device(): block = lax.all_to_all(grad, 'dp', 0, 0)  61.5 us
    all_gather x1, blocking collectives, gram_total(): flat = jnp.sum(lax.all_gather(flat, 'dp'), axis=0)  25.5 us
    dot_general x1, matrix products, on_device(): lax.dot_general(block, block, (((1, 2), (1, 2)), ((), ())), precision=lax...  13.9 us
    all_to_all x1, waiting for transfers between devices, gram_total(): flat = jnp.sum(lax.all_to_all(peers, 'tensor', 0, 0), axis=0)  11.6 us
    dot_general x1, matrix products, on_device(): grad = jnp.dot(part, out_grads, preferred_element_type=jnp.float32)  9.24 us
    all_to_all x1, starting transfers between devices, gram_total(): flat = jnp.sum(lax.all_to_all(peers, 'tensor', 0, 0), axis=0)  8.58 us
    all_to_all x1, starting transfers between devices, on_device(): block = lax.all_to_all(grad, 'dp', 0, 0)  7.6 us
  transfers between devices with their start and end apart: 3, of which 3 were waited for; matrix products, arithmetic and copies ran while one was open for 0% of the time, Pallas kernels for 0%

profile of v1, /device:TPU:1, one launch (start us, length us, event | category | flops | bytes accessed | tf_op | source)
XLA Modules:
  0.0 292.9 jit_solution(3494430623465237135)
XLA Ops:
  6.5 0.0 copy-start
  6.5 0.7 all-gather.2.cloned.1.call-update
  7.3 134.5 %all-gather.2.cloned.1.call-done = bf16[16,2,160,1024]{3,2,1,0:T(8,128)(2,1)} async-done(((bf16[1,2,160,1024]{3,2,1,0:T(8,128)(2,1)}), bf16[16,2,160,1024]{3,2,1,0:T(8,128)(2,1)}) %all-gather.2.cloned.1.call-update) | async-done | bytes 10485776 | tf_op jit(solution)/shard_map/all_gather | solution.py:51
  141.8 9.2 %fusion.5 = f32[32,160,256]{2,1,0:T(8,128)} fusion(bf16[32,160,1024]{2,1,0:T(8,128)(2,1)} %bitcast.11, bf16[1024,256]{1,0:T(8,128)(2,1)S(1)} %copy-done), kind=kOutput, calls=%fused_computation.4 | convolution fusion | flops 2684354560 | bytes 16252928 | tf_op jit(solution)/shard_map/dot_general | solution.py:53
  151.0 7.6 %all-to-all-start = ((f32[32,160,256]{2,1,0:T(8,128)}), f32[32,160,256]{2,1,0:T(8,128)}, u32[]{:S(2)}, u32[]{:S(2)}) async-start(f32[32,160,256]{2,1,0:T(8,128)} %fusion.5), calls=%async_computation | async-start | bytes 10485760 | tf_op jit(solution)/shard_map/all_to_all | solution.py:55
  158.7 61.5 %all-to-all-done = f32[32,160,256]{2,1,0:T(8,128)} async-done(((f32[32,160,256]{2,1,0:T(8,128)}), f32[32,160,256]{2,1,0:T(8,128)}, u32[]{:S(2)}, u32[]{:S(2)}) %all-to-all-start) | async-done | bytes 5242912 | tf_op jit(solution)/shard_map/all_to_all | solution.py:55
  220.1 13.9 %fusion.2 = f32[32,32]{1,0:T(8,128)S(1)} fusion(f32[32,160,256]{2,1,0:T(8,128)} %all-to-all-done), kind=kOutput, calls=%fused_computation.3 | convolution fusion | flops 503316480 | bytes 5246976 | tf_op jit(solution)/shard_map/dot_general | solution.py:57
  234.1 0.1 all_gather_reshape.3
  234.1 25.5 %all_gather.7 = f32[32,8,128]{2,1,0:T(8,128)S(1)} all-gather(f32[1,8,128]{2,1,0:T(8,128)S(1)} %all_gather_reshape.3), channel_id=1, replica_groups=mesh['dp'=32,'tensor'=16] {'dp'}, dimensions={0}, use_global_device_ids=true | all-gather | bytes 135168 | tf_op jit(solution)/shard_map/all_gather | solution.py:13
  259.7 0.6 broadcast_in_dim.119
  260.4 8.6 %all-to-all-start.1 = ((f32[16,8,128]{2,1,0:T(8,128)}), f32[16,8,128]{2,1,0:T(8,128)S(1)}, u32[]{:S(2)}, u32[]{:S(2)}) async-start(f32[16,8,128]{2,1,0:T(8,128)} %broadcast_in_dim.119), calls=%async_computation.1 | async-start | bytes 131072 | tf_op jit(solution)/shard_map/all_to_all | solution.py:15
  269.0 11.6 %all-to-all-done.1 = f32[16,8,128]{2,1,0:T(8,128)S(1)} async-done(((f32[16,8,128]{2,1,0:T(8,128)}), f32[16,8,128]{2,1,0:T(8,128)S(1)}, u32[]{:S(2)}, u32[]{:S(2)}) %all-to-all-start.1) | async-done | bytes 65568 | tf_op jit(solution)/shard_map/all_to_all | solution.py:15
  280.6 0.1 reshape.308
  280.6 0.1 select_reduce_fusion.5
  280.8 0.1 select_reduce_fusion.4
  280.9 0.2 fusion.8
  281.1 0.2 fusion.9
  281.3 0.2 fusion.11
  281.5 0.2 fusion.12
  281.7 0.2 fusion.14
  281.9 0.2 fusion.15
  282.1 0.2 fusion.17
  282.3 0.2 fusion.18
  282.5 3.6 %multiply_reduce_fusion = f32[160,256]{1,0:T(8,128)} fusion(f32[32,160,256]{2,1,0:T(8,128)} %all-to-all-done, f32[32]{0:T(128)S(1)} %subtract_multiply_fusion), kind=kLoop, calls=%fused_computation.2 | loop fusion | flops 2580480 | bytes 5406848 | tf_op jit(solution)/shard_map/reduce_sum | solution.py:62
  (14 shorter events, 0.1 us)
Async XLA Ops:
  6.5 135.3 %copy-start = (bf16[1024,256]{1,0:T(8,128)(2,1)S(1)}, bf16[1024,256]{1,0:T(8,128)(2,1)}, u32[]{:S(2)}) copy-start(bf16[1024,256]{1,0:T(8,128)(2,1)} %param.3) | copy-start | bytes 1572868
  6.5 135.2 %all-gather.2.cloned.1.call-start = ((), (), s32[]{:S(2)}) async-start(), calls=%async_computation.2 | async-start | bytes 11141120 | tf_op jit(solution)/shard_map/all_gather | solution.py:51
  151.0 69.1 %all-to-all-start = ((f32[32,160,256]{2,1,0:T(8,128)}), f32[32,160,256]{2,1,0:T(8,128)}, u32[]{:S(2)}, u32[]{:S(2)}) async-start(f32[32,160,256]{2,1,0:T(8,128)} %fusion.5), calls=%async_computation | async-start | bytes 10485760 | tf_op jit(solution)/shard_map/all_to_all | solution.py:55
  260.4 20.2 %all-to-all-start.1 = ((f32[16,8,128]{2,1,0:T(8,128)}), f32[16,8,128]{2,1,0:T(8,128)S(1)}, u32[]{:S(2)}, u32[]{:S(2)}) async-start(f32[16,8,128]{2,1,0:T(8,128)} %broadcast_in_dim.119), calls=%async_computation.1 | async-start | bytes 131072 | tf_op jit(solution)/shard_map/all_to_all | solution.py:15
Sparse Core Ops, SparseCore 0:
  9.4 132.3 all-gather.1

commit v2 on v1

--- a/solution.py
+++ b/solution.py
@@ -4,7 +4,7 @@
 from jax.sharding import PartitionSpec as P
 
 epsilon = 1e-06
-CHUNKS = 1
+CHUNKS = 4
 
 
 def gram_total(gram):

time: 295 us -> 400 us (1.36)
  starting transfers between devices: 16.2 us -> 72.1 us
  waiting for transfers between devices: 208 us -> 257 us
    all_gather x1 -> x4, waiting for transfers between devices: 135 us -> 231 us  [on_device(): part = lax.all_gather(x[:, chunk], 'tensor', axis=0)]
    all_to_all x1 -> x4, starting transfers between devices: 7.6 us -> 64.8 us  [on_device(): block = lax.all_to_all(grad, 'dp', 0, 0)]
    all_to_all x1 -> x4, waiting for transfers between devices: 61.5 us -> 12.7 us  [on_device(): block = lax.all_to_all(grad, 'dp', 0, 0)]
    dot_general x1 -> x4, matrix products: 9.24 us -> 14.8 us  [on_device(): grad = jnp.dot(part, out_grads, preferred_element_type=jnp.float32)]
    dot_general x1 -> x4, matrix products: 13.9 us -> 9.98 us  [on_device(): lax.dot_general(block, block, (((1, 2), (1, 2)), ((), ())), precision=lax...]
  transfers between devices with their start and end apart: 3 -> 9, of which waited for: 3 -> 6; matrix products, arithmetic and copies ran while one was open for 0% -> 5% of each run, Pallas kernels for 0% -> 0%
where the time goes in v2:
time: 400 us; the launch traced here: 398 us
  waiting for transfers between devices  257 us (64%)
  starting transfers between devices  72.1 us (18%)
  matrix products  24.8 us (6%)
  blocking collectives  23.5 us (6%)
  between operations  13.3 us (3%)
  other arithmetic  4.66 us (1%)
    all_gather x4, waiting for transfers between devices, on_device(): part = lax.all_gather(x[:, chunk], 'tensor', axis=0)  231 us
    all_to_all x4, starting transfers between devices, on_device(): block = lax.all_to_all(grad, 'dp', 0, 0)  64.8 us
    all_gather x1, blocking collectives, gram_total(): flat = jnp.sum(lax.all_gather(flat, 'dp'), axis=0)  23.5 us
    dot_general x4, matrix products, on_device(): grad = jnp.dot(part, out_grads, preferred_element_type=jnp.float32)  14.8 us
    all_to_all x4, waiting for transfers between devices, on_device(): block = lax.all_to_all(grad, 'dp', 0, 0)  12.7 us
    all_to_all x1, waiting for transfers between devices, gram_total(): flat = jnp.sum(lax.all_to_all(peers, 'tensor', 0, 0), axis=0)  11.6 us
    dot_general x4, matrix products, on_device(): lax.dot_general(block, block, (((1, 2), (1, 2)), ((), ())), precision=lax...  9.98 us
  transfers between devices with their start and end apart: 9, of which 6 were waited for; matrix products, arithmetic and copies ran while one was open for 5% of the time, Pallas kernels for 0%

profile of v2, /device:TPU:1, one launch (start us, length us, event | category | flops | bytes accessed | tf_op | source)
XLA Modules:
  0.0 398.3 jit_solution(17022049178003242474)
XLA Ops:
  6.5 2.0 fusion.54
  8.7 0.7 all-gather.11.cloned.1.call-update
  10.7 70.1 %all-gather.9.cloned.1.call-done = bf16[32,1,40,1024]{3,2,1,0:T(8,128)(2,1)} async-done(((bf16[2,1,40,1024]{3,2,1,0:T(8,128)(2,1)}), bf16[32,1,40,1024]{3,2,1,0:T(8,128)(2,1)}) %all-gather.9.cloned.1.call-update) | async-done | bytes 2621456 | tf_op jit(solution)/shard_map/all_gather | solution.py:51
  80.8 3.7 fusion.6
  84.5 16.5 %all-to-all-start = ((f32[32,40,256]{2,1,0:T(8,128)}), f32[32,40,256]{2,1,0:T(8,128)S(1)}, u32[]{:S(2)}, u32[]{:S(2)}) async-start(f32[32,40,256]{2,1,0:T(8,128)} %fusion.6), calls=%async_computation | async-start | bytes 2621440 | tf_op jit(solution)/shard_map/all_to_all | solution.py:55
  101.0 53.7 %all-gather.11.cloned.1.call-done = bf16[32,1,40,1024]{3,2,1,0:T(8,128)(2,1)} async-done(((bf16[2,1,40,1024]{3,2,1,0:T(8,128)(2,1)}), bf16[32,1,40,1024]{3,2,1,0:T(8,128)(2,1)}) %all-gather.11.cloned.1.call-update) | async-done | bytes 2621456 | tf_op jit(solution)/shard_map/all_gather | solution.py:51
  154.7 3.8 fusion.4
  158.5 16.1 %all-to-all-start.1 = ((f32[32,40,256]{2,1,0:T(8,128)}), f32[32,40,256]{2,1,0:T(8,128)S(1)}, u32[]{:S(2)}, u32[]{:S(2)}) async-start(f32[32,40,256]{2,1,0:T(8,128)} %fusion.4), calls=%async_computation.1 | async-start | bytes 2621440 | tf_op jit(solution)/shard_map/all_to_all | solution.py:55
  174.5 53.6 %all-gather.13.cloned.1.call-done = bf16[32,1,40,1024]{3,2,1,0:T(8,128)(2,1)} async-done(((bf16[2,1,40,1024]{3,2,1,0:T(8,128)(2,1)}), bf16[32,1,40,1024]{3,2,1,0:T(8,128)(2,1)}) %all-gather.13.cloned.1.call-update) | async-done | bytes 2621456 | tf_op jit(solution)/shard_map/all_gather | solution.py:51
  228.2 3.7 fusion.2
  231.9 16.1 %all-to-all-start.2 = ((f32[32,40,256]{2,1,0:T(8,128)}), f32[32,40,256]{2,1,0:T(8,128)}, u32[]{:S(2)}, u32[]{:S(2)}) async-start(f32[32,40,256]{2,1,0:T(8,128)} %fusion.2), calls=%async_computation.2 | async-start | bytes 2621440 | tf_op jit(solution)/shard_map/all_to_all | solution.py:55
  248.0 53.4 %all-gather.15.cloned.1.call-done = bf16[32,1,40,1024]{3,2,1,0:T(8,128)(2,1)} async-done(((bf16[2,1,40,1024]{3,2,1,0:T(8,128)(2,1)}), bf16[32,1,40,1024]{3,2,1,0:T(8,128)(2,1)}) %all-gather.15.cloned.1.call-update) | async-done | bytes 2621456 | tf_op jit(solution)/shard_map/all_gather | solution.py:51
  301.4 3.7 fusion
  305.1 16.2 %all-to-all-start.3 = ((f32[32,40,256]{2,1,0:T(8,128)}), f32[32,40,256]{2,1,0:T(8,128)}, u32[]{:S(2)}, u32[]{:S(2)}) async-start(f32[32,40,256]{2,1,0:T(8,128)} %fusion), calls=%async_computation.3 | async-start | bytes 2621440 | tf_op jit(solution)/shard_map/all_to_all | solution.py:55
  321.3 1.4 fusion.16
  322.7 1.4 fusion.34
  324.1 3.6 fusion.31
  327.7 12.7 %all-to-all-done.3 = f32[32,40,256]{2,1,0:T(8,128)} async-done(((f32[32,40,256]{2,1,0:T(8,128)}), f32[32,40,256]{2,1,0:T(8,128)}, u32[]{:S(2)}, u32[]{:S(2)}) %all-to-all-start.3) | async-done | bytes 1310752 | tf_op jit(solution)/shard_map/all_to_all | solution.py:55
  340.4 3.6 fusion.28
  344.1 23.5 %all_gather.19 = f32[32,8,128]{2,1,0:T(8,128)S(1)} all-gather(f32[1,8,128]{2,1,0:T(8,128)S(1)} %all_gather_reshape.3), channel_id=1, replica_groups=mesh['dp'=32,'tensor'=16] {'dp'}, dimensions={0}, use_global_device_ids=true | all-gather | bytes 135168 | tf_op jit(solution)/shard_map/all_gather | solution.py:13
  368.3 7.1 %all-to-all-start.4 = ((f32[16,8,128]{2,1,0:T(8,128)}), f32[16,8,128]{2,1,0:T(8,128)S(1)}, u32[]{:S(2)}, u32[]{:S(2)}) async-start(f32[16,8,128]{2,1,0:T(8,128)} %broadcast_in_dim.122), calls=%async_computation.4 | async-start | bytes 131072 | tf_op jit(solution)/shard_map/all_to_all | solution.py:15
  375.5 11.6 %all-to-all-done.4 = f32[16,8,128]{2,1,0:T(8,128)S(1)} async-done(((f32[16,8,128]{2,1,0:T(8,128)}), f32[16,8,128]{2,1,0:T(8,128)S(1)}, u32[]{:S(2)}, u32[]{:S(2)}) %all-to-all-start.4) | async-done | bytes 65568 | tf_op jit(solution)/shard_map/all_to_all | solution.py:15
  388.9 2.1 multiply_reduce_fusion.3
  391.1 0.7 pad_maximum_fusion
  (37 shorter events, 4.0 us)
Async XLA Ops:
  6.5 74.3 %copy-start = (bf16[1024,256]{1,0:T(8,128)(2,1)S(1)}, bf16[1024,256]{1,0:T(8,128)(2,1)}, u32[]{:S(2)}) copy-start(bf16[1024,256]{1,0:T(8,128)(2,1)} %param.3) | copy-start | bytes 1572868
  6.5 74.3 %all-gather.9.cloned.1.call-start = ((), (), s32[]{:S(2)}) async-start(), calls=%async_computation.5 | async-start | bytes 2785280 | tf_op jit(solution)/shard_map/all_gather | solution.py:51
  8.6 146.1 %all-gather.11.cloned.1.call-start = ((), (), s32[]{:S(2)}) async-start(), calls=%async_computation.6 | async-start | bytes 2785280 | tf_op jit(solution)/shard_map/all_gather | solution.py:51
  9.4 218.8 %all-gather.13.cloned.1.call-start = ((), (), s32[]{:S(2)}) async-start(), calls=%async_computation.7 | async-start | bytes 2785280 | tf_op jit(solution)/shard_map/all_gather | solution.py:51
  10.1 291.3 %all-gather.15.cloned.1.call-start = ((), (), s32[]{:S(2)}) async-start(), calls=%async_computation.8 | async-start | bytes 2785280 | tf_op jit(solution)/shard_map/all_gather | solution.py:51
  84.5 74.0 %all-to-all-start = ((f32[32,40,256]{2,1,0:T(8,128)}), f32[32,40,256]{2,1,0:T(8,128)S(1)}, u32[]{:S(2)}, u32[]{:S(2)}) async-start(f32[32,40,256]{2,1,0:T(8,128)} %fusion.6), calls=%async_computation | async-start | bytes 2621440 | tf_op jit(solution)/shard_map/all_to_all | solution.py:55
  158.5 73.4 %all-to-all-start.1 = ((f32[32,40,256]{2,1,0:T(8,128)}), f32[32,40,256]{2,1,0:T(8,128)S(1)}, u32[]{:S(2)}, u32[]{:S(2)}) async-start(f32[32,40,256]{2,1,0:T(8,128)} %fusion.4), calls=%async_computation.1 | async-start | bytes 2621440 | tf_op jit(solution)/shard_map/all_to_all | solution.py:55
  231.9 73.2 %all-to-all-start.2 = ((f32[32,40,256]{2,1,0:T(8,128)}), f32[32,40,256]{2,1,0:T(8,128)}, u32[]{:S(2)}, u32[]{:S(2)}) async-start(f32[32,40,256]{2,1,0:T(8,128)} %fusion.2), calls=%async_computation.2 | async-start | bytes 2621440 | tf_op jit(solution)/shard_map/all_to_all | solution.py:55
  305.1 35.3 %all-to-all-start.3 = ((f32[32,40,256]{2,1,0:T(8,128)}), f32[32,40,256]{2,1,0:T(8,128)}, u32[]{:S(2)}, u32[]{:S(2)}) async-start(f32[32,40,256]{2,1,0:T(8,128)} %fusion), calls=%async_computation.3 | async-start | bytes 2621440 | tf_op jit(solution)/shard_map/all_to_all | solution.py:55
  368.3 18.7 %all-to-all-start.4 = ((f32[16,8,128]{2,1,0:T(8,128)}), f32[16,8,128]{2,1,0:T(8,128)S(1)}, u32[]{:S(2)}, u32[]{:S(2)}) async-start(f32[16,8,128]{2,1,0:T(8,128)} %broadcast_in_dim.122), calls=%async_computation.4 | async-start | bytes 131072 | tf_op jit(solution)/shard_map/all_to_all | solution.py:15
Sparse Core Ops, SparseCore 0:
  9.4 71.3 all-gather.8
  82.9 71.7 all-gather.10
  156.8 71.3 all-gather.12
  230.1 71.2 all-gather.14

commit v3 on v2

v3 whole, which is shorter than its diff:
```python
import jax
import jax.numpy as jnp
from jax import lax
from jax.sharding import PartitionSpec as P

epsilon = 1e-06
GROUP_ENDS = (2, 4, 6, 8)


def gram_total(gram):
    n = gram.shape[0]
    flat = gram.reshape(-1, 128)
    flat = jnp.sum(lax.all_gather(flat, "dp"), axis=0)
    peers = jnp.broadcast_to(flat, (lax.axis_size("tensor"), *flat.shape))
    flat = jnp.sum(lax.all_to_all(peers, "tensor", 0, 0), axis=0)
    return flat.reshape(n, n)


def tree_weights(gram):
    n = gram.shape[0]
    index = jnp.arange(n)
    weights = jnp.ones((n,), jnp.float32)
    width = 1
    while width < n:
        scaled = gram * weights[:, None] * weights[None, :]
        item = index // width
        same = item[:, None] == item[None, :]
        partner = item[:, None] == (item ^ 1)[None, :]
        own = jnp.sum(jnp.where(same, scaled, 0.0), axis=1)
        cross = jnp.sum(jnp.where(partner, scaled, 0.0), axis=1)
        own = jnp.sum(jnp.where(same, own[None, :], 0.0), axis=1)
        cross = jnp.sum(jnp.where(same, cross[None, :], 0.0), axis=1)
        own = jnp.maximum(own, 0.0)
        weights = weights * (1.0 - cross / (2.0 * (own + epsilon)))
        width *= 2
    return weights


def on_device(activations, out_grads):
    replicas = lax.axis_size("dp")
    slabs = lax.axis_size("tensor")
    here = lax.axis_index("tensor")
    tokens, slab_rows = activations.shape
    columns = out_grads.shape[1]
    part = columns // replicas
    half = slabs // 2
    up = [(i, (i + 1) % slabs) for i in range(slabs)]
    down = [((i + 1) % slabs, i) for i in range(slabs)]

    slab = activations.T
    from_below = from_above = slab
    held, order = [slab], [0]
    blocks = []
    gram = jnp.zeros((replicas, replicas), jnp.float32)
    for step in range(1, half + 1):
        if step < half:
            from_below = lax.ppermute(from_below, "tensor", up)
            from_above = lax.ppermute(from_above, "tensor", down)
            held += [from_below, from_above]
            order += [slabs - step, step]
        else:
            cut = slab_rows // 2
            from_below = lax.ppermute(from_below[:cut], "tensor", up)
            from_above = lax.ppermute(from_above[cut:], "tensor", down)
            held += [from_below, from_above]
            order += [half]
        if step in GROUP_ENDS:
            group = jnp.concatenate(held, axis=0)
            grad = lax.dot_general(
                out_grads, group, (((0,), (1,)), ((), ())),
                preferred_element_type=jnp.float32,
            )
            block = lax.all_to_all(grad.reshape(replicas, part, -1), "dp", 0, 0)
            gram = gram + lax.dot_general(
                block, block, (((1, 2), (1, 2)), ((), ())),
                precision=lax.Precision.HIGHEST, preferred_element_type=jnp.float32,
            )
            blocks.append(block)
            held = []
    weights = tree_weights(gram_total(gram))
    sums = [jnp.sum(b * weights[:, None, None], axis=0) for b in blocks]
    by_slab = jnp.concatenate(sums, axis=1).reshape(part, slabs, slab_rows)
    by_slab = jnp.stack([by_slab[:, order.index(k)] for k in range(slabs)])
    by_slab = jnp.roll(by_slab, here, axis=0)
    home = by_slab.reshape(slabs, part, replicas // slabs, -1)
    home = home.transpose(0, 2, 1, 3).reshape(replicas, part, -1)
    home = lax.all_to_all(home, "dp", 0, 0)
    return home.reshape(columns, -1).T


def solution(mesh):
    return jax.shard_map(
        on_device,
        mesh=mesh,
        in_specs=(P("dp", "tensor"), P("dp", "tensor")),
        out_specs=P("dp", "tensor"),
        check_vma=False,
    )
```

time: 400 us -> 274 us (0.69)
  waiting for transfers between devices: 257 us -> 73.1 us
  starting transfers between devices: 72.1 us -> 108 us
  blocking collectives: 23.5 us -> 40 us
  between operations: 13.3 us -> 0.42 us
  other arithmetic: 4.66 us -> 17.2 us
  local copies, waits for them, and re-layouts: 2.83 us -> 11.7 us
    all_gather x4 -> x0, waiting for transfers between devices: 231 us -> none  [on_device(): part = lax.all_gather(x[:, chunk], 'tensor', axis=0)]
    ppermute x0 -> x16, starting transfers between devices: none -> 60.6 us  [the longest x7 37.9 us: on_device(): from_above = lax.ppermute(from_above, 'tensor', down)]
    ppermute x0 -> x16, waiting for transfers between devices: none -> 53.5 us  [the longest x7 23.1 us: on_device(): from_below = lax.ppermute(from_below, 'tensor', up)]
    all_to_all x4, starting transfers between devices: 64.8 us -> 39.8 us  [on_device(): block = lax.all_to_all(grad.reshape(replicas, part, -1), 'dp', 0, 0)]
    all_to_all x0 -> x1, blocking collectives: none -> 15.5 us  [on_device(): home = lax.all_to_all(home, 'dp', 0, 0)]
    dot_general x0 -> x2, local copies, waits for them, and re-layouts: none -> 4.16 us  [on_device(): lax.dot_general(out_grads, group, (((0,), (1,)), ((), ())), preferred_ele...]
  transfers between devices with their start and end apart: 9 -> 21, of which waited for: 6 -> 8; matrix products, arithmetic and copies ran while one was open for 5% -> 10% of each run, Pallas kernels for 0% -> 0%
where the time goes in v3:
time: 274 us; the launch traced here: 272 us
  starting transfers between devices  108 us (39%)
  waiting for transfers between devices  73.1 us (27%)
  blocking collectives  40 us (15%)
  matrix products  22.1 us (8%)
  other arithmetic  17.2 us (6%)
  local copies, waits for them, and re-layouts  11.7 us (4%)
    all_to_all x4, starting transfers between devices, on_device(): block = lax.all_to_all(grad.reshape(replicas, part, -1), 'dp', 0, 0)  39.8 us
    ppermute x7, starting transfers between devices, on_device(): from_above = lax.ppermute(from_above, 'tensor', down)  37.9 us
    all_gather x1, blocking collectives, gram_total(): flat = jnp.sum(lax.all_gather(flat, 'dp'), axis=0)  24.5 us
    ppermute x7, waiting for transfers between devices, on_device(): from_below = lax.ppermute(from_below, 'tensor', up)  23.1 us
    ppermute x7, waiting for transfers between devices, on_device(): from_above = lax.ppermute(from_above, 'tensor', down)  22 us
    ppermute x7, starting transfers between devices, on_device(): from_below = lax.ppermute(from_below, 'tensor', up)  16 us
    all_to_all x1, blocking collectives, on_device(): home = lax.all_to_all(home, 'dp', 0, 0)  15.5 us
    dot_general x4, matrix products, on_device(): lax.dot_general(out_grads, group, (((0,), (1,)), ((), ())), preferred_ele...  11.3 us
  transfers between devices with their start and end apart: 21, of which 8 were waited for; matrix products, arithmetic and copies ran while one was open for 10% of the time, Pallas kernels for 0%

profile of v3, /device:TPU:1, one launch (start us, length us, event | category | flops | bytes accessed | tf_op | source)
XLA Modules:
  0.0 272.4 jit_solution(7624751220594729995)
XLA Ops:
  0.0 4.5 %collective-permute-start = (bf16[320,1024]{1,0:T(8,128)(2,1)}, bf16[320,1024]{1,0:T(8,128)(2,1)S(1)}, u32[]{:S(2)}, u32[]{:S(2)}) collective-permute-start(bf16[320,1024]{1,0:T(8,128)(2,1)} %bitcast.75), channel_id=1, source_target_pairs={{0,1},{1,2},{2,3},{3,4},{4,5},{5,6},{6,7},{7,8},{8,9},{9,10},{10,1... | collective-permute-start | bytes 1966088 | tf_op jit(solution)/shard_map/ppermute | solution.py:57
  4.5 9.5 %collective-permute-start.1 = (bf16[320,1024]{1,0:T(8,128)(2,1)}, bf16[320,1024]{1,0:T(8,128)(2,1)S(1)}, u32[]{:S(2)}, u32[]{:S(2)}) collective-permute-start(bf16[320,1024]{1,0:T(8,128)(2,1)} %bitcast.76), channel_id=1, source_target_pairs={{1,0},{2,1},{3,2},{4,3},{5,4},{6,5},{7,6},{8,7},{9,8},{10,9},{11,1... | collective-permute-start | bytes 1966088 | tf_op jit(solution)/shard_map/ppermute | solution.py:58
  14.0 12.7 %collective-permute-done = bf16[320,1024]{1,0:T(8,128)(2,1)S(1)} collective-permute-done((bf16[320,1024]{1,0:T(8,128)(2,1)}, bf16[320,1024]{1,0:T(8,128)(2,1)S(1)}, u32[]{:S(2)}, u32[]{:S(2)}) %collective-permute-start) | collective-permute-done | bytes 655392 | tf_op jit(solution)/shard_map/ppermute | solution.py:57
  28.7 4.6 %collective-permute-start.3 = (bf16[320,1024]{1,0:T(8,128)(2,1)S(1)}, bf16[320,1024]{1,0:T(8,128)(2,1)S(1)}, u32[]{:S(2)}, u32[]{:S(2)}) collective-permute-start(bf16[320,1024]{1,0:T(8,128)(2,1)S(1)} %collective-permute-done.1), channel_id=1, source_target_pairs={{1,0},{2,1},{3,2},{4,3},{5,4},{6,5},{7,6},{8,7},{9,8},{10,9},{11,1... | collective-permute-start | bytes 1966088 | tf_op jit(solution)/shard_map/ppermute | solution.py:58
  34.5 10.3 %collective-permute-done.2 = bf16[320,1024]{1,0:T(8,128)(2,1)S(1)} collective-permute-done((bf16[320,1024]{1,0:T(8,128)(2,1)S(1)}, bf16[320,1024]{1,0:T(8,128)(2,1)S(1)}, u32[]{:S(2)}, u32[]{:S(2)}) %collective-permute-start.2) | collective-permute-done | bytes 655392 | tf_op jit(solution)/shard_map/ppermute | solution.py:57
  46.8 4.6 %collective-permute-start.5 = (bf16[320,1024]{1,0:T(8,128)(2,1)S(1)}, bf16[320,1024]{1,0:T(8,128)(2,1)}, u32[]{:S(2)}, u32[]{:S(2)}) collective-permute-start(bf16[320,1024]{1,0:T(8,128)(2,1)S(1)} %collective-permute-done.3), channel_id=1, source_target_pairs={{1,0},{2,1},{3,2},{4,3},{5,4},{6,5},{7,6},{8,7},{9,8},{10,9},{11,1... | collective-permute-start | bytes 1966088 | tf_op jit(solution)/shard_map/ppermute | solution.py:58
  54.1 9.8 %all-to-all-start = ((f32[32,8,1600]{2,1,0:T(8,128)}), f32[32,8,1600]{2,1,0:T(8,128)S(1)}, u32[]{:S(2)}, u32[]{:S(2)}) async-start(f32[32,8,1600]{2,1,0:T(8,128)} %bitcast.71), calls=%async_computation | async-start | bytes 3407872 | tf_op jit(solution)/shard_map/all_to_all | solution.py:73
  64.0 4.4 %collective-permute-start.7 = (bf16[320,1024]{1,0:T(8,128)(2,1)}, bf16[320,1024]{1,0:T(8,128)(2,1)}, u32[]{:S(2)}, u32[]{:S(2)}) collective-permute-start(bf16[320,1024]{1,0:T(8,128)(2,1)} %collective-permute-done.5), channel_id=1, source_target_pairs={{1,0},{2,1},{3,2},{4,3},{5,4},{6,5},{7,6},{8,7},{9,8},{10,9},{11,1... | collective-permute-start | bytes 1966088 | tf_op jit(solution)/shard_map/ppermute | solution.py:58
  70.3 9.7 %collective-permute-done.7 = bf16[320,1024]{1,0:T(8,128)(2,1)} collective-permute-done((bf16[320,1024]{1,0:T(8,128)(2,1)}, bf16[320,1024]{1,0:T(8,128)(2,1)}, u32[]{:S(2)}, u32[]{:S(2)}) %collective-permute-start.7) | collective-permute-done | bytes 655392 | tf_op jit(solution)/shard_map/ppermute | solution.py:58
  80.0 4.6 %collective-permute-start.9 = (bf16[320,1024]{1,0:T(8,128)(2,1)}, bf16[320,1024]{1,0:T(8,128)(2,1)}, u32[]{:S(2)}, u32[]{:S(2)}) collective-permute-start(bf16[320,1024]{1,0:T(8,128)(2,1)} %collective-permute-done.7), channel_id=1, source_target_pairs={{1,0},{2,1},{3,2},{4,3},{5,4},{6,5},{7,6},{8,7},{9,8},{10,9},{11,1... | collective-permute-start | bytes 1966088 | tf_op jit(solution)/shard_map/ppermute | solution.py:58
  90.2 11.6 %all-to-all-start.1 = ((f32[32,8,1280]{2,1,0:T(8,128)}), f32[32,8,1280]{2,1,0:T(8,128)S(1)}, u32[]{:S(2)}, u32[]{:S(2)}) async-start(f32[32,8,1280]{2,1,0:T(8,128)} %convolution_bitcast_fusion.1), calls=%async_computation.1 | async-start | bytes 2621440 | tf_op jit(solution)/shard_map/all_to_all | solution.py:73
  101.9 4.9 %collective-permute-start.11 = (bf16[320,1024]{1,0:T(8,128)(2,1)}, bf16[320,1024]{1,0:T(8,128)(2,1)}, u32[]{:S(2)}, u32[]{:S(2)}) collective-permute-start(bf16[320,1024]{1,0:T(8,128)(2,1)} %collective-permute-done.9), channel_id=1, source_target_pairs={{1,0},{2,1},{3,2},{4,3},{5,4},{6,5},{7,6},{8,7},{9,8},{10,9},{11,1... | collective-permute-start | bytes 1966088 | tf_op jit(solution)/shard_map/ppermute | solution.py:58
  108.7 12.3 %collective-permute-done.11 = bf16[320,1024]{1,0:T(8,128)(2,1)} collective-permute-done((bf16[320,1024]{1,0:T(8,128)(2,1)}, bf16[320,1024]{1,0:T(8,128)(2,1)}, u32[]{:S(2)}, u32[]{:S(2)}) %collective-permute-start.11) | collective-permute-done | bytes 655392 | tf_op jit(solution)/shard_map/ppermute | solution.py:58
  121.0 5.3 %collective-permute-start.13 = (bf16[320,1024]{1,0:T(8,128)(2,1)}, bf16[320,1024]{1,0:T(8,128)(2,1)}, u32[]{:S(2)}, u32[]{:S(2)}) collective-permute-start(bf16[320,1024]{1,0:T(8,128)(2,1)} %collective-permute-done.11), channel_id=1, source_target_pairs={{1,0},{2,1},{3,2},{4,3},{5,4},{6,5},{7,6},{8,7},{9,8},{10,9},{11,1... | collective-permute-start | bytes 1966088 | tf_op jit(solution)/shard_map/ppermute | solution.py:58
  131.9 8.4 %all-to-all-start.2 = ((f32[32,8,1280]{2,1,0:T(8,128)}), f32[32,8,1280]{2,1,0:T(8,128)}, u32[]{:S(2)}, u32[]{:S(2)}) async-start(f32[32,8,1280]{2,1,0:T(8,128)} %convolution_bitcast_fusion), calls=%async_computation.2 | async-start | bytes 2621440 | tf_op jit(solution)/shard_map/all_to_all | solution.py:73
  141.3 4.9 %collective-permute-start.15 = (bf16[160,1024]{1,0:T(8,128)(2,1)S(1)}, bf16[160,1024]{1,0:T(8,128)(2,1)S(1)}, u32[]{:S(2)}, u32[]{:S(2)}) collective-permute-start(bf16[160,1024]{1,0:T(8,128)(2,1)S(1)} %slice.81), channel_id=1, source_target_pairs={{1,0},{2,1},{3,2},{4,3},{5,4},{6,5},{7,6},{8,7},{9,8},{10,9},{11,1... | collective-permute-start | bytes 983048 | tf_op jit(solution)/shard_map/ppermute | solution.py:64
  151.4 6.1 %collective-permute-done.14 = bf16[160,1024]{1,0:T(8,128)(2,1)S(1)} collective-permute-done((bf16[160,1024]{1,0:T(8,128)(2,1)S(1)}, bf16[160,1024]{1,0:T(8,128)(2,1)S(1)}, u32[]{:S(2)}, u32[]{:S(2)}) %collective-permute-start.14) | collective-permute-done | bytes 327712 | tf_op jit(solution)/shard_map/ppermute | solution.py:63
  163.0 10.0 %all-to-all-start.3 = ((f32[32,8,960]{2,1,0:T(8,128)}), f32[32,8,960]{2,1,0:T(8,128)}, u32[]{:S(2)}, u32[]{:S(2)}) async-start(f32[32,8,960]{2,1,0:T(8,128)} %bitcast.72), calls=%async_computation.3 | async-start | bytes 2097152 | tf_op jit(solution)/shard_map/all_to_all | solution.py:73
  180.6 9.6 %all-to-all-done.3 = f32[32,8,960]{2,1,0:T(8,128)} async-done(((f32[32,8,960]{2,1,0:T(8,128)}), f32[32,8,960]{2,1,0:T(8,128)}, u32[]{:S(2)}, u32[]{:S(2)}) %all-to-all-start.3) | async-done | bytes 983072 | tf_op jit(solution)/shard_map/all_to_all | solution.py:73
  190.2 4.3 %fusion.40 = f32[32,32]{1,0:T(8,128)} fusion(f32[32,32]{1,0:T(8,128)S(1)} %fusion.44, f32[32,8,960]{2,1,0:T(8,128)} %all-to-all-done.3), kind=kOutput, calls=%fused_computation.39 | convolution fusion | flops 94372864 | bytes 991232 | tf_op jit(solution)/shard_map/dot_general | solution.py:74
  195.3 24.5 %all_gather.3 = f32[32,8,128]{2,1,0:T(8,128)} all-gather(f32[1,8,128]{2,1,0:T(8,128)S(1)} %all_gather_reshape.3), channel_id=1, replica_groups=mesh['dp'=32,'tensor'=16] {'dp'}, dimensions={0}, use_global_device_ids=true | all-gather | bytes 135168 | tf_op jit(solution)/shard_map/all_gather | solution.py:13
  221.4 7.5 %all-to-all-start.4 = ((f32[16,8,128]{2,1,0:T(8,128)}), f32[16,8,128]{2,1,0:T(8,128)}, u32[]{:S(2)}, u32[]{:S(2)}) async-start(f32[16,8,128]{2,1,0:T(8,128)} %broadcast_in_dim.122), calls=%async_computation.4 | async-start | bytes 131072 | tf_op jit(solution)/shard_map/all_to_all | solution.py:15
  230.5 10.0 %all-to-all-done.4 = f32[16,8,128]{2,1,0:T(8,128)} async-done(((f32[16,8,128]{2,1,0:T(8,128)}), f32[16,8,128]{2,1,0:T(8,128)}, u32[]{:S(2)}, u32[]{:S(2)}) %all-to-all-start.4) | async-done | bytes 65568 | tf_op jit(solution)/shard_map/all_to_all | solution.py:15
  256.1 15.5 %all_to_all.30 = f32[32,8,160]{2,1,0:T(8,128)S(1)} all-to-all(f32[32,8,160]{2,1,0:T(8,128)S(1)} %bitcast.73), channel_id=1, replica_groups=mesh['dp'=32,'tensor'=16] {'dp'}, dimensions={0} | all-to-all | bytes 327680 | tf_op jit(solution)/shard_map/all_to_all | solution.py:87
  (77 shorter events, 62.5 us)
Async XLA Ops:
  0.0 51.4 %copy-start = (bf16[1024,256]{1,0:T(8,128)(2,1)S(1)}, bf16[1024,256]{1,0:T(8,128)(2,1)}, u32[]{:S(2)}) copy-start(bf16[1024,256]{1,0:T(8,128)(2,1)} %param.3) | copy-start | bytes 1572868
  0.0 26.7 %collective-permute-start = (bf16[320,1024]{1,0:T(8,128)(2,1)}, bf16[320,1024]{1,0:T(8,128)(2,1)S(1)}, u32[]{:S(2)}, u32[]{:S(2)}) collective-permute-start(bf16[320,1024]{1,0:T(8,128)(2,1)} %bitcast.75), channel_id=1, source_target_pairs={{0,1},{1,2},{2,3},{3,4},{4,5},{5,6},{6,7},{7,8},{8,9},{9,10},{10,1... | collective-permute-start | bytes 1966088 | tf_op jit(solution)/shard_map/ppermute | solution.py:57
  4.5 24.1 %collective-permute-start.1 = (bf16[320,1024]{1,0:T(8,128)(2,1)}, bf16[320,1024]{1,0:T(8,128)(2,1)S(1)}, u32[]{:S(2)}, u32[]{:S(2)}) collective-permute-start(bf16[320,1024]{1,0:T(8,128)(2,1)} %bitcast.76), channel_id=1, source_target_pairs={{1,0},{2,1},{3,2},{4,3},{5,4},{6,5},{7,6},{8,7},{9,8},{10,9},{11,1... | collective-permute-start | bytes 1966088 | tf_op jit(solution)/shard_map/ppermute | solution.py:58
  26.7 18.1 %collective-permute-start.2 = (bf16[320,1024]{1,0:T(8,128)(2,1)S(1)}, bf16[320,1024]{1,0:T(8,128)(2,1)S(1)}, u32[]{:S(2)}, u32[]{:S(2)}) collective-permute-start(bf16[320,1024]{1,0:T(8,128)(2,1)S(1)} %collective-permute-done), channel_id=1, source_target_pairs={{0,1},{1,2},{2,3},{3,4},{4,5},{5,6},{6,7},{7,8},{8,9},{9,10},{10,1... | collective-permute-start | bytes 1966088 | tf_op jit(solution)/shard_map/ppermute | solution.py:57
  28.7 18.1 %collective-permute-start.3 = (bf16[320,1024]{1,0:T(8,128)(2,1)S(1)}, bf16[320,1024]{1,0:T(8,128)(2,1)S(1)}, u32[]{:S(2)}, u32[]{:S(2)}) collective-permute-start(bf16[320,1024]{1,0:T(8,128)(2,1)S(1)} %collective-permute-done.1), channel_id=1, source_target_pairs={{1,0},{2,1},{3,2},{4,3},{5,4},{6,5},{7,6},{8,7},{9,8},{10,9},{11,1... | collective-permute-start | bytes 1966088 | tf_op jit(solution)/shard_map/ppermute | solution.py:58
  44.8 23.6 %collective-permute-start.4 = (bf16[320,1024]{1,0:T(8,128)(2,1)S(1)}, bf16[320,1024]{1,0:T(8,128)(2,1)}, u32[]{:S(2)}, u32[]{:S(2)}) collective-permute-start(bf16[320,1024]{1,0:T(8,128)(2,1)S(1)} %collective-permute-done.2), channel_id=1, source_target_pairs={{0,1},{1,2},{2,3},{3,4},{4,5},{5,6},{6,7},{7,8},{8,9},{9,10},{10,1... | collective-permute-start | bytes 1966088 | tf_op jit(solution)/shard_map/ppermute | solution.py:57
  46.8 17.1 %collective-permute-start.5 = (bf16[320,1024]{1,0:T(8,128)(2,1)S(1)}, bf16[320,1024]{1,0:T(8,128)(2,1)}, u32[]{:S(2)}, u32[]{:S(2)}) collective-permute-start(bf16[320,1024]{1,0:T(8,128)(2,1)S(1)} %collective-permute-done.3), channel_id=1, source_target_pairs={{1,0},{2,1},{3,2},{4,3},{5,4},{6,5},{7,6},{8,7},{9,8},{10,9},{11,1... | collective-permute-start | bytes 1966088 | tf_op jit(solution)/shard_map/ppermute | solution.py:58
  54.1 36.1 %all-to-all-start = ((f32[32,8,1600]{2,1,0:T(8,128)}), f32[32,8,1600]{2,1,0:T(8,128)S(1)}, u32[]{:S(2)}, u32[]{:S(2)}) async-start(f32[32,8,1600]{2,1,0:T(8,128)} %bitcast.71), calls=%async_computation | async-start | bytes 3407872 | tf_op jit(solution)/shard_map/all_to_all | solution.py:73
  64.0 16.1 %collective-permute-start.7 = (bf16[320,1024]{1,0:T(8,128)(2,1)}, bf16[320,1024]{1,0:T(8,128)(2,1)}, u32[]{:S(2)}, u32[]{:S(2)}) collective-permute-start(bf16[320,1024]{1,0:T(8,128)(2,1)} %collective-permute-done.5), channel_id=1, source_target_pairs={{1,0},{2,1},{3,2},{4,3},{5,4},{6,5},{7,6},{8,7},{9,8},{10,9},{11,1... | collective-permute-start | bytes 1966088 | tf_op jit(solution)/shard_map/ppermute | solution.py:58
  68.4 16.3 %collective-permute-start.6 = (bf16[320,1024]{1,0:T(8,128)(2,1)}, bf16[320,1024]{1,0:T(8,128)(2,1)}, u32[]{:S(2)}, u32[]{:S(2)}) collective-permute-start(bf16[320,1024]{1,0:T(8,128)(2,1)} %collective-permute-done.4), channel_id=1, source_target_pairs={{0,1},{1,2},{2,3},{3,4},{4,5},{5,6},{6,7},{7,8},{8,9},{9,10},{10,1... | collective-permute-start | bytes 1966088 | tf_op jit(solution)/shard_map/ppermute | solution.py:57
  80.0 21.9 %collective-permute-start.9 = (bf16[320,1024]{1,0:T(8,128)(2,1)}, bf16[320,1024]{1,0:T(8,128)(2,1)}, u32[]{:S(2)}, u32[]{:S(2)}) collective-permute-start(bf16[320,1024]{1,0:T(8,128)(2,1)} %collective-permute-done.7), channel_id=1, source_target_pairs={{1,0},{2,1},{3,2},{4,3},{5,4},{6,5},{7,6},{8,7},{9,8},{10,9},{11,1... | collective-permute-start | bytes 1966088 | tf_op jit(solution)/shard_map/ppermute | solution.py:58
  84.7 22.1 %collective-permute-start.8 = (bf16[320,1024]{1,0:T(8,128)(2,1)}, bf16[320,1024]{1,0:T(8,128)(2,1)}, u32[]{:S(2)}, u32[]{:S(2)}) collective-permute-start(bf16[320,1024]{1,0:T(8,128)(2,1)} %collective-permute-done.6), channel_id=1, source_target_pairs={{0,1},{1,2},{2,3},{3,4},{4,5},{5,6},{6,7},{7,8},{8,9},{9,10},{10,1... | collective-permute-start | bytes 1966088 | tf_op jit(solution)/shard_map/ppermute | solution.py:57
  90.2 41.6 %all-to-all-start.1 = ((f32[32,8,1280]{2,1,0:T(8,128)}), f32[32,8,1280]{2,1,0:T(8,128)S(1)}, u32[]{:S(2)}, u32[]{:S(2)}) async-start(f32[32,8,1280]{2,1,0:T(8,128)} %convolution_bitcast_fusion.1), calls=%async_computation.1 | async-start | bytes 2621440 | tf_op jit(solution)/shard_map/all_to_all | solution.py:73
  101.9 19.1 %collective-permute-start.11 = (bf16[320,1024]{1,0:T(8,128)(2,1)}, bf16[320,1024]{1,0:T(8,128)(2,1)}, u32[]{:S(2)}, u32[]{:S(2)}) collective-permute-start(bf16[320,1024]{1,0:T(8,128)(2,1)} %collective-permute-done.9), channel_id=1, source_target_pairs={{1,0},{2,1},{3,2},{4,3},{5,4},{6,5},{7,6},{8,7},{9,8},{10,9},{11,1... | collective-permute-start | bytes 1966088 | tf_op jit(solution)/shard_map/ppermute | solution.py:58
  106.8 19.5 %collective-permute-start.10 = (bf16[320,1024]{1,0:T(8,128)(2,1)}, bf16[320,1024]{1,0:T(8,128)(2,1)}, u32[]{:S(2)}, u32[]{:S(2)}) collective-permute-start(bf16[320,1024]{1,0:T(8,128)(2,1)} %collective-permute-done.8), channel_id=1, source_target_pairs={{0,1},{1,2},{2,3},{3,4},{4,5},{5,6},{6,7},{7,8},{8,9},{9,10},{10,1... | collective-permute-start | bytes 1966088 | tf_op jit(solution)/shard_map/ppermute | solution.py:57
  121.0 19.3 %collective-permute-start.13 = (bf16[320,1024]{1,0:T(8,128)(2,1)}, bf16[320,1024]{1,0:T(8,128)(2,1)}, u32[]{:S(2)}, u32[]{:S(2)}) collective-permute-start(bf16[320,1024]{1,0:T(8,128)(2,1)} %collective-permute-done.11), channel_id=1, source_target_pairs={{1,0},{2,1},{3,2},{4,3},{5,4},{6,5},{7,6},{8,7},{9,8},{10,9},{11,1... | collective-permute-start | bytes 1966088 | tf_op jit(solution)/shard_map/ppermute | solution.py:58
  126.3 19.9 %collective-permute-start.12 = (bf16[320,1024]{1,0:T(8,128)(2,1)}, bf16[320,1024]{1,0:T(8,128)(2,1)}, u32[]{:S(2)}, u32[]{:S(2)}) collective-permute-start(bf16[320,1024]{1,0:T(8,128)(2,1)} %collective-permute-done.10), channel_id=1, source_target_pairs={{0,1},{1,2},{2,3},{3,4},{4,5},{5,6},{6,7},{7,8},{8,9},{9,10},{10,1... | collective-permute-start | bytes 1966088 | tf_op jit(solution)/shard_map/ppermute | solution.py:57
  131.9 31.1 %all-to-all-start.2 = ((f32[32,8,1280]{2,1,0:T(8,128)}), f32[32,8,1280]{2,1,0:T(8,128)}, u32[]{:S(2)}, u32[]{:S(2)}) async-start(f32[32,8,1280]{2,1,0:T(8,128)} %convolution_bitcast_fusion), calls=%async_computation.2 | async-start | bytes 2621440 | tf_op jit(solution)/shard_map/all_to_all | solution.py:73
  141.3 10.2 %collective-permute-start.15 = (bf16[160,1024]{1,0:T(8,128)(2,1)S(1)}, bf16[160,1024]{1,0:T(8,128)(2,1)S(1)}, u32[]{:S(2)}, u32[]{:S(2)}) collective-permute-start(bf16[160,1024]{1,0:T(8,128)(2,1)S(1)} %slice.81), channel_id=1, source_target_pairs={{1,0},{2,1},{3,2},{4,3},{5,4},{6,5},{7,6},{8,7},{9,8},{10,9},{11,1... | collective-permute-start | bytes 983048 | tf_op jit(solution)/shard_map/ppermute | solution.py:64
  147.2 10.3 %collective-permute-start.14 = (bf16[160,1024]{1,0:T(8,128)(2,1)S(1)}, bf16[160,1024]{1,0:T(8,128)(2,1)S(1)}, u32[]{:S(2)}, u32[]{:S(2)}) collective-permute-start(bf16[160,1024]{1,0:T(8,128)(2,1)S(1)} %slice.80), channel_id=1, source_target_pairs={{0,1},{1,2},{2,3},{3,4},{4,5},{5,6},{6,7},{7,8},{8,9},{9,10},{10,1... | collective-permute-start | bytes 983048 | tf_op jit(solution)/shard_map/ppermute | solution.py:63
  163.0 27.2 %all-to-all-start.3 = ((f32[32,8,960]{2,1,0:T(8,128)}), f32[32,8,960]{2,1,0:T(8,128)}, u32[]{:S(2)}, u32[]{:S(2)}) async-start(f32[32,8,960]{2,1,0:T(8,128)} %bitcast.72), calls=%async_computation.3 | async-start | bytes 2097152 | tf_op jit(solution)/shard_map/all_to_all | solution.py:73
  221.4 19.1 %all-to-all-start.4 = ((f32[16,8,128]{2,1,0:T(8,128)}), f32[16,8,128]{2,1,0:T(8,128)}, u32[]{:S(2)}, u32[]{:S(2)}) async-start(f32[16,8,128]{2,1,0:T(8,128)} %broadcast_in_dim.122), calls=%async_computation.4 | async-start | bytes 131072 | tf_op jit(solution)/shard_map/all_to_all | solution.py:15
  251.8 3.0 %copy-start.1 = (f32[8,1600]{1,0:T(8,128)S(1)}, f32[8,1600]{1,0:T(8,128)}, u32[]{:S(2)}) copy-start(f32[8,1600]{1,0:T(8,128)} %multiply_reduce_fusion) | copy-start | bytes 153604

commit v4 on v3

v4 whole, which is shorter than its diff:
```python
import functools

import jax
import jax.numpy as jnp
from jax import lax
from jax.experimental import pallas as pl
from jax.experimental.pallas import tpu as pltpu
from jax.sharding import PartitionSpec as P

epsilon = 1e-06
GROUPS = (6, 6, 4)
VMEM = pltpu.VMEM
LIMIT = 48 * 1024 * 1024
EXACT = lax.Precision.HIGHEST


def gram_kernel(replicas, block_ref, before_ref, out_ref):
    rows, cols = block_ref.shape
    part = rows // replicas
    whole = lax.dot_general(
        block_ref[...], block_ref[...], (((1,), (1,)), ((), ())),
        precision=EXACT, preferred_element_type=jnp.float32,
    )
    i = lax.broadcasted_iota(jnp.int32, (rows, rows), 0)
    j = lax.broadcasted_iota(jnp.int32, (rows, rows), 1)
    whole = jnp.where(i % part == j % part, whole, 0.0)
    thin = jnp.sum(whole.reshape(replicas, part, rows), axis=1)
    c = lax.broadcasted_iota(jnp.int32, (rows, 128), 0)
    lane = lax.broadcasted_iota(jnp.int32, (rows, 128), 1)
    total = before_ref[...]
    for k in range(replicas // 8):
        pick = jnp.where(lane == c // part + k * replicas, 1.0, 0.0)
        total = total + jnp.dot(
            thin[k * 8:(k + 1) * 8], pick,
            precision=EXACT, preferred_element_type=jnp.float32,
        )
    out_ref[...] = total


def gram_add(replicas, block, before):
    rows = block.shape[0] * block.shape[1]
    block = block.reshape(rows, -1)
    cols = block.shape[1]
    return pl.pallas_call(
        functools.partial(gram_kernel, replicas),
        out_shape=jax.ShapeDtypeStruct((8, 128), jnp.float32),
        in_specs=[pl.BlockSpec(memory_space=VMEM)] * 2,
        out_specs=pl.BlockSpec(memory_space=VMEM),
        cost_estimate=pl.CostEstimate(
            flops=12 * rows * rows * cols, bytes_accessed=4 * rows * cols, transcendentals=0
        ),
        compiler_params=pltpu.CompilerParams(vmem_limit_bytes=LIMIT),
    )(block, before)


def spread_kernel(parts_ref, out_ref):
    total = jnp.sum(parts_ref[...], axis=0)
    out_ref[...] = jnp.broadcast_to(total[None], out_ref.shape)


def sum_and_spread(parts, copies):
    return pl.pallas_call(
        spread_kernel,
        out_shape=jax.ShapeDtypeStruct((copies, *parts.shape[1:]), jnp.float32),
        in_specs=[pl.BlockSpec(memory_space=VMEM)],
        out_specs=pl.BlockSpec(memory_space=VMEM),
    )(parts)


def combine_kernel(replicas, slabs, order, here_ref, parts_ref, *refs):
    blocks, out_ref = refs[:-1], refs[-1]
    packed = jnp.sum(parts_ref[...], axis=0)
    gram = jnp.concatenate(
        [packed[:, k * replicas:(k + 1) * replicas] for k in range(replicas // 8)], axis=0
    )
    i = lax.broadcasted_iota(jnp.int32, (replicas, replicas), 0)
    j = lax.broadcasted_iota(jnp.int32, (replicas, replicas), 1)
    down = jnp.ones((replicas, 1), jnp.float32)
    across = jnp.ones((1, replicas), jnp.float32)
    width = 1
    while width < replicas:
        scaled = gram * down * across
        same = i // width == j // width
        partner = i // width == (j // width ^ 1)
        mine = jnp.where(same, scaled, 0.0)
        other = jnp.where(partner, scaled, 0.0)
        own_down = jnp.sum(mine, axis=1, keepdims=True)
        own_across = jnp.sum(mine, axis=0, keepdims=True)
        cross_down = jnp.sum(other, axis=1, keepdims=True)
        cross_across = jnp.sum(other, axis=0, keepdims=True)

        def factor(cross, own, axis):
            cross = jnp.sum(jnp.where(same, cross, 0.0), axis=axis, keepdims=True)
            own = jnp.sum(jnp.where(same, own, 0.0), axis=axis, keepdims=True)
            return 1.0 - cross / (2.0 * (jnp.maximum(own, 0.0) + epsilon))

        new_down = down * factor(cross_across, own_across, 1)
        across = across * factor(cross_down, own_down, 0)
        down = new_down
        width *= 2
    sums = []
    for block_ref in blocks:
        total = block_ref[0] * down[0:1]
        for r in range(1, replicas):
            total = total + block_ref[r] * down[r:r + 1]
        sums.append(total)
    each = replicas // slabs
    width = out_ref.shape[2]
    place = 0
    for total in sums:
        for k in range(total.shape[1] // (width * each)):
            slab = lax.rem(here_ref[0] + order[place], slabs)
            for h in range(each):
                start = (k * each + h) * width
                out_ref[slab * each + h] = total[:, start:start + width]
            place += 1


def weighted_sums(replicas, slabs, order, here, parts, blocks):
    part = blocks[0].shape[1]
    total = sum(b.shape[2] for b in blocks)
    size = replicas * part * total
    return pl.pallas_call(
        functools.partial(combine_kernel, replicas, slabs, order),
        out_shape=jax.ShapeDtypeStruct((replicas, part, total // replicas), jnp.float32),
        in_specs=[pl.BlockSpec(memory_space=pltpu.SMEM)]
        + [pl.BlockSpec(memory_space=VMEM)] * (1 + len(blocks)),
        out_specs=pl.BlockSpec(memory_space=VMEM),
        cost_estimate=pl.CostEstimate(flops=2 * size, bytes_accessed=4 * size, transcendentals=0),
        compiler_params=pltpu.CompilerParams(vmem_limit_bytes=LIMIT),
    )(here.reshape(1), parts, *blocks)


def on_device(activations, out_grads):
    replicas = lax.axis_size("dp")
    slabs = lax.axis_size("tensor")
    here = lax.axis_index("tensor").astype(jnp.int32)
    even = lax.axis_index("dp") % 2 == 0
    columns = out_grads.shape[1]
    part = columns // replicas
    half = slabs // 2
    up = [(i, (i + 1) % slabs) for i in range(slabs)]
    down = [((i + 1) % slabs, i) for i in range(slabs)]
    split = [
        (r * slabs + i, r * slabs + (i + (-1 if r % 2 else 1)) % slabs)
        for r in range(replicas) for i in range(slabs)
    ]

    slab = activations.T
    from_below = from_above = slab
    held, order = [slab], [0]
    blocks = []
    gram = jnp.zeros((8, 128), jnp.float32)
    sizes = list(GROUPS)
    for step in range(1, half + 1):
        if step < half:
            from_below = lax.ppermute(from_below, "tensor", up)
            from_above = lax.ppermute(from_above, "tensor", down)
            held += [from_below, from_above]
            order += [slabs - step, step]
        else:
            onward = jnp.where(even, from_below, from_above)
            held += [lax.ppermute(onward, ("dp", "tensor"), split)]
            order += [half]
        if len(held) >= sizes[0]:
            group, held = held[:sizes[0]], held[sizes.pop(0):]
            grad = lax.dot_general(
                out_grads, jnp.concatenate(group, axis=0), (((0,), (1,)), ((), ())),
                preferred_element_type=jnp.float32,
            )
            block = lax.all_to_all(grad.reshape(replicas, part, -1), "dp", 0, 0)
            gram = gram_add(replicas, block, gram)
            blocks.append(block)
    peers = jnp.broadcast_to(gram, (replicas, *gram.shape))
    parts = sum_and_spread(lax.all_to_all(peers, "dp", 0, 0), slabs)
    parts = lax.all_to_all(parts, "tensor", 0, 0)
    home = weighted_sums(replicas, slabs, tuple(order), here, parts, blocks)
    home = lax.all_to_all(home, "dp", 0, 0)
    return home.reshape(columns, -1).T


def solution(mesh):
    return jax.shard_map(
        on_device,
        mesh=mesh,
        in_specs=(P("dp", "tensor"), P("dp", "tensor")),
        out_specs=P("dp", "tensor"),
        check_vma=False,
    )
```

time: 274 us -> 248 us (0.905)
  waiting for transfers between devices: 73.1 us -> 95.6 us
  other arithmetic: 17.2 us -> 1.17 us
  starting transfers between devices: 108 us -> 92.6 us
  Pallas kernels: 0 us -> 14.2 us
  matrix products: 22.1 us -> 8.66 us
  blocking collectives: 40 us -> 27.1 us
  local copies, waits for them, and re-layouts: 11.7 us -> 6.78 us
    ppermute x7, waiting for transfers between devices: 23.1 us -> 54.9 us  [on_device(): from_below = lax.ppermute(from_below, 'tensor', up)]
    all_gather x1 -> x0, blocking collectives: 24.5 us -> none  [gram_total(): flat = jnp.sum(lax.all_gather(flat, 'dp'), axis=0)]
    ppermute x7, waiting for transfers between devices: 22 us -> 0.02 us  [on_device(): from_above = lax.ppermute(from_above, 'tensor', down)]
    reduce_sum x15 -> x0, other arithmetic: 14.4 us -> none  [the longest x5 4.44 us: tree_weights(): own = jnp.sum(jnp.where(same, scaled, 0.0), axis=1)]
    pallas_call x0 -> x5, Pallas kernels: none -> 14.2 us  [the longest x3 9.8 us: gram_add(): pl.pallas_call(functools.partial(gram_kernel, replicas), out_shape=jax.Sh...]
    dot_general x8 -> x3, matrix products: 22.1 us -> 8.66 us  [on_device(): lax.dot_general(out_grads, jnp.concatenate(group, axis=0), (((0,), (1,)),...]
    all_to_all x4 -> x3, starting transfers between devices: 39.8 us -> 26.8 us  [on_device(): block = lax.all_to_all(grad.reshape(replicas, part, -1), 'dp', 0, 0)]
    all_to_all x0 -> x1, blocking collectives: none -> 13 us  [on_device(): parts = sum_and_spread(lax.all_to_all(peers, 'dp', 0, 0), slabs)]
  transfers between devices with their start and end apart: 21 -> 19, of which waited for: 8 -> 9; matrix products, arithmetic and copies ran while one was open for 10% -> 6% of each run, Pallas kernels for 0% -> 3%
where the time goes in v4:
time: 248 us; the launch traced here: 247 us
  waiting for transfers between devices  95.6 us (39%)
  starting transfers between devices  92.6 us (37%)
  blocking collectives  27.1 us (11%)
  Pallas kernels  14.2 us (6%)
  matrix products  8.66 us (3%)
  local copies, waits for them, and re-layouts  6.78 us (3%)
    ppermute x7, waiting for transfers between devices, on_device(): from_below = lax.ppermute(from_below, 'tensor', up)  54.9 us
    ppermute x7, starting transfers between devices, on_device(): from_above = lax.ppermute(from_above, 'tensor', down)  36.9 us
    all_to_all x3, starting transfers between devices, on_device(): block = lax.all_to_all(grad.reshape(replicas, part, -1), 'dp', 0, 0)  26.8 us
    all_to_all x3, waiting for transfers between devices, on_device(): block = lax.all_to_all(grad.reshape(replicas, part, -1), 'dp', 0, 0)  21.6 us
    ppermute x7, starting transfers between devices, on_device(): from_below = lax.ppermute(from_below, 'tensor', up)  16 us
    all_to_all x1, blocking collectives, on_device(): home = lax.all_to_all(home, 'dp', 0, 0)  14.1 us
    all_to_all x1, blocking collectives, on_device(): parts = sum_and_spread(lax.all_to_all(peers, 'dp', 0, 0), slabs)  13 us
    all_to_all x1, waiting for transfers between devices, on_device(): parts = lax.all_to_all(parts, 'tensor', 0, 0)  11.6 us
  transfers between devices with their start and end apart: 19, of which 9 were waited for; matrix products, arithmetic and copies ran while one was open for 6% of the time, Pallas kernels for 3%

profile of v4, /device:TPU:1, one launch (start us, length us, event | category | flops | bytes accessed | tf_op | source)
XLA Modules:
  0.0 246.5 jit_solution(7324759128799990912)
XLA Ops:
  0.0 4.5 %collective-permute-start.6 = (bf16[320,1024]{1,0:T(8,128)(2,1)}, bf16[320,1024]{1,0:T(8,128)(2,1)S(1)}, u32[]{:S(2)}, u32[]{:S(2)}) collective-permute-start(bf16[320,1024]{1,0:T(8,128)(2,1)} %bitcast.27), channel_id=1, source_target_pairs={{0,1},{1,2},{2,3},{3,4},{4,5},{5,6},{6,7},{7,8},{8,9},{9,10},{10,1... | collective-permute-start | bytes 1966088 | tf_op jit(solution)/shard_map/ppermute | solution.py:157
  4.5 9.5 %collective-permute-start = (bf16[320,1024]{1,0:T(8,128)(2,1)}, bf16[320,1024]{1,0:T(8,128)(2,1)S(1)}, u32[]{:S(2)}, u32[]{:S(2)}) collective-permute-start(bf16[320,1024]{1,0:T(8,128)(2,1)} %bitcast.28), channel_id=1, source_target_pairs={{1,0},{2,1},{3,2},{4,3},{5,4},{6,5},{7,6},{8,7},{9,8},{10,9},{11,1... | collective-permute-start | bytes 1966088 | tf_op jit(solution)/shard_map/ppermute | solution.py:158
  14.0 12.7 %collective-permute-done.6 = bf16[320,1024]{1,0:T(8,128)(2,1)S(1)} collective-permute-done((bf16[320,1024]{1,0:T(8,128)(2,1)}, bf16[320,1024]{1,0:T(8,128)(2,1)S(1)}, u32[]{:S(2)}, u32[]{:S(2)}) %collective-permute-start.6) | collective-permute-done | bytes 655392 | tf_op jit(solution)/shard_map/ppermute | solution.py:157
  28.7 4.6 %collective-permute-start.1 = (bf16[320,1024]{1,0:T(8,128)(2,1)S(1)}, bf16[320,1024]{1,0:T(8,128)(2,1)S(1)}, u32[]{:S(2)}, u32[]{:S(2)}) collective-permute-start(bf16[320,1024]{1,0:T(8,128)(2,1)S(1)} %collective-permute-done), channel_id=1, source_target_pairs={{1,0},{2,1},{3,2},{4,3},{5,4},{6,5},{7,6},{8,7},{9,8},{10,9},{11,1... | collective-permute-start | bytes 1966088 | tf_op jit(solution)/shard_map/ppermute | solution.py:158
  33.2 11.6 %collective-permute-done.7 = bf16[320,1024]{1,0:T(8,128)(2,1)S(1)} collective-permute-done((bf16[320,1024]{1,0:T(8,128)(2,1)S(1)}, bf16[320,1024]{1,0:T(8,128)(2,1)S(1)}, u32[]{:S(2)}, u32[]{:S(2)}) %collective-permute-start.7) | collective-permute-done | bytes 655392 | tf_op jit(solution)/shard_map/ppermute | solution.py:157
  46.8 4.6 %collective-permute-start.2 = (bf16[320,1024]{1,0:T(8,128)(2,1)S(1)}, bf16[320,1024]{1,0:T(8,128)(2,1)S(1)}, u32[]{:S(2)}, u32[]{:S(2)}) collective-permute-start(bf16[320,1024]{1,0:T(8,128)(2,1)S(1)} %collective-permute-done.1), channel_id=1, source_target_pairs={{1,0},{2,1},{3,2},{4,3},{5,4},{6,5},{7,6},{8,7},{9,8},{10,9},{11,1... | collective-permute-start | bytes 1966088 | tf_op jit(solution)/shard_map/ppermute | solution.py:158
  52.6 9.5 %collective-permute-done.8 = bf16[320,1024]{1,0:T(8,128)(2,1)} collective-permute-done((bf16[320,1024]{1,0:T(8,128)(2,1)S(1)}, bf16[320,1024]{1,0:T(8,128)(2,1)}, u32[]{:S(2)}, u32[]{:S(2)}) %collective-permute-start.8) | collective-permute-done | bytes 655392 | tf_op jit(solution)/shard_map/ppermute | solution.py:157
  64.0 4.6 %collective-permute-start.3 = (bf16[320,1024]{1,0:T(8,128)(2,1)S(1)}, bf16[320,1024]{1,0:T(8,128)(2,1)}, u32[]{:S(2)}, u32[]{:S(2)}) collective-permute-start(bf16[320,1024]{1,0:T(8,128)(2,1)S(1)} %collective-permute-done.2), channel_id=1, source_target_pairs={{1,0},{2,1},{3,2},{4,3},{5,4},{6,5},{7,6},{8,7},{9,8},{10,9},{11,1... | collective-permute-start | bytes 1966088 | tf_op jit(solution)/shard_map/ppermute | solution.py:158
  72.4 10.7 %all-to-all-start.2 = ((f32[32,8,1920]{2,1,0:T(8,128)}), f32[32,8,1920]{2,1,0:T(8,128)S(1)}, u32[]{:S(2)}, u32[]{:S(2)}) async-start(f32[32,8,1920]{2,1,0:T(8,128)} %convolution_bitcast_fusion), calls=%async_computation.2 | async-start | bytes 3932160 | tf_op jit(solution)/shard_map/all_to_all | solution.py:171
  85.1 4.6 %collective-permute-start.4 = (bf16[320,1024]{1,0:T(8,128)(2,1)}, bf16[320,1024]{1,0:T(8,128)(2,1)S(1)}, u32[]{:S(2)}, u32[]{:S(2)}) collective-permute-start(bf16[320,1024]{1,0:T(8,128)(2,1)} %collective-permute-done.3), channel_id=1, source_target_pairs={{1,0},{2,1},{3,2},{4,3},{5,4},{6,5},{7,6},{8,7},{9,8},{10,9},{11,1... | collective-permute-start | bytes 1966088 | tf_op jit(solution)/shard_map/ppermute | solution.py:158
  89.7 12.9 %collective-permute-done.10 = bf16[320,1024]{1,0:T(8,128)(2,1)S(1)} collective-permute-done((bf16[320,1024]{1,0:T(8,128)(2,1)}, bf16[320,1024]{1,0:T(8,128)(2,1)S(1)}, u32[]{:S(2)}, u32[]{:S(2)}) %collective-permute-start.10) | collective-permute-done | bytes 655392 | tf_op jit(solution)/shard_map/ppermute | solution.py:157
  104.5 4.6 %collective-permute-start.5 = (bf16[320,1024]{1,0:T(8,128)(2,1)S(1)}, bf16[320,1024]{1,0:T(8,128)(2,1)}, u32[]{:S(2)}, u32[]{:S(2)}) collective-permute-start(bf16[320,1024]{1,0:T(8,128)(2,1)S(1)} %collective-permute-done.4), channel_id=1, source_target_pairs={{1,0},{2,1},{3,2},{4,3},{5,4},{6,5},{7,6},{8,7},{9,8},{10,9},{11,1... | collective-permute-start | bytes 1966088 | tf_op jit(solution)/shard_map/ppermute | solution.py:158
  112.6 8.3 %collective-permute-done.11 = bf16[320,1024]{1,0:T(8,128)(2,1)S(1)} collective-permute-done((bf16[320,1024]{1,0:T(8,128)(2,1)S(1)}, bf16[320,1024]{1,0:T(8,128)(2,1)S(1)}, u32[]{:S(2)}, u32[]{:S(2)}) %collective-permute-start.11) | collective-permute-done | bytes 655392 | tf_op jit(solution)/shard_map/ppermute | solution.py:157
  122.8 4.6 %collective-permute-start.13 = (bf16[320,1024]{1,0:T(8,128)(2,1)}, bf16[320,1024]{1,0:T(8,128)(2,1)}, u32[]{:S(2)}, u32[]{:S(2)}) collective-permute-start(bf16[320,1024]{1,0:T(8,128)(2,1)} %collective-permute-done.5), channel_id=1, source_target_pairs={{1,0},{2,1},{3,2},{4,3},{5,4},{6,5},{7,6},{8,7},{9,8},{10,9},{11,1... | collective-permute-start | bytes 1966088 | tf_op jit(solution)/shard_map/ppermute | solution.py:158
  130.0 9.5 %all-to-all-start.1 = ((f32[32,8,1920]{2,1,0:T(8,128)}), f32[32,8,1920]{2,1,0:T(8,128)}, u32[]{:S(2)}, u32[]{:S(2)}) async-start(f32[32,8,1920]{2,1,0:T(8,128)} %convolution_bitcast_fusion.1), calls=%async_computation.1 | async-start | bytes 3932160 | tf_op jit(solution)/shard_map/all_to_all | solution.py:171
  140.7 5.3 %collective-permute-start.14 = (bf16[320,1024]{1,0:T(8,128)(2,1)S(1)}, bf16[320,1024]{1,0:T(8,128)(2,1)S(1)}, u32[]{:S(2)}, u32[]{:S(2)}) collective-permute-start(bf16[320,1024]{1,0:T(8,128)(2,1)S(1)} %broadcast_select_fusion), channel_id=1, source_target_pairs={{0,1},{1,2},{2,3},{3,4},{4,5},{5,6},{6,7},{7,8},{8,9},{9,10},{10,1... | collective-permute-start | bytes 1966088 | tf_op jit(solution)/shard_map/ppermute | solution.py:163
  145.9 7.5 %collective-permute-done.14 = bf16[320,1024]{1,0:T(8,128)(2,1)S(1)} collective-permute-done((bf16[320,1024]{1,0:T(8,128)(2,1)S(1)}, bf16[320,1024]{1,0:T(8,128)(2,1)S(1)}, u32[]{:S(2)}, u32[]{:S(2)}) %collective-permute-start.14) | collective-permute-done | bytes 655392 | tf_op jit(solution)/shard_map/ppermute | solution.py:163
  156.9 8.9 %all-to-all-done.1.refs_1_ = f32[32,8,1920]{2,1,0:T(8,128)} async-done(((f32[32,8,1920]{2,1,0:T(8,128)}), f32[32,8,1920]{2,1,0:T(8,128)}, u32[]{:S(2)}, u32[]{:S(2)}) %all-to-all-start.1) | async-done | bytes 1966112 | tf_op jit(solution)/shard_map/all_to_all | solution.py:171
  165.8 6.6 %all-to-all-start = ((f32[32,8,1280]{2,1,0:T(8,128)}), f32[32,8,1280]{2,1,0:T(8,128)}, u32[]{:S(2)}, u32[]{:S(2)}) async-start(f32[32,8,1280]{2,1,0:T(8,128)} %convolution_bitcast_fusion.2), calls=%async_computation | async-start | bytes 2621440 | tf_op jit(solution)/shard_map/all_to_all | solution.py:171
  179.0 12.7 %all-to-all-done.refs_2_ = f32[32,8,1280]{2,1,0:T(8,128)} async-done(((f32[32,8,1280]{2,1,0:T(8,128)}), f32[32,8,1280]{2,1,0:T(8,128)}, u32[]{:S(2)}, u32[]{:S(2)}) %all-to-all-start) | async-done | bytes 1310752 | tf_op jit(solution)/shard_map/all_to_all | solution.py:171
  194.9 13.0 %all_to_all.30.parts_ref = f32[32,8,128]{2,1,0:T(8,128)} all-to-all(f32[32,8,128]{2,1,0:T(8,128)S(1)} %broadcast_in_dim.7), channel_id=1, replica_groups=mesh['dp'=32,'tensor'=16] {'dp'}, dimensions={0} | all-to-all | bytes 262144 | tf_op jit(solution)/shard_map/all_to_all | solution.py:175
  209.5 7.7 %all-to-all-start.4 = ((f32[16,8,128]{2,1,0:T(8,128)}), f32[16,8,128]{2,1,0:T(8,128)S(1)}, u32[]{:S(2)}, u32[]{:S(2)}) async-start(f32[16,8,128]{2,1,0:T(8,128)} %shard_map.31), calls=%async_computation.4 | async-start | bytes 131072 | tf_op jit(solution)/shard_map/all_to_all | solution.py:176
  217.2 11.6 %all-to-all-done.4.parts_ref = f32[16,8,128]{2,1,0:T(8,128)S(1)} async-done(((f32[16,8,128]{2,1,0:T(8,128)}), f32[16,8,128]{2,1,0:T(8,128)S(1)}, u32[]{:S(2)}, u32[]{:S(2)}) %all-to-all-start.4) | async-done | bytes 65568 | tf_op jit(solution)/shard_map/all_to_all | solution.py:176
  231.7 14.1 %all_to_all.31 = f32[32,8,160]{2,1,0:T(8,128)S(1)} all-to-all(f32[32,8,160]{2,1,0:T(8,128)S(1)} %shard_map.32), channel_id=1, replica_groups=mesh['dp'=32,'tensor'=16] {'dp'}, dimensions={0} | all-to-all | bytes 327680 | tf_op jit(solution)/shard_map/all_to_all | solution.py:178
  (44 shorter events, 42.4 us)
Async XLA Ops:
  0.0 69.8 %copy-start = (bf16[1024,256]{1,0:T(8,128)(2,1)S(1)}, bf16[1024,256]{1,0:T(8,128)(2,1)}, u32[]{:S(2)}) copy-start(bf16[1024,256]{1,0:T(8,128)(2,1)} %param.3) | copy-start | bytes 1572868
  0.0 26.7 %collective-permute-start.6 = (bf16[320,1024]{1,0:T(8,128)(2,1)}, bf16[320,1024]{1,0:T(8,128)(2,1)S(1)}, u32[]{:S(2)}, u32[]{:S(2)}) collective-permute-start(bf16[320,1024]{1,0:T(8,128)(2,1)} %bitcast.27), channel_id=1, source_target_pairs={{0,1},{1,2},{2,3},{3,4},{4,5},{5,6},{6,7},{7,8},{8,9},{9,10},{10,1... | collective-permute-start | bytes 1966088 | tf_op jit(solution)/shard_map/ppermute | solution.py:157
  4.5 24.1 %collective-permute-start = (bf16[320,1024]{1,0:T(8,128)(2,1)}, bf16[320,1024]{1,0:T(8,128)(2,1)S(1)}, u32[]{:S(2)}, u32[]{:S(2)}) collective-permute-start(bf16[320,1024]{1,0:T(8,128)(2,1)} %bitcast.28), channel_id=1, source_target_pairs={{1,0},{2,1},{3,2},{4,3},{5,4},{6,5},{7,6},{8,7},{9,8},{10,9},{11,1... | collective-permute-start | bytes 1966088 | tf_op jit(solution)/shard_map/ppermute | solution.py:158
  26.7 18.1 %collective-permute-start.7 = (bf16[320,1024]{1,0:T(8,128)(2,1)S(1)}, bf16[320,1024]{1,0:T(8,128)(2,1)S(1)}, u32[]{:S(2)}, u32[]{:S(2)}) collective-permute-start(bf16[320,1024]{1,0:T(8,128)(2,1)S(1)} %collective-permute-done.6), channel_id=1, source_target_pairs={{0,1},{1,2},{2,3},{3,4},{4,5},{5,6},{6,7},{7,8},{8,9},{9,10},{10,1... | collective-permute-start | bytes 1966088 | tf_op jit(solution)/shard_map/ppermute | solution.py:157
  28.7 18.1 %collective-permute-start.1 = (bf16[320,1024]{1,0:T(8,128)(2,1)S(1)}, bf16[320,1024]{1,0:T(8,128)(2,1)S(1)}, u32[]{:S(2)}, u32[]{:S(2)}) collective-permute-start(bf16[320,1024]{1,0:T(8,128)(2,1)S(1)} %collective-permute-done), channel_id=1, source_target_pairs={{1,0},{2,1},{3,2},{4,3},{5,4},{6,5},{7,6},{8,7},{9,8},{10,9},{11,1... | collective-permute-start | bytes 1966088 | tf_op jit(solution)/shard_map/ppermute | solution.py:158
  44.8 17.3 %collective-permute-start.8 = (bf16[320,1024]{1,0:T(8,128)(2,1)S(1)}, bf16[320,1024]{1,0:T(8,128)(2,1)}, u32[]{:S(2)}, u32[]{:S(2)}) collective-permute-start(bf16[320,1024]{1,0:T(8,128)(2,1)S(1)} %collective-permute-done.7), channel_id=1, source_target_pairs={{0,1},{1,2},{2,3},{3,4},{4,5},{5,6},{6,7},{7,8},{8,9},{9,10},{10,1... | collective-permute-start | bytes 1966088 | tf_op jit(solution)/shard_map/ppermute | solution.py:157
  46.8 17.3 %collective-permute-start.2 = (bf16[320,1024]{1,0:T(8,128)(2,1)S(1)}, bf16[320,1024]{1,0:T(8,128)(2,1)S(1)}, u32[]{:S(2)}, u32[]{:S(2)}) collective-permute-start(bf16[320,1024]{1,0:T(8,128)(2,1)S(1)} %collective-permute-done.1), channel_id=1, source_target_pairs={{1,0},{2,1},{3,2},{4,3},{5,4},{6,5},{7,6},{8,7},{9,8},{10,9},{11,1... | collective-permute-start | bytes 1966088 | tf_op jit(solution)/shard_map/ppermute | solution.py:158
  62.1 21.0 %collective-permute-start.9 = (bf16[320,1024]{1,0:T(8,128)(2,1)}, bf16[320,1024]{1,0:T(8,128)(2,1)}, u32[]{:S(2)}, u32[]{:S(2)}) collective-permute-start(bf16[320,1024]{1,0:T(8,128)(2,1)} %collective-permute-done.8), channel_id=1, source_target_pairs={{0,1},{1,2},{2,3},{3,4},{4,5},{5,6},{6,7},{7,8},{8,9},{9,10},{10,1... | collective-permute-start | bytes 1966088 | tf_op jit(solution)/shard_map/ppermute | solution.py:157
  64.0 8.4 %copy-start.1 = (bf16[320,1024]{1,0:T(8,128)(2,1)}, bf16[320,1024]{1,0:T(8,128)(2,1)S(1)}, u32[]{:S(2)}) copy-start(bf16[320,1024]{1,0:T(8,128)(2,1)S(1)} %collective-permute-done.2) | copy-start | bytes 1966084
  64.0 21.0 %collective-permute-start.3 = (bf16[320,1024]{1,0:T(8,128)(2,1)S(1)}, bf16[320,1024]{1,0:T(8,128)(2,1)}, u32[]{:S(2)}, u32[]{:S(2)}) collective-permute-start(bf16[320,1024]{1,0:T(8,128)(2,1)S(1)} %collective-permute-done.2), channel_id=1, source_target_pairs={{1,0},{2,1},{3,2},{4,3},{5,4},{6,5},{7,6},{8,7},{9,8},{10,9},{11,1... | collective-permute-start | bytes 1966088 | tf_op jit(solution)/shard_map/ppermute | solution.py:158
  72.4 57.6 %all-to-all-start.2 = ((f32[32,8,1920]{2,1,0:T(8,128)}), f32[32,8,1920]{2,1,0:T(8,128)S(1)}, u32[]{:S(2)}, u32[]{:S(2)}) async-start(f32[32,8,1920]{2,1,0:T(8,128)} %convolution_bitcast_fusion), calls=%async_computation.2 | async-start | bytes 3932160 | tf_op jit(solution)/shard_map/all_to_all | solution.py:171
  83.2 19.4 %collective-permute-start.10 = (bf16[320,1024]{1,0:T(8,128)(2,1)}, bf16[320,1024]{1,0:T(8,128)(2,1)S(1)}, u32[]{:S(2)}, u32[]{:S(2)}) collective-permute-start(bf16[320,1024]{1,0:T(8,128)(2,1)} %collective-permute-done.9), channel_id=1, source_target_pairs={{0,1},{1,2},{2,3},{3,4},{4,5},{5,6},{6,7},{7,8},{8,9},{9,10},{10,1... | collective-permute-start | bytes 1966088 | tf_op jit(solution)/shard_map/ppermute | solution.py:157
  85.1 19.4 %collective-permute-start.4 = (bf16[320,1024]{1,0:T(8,128)(2,1)}, bf16[320,1024]{1,0:T(8,128)(2,1)S(1)}, u32[]{:S(2)}, u32[]{:S(2)}) collective-permute-start(bf16[320,1024]{1,0:T(8,128)(2,1)} %collective-permute-done.3), channel_id=1, source_target_pairs={{1,0},{2,1},{3,2},{4,3},{5,4},{6,5},{7,6},{8,7},{9,8},{10,9},{11,1... | collective-permute-start | bytes 1966088 | tf_op jit(solution)/shard_map/ppermute | solution.py:158
  102.6 18.3 %collective-permute-start.11 = (bf16[320,1024]{1,0:T(8,128)(2,1)S(1)}, bf16[320,1024]{1,0:T(8,128)(2,1)S(1)}, u32[]{:S(2)}, u32[]{:S(2)}) collective-permute-start(bf16[320,1024]{1,0:T(8,128)(2,1)S(1)} %collective-permute-done.10), channel_id=1, source_target_pairs={{0,1},{1,2},{2,3},{3,4},{4,5},{5,6},{6,7},{7,8},{8,9},{9,10},{10,1... | collective-permute-start | bytes 1966088 | tf_op jit(solution)/shard_map/ppermute | solution.py:157
  104.5 18.3 %collective-permute-start.5 = (bf16[320,1024]{1,0:T(8,128)(2,1)S(1)}, bf16[320,1024]{1,0:T(8,128)(2,1)}, u32[]{:S(2)}, u32[]{:S(2)}) collective-permute-start(bf16[320,1024]{1,0:T(8,128)(2,1)S(1)} %collective-permute-done.4), channel_id=1, source_target_pairs={{1,0},{2,1},{3,2},{4,3},{5,4},{6,5},{7,6},{8,7},{9,8},{10,9},{11,1... | collective-permute-start | bytes 1966088 | tf_op jit(solution)/shard_map/ppermute | solution.py:158
  120.8 18.6 %collective-permute-start.12 = (bf16[320,1024]{1,0:T(8,128)(2,1)S(1)}, bf16[320,1024]{1,0:T(8,128)(2,1)}, u32[]{:S(2)}, u32[]{:S(2)}) collective-permute-start(bf16[320,1024]{1,0:T(8,128)(2,1)S(1)} %collective-permute-done.11), channel_id=1, source_target_pairs={{0,1},{1,2},{2,3},{3,4},{4,5},{5,6},{6,7},{7,8},{8,9},{9,10},{10,1... | collective-permute-start | bytes 1966088 | tf_op jit(solution)/shard_map/ppermute | solution.py:157
  122.8 16.7 %collective-permute-start.13 = (bf16[320,1024]{1,0:T(8,128)(2,1)}, bf16[320,1024]{1,0:T(8,128)(2,1)}, u32[]{:S(2)}, u32[]{:S(2)}) collective-permute-start(bf16[320,1024]{1,0:T(8,128)(2,1)} %collective-permute-done.5), channel_id=1, source_target_pairs={{1,0},{2,1},{3,2},{4,3},{5,4},{6,5},{7,6},{8,7},{9,8},{10,9},{11,1... | collective-permute-start | bytes 1966088 | tf_op jit(solution)/shard_map/ppermute | solution.py:158
  130.0 35.8 %all-to-all-start.1 = ((f32[32,8,1920]{2,1,0:T(8,128)}), f32[32,8,1920]{2,1,0:T(8,128)}, u32[]{:S(2)}, u32[]{:S(2)}) async-start(f32[32,8,1920]{2,1,0:T(8,128)} %convolution_bitcast_fusion.1), calls=%async_computation.1 | async-start | bytes 3932160 | tf_op jit(solution)/shard_map/all_to_all | solution.py:171
  140.7 12.8 %collective-permute-start.14 = (bf16[320,1024]{1,0:T(8,128)(2,1)S(1)}, bf16[320,1024]{1,0:T(8,128)(2,1)S(1)}, u32[]{:S(2)}, u32[]{:S(2)}) collective-permute-start(bf16[320,1024]{1,0:T(8,128)(2,1)S(1)} %broadcast_select_fusion), channel_id=1, source_target_pairs={{0,1},{1,2},{2,3},{3,4},{4,5},{5,6},{6,7},{7,8},{8,9},{9,10},{10,1... | collective-permute-start | bytes 1966088 | tf_op jit(solution)/shard_map/ppermute | solution.py:163
  165.8 25.8 %all-to-all-start = ((f32[32,8,1280]{2,1,0:T(8,128)}), f32[32,8,1280]{2,1,0:T(8,128)}, u32[]{:S(2)}, u32[]{:S(2)}) async-start(f32[32,8,1280]{2,1,0:T(8,128)} %convolution_bitcast_fusion.2), calls=%async_computation | async-start | bytes 2621440 | tf_op jit(solution)/shard_map/all_to_all | solution.py:171
  209.5 19.3 %all-to-all-start.4 = ((f32[16,8,128]{2,1,0:T(8,128)}), f32[16,8,128]{2,1,0:T(8,128)S(1)}, u32[]{:S(2)}, u32[]{:S(2)}) async-start(f32[16,8,128]{2,1,0:T(8,128)} %shard_map.31), calls=%async_computation.4 | async-start | bytes 131072 | tf_op jit(solution)/shard_map/all_to_all | solution.py:176

commit v5 on v4

--- a/solution.py
+++ b/solution.py
@@ -8,7 +8,8 @@
 from jax.sharding import PartitionSpec as P
 
 epsilon = 1e-06
-GROUPS = (6, 6, 4)
+PIECES = 2
+GROUPS = (8, 8, 8, 8)
 VMEM = pltpu.VMEM
 LIMIT = 48 * 1024 * 1024
 EXACT = lax.Precision.HIGHEST
@@ -98,21 +99,16 @@
         across = across * factor(cross_down, own_down, 0)
         down = new_down
         width *= 2
-    sums = []
+    width = out_ref.shape[2]
+    place = 0
     for block_ref in blocks:
         total = block_ref[0] * down[0:1]
         for r in range(1, replicas):
             total = total + block_ref[r] * down[r:r + 1]
-        sums.append(total)
-    each = replicas // slabs
-    width = out_ref.shape[2]
-    place = 0
-    for total in sums:
-        for k in range(total.shape[1] // (width * each)):
-            slab = lax.rem(here_ref[0] + order[place], slabs)
-            for h in range(each):
-                start = (k * each + h) * width
-                out_ref[slab * each + h] = total[:, start:start + width]
+        for start in range(0, total.shape[1], width):
+            away, piece = order[place]
+            slab = lax.rem(here_ref[0] + away, slabs)
+            out_ref[slab * PIECES + piece] = total[:, start:start + width]
             place += 1
 
 
@@ -135,33 +131,29 @@
     replicas = lax.axis_size("dp")
     slabs = lax.axis_size("tensor")
     here = lax.axis_index("tensor").astype(jnp.int32)
-    even = lax.axis_index("dp") % 2 == 0
     columns = out_grads.shape[1]
     part = columns // replicas
     half = slabs // 2
     up = [(i, (i + 1) % slabs) for i in range(slabs)]
     down = [((i + 1) % slabs, i) for i in range(slabs)]
-    split = [
-        (r * slabs + i, r * slabs + (i + (-1 if r % 2 else 1)) % slabs)
-        for r in range(replicas) for i in range(slabs)
-    ]
-
     slab = activations.T
-    from_below = from_above = slab
-    held, order = [slab], [0]
+    rows = slab.shape[0] // PIECES
+    pieces = [slab[i * rows:(i + 1) * rows] for i in range(PIECES)]
+    below, above = list(pieces), list(pieces)
+    held, order = list(pieces), [(0, i) for i in range(PIECES)]
     blocks = []
     gram = jnp.zeros((8, 128), jnp.float32)
     sizes = list(GROUPS)
     for step in range(1, half + 1):
-        if step < half:
-            from_below = lax.ppermute(from_below, "tensor", up)
-            from_above = lax.ppermute(from_above, "tensor", down)
-            held += [from_below, from_above]
-            order += [slabs - step, step]
-        else:
-            onward = jnp.where(even, from_below, from_above)
-            held += [lax.ppermute(onward, ("dp", "tensor"), split)]
-            order += [half]
+        for i in range(PIECES):
+            if step < half or i < PIECES // 2:
+                below[i] = lax.ppermute(below[i], "tensor", up)
+                held.append(below[i])
+                order.append((slabs - step, i))
+            if step < half or i >= PIECES // 2:
+                above[i] = lax.ppermute(above[i], "tensor", down)
+                held.append(above[i])
+                order.append((step, i))
         if len(held) >= sizes[0]:
             group, held = held[:sizes[0]], held[sizes.pop(0):]
             grad = lax.dot_general(

time: 248 us -> 258 us (1.040)
  waiting for transfers between devices: 95.6 us -> 35.9 us
  starting transfers between devices: 92.6 us -> 151 us
  local copies, waits for them, and re-layouts: 6.78 us -> 19.1 us
    ppermute x15 -> x30, waiting for transfers between devices: 62.5 us -> 12.2 us  [the longest x15 9.96 us: on_device(): below[i] = lax.ppermute(below[i], 'tensor', up)]
    ppermute x15 -> x30, starting transfers between devices: 58.2 us -> 104 us  [the longest x15 71.6 us: on_device(): above[i] = lax.ppermute(above[i], 'tensor', down)]
    all_to_all x3 -> x4, starting transfers between devices: 26.8 us -> 37.4 us  [on_device(): block = lax.all_to_all(grad.reshape(replicas, part, -1), 'dp', 0, 0)]
    unnamed x14 -> x31, local copies, waits for them, and re-layouts: 4.8 us -> 15.1 us
    all_to_all x3 -> x4, waiting for transfers between devices: 21.6 us -> 12.1 us  [on_device(): block = lax.all_to_all(grad.reshape(replicas, part, -1), 'dp', 0, 0)]
    dot_general x3 -> x4, matrix products: 8.66 us -> 8.13 us  [on_device(): lax.dot_general(out_grads, jnp.concatenate(group, axis=0), (((0,), (1,)),...]
    pallas_call x3 -> x4, Pallas kernels: 9.8 us -> 10.3 us  [gram_add(): pl.pallas_call(functools.partial(gram_kernel, replicas), out_shape=jax.Sh...]
  transfers between devices with their start and end apart: 19 -> 35, of which waited for: 9 -> 5; matrix products, arithmetic and copies ran while one was open for 6% -> 10% of each run, Pallas kernels for 3% -> 3%
where the time goes in v5:
time: 258 us; the launch traced here: 256 us
  starting transfers between devices  151 us (59%)
  waiting for transfers between devices  35.9 us (14%)
  blocking collectives  27 us (10%)
  local copies, waits for them, and re-layouts  19.1 us (7%)
  Pallas kernels  14.6 us (6%)
  matrix products  8.13 us (3%)
    ppermute x15, starting transfers between devices, on_device(): above[i] = lax.ppermute(above[i], 'tensor', down)  71.6 us
    all_to_all x4, starting transfers between devices, on_device(): block = lax.all_to_all(grad.reshape(replicas, part, -1), 'dp', 0, 0)  37.4 us
    ppermute x15, starting transfers between devices, on_device(): below[i] = lax.ppermute(below[i], 'tensor', up)  32.7 us
    unnamed x31, local copies, waits for them, and re-layouts  15.1 us
    all_to_all x1, blocking collectives, on_device(): home = lax.all_to_all(home, 'dp', 0, 0)  14.1 us
    all_to_all x1, blocking collectives, on_device(): parts = sum_and_spread(lax.all_to_all(peers, 'dp', 0, 0), slabs)  13 us
    all_to_all x4, waiting for transfers between devices, on_device(): block = lax.all_to_all(grad.reshape(replicas, part, -1), 'dp', 0, 0)  12.1 us
    all_to_all x1, waiting for transfers between devices, on_device(): parts = lax.all_to_all(parts, 'tensor', 0, 0)  11.6 us
  transfers between devices with their start and end apart: 35, of which 5 were waited for; matrix products, arithmetic and copies ran while one was open for 10% of the time, Pallas kernels for 3%

profile of v5, /device:TPU:1, one launch (start us, length us, event | category | flops | bytes accessed | tf_op | source)
XLA Modules:
  0.0 256.0 jit_solution(8350885855997760013)
XLA Ops:
  5.6 9.5 %collective-permute-start.6 = (bf16[160,1024]{1,0:T(8,128)(2,1)S(1)}, bf16[160,1024]{1,0:T(8,128)(2,1)S(1)}, u32[]{:S(2)}, u32[]{:S(2)}) collective-permute-start(bf16[160,1024]{1,0:T(8,128)(2,1)S(1)} %get-tuple-element.6), channel_id=1, source_target_pairs={{1,0},{2,1},{3,2},{4,3},{5,4},{6,5},{7,6},{8,7},{9,8},{10,9},{11,1... | collective-permute-start | bytes 983048 | tf_op jit(solution)/shard_map/ppermute | solution.py:154
  17.0 4.6 %collective-permute-start.19 = (bf16[160,1024]{1,0:T(8,128)(2,1)S(1)}, bf16[160,1024]{1,0:T(8,128)(2,1)S(1)}, u32[]{:S(2)}, u32[]{:S(2)}) collective-permute-start(bf16[160,1024]{1,0:T(8,128)(2,1)S(1)} %get-tuple-element.5), channel_id=1, source_target_pairs={{1,0},{2,1},{3,2},{4,3},{5,4},{6,5},{7,6},{8,7},{9,8},{10,9},{11,1... | collective-permute-start | bytes 983048 | tf_op jit(solution)/shard_map/ppermute | solution.py:154
  24.7 4.6 %collective-permute-start.7 = (bf16[160,1024]{1,0:T(8,128)(2,1)S(1)}, bf16[160,1024]{1,0:T(8,128)(2,1)}, u32[]{:S(2)}, u32[]{:S(2)}) collective-permute-start(bf16[160,1024]{1,0:T(8,128)(2,1)S(1)} %collective-permute-done.6), channel_id=1, source_target_pairs={{1,0},{2,1},{3,2},{4,3},{5,4},{6,5},{7,6},{8,7},{9,8},{10,9},{11,1... | collective-permute-start | bytes 983048 | tf_op jit(solution)/shard_map/ppermute | solution.py:154
  31.2 4.6 %collective-permute-start.20 = (bf16[160,1024]{1,0:T(8,128)(2,1)S(1)}, bf16[160,1024]{1,0:T(8,128)(2,1)}, u32[]{:S(2)}, u32[]{:S(2)}) collective-permute-start(bf16[160,1024]{1,0:T(8,128)(2,1)S(1)} %collective-permute-done.19), channel_id=1, source_target_pairs={{1,0},{2,1},{3,2},{4,3},{5,4},{6,5},{7,6},{8,7},{9,8},{10,9},{11,1... | collective-permute-start | bytes 983048 | tf_op jit(solution)/shard_map/ppermute | solution.py:154
  42.4 4.6 %collective-permute-start.21 = (bf16[160,1024]{1,0:T(8,128)(2,1)}, bf16[160,1024]{1,0:T(8,128)(2,1)S(1)}, u32[]{:S(2)}, u32[]{:S(2)}) collective-permute-start(bf16[160,1024]{1,0:T(8,128)(2,1)} %collective-permute-done.20), channel_id=1, source_target_pairs={{1,0},{2,1},{3,2},{4,3},{5,4},{6,5},{7,6},{8,7},{9,8},{10,9},{11,1... | collective-permute-start | bytes 983048 | tf_op jit(solution)/shard_map/ppermute | solution.py:154
  48.9 4.6 %collective-permute-start.8 = (bf16[160,1024]{1,0:T(8,128)(2,1)}, bf16[160,1024]{1,0:T(8,128)(2,1)}, u32[]{:S(2)}, u32[]{:S(2)}) collective-permute-start(bf16[160,1024]{1,0:T(8,128)(2,1)} %collective-permute-done.7), channel_id=1, source_target_pairs={{1,0},{2,1},{3,2},{4,3},{5,4},{6,5},{7,6},{8,7},{9,8},{10,9},{11,1... | collective-permute-start | bytes 983048 | tf_op jit(solution)/shard_map/ppermute | solution.py:154
  56.6 10.7 %all-to-all-start.3 = ((f32[32,8,1280]{2,1,0:T(8,128)}), f32[32,8,1280]{2,1,0:T(8,128)S(1)}, u32[]{:S(2)}, u32[]{:S(2)}) async-start(f32[32,8,1280]{2,1,0:T(8,128)} %convolution_bitcast_fusion), calls=%async_computation.3 | async-start | bytes 2621440 | tf_op jit(solution)/shard_map/all_to_all | solution.py:163
  70.3 4.6 %collective-permute-start.22 = (bf16[160,1024]{1,0:T(8,128)(2,1)S(1)}, bf16[160,1024]{1,0:T(8,128)(2,1)}, u32[]{:S(2)}, u32[]{:S(2)}) collective-permute-start(bf16[160,1024]{1,0:T(8,128)(2,1)S(1)} %collective-permute-done.21), channel_id=1, source_target_pairs={{1,0},{2,1},{3,2},{4,3},{5,4},{6,5},{7,6},{8,7},{9,8},{10,9},{11,1... | collective-permute-start | bytes 983048 | tf_op jit(solution)/shard_map/ppermute | solution.py:154
  76.8 4.6 %collective-permute-start.9 = (bf16[160,1024]{1,0:T(8,128)(2,1)}, bf16[160,1024]{1,0:T(8,128)(2,1)}, u32[]{:S(2)}, u32[]{:S(2)}) collective-permute-start(bf16[160,1024]{1,0:T(8,128)(2,1)} %collective-permute-done.8), channel_id=1, source_target_pairs={{1,0},{2,1},{3,2},{4,3},{5,4},{6,5},{7,6},{8,7},{9,8},{10,9},{11,1... | collective-permute-start | bytes 983048 | tf_op jit(solution)/shard_map/ppermute | solution.py:154
  84.4 4.6 %collective-permute-start.23 = (bf16[160,1024]{1,0:T(8,128)(2,1)}, bf16[160,1024]{1,0:T(8,128)(2,1)}, u32[]{:S(2)}, u32[]{:S(2)}) collective-permute-start(bf16[160,1024]{1,0:T(8,128)(2,1)} %collective-permute-done.22), channel_id=1, source_target_pairs={{1,0},{2,1},{3,2},{4,3},{5,4},{6,5},{7,6},{8,7},{9,8},{10,9},{11,1... | collective-permute-start | bytes 983048 | tf_op jit(solution)/shard_map/ppermute | solution.py:154
  91.0 4.6 %collective-permute-start.10 = (bf16[160,1024]{1,0:T(8,128)(2,1)}, bf16[160,1024]{1,0:T(8,128)(2,1)}, u32[]{:S(2)}, u32[]{:S(2)}) collective-permute-start(bf16[160,1024]{1,0:T(8,128)(2,1)} %collective-permute-done.9), channel_id=1, source_target_pairs={{1,0},{2,1},{3,2},{4,3},{5,4},{6,5},{7,6},{8,7},{9,8},{10,9},{11,1... | collective-permute-start | bytes 983048 | tf_op jit(solution)/shard_map/ppermute | solution.py:154
  99.6 9.6 %all-to-all-start.2 = ((f32[32,8,1280]{2,1,0:T(8,128)}), f32[32,8,1280]{2,1,0:T(8,128)S(1)}, u32[]{:S(2)}, u32[]{:S(2)}) async-start(f32[32,8,1280]{2,1,0:T(8,128)} %convolution_bitcast_fusion.1), calls=%async_computation.2 | async-start | bytes 2621440 | tf_op jit(solution)/shard_map/all_to_all | solution.py:163
  113.2 4.6 %collective-permute-start.24 = (bf16[160,1024]{1,0:T(8,128)(2,1)}, bf16[160,1024]{1,0:T(8,128)(2,1)S(1)}, u32[]{:S(2)}, u32[]{:S(2)}) collective-permute-start(bf16[160,1024]{1,0:T(8,128)(2,1)} %collective-permute-done.23), channel_id=1, source_target_pairs={{1,0},{2,1},{3,2},{4,3},{5,4},{6,5},{7,6},{8,7},{9,8},{10,9},{11,1... | collective-permute-start | bytes 983048 | tf_op jit(solution)/shard_map/ppermute | solution.py:154
  119.7 4.6 %collective-permute-start.11 = (bf16[160,1024]{1,0:T(8,128)(2,1)}, bf16[160,1024]{1,0:T(8,128)(2,1)}, u32[]{:S(2)}, u32[]{:S(2)}) collective-permute-start(bf16[160,1024]{1,0:T(8,128)(2,1)} %collective-permute-done.10), channel_id=1, source_target_pairs={{1,0},{2,1},{3,2},{4,3},{5,4},{6,5},{7,6},{8,7},{9,8},{10,9},{11,1... | collective-permute-start | bytes 983048 | tf_op jit(solution)/shard_map/ppermute | solution.py:154
  131.5 5.3 %collective-permute-start.27 = (bf16[160,1024]{1,0:T(8,128)(2,1)}, bf16[160,1024]{1,0:T(8,128)(2,1)}, u32[]{:S(2)}, u32[]{:S(2)}) collective-permute-start(bf16[160,1024]{1,0:T(8,128)(2,1)} %collective-permute-done.11), channel_id=1, source_target_pairs={{1,0},{2,1},{3,2},{4,3},{5,4},{6,5},{7,6},{8,7},{9,8},{10,9},{11,1... | collective-permute-start | bytes 983048 | tf_op jit(solution)/shard_map/ppermute | solution.py:154
  140.6 8.9 %all-to-all-start.1 = ((f32[32,8,1280]{2,1,0:T(8,128)}), f32[32,8,1280]{2,1,0:T(8,128)}, u32[]{:S(2)}, u32[]{:S(2)}) async-start(f32[32,8,1280]{2,1,0:T(8,128)} %convolution_bitcast_fusion.2), calls=%async_computation.1 | async-start | bytes 2621440 | tf_op jit(solution)/shard_map/all_to_all | solution.py:163
  158.7 4.6 %collective-permute-start.29 = (bf16[160,1024]{1,0:T(8,128)(2,1)}, bf16[160,1024]{1,0:T(8,128)(2,1)S(1)}, u32[]{:S(2)}, u32[]{:S(2)}) collective-permute-start(bf16[160,1024]{1,0:T(8,128)(2,1)} %collective-permute-done.27), channel_id=1, source_target_pairs={{1,0},{2,1},{3,2},{4,3},{5,4},{6,5},{7,6},{8,7},{9,8},{10,9},{11,1... | collective-permute-start | bytes 983048 | tf_op jit(solution)/shard_map/ppermute | solution.py:154
  165.4 5.4 %collective-permute-done.28 = bf16[160,1024]{1,0:T(8,128)(2,1)S(1)} collective-permute-done((bf16[160,1024]{1,0:T(8,128)(2,1)}, bf16[160,1024]{1,0:T(8,128)(2,1)S(1)}, u32[]{:S(2)}, u32[]{:S(2)}) %collective-permute-start.28) | collective-permute-done | bytes 327712 | tf_op jit(solution)/shard_map/ppermute | solution.py:150
  172.8 8.2 %all-to-all-start = ((f32[32,8,1280]{2,1,0:T(8,128)}), f32[32,8,1280]{2,1,0:T(8,128)}, u32[]{:S(2)}, u32[]{:S(2)}) async-start(f32[32,8,1280]{2,1,0:T(8,128)} %convolution_bitcast_fusion.3), calls=%async_computation | async-start | bytes 2621440 | tf_op jit(solution)/shard_map/all_to_all | solution.py:163
  188.1 12.1 %all-to-all-done.refs_3_ = f32[32,8,1280]{2,1,0:T(8,128)} async-done(((f32[32,8,1280]{2,1,0:T(8,128)}), f32[32,8,1280]{2,1,0:T(8,128)}, u32[]{:S(2)}, u32[]{:S(2)}) %all-to-all-start) | async-done | bytes 1310752 | tf_op jit(solution)/shard_map/all_to_all | solution.py:163
  203.5 13.0 %all_to_all.35.parts_ref = f32[32,8,128]{2,1,0:T(8,128)} all-to-all(f32[32,8,128]{2,1,0:T(8,128)S(1)} %broadcast_in_dim.7), channel_id=1, replica_groups=mesh['dp'=32,'tensor'=16] {'dp'}, dimensions={0} | all-to-all | bytes 262144 | tf_op jit(solution)/shard_map/all_to_all | solution.py:167
  218.0 8.9 %all-to-all-start.5 = ((f32[16,8,128]{2,1,0:T(8,128)}), f32[16,8,128]{2,1,0:T(8,128)S(1)}, u32[]{:S(2)}, u32[]{:S(2)}) async-start(f32[16,8,128]{2,1,0:T(8,128)} %shard_map.32), calls=%async_computation.5 | async-start | bytes 131072 | tf_op jit(solution)/shard_map/all_to_all | solution.py:168
  226.9 11.6 %all-to-all-done.5.parts_ref = f32[16,8,128]{2,1,0:T(8,128)S(1)} async-done(((f32[16,8,128]{2,1,0:T(8,128)}), f32[16,8,128]{2,1,0:T(8,128)S(1)}, u32[]{:S(2)}, u32[]{:S(2)}) %all-to-all-start.5) | async-done | bytes 65568 | tf_op jit(solution)/shard_map/all_to_all | solution.py:168
  241.2 14.1 %all_to_all.36 = f32[32,8,160]{2,1,0:T(8,128)S(1)} all-to-all(f32[32,8,160]{2,1,0:T(8,128)S(1)} %shard_map.33), channel_id=1, replica_groups=mesh['dp'=32,'tensor'=16] {'dp'}, dimensions={0} | all-to-all | bytes 327680 | tf_op jit(solution)/shard_map/all_to_all | solution.py:170
  (97 shorter events, 83.3 us)
Async XLA Ops:
  1.2 21.5 %collective-permute-start = (bf16[160,1024]{1,0:T(8,128)(2,1)S(1)}, bf16[160,1024]{1,0:T(8,128)(2,1)S(1)}, u32[]{:S(2)}, u32[]{:S(2)}) collective-permute-start(bf16[160,1024]{1,0:T(8,128)(2,1)S(1)} %get-tuple-element.6), channel_id=1, source_target_pairs={{0,1},{1,2},{2,3},{3,4},{4,5},{5,6},{6,7},{7,8},{8,9},{9,10},{10,1... | collective-permute-start | bytes 983048 | tf_op jit(solution)/shard_map/ppermute | solution.py:150
  5.6 19.1 %collective-permute-start.6 = (bf16[160,1024]{1,0:T(8,128)(2,1)S(1)}, bf16[160,1024]{1,0:T(8,128)(2,1)S(1)}, u32[]{:S(2)}, u32[]{:S(2)}) collective-permute-start(bf16[160,1024]{1,0:T(8,128)(2,1)S(1)} %get-tuple-element.6), channel_id=1, source_target_pairs={{1,0},{2,1},{3,2},{4,3},{5,4},{6,5},{7,6},{8,7},{9,8},{10,9},{11,1... | collective-permute-start | bytes 983048 | tf_op jit(solution)/shard_map/ppermute | solution.py:154
  17.0 14.2 %collective-permute-start.19 = (bf16[160,1024]{1,0:T(8,128)(2,1)S(1)}, bf16[160,1024]{1,0:T(8,128)(2,1)S(1)}, u32[]{:S(2)}, u32[]{:S(2)}) collective-permute-start(bf16[160,1024]{1,0:T(8,128)(2,1)S(1)} %get-tuple-element.5), channel_id=1, source_target_pairs={{1,0},{2,1},{3,2},{4,3},{5,4},{6,5},{7,6},{8,7},{9,8},{10,9},{11,1... | collective-permute-start | bytes 983048 | tf_op jit(solution)/shard_map/ppermute | solution.py:154
  22.7 24.3 %collective-permute-start.1 = (bf16[160,1024]{1,0:T(8,128)(2,1)S(1)}, bf16[160,1024]{1,0:T(8,128)(2,1)S(1)}, u32[]{:S(2)}, u32[]{:S(2)}) collective-permute-start(bf16[160,1024]{1,0:T(8,128)(2,1)S(1)} %collective-permute-done), channel_id=1, source_target_pairs={{0,1},{1,2},{2,3},{3,4},{4,5},{5,6},{6,7},{7,8},{8,9},{9,10},{10,1... | collective-permute-start | bytes 983048 | tf_op jit(solution)/shard_map/ppermute | solution.py:150
  24.7 24.3 %collective-permute-start.7 = (bf16[160,1024]{1,0:T(8,128)(2,1)S(1)}, bf16[160,1024]{1,0:T(8,128)(2,1)}, u32[]{:S(2)}, u32[]{:S(2)}) collective-permute-start(bf16[160,1024]{1,0:T(8,128)(2,1)S(1)} %collective-permute-done.6), channel_id=1, source_target_pairs={{1,0},{2,1},{3,2},{4,3},{5,4},{6,5},{7,6},{8,7},{9,8},{10,9},{11,1... | collective-permute-start | bytes 983048 | tf_op jit(solution)/shard_map/ppermute | solution.py:154
  40.5 27.9 %collective-permute-start.14 = (bf16[160,1024]{1,0:T(8,128)(2,1)S(1)}, bf16[160,1024]{1,0:T(8,128)(2,1)S(1)}, u32[]{:S(2)}, u32[]{:S(2)}) collective-permute-start(bf16[160,1024]{1,0:T(8,128)(2,1)S(1)} %collective-permute-done.13), channel_id=1, source_target_pairs={{0,1},{1,2},{2,3},{3,4},{4,5},{5,6},{6,7},{7,8},{8,9},{9,10},{10,1... | collective-permute-start | bytes 983048 | tf_op jit(solution)/shard_map/ppermute | solution.py:150
  42.4 27.9 %collective-permute-start.21 = (bf16[160,1024]{1,0:T(8,128)(2,1)}, bf16[160,1024]{1,0:T(8,128)(2,1)S(1)}, u32[]{:S(2)}, u32[]{:S(2)}) collective-permute-start(bf16[160,1024]{1,0:T(8,128)(2,1)} %collective-permute-done.20), channel_id=1, source_target_pairs={{1,0},{2,1},{3,2},{4,3},{5,4},{6,5},{7,6},{8,7},{9,8},{10,9},{11,1... | collective-permute-start | bytes 983048 | tf_op jit(solution)/shard_map/ppermute | solution.py:154
  47.0 27.9 %collective-permute-start.2 = (bf16[160,1024]{1,0:T(8,128)(2,1)S(1)}, bf16[160,1024]{1,0:T(8,128)(2,1)S(1)}, u32[]{:S(2)}, u32[]{:S(2)}) collective-permute-start(bf16[160,1024]{1,0:T(8,128)(2,1)S(1)} %collective-permute-done.1), channel_id=1, source_target_pairs={{0,1},{1,2},{2,3},{3,4},{4,5},{5,6},{6,7},{7,8},{8,9},{9,10},{10,1... | collective-permute-start | bytes 983048 | tf_op jit(solution)/shard_map/ppermute | solution.py:150
  48.9 27.9 %collective-permute-start.8 = (bf16[160,1024]{1,0:T(8,128)(2,1)}, bf16[160,1024]{1,0:T(8,128)(2,1)}, u32[]{:S(2)}, u32[]{:S(2)}) collective-permute-start(bf16[160,1024]{1,0:T(8,128)(2,1)} %collective-permute-done.7), channel_id=1, source_target_pairs={{1,0},{2,1},{3,2},{4,3},{5,4},{6,5},{7,6},{8,7},{9,8},{10,9},{11,1... | collective-permute-start | bytes 983048 | tf_op jit(solution)/shard_map/ppermute | solution.py:154
  56.6 43.0 %all-to-all-start.3 = ((f32[32,8,1280]{2,1,0:T(8,128)}), f32[32,8,1280]{2,1,0:T(8,128)S(1)}, u32[]{:S(2)}, u32[]{:S(2)}) async-start(f32[32,8,1280]{2,1,0:T(8,128)} %convolution_bitcast_fusion), calls=%async_computation.3 | async-start | bytes 2621440 | tf_op jit(solution)/shard_map/all_to_all | solution.py:163
  82.5 28.7 %collective-permute-start.16 = (bf16[160,1024]{1,0:T(8,128)(2,1)}, bf16[160,1024]{1,0:T(8,128)(2,1)}, u32[]{:S(2)}, u32[]{:S(2)}) collective-permute-start(bf16[160,1024]{1,0:T(8,128)(2,1)} %collective-permute-done.15), channel_id=1, source_target_pairs={{0,1},{1,2},{2,3},{3,4},{4,5},{5,6},{6,7},{7,8},{8,9},{9,10},{10,1... | collective-permute-start | bytes 983048 | tf_op jit(solution)/shard_map/ppermute | solution.py:150
  84.4 28.7 %collective-permute-start.23 = (bf16[160,1024]{1,0:T(8,128)(2,1)}, bf16[160,1024]{1,0:T(8,128)(2,1)}, u32[]{:S(2)}, u32[]{:S(2)}) collective-permute-start(bf16[160,1024]{1,0:T(8,128)(2,1)} %collective-permute-done.22), channel_id=1, source_target_pairs={{1,0},{2,1},{3,2},{4,3},{5,4},{6,5},{7,6},{8,7},{9,8},{10,9},{11,1... | collective-permute-start | bytes 983048 | tf_op jit(solution)/shard_map/ppermute | solution.py:154
  89.0 28.7 %collective-permute-start.4 = (bf16[160,1024]{1,0:T(8,128)(2,1)}, bf16[160,1024]{1,0:T(8,128)(2,1)S(1)}, u32[]{:S(2)}, u32[]{:S(2)}) collective-permute-start(bf16[160,1024]{1,0:T(8,128)(2,1)} %collective-permute-done.3), channel_id=1, source_target_pairs={{0,1},{1,2},{2,3},{3,4},{4,5},{5,6},{6,7},{7,8},{8,9},{9,10},{10,1... | collective-permute-start | bytes 983048 | tf_op jit(solution)/shard_map/ppermute | solution.py:150
  91.0 28.7 %collective-permute-start.10 = (bf16[160,1024]{1,0:T(8,128)(2,1)}, bf16[160,1024]{1,0:T(8,128)(2,1)}, u32[]{:S(2)}, u32[]{:S(2)}) collective-permute-start(bf16[160,1024]{1,0:T(8,128)(2,1)} %collective-permute-done.9), channel_id=1, source_target_pairs={{1,0},{2,1},{3,2},{4,3},{5,4},{6,5},{7,6},{8,7},{9,8},{10,9},{11,1... | collective-permute-start | bytes 983048 | tf_op jit(solution)/shard_map/ppermute | solution.py:154
  99.6 41.0 %all-to-all-start.2 = ((f32[32,8,1280]{2,1,0:T(8,128)}), f32[32,8,1280]{2,1,0:T(8,128)S(1)}, u32[]{:S(2)}, u32[]{:S(2)}) async-start(f32[32,8,1280]{2,1,0:T(8,128)} %convolution_bitcast_fusion.1), calls=%async_computation.2 | async-start | bytes 2621440 | tf_op jit(solution)/shard_map/all_to_all | solution.py:163
  111.2 16.1 %collective-permute-start.17 = (bf16[160,1024]{1,0:T(8,128)(2,1)}, bf16[160,1024]{1,0:T(8,128)(2,1)}, u32[]{:S(2)}, u32[]{:S(2)}) collective-permute-start(bf16[160,1024]{1,0:T(8,128)(2,1)} %collective-permute-done.16), channel_id=1, source_target_pairs={{0,1},{1,2},{2,3},{3,4},{4,5},{5,6},{6,7},{7,8},{8,9},{9,10},{10,1... | collective-permute-start | bytes 983048 | tf_op jit(solution)/shard_map/ppermute | solution.py:150
  113.2 24.6 %collective-permute-start.24 = (bf16[160,1024]{1,0:T(8,128)(2,1)}, bf16[160,1024]{1,0:T(8,128)(2,1)S(1)}, u32[]{:S(2)}, u32[]{:S(2)}) collective-permute-start(bf16[160,1024]{1,0:T(8,128)(2,1)} %collective-permute-done.23), channel_id=1, source_target_pairs={{1,0},{2,1},{3,2},{4,3},{5,4},{6,5},{7,6},{8,7},{9,8},{10,9},{11,1... | collective-permute-start | bytes 983048 | tf_op jit(solution)/shard_map/ppermute | solution.py:154
  117.8 33.6 %collective-permute-start.5 = (bf16[160,1024]{1,0:T(8,128)(2,1)S(1)}, bf16[160,1024]{1,0:T(8,128)(2,1)}, u32[]{:S(2)}, u32[]{:S(2)}) collective-permute-start(bf16[160,1024]{1,0:T(8,128)(2,1)S(1)} %collective-permute-done.4), channel_id=1, source_target_pairs={{0,1},{1,2},{2,3},{3,4},{4,5},{5,6},{6,7},{7,8},{8,9},{9,10},{10,1... | collective-permute-start | bytes 983048 | tf_op jit(solution)/shard_map/ppermute | solution.py:150
  127.3 29.5 %collective-permute-start.18 = (bf16[160,1024]{1,0:T(8,128)(2,1)}, bf16[160,1024]{1,0:T(8,128)(2,1)}, u32[]{:S(2)}, u32[]{:S(2)}) collective-permute-start(bf16[160,1024]{1,0:T(8,128)(2,1)} %collective-permute-done.17), channel_id=1, source_target_pairs={{0,1},{1,2},{2,3},{3,4},{4,5},{5,6},{6,7},{7,8},{8,9},{9,10},{10,1... | collective-permute-start | bytes 983048 | tf_op jit(solution)/shard_map/ppermute | solution.py:150
  131.5 27.2 %collective-permute-start.27 = (bf16[160,1024]{1,0:T(8,128)(2,1)}, bf16[160,1024]{1,0:T(8,128)(2,1)}, u32[]{:S(2)}, u32[]{:S(2)}) collective-permute-start(bf16[160,1024]{1,0:T(8,128)(2,1)} %collective-permute-done.11), channel_id=1, source_target_pairs={{1,0},{2,1},{3,2},{4,3},{5,4},{6,5},{7,6},{8,7},{9,8},{10,9},{11,1... | collective-permute-start | bytes 983048 | tf_op jit(solution)/shard_map/ppermute | solution.py:154
  140.6 32.2 %all-to-all-start.1 = ((f32[32,8,1280]{2,1,0:T(8,128)}), f32[32,8,1280]{2,1,0:T(8,128)}, u32[]{:S(2)}, u32[]{:S(2)}) async-start(f32[32,8,1280]{2,1,0:T(8,128)} %convolution_bitcast_fusion.2), calls=%async_computation.1 | async-start | bytes 2621440 | tf_op jit(solution)/shard_map/all_to_all | solution.py:163
  149.5 14.8 %collective-permute-start.25 = (bf16[160,1024]{1,0:T(8,128)(2,1)}, bf16[160,1024]{1,0:T(8,128)(2,1)S(1)}, u32[]{:S(2)}, u32[]{:S(2)}) collective-permute-start(bf16[160,1024]{1,0:T(8,128)(2,1)} %copy-done.1), channel_id=1, source_target_pairs={{1,0},{2,1},{3,2},{4,3},{5,4},{6,5},{7,6},{8,7},{9,8},{10,9},{11,1... | collective-permute-start | bytes 983048 | tf_op jit(solution)/shard_map/ppermute | solution.py:154
  172.8 27.4 %all-to-all-start = ((f32[32,8,1280]{2,1,0:T(8,128)}), f32[32,8,1280]{2,1,0:T(8,128)}, u32[]{:S(2)}, u32[]{:S(2)}) async-start(f32[32,8,1280]{2,1,0:T(8,128)} %convolution_bitcast_fusion.3), calls=%async_computation | async-start | bytes 2621440 | tf_op jit(solution)/shard_map/all_to_all | solution.py:163
  218.0 20.5 %all-to-all-start.5 = ((f32[16,8,128]{2,1,0:T(8,128)}), f32[16,8,128]{2,1,0:T(8,128)S(1)}, u32[]{:S(2)}, u32[]{:S(2)}) async-start(f32[16,8,128]{2,1,0:T(8,128)} %shard_map.32), calls=%async_computation.5 | async-start | bytes 131072 | tf_op jit(solution)/shard_map/all_to_all | solution.py:168
  (13 other events, 199.2 us)

commit v6 on v4

--- a/solution.py
+++ b/solution.py
@@ -8,21 +8,26 @@
 from jax.sharding import PartitionSpec as P
 
 epsilon = 1e-06
-GROUPS = (6, 6, 4)
+GROUPS = (4, 4, 4, 4)
 VMEM = pltpu.VMEM
 LIMIT = 48 * 1024 * 1024
 EXACT = lax.Precision.HIGHEST
 
 
 def gram_kernel(replicas, block_ref, before_ref, out_ref):
-    rows, cols = block_ref.shape
-    part = rows // replicas
-    whole = lax.dot_general(
-        block_ref[...], block_ref[...], (((1,), (1,)), ((), ())),
-        precision=EXACT, preferred_element_type=jnp.float32,
-    )
+    part = block_ref.shape[1] // 4
+    rows = replicas * part
     i = lax.broadcasted_iota(jnp.int32, (rows, rows), 0)
     j = lax.broadcasted_iota(jnp.int32, (rows, rows), 1)
+    whole = jnp.zeros((rows, rows), jnp.float32)
+    for core in range(2):
+        first = block_ref[:, (3 * core) * part:(3 * core + 1) * part]
+        second = block_ref[:, (1 + core) * part:(2 + core) * part]
+        both = jnp.concatenate([first, second], axis=1).reshape(rows, -1)
+        whole = whole + lax.dot_general(
+            both, both, (((1,), (1,)), ((), ())),
+            precision=EXACT, preferred_element_type=jnp.float32,
+        )
     whole = jnp.where(i % part == j % part, whole, 0.0)
     thin = jnp.sum(whole.reshape(replicas, part, rows), axis=1)
     c = lax.broadcasted_iota(jnp.int32, (rows, 128), 0)
@@ -38,16 +43,15 @@
 
 
 def gram_add(replicas, block, before):
-    rows = block.shape[0] * block.shape[1]
-    block = block.reshape(rows, -1)
-    cols = block.shape[1]
+    block = block.reshape(replicas // 2, 2 * block.shape[1], -1)
+    size = block.size
     return pl.pallas_call(
         functools.partial(gram_kernel, replicas),
         out_shape=jax.ShapeDtypeStruct((8, 128), jnp.float32),
         in_specs=[pl.BlockSpec(memory_space=VMEM)] * 2,
         out_specs=pl.BlockSpec(memory_space=VMEM),
         cost_estimate=pl.CostEstimate(
-            flops=12 * rows * rows * cols, bytes_accessed=4 * rows * cols, transcendentals=0
+            flops=12 * size * replicas * 8, bytes_accessed=4 * size, transcendentals=0
         ),
         compiler_params=pltpu.CompilerParams(vmem_limit_bytes=LIMIT),
     )(block, before)
@@ -98,27 +102,24 @@
         across = across * factor(cross_down, own_down, 0)
         down = new_down
         width *= 2
-    sums = []
-    for block_ref in blocks:
-        total = block_ref[0] * down[0:1]
-        for r in range(1, replicas):
-            total = total + block_ref[r] * down[r:r + 1]
-        sums.append(total)
-    each = replicas // slabs
-    width = out_ref.shape[2]
-    place = 0
-    for total in sums:
-        for k in range(total.shape[1] // (width * each)):
-            slab = lax.rem(here_ref[0] + order[place], slabs)
-            for h in range(each):
-                start = (k * each + h) * width
-                out_ref[slab * each + h] = total[:, start:start + width]
-            place += 1
+    part, width = out_ref.shape[1:]
+    for core in range(2):
+        place = 0
+        for block_ref in blocks:
+            total = 0.0
+            for r in range(replicas):
+                row = (r + core) % 2 * part
+                total = total + block_ref[r // 2 * 2 + core, row:row + part] * down[r:r + 1]
+            for start in range(0, total.shape[1], width):
+                away, piece = order[core][place]
+                slab = lax.rem(here_ref[0] + away, slabs)
+                out_ref[slab * 2 + piece] = total[:, start:start + width]
+                place += 1
 
 
 def weighted_sums(replicas, slabs, order, here, parts, blocks):
-    part = blocks[0].shape[1]
-    total = sum(b.shape[2] for b in blocks)
+    part = blocks[0].shape[1] // 2
+    total = 2 * sum(b.shape[2] for b in blocks)
     size = replicas * part * total
     return pl.pallas_call(
         functools.partial(combine_kernel, replicas, slabs, order),
@@ -135,46 +136,60 @@
     replicas = lax.axis_size("dp")
     slabs = lax.axis_size("tensor")
     here = lax.axis_index("tensor").astype(jnp.int32)
-    even = lax.axis_index("dp") % 2 == 0
+    core = lax.axis_index("dp") % 2
+    tokens, slab_rows = activations.shape
     columns = out_grads.shape[1]
     part = columns // replicas
     half = slabs // 2
-    up = [(i, (i + 1) % slabs) for i in range(slabs)]
-    down = [((i + 1) % slabs, i) for i in range(slabs)]
-    split = [
+    rows = slab_rows // 2
+    sibling = [(r, r ^ 1) for r in range(replicas)]
+    onward = [
         (r * slabs + i, r * slabs + (i + (-1 if r % 2 else 1)) % slabs)
         for r in range(replicas) for i in range(slabs)
     ]
 
-    slab = activations.T
-    from_below = from_above = slab
-    held, order = [slab], [0]
+    def own_half(slab):
+        return lax.dynamic_slice(slab, (core * rows, 0), (rows, tokens))
+
+    def move(slab):
+        return lax.ppermute(slab, ("dp", "tensor"), onward)
+
+    mine = activations.T
+    chains = [mine, lax.ppermute(mine, "dp", sibling)]
+    grads = [out_grads, lax.ppermute(out_grads, "dp", sibling)]
+    held = [[own_half(slab)] for slab in chains]
+    order = [[(0, 0)], [(0, 1)]]
     blocks = []
     gram = jnp.zeros((8, 128), jnp.float32)
     sizes = list(GROUPS)
     for step in range(1, half + 1):
         if step < half:
-            from_below = lax.ppermute(from_below, "tensor", up)
-            from_above = lax.ppermute(from_above, "tensor", down)
-            held += [from_below, from_above]
-            order += [slabs - step, step]
+            chains = [move(slab) for slab in chains]
+            for k in range(2):
+                held[k] += [chains[k][:rows], chains[k][rows:]]
+            order[0] += [(slabs - step, 0), (slabs - step, 1)]
+            order[1] += [(step, 0), (step, 1)]
         else:
-            onward = jnp.where(even, from_below, from_above)
-            held += [lax.ppermute(onward, ("dp", "tensor"), split)]
-            order += [half]
-        if len(held) >= sizes[0]:
-            group, held = held[:sizes[0]], held[sizes.pop(0):]
-            grad = lax.dot_general(
-                out_grads, jnp.concatenate(group, axis=0), (((0,), (1,)), ((), ())),
-                preferred_element_type=jnp.float32,
-            )
-            block = lax.all_to_all(grad.reshape(replicas, part, -1), "dp", 0, 0)
+            for k in range(2):
+                held[k].append(move(own_half(chains[k])))
+                order[k].append((half, k))
+        if len(held[0]) >= sizes[0]:
+            count = sizes.pop(0)
+            parts = []
+            for k in range(2):
+                group, held[k] = held[k][:count], held[k][count:]
+                grad = lax.dot_general(
+                    grads[k], jnp.concatenate(group, axis=0), (((0,), (1,)), ((), ())),
+                    preferred_element_type=jnp.float32,
+                )
+                parts.append(grad.reshape(replicas, part, -1))
+            block = lax.all_to_all(jnp.concatenate(parts, axis=1), "dp", 0, 0)
             gram = gram_add(replicas, block, gram)
             blocks.append(block)
     peers = jnp.broadcast_to(gram, (replicas, *gram.shape))
     parts = sum_and_spread(lax.all_to_all(peers, "dp", 0, 0), slabs)
     parts = lax.all_to_all(parts, "tensor", 0, 0)
-    home = weighted_sums(replicas, slabs, tuple(order), here, parts, blocks)
+    home = weighted_sums(replicas, slabs, order, here, parts, blocks)
     home = lax.all_to_all(home, "dp", 0, 0)
     return home.reshape(columns, -1).T
 

time: 248 us -> 230 us (0.927)
  waiting for transfers between devices: 95.6 us -> 48.2 us
  starting transfers between devices: 92.6 us -> 111 us
  matrix products: 8.66 us -> 13.2 us
  other arithmetic: 1.17 us -> 4.66 us
    ppermute x15 -> x18, waiting for transfers between devices: 62.5 us -> 18.2 us  [the longest x16 18.2 us: move(): return lax.ppermute(slab, ('dp', 'tensor'), onward)]
    ppermute x15 -> x18, starting transfers between devices: 58.2 us -> 76.3 us  [the longest x16 65.6 us: move(): return lax.ppermute(slab, ('dp', 'tensor'), onward)]
    slice x0 -> x6, local copies, waits for them, and re-layouts: none -> 5.03 us  [on_device(): held[k] += [chains[k][:rows], chains[k][rows:]]]
    unnamed x14 -> x24, local copies, waits for them, and re-layouts: 4.8 us -> 0.06 us
    concatenate x0 -> x4, other arithmetic: none -> 4.66 us  [on_device(): block = lax.all_to_all(jnp.concatenate(parts, axis=1), 'dp', 0, 0)]
    dot_general x3 -> x8, matrix products: 8.66 us -> 13.2 us  [on_device(): lax.dot_general(grads[k], jnp.concatenate(group, axis=0), (((0,), (1,)),...]
    dynamic_slice x0 -> x4, local copies, waits for them, and re-layouts: none -> 3.2 us  [own_half(): return lax.dynamic_slice(slab, (core * rows, 0), (rows, tokens))]
    all_to_all x3 -> x4, waiting for transfers between devices: 21.6 us -> 18.4 us  [on_device(): block = lax.all_to_all(jnp.concatenate(parts, axis=1), 'dp', 0, 0)]
  transfers between devices with their start and end apart: 19 -> 23, of which waited for: 9 -> 14; matrix products, arithmetic and copies ran while one was open for 6% -> 11% of each run, Pallas kernels for 3% -> 3%
where the time goes in v6:
time: 230 us; the launch traced here: 229 us
  starting transfers between devices  111 us (48%)
  waiting for transfers between devices  48.2 us (21%)
  blocking collectives  27 us (12%)
  Pallas kernels  15.4 us (7%)
  matrix products  13.2 us (6%)
  local copies, waits for them, and re-layouts  9.08 us (4%)
  other arithmetic  4.66 us (2%)
    ppermute x16, starting transfers between devices, move(): return lax.ppermute(slab, ('dp', 'tensor'), onward)  65.6 us
    all_to_all x4, starting transfers between devices, on_device(): block = lax.all_to_all(jnp.concatenate(parts, axis=1), 'dp', 0, 0)  25.7 us
    all_to_all x4, waiting for transfers between devices, on_device(): block = lax.all_to_all(jnp.concatenate(parts, axis=1), 'dp', 0, 0)  18.4 us
    ppermute x16, waiting for transfers between devices, move(): return lax.ppermute(slab, ('dp', 'tensor'), onward)  18.2 us
    all_to_all x1, blocking collectives, on_device(): home = lax.all_to_all(home, 'dp', 0, 0)  14.1 us
    dot_general x8, matrix products, on_device(): lax.dot_general(grads[k], jnp.concatenate(group, axis=0), (((0,), (1,)),...  13.2 us
    all_to_all x1, blocking collectives, on_device(): parts = sum_and_spread(lax.all_to_all(peers, 'dp', 0, 0), slabs)  13 us
    all_to_all x1, waiting for transfers between devices, on_device(): parts = lax.all_to_all(parts, 'tensor', 0, 0)  11.6 us
  transfers between devices with their start and end apart: 23, of which 14 were waited for; matrix products, arithmetic and copies ran while one was open for 11% of the time, Pallas kernels for 3%

profile of v6, /device:TPU:1, one launch (start us, length us, event | category | flops | bytes accessed | tf_op | source)
XLA Modules:
  0.0 228.5 jit_solution(4914327571803013967)
XLA Ops:
  0.0 8.8 %collective-permute-start.8 = (bf16[320,1024]{1,0:T(8,128)(2,1)}, bf16[320,1024]{1,0:T(8,128)(2,1)S(1)}, u32[]{:S(2)}, u32[]{:S(2)}) collective-permute-start(bf16[320,1024]{1,0:T(8,128)(2,1)} %bitcast.53), channel_id=1, source_target_pairs={{0,16},{16,0},{32,48},{48,32},{64,80},{80,64},{96,112},{112,96},{1... | collective-permute-start | bytes 1966088 | tf_op jit(solution)/shard_map/ppermute | solution.py:158
  8.8 5.7 %collective-permute-start = (bf16[320,1024]{1,0:T(8,128)(2,1)}, bf16[320,1024]{1,0:T(8,128)(2,1)S(1)}, u32[]{:S(2)}, u32[]{:S(2)}) collective-permute-start(bf16[320,1024]{1,0:T(8,128)(2,1)} %bitcast.54), channel_id=1, source_target_pairs={{0,1},{1,2},{2,3},{3,4},{4,5},{5,6},{6,7},{7,8},{8,9},{9,10},{10,1... | collective-permute-start | bytes 1966088 | tf_op jit(solution)/shard_map/ppermute | solution.py:155
  17.2 5.2 %collective-permute-done = bf16[320,1024]{1,0:T(8,128)(2,1)S(1)} collective-permute-done((bf16[320,1024]{1,0:T(8,128)(2,1)}, bf16[320,1024]{1,0:T(8,128)(2,1)S(1)}, u32[]{:S(2)}, u32[]{:S(2)}) %collective-permute-start) | collective-permute-done | bytes 655392 | tf_op jit(solution)/shard_map/ppermute | solution.py:155
  22.4 4.9 %collective-permute-start.1 = (bf16[320,1024]{1,0:T(8,128)(2,1)S(1)}, bf16[320,1024]{1,0:T(8,128)(2,1)S(1)}, u32[]{:S(2)}, u32[]{:S(2)}) collective-permute-start(bf16[320,1024]{1,0:T(8,128)(2,1)S(1)} %collective-permute-done), channel_id=1, source_target_pairs={{0,1},{1,2},{2,3},{3,4},{4,5},{5,6},{6,7},{7,8},{8,9},{9,10},{10,1... | collective-permute-start | bytes 1966088 | tf_op jit(solution)/shard_map/ppermute | solution.py:155
  29.3 5.0 %collective-permute-start.10 = (bf16[320,1024]{1,0:T(8,128)(2,1)S(1)}, bf16[320,1024]{1,0:T(8,128)(2,1)S(1)}, u32[]{:S(2)}, u32[]{:S(2)}) collective-permute-start(bf16[320,1024]{1,0:T(8,128)(2,1)S(1)} %collective-permute-done.9), channel_id=1, source_target_pairs={{0,1},{1,2},{2,3},{3,4},{4,5},{5,6},{6,7},{7,8},{8,9},{9,10},{10,1... | collective-permute-start | bytes 1966088 | tf_op jit(solution)/shard_map/ppermute | solution.py:155
  36.3 5.0 %collective-permute-start.2 = (bf16[320,1024]{1,0:T(8,128)(2,1)S(1)}, bf16[320,1024]{1,0:T(8,128)(2,1)}, u32[]{:S(2)}, u32[]{:S(2)}) collective-permute-start(bf16[320,1024]{1,0:T(8,128)(2,1)S(1)} %collective-permute-done.1), channel_id=1, source_target_pairs={{0,1},{1,2},{2,3},{3,4},{4,5},{5,6},{6,7},{7,8},{8,9},{9,10},{10,1... | collective-permute-start | bytes 1966088 | tf_op jit(solution)/shard_map/ppermute | solution.py:155
  44.5 3.9 %collective-permute-start.11 = (bf16[320,1024]{1,0:T(8,128)(2,1)S(1)}, bf16[320,1024]{1,0:T(8,128)(2,1)}, u32[]{:S(2)}, u32[]{:S(2)}) collective-permute-start(bf16[320,1024]{1,0:T(8,128)(2,1)S(1)} %collective-permute-done.10), channel_id=1, source_target_pairs={{0,1},{1,2},{2,3},{3,4},{4,5},{5,6},{6,7},{7,8},{8,9},{9,10},{10,1... | collective-permute-start | bytes 1966088 | tf_op jit(solution)/shard_map/ppermute | solution.py:155
  50.3 5.1 %collective-permute-start.3 = (bf16[320,1024]{1,0:T(8,128)(2,1)}, bf16[320,1024]{1,0:T(8,128)(2,1)S(1)}, u32[]{:S(2)}, u32[]{:S(2)}) collective-permute-start(bf16[320,1024]{1,0:T(8,128)(2,1)} %collective-permute-done.2), channel_id=1, source_target_pairs={{0,1},{1,2},{2,3},{3,4},{4,5},{5,6},{6,7},{7,8},{8,9},{9,10},{10,1... | collective-permute-start | bytes 1966088 | tf_op jit(solution)/shard_map/ppermute | solution.py:155
  57.4 5.1 %collective-permute-start.12 = (bf16[320,1024]{1,0:T(8,128)(2,1)}, bf16[320,1024]{1,0:T(8,128)(2,1)S(1)}, u32[]{:S(2)}, u32[]{:S(2)}) collective-permute-start(bf16[320,1024]{1,0:T(8,128)(2,1)} %collective-permute-done.11), channel_id=1, source_target_pairs={{0,1},{1,2},{2,3},{3,4},{4,5},{5,6},{6,7},{7,8},{8,9},{9,10},{10,1... | collective-permute-start | bytes 1966088 | tf_op jit(solution)/shard_map/ppermute | solution.py:155
  64.5 4.9 %collective-permute-start.4 = (bf16[320,1024]{1,0:T(8,128)(2,1)S(1)}, bf16[320,1024]{1,0:T(8,128)(2,1)}, u32[]{:S(2)}, u32[]{:S(2)}) collective-permute-start(bf16[320,1024]{1,0:T(8,128)(2,1)S(1)} %collective-permute-done.3), channel_id=1, source_target_pairs={{0,1},{1,2},{2,3},{3,4},{4,5},{5,6},{6,7},{7,8},{8,9},{9,10},{10,1... | collective-permute-start | bytes 1966088 | tf_op jit(solution)/shard_map/ppermute | solution.py:155
  70.6 7.2 %all-to-all-start.3 = ((f32[32,16,640]{2,1,0:T(8,128)}), f32[32,16,640]{2,1,0:T(8,128)S(1)}, u32[]{:S(2)}, u32[]{:S(2)}) async-start(f32[32,16,640]{2,1,0:T(8,128)} %pad_maximum_fusion.3), calls=%async_computation.3 | async-start | bytes 2621440 | tf_op jit(solution)/shard_map/all_to_all | solution.py:186
  90.3 4.1 %collective-permute-start.14 = (bf16[320,1024]{1,0:T(8,128)(2,1)}, bf16[320,1024]{1,0:T(8,128)(2,1)}, u32[]{:S(2)}, u32[]{:S(2)}) collective-permute-start(bf16[320,1024]{1,0:T(8,128)(2,1)} %collective-permute-done.13), channel_id=1, source_target_pairs={{0,1},{1,2},{2,3},{3,4},{4,5},{5,6},{6,7},{7,8},{8,9},{9,10},{10,1... | collective-permute-start | bytes 1966088 | tf_op jit(solution)/shard_map/ppermute | solution.py:155
  96.9 6.0 %all-to-all-start.2 = ((f32[32,16,640]{2,1,0:T(8,128)}), f32[32,16,640]{2,1,0:T(8,128)S(1)}, u32[]{:S(2)}, u32[]{:S(2)}) async-start(f32[32,16,640]{2,1,0:T(8,128)} %pad_maximum_fusion.2), calls=%async_computation.2 | async-start | bytes 2621440 | tf_op jit(solution)/shard_map/all_to_all | solution.py:186
  102.9 5.0 %collective-permute-start.6 = (bf16[320,1024]{1,0:T(8,128)(2,1)S(1)}, bf16[320,1024]{1,0:T(8,128)(2,1)}, u32[]{:S(2)}, u32[]{:S(2)}) collective-permute-start(bf16[320,1024]{1,0:T(8,128)(2,1)S(1)} %collective-permute-done.5), channel_id=1, source_target_pairs={{0,1},{1,2},{2,3},{3,4},{4,5},{5,6},{6,7},{7,8},{8,9},{9,10},{10,1... | collective-permute-start | bytes 1966088 | tf_op jit(solution)/shard_map/ppermute | solution.py:155
  117.3 4.7 %all-to-all-done.2.refs_1_ = f32[32,16,640]{2,1,0:T(8,128)S(1)} async-done(((f32[32,16,640]{2,1,0:T(8,128)}), f32[32,16,640]{2,1,0:T(8,128)S(1)}, u32[]{:S(2)}, u32[]{:S(2)}) %all-to-all-start.2) | async-done | bytes 1310752 | tf_op jit(solution)/shard_map/all_to_all | solution.py:186
  121.9 6.2 %all-to-all-start.1 = ((f32[32,16,640]{2,1,0:T(8,128)}), f32[32,16,640]{2,1,0:T(8,128)}, u32[]{:S(2)}, u32[]{:S(2)}) async-start(f32[32,16,640]{2,1,0:T(8,128)} %pad_maximum_fusion.1), calls=%async_computation.1 | async-start | bytes 2621440 | tf_op jit(solution)/shard_map/all_to_all | solution.py:186
  129.3 4.9 %collective-permute-start.7 = (bf16[160,1024]{1,0:T(8,128)(2,1)S(1)}, bf16[160,1024]{1,0:T(8,128)(2,1)S(1)}, u32[]{:S(2)}, u32[]{:S(2)}) collective-permute-start(bf16[160,1024]{1,0:T(8,128)(2,1)S(1)} %constant_dynamic-slice_fusion.2), channel_id=1, source_target_pairs={{0,1},{1,2},{2,3},{3,4},{4,5},{5,6},{6,7},{7,8},{8,9},{9,10},{10,1... | collective-permute-start | bytes 983048 | tf_op jit(solution)/shard_map/ppermute | solution.py:155
  147.4 6.3 %all-to-all-start = ((f32[32,16,640]{2,1,0:T(8,128)}), f32[32,16,640]{2,1,0:T(8,128)}, u32[]{:S(2)}, u32[]{:S(2)}) async-start(f32[32,16,640]{2,1,0:T(8,128)} %pad_maximum_fusion), calls=%async_computation | async-start | bytes 2621440 | tf_op jit(solution)/shard_map/all_to_all | solution.py:186
  158.0 3.5 %shard_map.30.before_ref = f32[8,128]{1,0:T(8,128)S(1)} custom-call(f32[16,32,640]{2,1,0:T(8,128)} %bitcast.11.block_ref, f32[8,128]{1,0:T(8,128)S(1)} %shard_map.29.before_ref), custom_call_target="tpu_custom_call" | custom-call | flops 1006632960 | bytes 1310720 | tf_op jit(solution)/shard_map/pallas_call | solution.py:48
  161.5 11.4 %all-to-all-done.refs_3_ = f32[32,16,640]{2,1,0:T(8,128)} async-done(((f32[32,16,640]{2,1,0:T(8,128)}), f32[32,16,640]{2,1,0:T(8,128)}, u32[]{:S(2)}, u32[]{:S(2)}) %all-to-all-start) | async-done | bytes 1310752 | tf_op jit(solution)/shard_map/all_to_all | solution.py:186
  176.4 13.0 %all_to_all.35.parts_ref = f32[32,8,128]{2,1,0:T(8,128)} all-to-all(f32[32,8,128]{2,1,0:T(8,128)S(1)} %broadcast_in_dim.7), channel_id=1, replica_groups=mesh['dp'=32,'tensor'=16] {'dp'}, dimensions={0} | all-to-all | bytes 262144 | tf_op jit(solution)/shard_map/all_to_all | solution.py:190
  190.9 8.5 %all-to-all-start.5 = ((f32[16,8,128]{2,1,0:T(8,128)}), f32[16,8,128]{2,1,0:T(8,128)S(1)}, u32[]{:S(2)}, u32[]{:S(2)}) async-start(f32[16,8,128]{2,1,0:T(8,128)} %shard_map.32), calls=%async_computation.5 | async-start | bytes 131072 | tf_op jit(solution)/shard_map/all_to_all | solution.py:191
  199.4 11.6 %all-to-all-done.5.parts_ref = f32[16,8,128]{2,1,0:T(8,128)S(1)} async-done(((f32[16,8,128]{2,1,0:T(8,128)}), f32[16,8,128]{2,1,0:T(8,128)S(1)}, u32[]{:S(2)}, u32[]{:S(2)}) %all-to-all-start.5) | async-done | bytes 65568 | tf_op jit(solution)/shard_map/all_to_all | solution.py:191
  213.7 14.1 %all_to_all.36 = f32[32,8,160]{2,1,0:T(8,128)S(1)} all-to-all(f32[32,8,160]{2,1,0:T(8,128)S(1)} %shard_map.33), channel_id=1, replica_groups=mesh['dp'=32,'tensor'=16] {'dp'}, dimensions={0} | all-to-all | bytes 327680 | tf_op jit(solution)/shard_map/all_to_all | solution.py:193
  (79 shorter events, 68.1 us)
Async XLA Ops:
  0.0 14.5 %collective-permute-start.8 = (bf16[320,1024]{1,0:T(8,128)(2,1)}, bf16[320,1024]{1,0:T(8,128)(2,1)S(1)}, u32[]{:S(2)}, u32[]{:S(2)}) collective-permute-start(bf16[320,1024]{1,0:T(8,128)(2,1)} %bitcast.53), channel_id=1, source_target_pairs={{0,16},{16,0},{32,48},{48,32},{64,80},{80,64},{96,112},{112,96},{1... | collective-permute-start | bytes 1966088 | tf_op jit(solution)/shard_map/ppermute | solution.py:158
  8.8 13.6 %collective-permute-start = (bf16[320,1024]{1,0:T(8,128)(2,1)}, bf16[320,1024]{1,0:T(8,128)(2,1)S(1)}, u32[]{:S(2)}, u32[]{:S(2)}) collective-permute-start(bf16[320,1024]{1,0:T(8,128)(2,1)} %bitcast.54), channel_id=1, source_target_pairs={{0,1},{1,2},{2,3},{3,4},{4,5},{5,6},{6,7},{7,8},{8,9},{9,10},{10,1... | collective-permute-start | bytes 1966088 | tf_op jit(solution)/shard_map/ppermute | solution.py:155
  14.5 14.7 %collective-permute-start.9 = (bf16[320,1024]{1,0:T(8,128)(2,1)S(1)}, bf16[320,1024]{1,0:T(8,128)(2,1)S(1)}, u32[]{:S(2)}, u32[]{:S(2)}) collective-permute-start(bf16[320,1024]{1,0:T(8,128)(2,1)S(1)} %collective-permute-done.8), channel_id=1, source_target_pairs={{0,1},{1,2},{2,3},{3,4},{4,5},{5,6},{6,7},{7,8},{8,9},{9,10},{10,1... | collective-permute-start | bytes 1966088 | tf_op jit(solution)/shard_map/ppermute | solution.py:155
  22.4 13.9 %collective-permute-start.1 = (bf16[320,1024]{1,0:T(8,128)(2,1)S(1)}, bf16[320,1024]{1,0:T(8,128)(2,1)S(1)}, u32[]{:S(2)}, u32[]{:S(2)}) collective-permute-start(bf16[320,1024]{1,0:T(8,128)(2,1)S(1)} %collective-permute-done), channel_id=1, source_target_pairs={{0,1},{1,2},{2,3},{3,4},{4,5},{5,6},{6,7},{7,8},{8,9},{9,10},{10,1... | collective-permute-start | bytes 1966088 | tf_op jit(solution)/shard_map/ppermute | solution.py:155
  29.3 15.2 %copy-start.5 = (bf16[320,1024]{1,0:T(8,128)(2,1)}, bf16[320,1024]{1,0:T(8,128)(2,1)S(1)}, u32[]{:S(2)}) copy-start(bf16[320,1024]{1,0:T(8,128)(2,1)S(1)} %collective-permute-done.9) | copy-start | bytes 1966084
  29.3 15.2 %collective-permute-start.10 = (bf16[320,1024]{1,0:T(8,128)(2,1)S(1)}, bf16[320,1024]{1,0:T(8,128)(2,1)S(1)}, u32[]{:S(2)}, u32[]{:S(2)}) collective-permute-start(bf16[320,1024]{1,0:T(8,128)(2,1)S(1)} %collective-permute-done.9), channel_id=1, source_target_pairs={{0,1},{1,2},{2,3},{3,4},{4,5},{5,6},{6,7},{7,8},{8,9},{9,10},{10,1... | collective-permute-start | bytes 1966088 | tf_op jit(solution)/shard_map/ppermute | solution.py:155
  36.3 14.0 %collective-permute-start.2 = (bf16[320,1024]{1,0:T(8,128)(2,1)S(1)}, bf16[320,1024]{1,0:T(8,128)(2,1)}, u32[]{:S(2)}, u32[]{:S(2)}) collective-permute-start(bf16[320,1024]{1,0:T(8,128)(2,1)S(1)} %collective-permute-done.1), channel_id=1, source_target_pairs={{0,1},{1,2},{2,3},{3,4},{4,5},{5,6},{6,7},{7,8},{8,9},{9,10},{10,1... | collective-permute-start | bytes 1966088 | tf_op jit(solution)/shard_map/ppermute | solution.py:155
  41.3 21.2 %collective-permute-start.17 = (bf16[1024,256]{1,0:T(8,128)(2,1)}, bf16[1024,256]{1,0:T(8,128)(2,1)}, u32[]{:S(2)}, u32[]{:S(2)}) collective-permute-start(bf16[1024,256]{1,0:T(8,128)(2,1)} %param.3), channel_id=1, source_target_pairs={{0,16},{16,0},{32,48},{48,32},{64,80},{80,64},{96,112},{112,96},{1... | collective-permute-start | bytes 1572872 | tf_op jit(solution)/shard_map/ppermute | solution.py:159
  44.5 12.9 %collective-permute-start.11 = (bf16[320,1024]{1,0:T(8,128)(2,1)S(1)}, bf16[320,1024]{1,0:T(8,128)(2,1)}, u32[]{:S(2)}, u32[]{:S(2)}) collective-permute-start(bf16[320,1024]{1,0:T(8,128)(2,1)S(1)} %collective-permute-done.10), channel_id=1, source_target_pairs={{0,1},{1,2},{2,3},{3,4},{4,5},{5,6},{6,7},{7,8},{8,9},{9,10},{10,1... | collective-permute-start | bytes 1966088 | tf_op jit(solution)/shard_map/ppermute | solution.py:155
  50.3 14.1 %collective-permute-start.3 = (bf16[320,1024]{1,0:T(8,128)(2,1)}, bf16[320,1024]{1,0:T(8,128)(2,1)S(1)}, u32[]{:S(2)}, u32[]{:S(2)}) collective-permute-start(bf16[320,1024]{1,0:T(8,128)(2,1)} %collective-permute-done.2), channel_id=1, source_target_pairs={{0,1},{1,2},{2,3},{3,4},{4,5},{5,6},{6,7},{7,8},{8,9},{9,10},{10,1... | collective-permute-start | bytes 1966088 | tf_op jit(solution)/shard_map/ppermute | solution.py:155
  57.4 21.2 %collective-permute-start.12 = (bf16[320,1024]{1,0:T(8,128)(2,1)}, bf16[320,1024]{1,0:T(8,128)(2,1)S(1)}, u32[]{:S(2)}, u32[]{:S(2)}) collective-permute-start(bf16[320,1024]{1,0:T(8,128)(2,1)} %collective-permute-done.11), channel_id=1, source_target_pairs={{0,1},{1,2},{2,3},{3,4},{4,5},{5,6},{6,7},{7,8},{8,9},{9,10},{10,1... | collective-permute-start | bytes 1966088 | tf_op jit(solution)/shard_map/ppermute | solution.py:155
  64.5 18.8 %collective-permute-start.4 = (bf16[320,1024]{1,0:T(8,128)(2,1)S(1)}, bf16[320,1024]{1,0:T(8,128)(2,1)}, u32[]{:S(2)}, u32[]{:S(2)}) collective-permute-start(bf16[320,1024]{1,0:T(8,128)(2,1)S(1)} %collective-permute-done.3), channel_id=1, source_target_pairs={{0,1},{1,2},{2,3},{3,4},{4,5},{5,6},{6,7},{7,8},{8,9},{9,10},{10,1... | collective-permute-start | bytes 1966088 | tf_op jit(solution)/shard_map/ppermute | solution.py:155
  70.6 26.3 %all-to-all-start.3 = ((f32[32,16,640]{2,1,0:T(8,128)}), f32[32,16,640]{2,1,0:T(8,128)S(1)}, u32[]{:S(2)}, u32[]{:S(2)}) async-start(f32[32,16,640]{2,1,0:T(8,128)} %pad_maximum_fusion.3), calls=%async_computation.3 | async-start | bytes 2621440 | tf_op jit(solution)/shard_map/all_to_all | solution.py:186
  78.6 11.7 %collective-permute-start.13 = (bf16[320,1024]{1,0:T(8,128)(2,1)S(1)}, bf16[320,1024]{1,0:T(8,128)(2,1)}, u32[]{:S(2)}, u32[]{:S(2)}) collective-permute-start(bf16[320,1024]{1,0:T(8,128)(2,1)S(1)} %collective-permute-done.12), channel_id=1, source_target_pairs={{0,1},{1,2},{2,3},{3,4},{4,5},{5,6},{6,7},{7,8},{8,9},{9,10},{10,1... | collective-permute-start | bytes 1966088 | tf_op jit(solution)/shard_map/ppermute | solution.py:155
  83.3 19.6 %collective-permute-start.5 = (bf16[320,1024]{1,0:T(8,128)(2,1)}, bf16[320,1024]{1,0:T(8,128)(2,1)S(1)}, u32[]{:S(2)}, u32[]{:S(2)}) collective-permute-start(bf16[320,1024]{1,0:T(8,128)(2,1)} %collective-permute-done.4), channel_id=1, source_target_pairs={{0,1},{1,2},{2,3},{3,4},{4,5},{5,6},{6,7},{7,8},{8,9},{9,10},{10,1... | collective-permute-start | bytes 1966088 | tf_op jit(solution)/shard_map/ppermute | solution.py:155
  90.3 20.1 %collective-permute-start.14 = (bf16[320,1024]{1,0:T(8,128)(2,1)}, bf16[320,1024]{1,0:T(8,128)(2,1)}, u32[]{:S(2)}, u32[]{:S(2)}) collective-permute-start(bf16[320,1024]{1,0:T(8,128)(2,1)} %collective-permute-done.13), channel_id=1, source_target_pairs={{0,1},{1,2},{2,3},{3,4},{4,5},{5,6},{6,7},{7,8},{8,9},{9,10},{10,1... | collective-permute-start | bytes 1966088 | tf_op jit(solution)/shard_map/ppermute | solution.py:155
  96.9 25.1 %all-to-all-start.2 = ((f32[32,16,640]{2,1,0:T(8,128)}), f32[32,16,640]{2,1,0:T(8,128)S(1)}, u32[]{:S(2)}, u32[]{:S(2)}) async-start(f32[32,16,640]{2,1,0:T(8,128)} %pad_maximum_fusion.2), calls=%async_computation.2 | async-start | bytes 2621440 | tf_op jit(solution)/shard_map/all_to_all | solution.py:186
  102.9 25.3 %collective-permute-start.6 = (bf16[320,1024]{1,0:T(8,128)(2,1)S(1)}, bf16[320,1024]{1,0:T(8,128)(2,1)}, u32[]{:S(2)}, u32[]{:S(2)}) collective-permute-start(bf16[320,1024]{1,0:T(8,128)(2,1)S(1)} %collective-permute-done.5), channel_id=1, source_target_pairs={{0,1},{1,2},{2,3},{3,4},{4,5},{5,6},{6,7},{7,8},{8,9},{9,10},{10,1... | collective-permute-start | bytes 1966088 | tf_op jit(solution)/shard_map/ppermute | solution.py:155
  112.3 21.8 %collective-permute-start.15 = (bf16[320,1024]{1,0:T(8,128)(2,1)}, bf16[320,1024]{1,0:T(8,128)(2,1)}, u32[]{:S(2)}, u32[]{:S(2)}) collective-permute-start(bf16[320,1024]{1,0:T(8,128)(2,1)} %collective-permute-done.14), channel_id=1, source_target_pairs={{0,1},{1,2},{2,3},{3,4},{4,5},{5,6},{6,7},{7,8},{8,9},{9,10},{10,1... | collective-permute-start | bytes 1966088 | tf_op jit(solution)/shard_map/ppermute | solution.py:155
  121.9 25.4 %all-to-all-start.1 = ((f32[32,16,640]{2,1,0:T(8,128)}), f32[32,16,640]{2,1,0:T(8,128)}, u32[]{:S(2)}, u32[]{:S(2)}) async-start(f32[32,16,640]{2,1,0:T(8,128)} %pad_maximum_fusion.1), calls=%async_computation.1 | async-start | bytes 2621440 | tf_op jit(solution)/shard_map/all_to_all | solution.py:186
  129.3 8.9 %collective-permute-start.7 = (bf16[160,1024]{1,0:T(8,128)(2,1)S(1)}, bf16[160,1024]{1,0:T(8,128)(2,1)S(1)}, u32[]{:S(2)}, u32[]{:S(2)}) collective-permute-start(bf16[160,1024]{1,0:T(8,128)(2,1)S(1)} %constant_dynamic-slice_fusion.2), channel_id=1, source_target_pairs={{0,1},{1,2},{2,3},{3,4},{4,5},{5,6},{6,7},{7,8},{8,9},{9,10},{10,1... | collective-permute-start | bytes 983048 | tf_op jit(solution)/shard_map/ppermute | solution.py:155
  135.1 8.2 %collective-permute-start.16 = (bf16[160,1024]{1,0:T(8,128)(2,1)S(1)}, bf16[160,1024]{1,0:T(8,128)(2,1)S(1)}, u32[]{:S(2)}, u32[]{:S(2)}) collective-permute-start(bf16[160,1024]{1,0:T(8,128)(2,1)S(1)} %constant_dynamic-slice_fusion.1), channel_id=1, source_target_pairs={{0,1},{1,2},{2,3},{3,4},{4,5},{5,6},{6,7},{7,8},{8,9},{9,10},{10,1... | collective-permute-start | bytes 983048 | tf_op jit(solution)/shard_map/ppermute | solution.py:155
  147.4 25.5 %all-to-all-start = ((f32[32,16,640]{2,1,0:T(8,128)}), f32[32,16,640]{2,1,0:T(8,128)}, u32[]{:S(2)}, u32[]{:S(2)}) async-start(f32[32,16,640]{2,1,0:T(8,128)} %pad_maximum_fusion), calls=%async_computation | async-start | bytes 2621440 | tf_op jit(solution)/shard_map/all_to_all | solution.py:186
  190.9 20.1 %all-to-all-start.5 = ((f32[16,8,128]{2,1,0:T(8,128)}), f32[16,8,128]{2,1,0:T(8,128)S(1)}, u32[]{:S(2)}, u32[]{:S(2)}) async-start(f32[16,8,128]{2,1,0:T(8,128)} %shard_map.32), calls=%async_computation.5 | async-start | bytes 131072 | tf_op jit(solution)/shard_map/all_to_all | solution.py:191
  (11 other events, 88.7 us)

commit v7 on v6

--- a/solution.py
+++ b/solution.py
@@ -157,14 +157,20 @@
     mine = activations.T
     chains = [mine, lax.ppermute(mine, "dp", sibling)]
     grads = [out_grads, lax.ppermute(out_grads, "dp", sibling)]
+    chains[1], grads[1] = lax.optimization_barrier((chains[1], grads[1]))
     held = [[own_half(slab)] for slab in chains]
     order = [[(0, 0)], [(0, 1)]]
     blocks = []
     gram = jnp.zeros((8, 128), jnp.float32)
     sizes = list(GROUPS)
+    ready = None
     for step in range(1, half + 1):
         if step < half:
             chains = [move(slab) for slab in chains]
+            if ready is not None:
+                chains[0], ready = lax.optimization_barrier((chains[0], ready))
+                blocks.append(lax.all_to_all(ready, "dp", 0, 0))
+                ready = None
             for k in range(2):
                 held[k] += [chains[k][:rows], chains[k][rows:]]
             order[0] += [(slabs - step, 0), (slabs - step, 1)]
@@ -183,9 +189,10 @@
                     preferred_element_type=jnp.float32,
                 )
                 parts.append(grad.reshape(replicas, part, -1))
-            block = lax.all_to_all(jnp.concatenate(parts, axis=1), "dp", 0, 0)
-            gram = gram_add(replicas, block, gram)
-            blocks.append(block)
+            ready = jnp.concatenate(parts, axis=1)
+    blocks.append(lax.all_to_all(ready, "dp", 0, 0))
+    for block in blocks:
+        gram = gram_add(replicas, block, gram)
     peers = jnp.broadcast_to(gram, (replicas, *gram.shape))
     parts = sum_and_spread(lax.all_to_all(peers, "dp", 0, 0), slabs)
     parts = lax.all_to_all(parts, "tensor", 0, 0)

time: 230 us -> 230 us (level)
  transfers between devices with their start and end apart: 23 -> 23, of which waited for: 14 -> 13; matrix products, arithmetic and copies ran while one was open for 11% -> 11% of each run, Pallas kernels for 3% -> 3%
where the time goes in v7:
time: 230 us; the launch traced here: 228 us
  starting transfers between devices  113 us (49%)
  waiting for transfers between devices  46.5 us (20%)
  blocking collectives  27.1 us (12%)
  Pallas kernels  15.4 us (7%)
  matrix products  12.7 us (6%)
  local copies, waits for them, and re-layouts  8.23 us (4%)
  other arithmetic  4.65 us (2%)
    ppermute x16, starting transfers between devices, move(): return lax.ppermute(slab, ('dp', 'tensor'), onward)  66.8 us
    all_to_all x4, starting transfers between devices, on_device(): blocks.append(lax.all_to_all(ready, 'dp', 0, 0))  26.6 us
    all_to_all x4, waiting for transfers between devices, on_device(): blocks.append(lax.all_to_all(ready, 'dp', 0, 0))  17.7 us
    ppermute x16, waiting for transfers between devices, move(): return lax.ppermute(slab, ('dp', 'tensor'), onward)  17.3 us
    all_to_all x1, blocking collectives, on_device(): home = lax.all_to_all(home, 'dp', 0, 0)  14.1 us
    all_to_all x1, blocking collectives, on_device(): parts = sum_and_spread(lax.all_to_all(peers, 'dp', 0, 0), slabs)  13 us
    dot_general x8, matrix products, on_device(): lax.dot_general(grads[k], jnp.concatenate(group, axis=0), (((0,), (1,)),...  12.7 us
    all_to_all x1, waiting for transfers between devices, on_device(): parts = lax.all_to_all(parts, 'tensor', 0, 0)  11.6 us
  transfers between devices with their start and end apart: 23, of which 13 were waited for; matrix products, arithmetic and copies ran while one was open for 11% of the time, Pallas kernels for 3%

profile of v7, /device:TPU:1, one launch (start us, length us, event | category | flops | bytes accessed | tf_op | source)
XLA Modules:
  0.0 227.9 jit_solution(8481530324907197324)
XLA Ops:
  0.0 8.8 %collective-permute-start.3 = (bf16[320,1024]{1,0:T(8,128)(2,1)}, bf16[320,1024]{1,0:T(8,128)(2,1)S(1)}, u32[]{:S(2)}, u32[]{:S(2)}) collective-permute-start(bf16[320,1024]{1,0:T(8,128)(2,1)} %bitcast.45), channel_id=1, source_target_pairs={{0,16},{16,0},{32,48},{48,32},{64,80},{80,64},{96,112},{112,96},{1... | collective-permute-start | bytes 1966088 | tf_op jit(solution)/shard_map/ppermute | solution.py:158
  10.7 5.8 %collective-permute-start = (bf16[320,1024]{1,0:T(8,128)(2,1)}, bf16[320,1024]{1,0:T(8,128)(2,1)}, u32[]{:S(2)}, u32[]{:S(2)}) collective-permute-start(bf16[320,1024]{1,0:T(8,128)(2,1)} %bitcast.46), channel_id=1, source_target_pairs={{0,1},{1,2},{2,3},{3,4},{4,5},{5,6},{6,7},{7,8},{8,9},{9,10},{10,1... | collective-permute-start | bytes 1966088 | tf_op jit(solution)/shard_map/ppermute | solution.py:155
  19.1 5.1 %collective-permute-done = bf16[320,1024]{1,0:T(8,128)(2,1)} collective-permute-done((bf16[320,1024]{1,0:T(8,128)(2,1)}, bf16[320,1024]{1,0:T(8,128)(2,1)}, u32[]{:S(2)}, u32[]{:S(2)}) %collective-permute-start) | collective-permute-done | bytes 655392 | tf_op jit(solution)/shard_map/ppermute | solution.py:155
  24.3 5.0 %collective-permute-start.1 = (bf16[320,1024]{1,0:T(8,128)(2,1)}, bf16[320,1024]{1,0:T(8,128)(2,1)S(1)}, u32[]{:S(2)}, u32[]{:S(2)}) collective-permute-start(bf16[320,1024]{1,0:T(8,128)(2,1)} %collective-permute-done), channel_id=1, source_target_pairs={{0,1},{1,2},{2,3},{3,4},{4,5},{5,6},{6,7},{7,8},{8,9},{9,10},{10,1... | collective-permute-start | bytes 1966088 | tf_op jit(solution)/shard_map/ppermute | solution.py:155
  31.2 5.0 %collective-permute-start.6 = (bf16[320,1024]{1,0:T(8,128)(2,1)S(1)}, bf16[320,1024]{1,0:T(8,128)(2,1)S(1)}, u32[]{:S(2)}, u32[]{:S(2)}) collective-permute-start(bf16[320,1024]{1,0:T(8,128)(2,1)S(1)} %collective-permute-done.5), channel_id=1, source_target_pairs={{0,1},{1,2},{2,3},{3,4},{4,5},{5,6},{6,7},{7,8},{8,9},{9,10},{10,1... | collective-permute-start | bytes 1966088 | tf_op jit(solution)/shard_map/ppermute | solution.py:155
  38.3 4.9 %collective-permute-start.2 = (bf16[320,1024]{1,0:T(8,128)(2,1)S(1)}, bf16[320,1024]{1,0:T(8,128)(2,1)}, u32[]{:S(2)}, u32[]{:S(2)}) collective-permute-start(bf16[320,1024]{1,0:T(8,128)(2,1)S(1)} %collective-permute-done.1), channel_id=1, source_target_pairs={{0,1},{1,2},{2,3},{3,4},{4,5},{5,6},{6,7},{7,8},{8,9},{9,10},{10,1... | collective-permute-start | bytes 1966088 | tf_op jit(solution)/shard_map/ppermute | solution.py:155
  45.3 5.0 %collective-permute-start.9 = (bf16[320,1024]{1,0:T(8,128)(2,1)S(1)}, bf16[320,1024]{1,0:T(8,128)(2,1)}, u32[]{:S(2)}, u32[]{:S(2)}) collective-permute-start(bf16[320,1024]{1,0:T(8,128)(2,1)S(1)} %collective-permute-done.6), channel_id=1, source_target_pairs={{0,1},{1,2},{2,3},{3,4},{4,5},{5,6},{6,7},{7,8},{8,9},{9,10},{10,1... | collective-permute-start | bytes 1966088 | tf_op jit(solution)/shard_map/ppermute | solution.py:155
  52.3 5.1 %collective-permute-start.7 = (bf16[320,1024]{1,0:T(8,128)(2,1)}, bf16[320,1024]{1,0:T(8,128)(2,1)S(1)}, u32[]{:S(2)}, u32[]{:S(2)}) collective-permute-start(bf16[320,1024]{1,0:T(8,128)(2,1)} %collective-permute-done.2), channel_id=1, source_target_pairs={{0,1},{1,2},{2,3},{3,4},{4,5},{5,6},{6,7},{7,8},{8,9},{9,10},{10,1... | collective-permute-start | bytes 1966088 | tf_op jit(solution)/shard_map/ppermute | solution.py:155
  59.3 5.1 %collective-permute-start.10 = (bf16[320,1024]{1,0:T(8,128)(2,1)}, bf16[320,1024]{1,0:T(8,128)(2,1)S(1)}, u32[]{:S(2)}, u32[]{:S(2)}) collective-permute-start(bf16[320,1024]{1,0:T(8,128)(2,1)} %collective-permute-done.9), channel_id=1, source_target_pairs={{0,1},{1,2},{2,3},{3,4},{4,5},{5,6},{6,7},{7,8},{8,9},{9,10},{10,1... | collective-permute-start | bytes 1966088 | tf_op jit(solution)/shard_map/ppermute | solution.py:155
  64.4 7.2 %all-to-all-start.3 = ((f32[32,16,640]{2,1,0:T(8,128)}), f32[32,16,640]{2,1,0:T(8,128)S(1)}, u32[]{:S(2)}, u32[]{:S(2)}) async-start(f32[32,16,640]{2,1,0:T(8,128)} %pad_maximum_fusion), calls=%async_computation.3 | async-start | bytes 2621440 | tf_op jit(solution)/shard_map/all_to_all | solution.py:172
  71.7 3.6 %collective-permute-start.8 = (bf16[320,1024]{1,0:T(8,128)(2,1)S(1)}, bf16[320,1024]{1,0:T(8,128)(2,1)}, u32[]{:S(2)}, u32[]{:S(2)}) collective-permute-start(bf16[320,1024]{1,0:T(8,128)(2,1)S(1)} %collective-permute-done.7), channel_id=1, source_target_pairs={{0,1},{1,2},{2,3},{3,4},{4,5},{5,6},{6,7},{7,8},{8,9},{9,10},{10,1... | collective-permute-start | bytes 1966088 | tf_op jit(solution)/shard_map/ppermute | solution.py:155
  84.1 4.0 %collective-permute-start.11 = (bf16[320,1024]{1,0:T(8,128)(2,1)}, bf16[320,1024]{1,0:T(8,128)(2,1)}, u32[]{:S(2)}, u32[]{:S(2)}) collective-permute-start(bf16[320,1024]{1,0:T(8,128)(2,1)} %collective-permute-done.8), channel_id=1, source_target_pairs={{0,1},{1,2},{2,3},{3,4},{4,5},{5,6},{6,7},{7,8},{8,9},{9,10},{10,1... | collective-permute-start | bytes 1966088 | tf_op jit(solution)/shard_map/ppermute | solution.py:155
  90.6 4.5 %collective-permute-start.14 = (bf16[320,1024]{1,0:T(8,128)(2,1)}, bf16[320,1024]{1,0:T(8,128)(2,1)S(1)}, u32[]{:S(2)}, u32[]{:S(2)}) collective-permute-start(bf16[320,1024]{1,0:T(8,128)(2,1)} %collective-permute-done.13), channel_id=1, source_target_pairs={{0,1},{1,2},{2,3},{3,4},{4,5},{5,6},{6,7},{7,8},{8,9},{9,10},{10,1... | collective-permute-start | bytes 1966088 | tf_op jit(solution)/shard_map/ppermute | solution.py:155
  95.1 7.0 %all-to-all-start.2 = ((f32[32,16,640]{2,1,0:T(8,128)}), f32[32,16,640]{2,1,0:T(8,128)S(1)}, u32[]{:S(2)}, u32[]{:S(2)}) async-start(f32[32,16,640]{2,1,0:T(8,128)} %pad_maximum_fusion.1), calls=%async_computation.2 | async-start | bytes 2621440 | tf_op jit(solution)/shard_map/all_to_all | solution.py:172
  102.1 4.8 %collective-permute-start.12 = (bf16[320,1024]{1,0:T(8,128)(2,1)}, bf16[320,1024]{1,0:T(8,128)(2,1)}, u32[]{:S(2)}, u32[]{:S(2)}) collective-permute-start(bf16[320,1024]{1,0:T(8,128)(2,1)} %collective-permute-done.11), channel_id=1, source_target_pairs={{0,1},{1,2},{2,3},{3,4},{4,5},{5,6},{6,7},{7,8},{8,9},{9,10},{10,1... | collective-permute-start | bytes 1966088 | tf_op jit(solution)/shard_map/ppermute | solution.py:155
  116.3 4.9 %all-to-all-done.2.refs_1_ = f32[32,16,640]{2,1,0:T(8,128)S(1)} async-done(((f32[32,16,640]{2,1,0:T(8,128)}), f32[32,16,640]{2,1,0:T(8,128)S(1)}, u32[]{:S(2)}, u32[]{:S(2)}) %all-to-all-start.2) | async-done | bytes 1310752 | tf_op jit(solution)/shard_map/all_to_all | solution.py:172
  121.2 6.2 %all-to-all-start.1 = ((f32[32,16,640]{2,1,0:T(8,128)}), f32[32,16,640]{2,1,0:T(8,128)}, u32[]{:S(2)}, u32[]{:S(2)}) async-start(f32[32,16,640]{2,1,0:T(8,128)} %pad_maximum_fusion.2), calls=%async_computation.1 | async-start | bytes 2621440 | tf_op jit(solution)/shard_map/all_to_all | solution.py:172
  128.5 4.7 %collective-permute-start.15 = (bf16[160,1024]{1,0:T(8,128)(2,1)S(1)}, bf16[160,1024]{1,0:T(8,128)(2,1)S(1)}, u32[]{:S(2)}, u32[]{:S(2)}) collective-permute-start(bf16[160,1024]{1,0:T(8,128)(2,1)S(1)} %constant_dynamic-slice_fusion.1), channel_id=1, source_target_pairs={{0,1},{1,2},{2,3},{3,4},{4,5},{5,6},{6,7},{7,8},{8,9},{9,10},{10,1... | collective-permute-start | bytes 983048 | tf_op jit(solution)/shard_map/ppermute | solution.py:155
  146.6 6.3 %all-to-all-start = ((f32[32,16,640]{2,1,0:T(8,128)}), f32[32,16,640]{2,1,0:T(8,128)}, u32[]{:S(2)}, u32[]{:S(2)}) async-start(f32[32,16,640]{2,1,0:T(8,128)} %pad_maximum_fusion.3), calls=%async_computation | async-start | bytes 2621440 | tf_op jit(solution)/shard_map/all_to_all | solution.py:193
  160.6 11.5 %all-to-all-done.refs_3_ = f32[32,16,640]{2,1,0:T(8,128)} async-done(((f32[32,16,640]{2,1,0:T(8,128)}), f32[32,16,640]{2,1,0:T(8,128)}, u32[]{:S(2)}, u32[]{:S(2)}) %all-to-all-start) | async-done | bytes 1310752 | tf_op jit(solution)/shard_map/all_to_all | solution.py:193
  175.6 13.0 %all_to_all.35.parts_ref = f32[32,8,128]{2,1,0:T(8,128)} all-to-all(f32[32,8,128]{2,1,0:T(8,128)S(1)} %broadcast_in_dim.7), channel_id=1, replica_groups=mesh['dp'=32,'tensor'=16] {'dp'}, dimensions={0} | all-to-all | bytes 262144 | tf_op jit(solution)/shard_map/all_to_all | solution.py:197
  190.1 8.6 %all-to-all-start.5 = ((f32[16,8,128]{2,1,0:T(8,128)}), f32[16,8,128]{2,1,0:T(8,128)S(1)}, u32[]{:S(2)}, u32[]{:S(2)}) async-start(f32[16,8,128]{2,1,0:T(8,128)} %shard_map.32), calls=%async_computation.5 | async-start | bytes 131072 | tf_op jit(solution)/shard_map/all_to_all | solution.py:198
  198.8 11.6 %all-to-all-done.5.parts_ref = f32[16,8,128]{2,1,0:T(8,128)S(1)} async-done(((f32[16,8,128]{2,1,0:T(8,128)}), f32[16,8,128]{2,1,0:T(8,128)S(1)}, u32[]{:S(2)}, u32[]{:S(2)}) %all-to-all-start.5) | async-done | bytes 65568 | tf_op jit(solution)/shard_map/all_to_all | solution.py:198
  213.1 14.1 %all_to_all.36 = f32[32,8,160]{2,1,0:T(8,128)S(1)} all-to-all(f32[32,8,160]{2,1,0:T(8,128)S(1)} %shard_map.33), channel_id=1, replica_groups=mesh['dp'=32,'tensor'=16] {'dp'}, dimensions={0} | all-to-all | bytes 327680 | tf_op jit(solution)/shard_map/all_to_all | solution.py:200
  (79 shorter events, 65.6 us)
Async XLA Ops:
  0.0 16.5 %collective-permute-start.3 = (bf16[320,1024]{1,0:T(8,128)(2,1)}, bf16[320,1024]{1,0:T(8,128)(2,1)S(1)}, u32[]{:S(2)}, u32[]{:S(2)}) collective-permute-start(bf16[320,1024]{1,0:T(8,128)(2,1)} %bitcast.45), channel_id=1, source_target_pairs={{0,16},{16,0},{32,48},{48,32},{64,80},{80,64},{96,112},{112,96},{1... | collective-permute-start | bytes 1966088 | tf_op jit(solution)/shard_map/ppermute | solution.py:158
  8.8 7.7 %collective-permute-start.4 = (bf16[1024,256]{1,0:T(8,128)(2,1)}, bf16[1024,256]{1,0:T(8,128)(2,1)S(1)}, u32[]{:S(2)}, u32[]{:S(2)}) collective-permute-start(bf16[1024,256]{1,0:T(8,128)(2,1)} %param.3), channel_id=1, source_target_pairs={{0,16},{16,0},{32,48},{48,32},{64,80},{80,64},{96,112},{112,96},{1... | collective-permute-start | bytes 1572872 | tf_op jit(solution)/shard_map/ppermute | solution.py:159
  10.7 13.6 %collective-permute-start = (bf16[320,1024]{1,0:T(8,128)(2,1)}, bf16[320,1024]{1,0:T(8,128)(2,1)}, u32[]{:S(2)}, u32[]{:S(2)}) collective-permute-start(bf16[320,1024]{1,0:T(8,128)(2,1)} %bitcast.46), channel_id=1, source_target_pairs={{0,1},{1,2},{2,3},{3,4},{4,5},{5,6},{6,7},{7,8},{8,9},{9,10},{10,1... | collective-permute-start | bytes 1966088 | tf_op jit(solution)/shard_map/ppermute | solution.py:155
  16.5 33.9 %copy-start.8 = (bf16[1024,256]{1,0:T(8,128)(2,1)}, bf16[1024,256]{1,0:T(8,128)(2,1)S(1)}, u32[]{:S(2)}) copy-start(bf16[1024,256]{1,0:T(8,128)(2,1)S(1)} %collective-permute-done.4) | copy-start | bytes 1572868
  16.5 14.7 %collective-permute-start.5 = (bf16[320,1024]{1,0:T(8,128)(2,1)S(1)}, bf16[320,1024]{1,0:T(8,128)(2,1)S(1)}, u32[]{:S(2)}, u32[]{:S(2)}) collective-permute-start(bf16[320,1024]{1,0:T(8,128)(2,1)S(1)} %collective-permute-done.3), channel_id=1, source_target_pairs={{0,1},{1,2},{2,3},{3,4},{4,5},{5,6},{6,7},{7,8},{8,9},{9,10},{10,1... | collective-permute-start | bytes 1966088 | tf_op jit(solution)/shard_map/ppermute | solution.py:155
  24.3 14.0 %collective-permute-start.1 = (bf16[320,1024]{1,0:T(8,128)(2,1)}, bf16[320,1024]{1,0:T(8,128)(2,1)S(1)}, u32[]{:S(2)}, u32[]{:S(2)}) collective-permute-start(bf16[320,1024]{1,0:T(8,128)(2,1)} %collective-permute-done), channel_id=1, source_target_pairs={{0,1},{1,2},{2,3},{3,4},{4,5},{5,6},{6,7},{7,8},{8,9},{9,10},{10,1... | collective-permute-start | bytes 1966088 | tf_op jit(solution)/shard_map/ppermute | solution.py:155
  31.2 14.0 %collective-permute-start.6 = (bf16[320,1024]{1,0:T(8,128)(2,1)S(1)}, bf16[320,1024]{1,0:T(8,128)(2,1)S(1)}, u32[]{:S(2)}, u32[]{:S(2)}) collective-permute-start(bf16[320,1024]{1,0:T(8,128)(2,1)S(1)} %collective-permute-done.5), channel_id=1, source_target_pairs={{0,1},{1,2},{2,3},{3,4},{4,5},{5,6},{6,7},{7,8},{8,9},{9,10},{10,1... | collective-permute-start | bytes 1966088 | tf_op jit(solution)/shard_map/ppermute | solution.py:155
  38.3 13.9 %collective-permute-start.2 = (bf16[320,1024]{1,0:T(8,128)(2,1)S(1)}, bf16[320,1024]{1,0:T(8,128)(2,1)}, u32[]{:S(2)}, u32[]{:S(2)}) collective-permute-start(bf16[320,1024]{1,0:T(8,128)(2,1)S(1)} %collective-permute-done.1), channel_id=1, source_target_pairs={{0,1},{1,2},{2,3},{3,4},{4,5},{5,6},{6,7},{7,8},{8,9},{9,10},{10,1... | collective-permute-start | bytes 1966088 | tf_op jit(solution)/shard_map/ppermute | solution.py:155
  45.3 14.0 %collective-permute-start.9 = (bf16[320,1024]{1,0:T(8,128)(2,1)S(1)}, bf16[320,1024]{1,0:T(8,128)(2,1)}, u32[]{:S(2)}, u32[]{:S(2)}) collective-permute-start(bf16[320,1024]{1,0:T(8,128)(2,1)S(1)} %collective-permute-done.6), channel_id=1, source_target_pairs={{0,1},{1,2},{2,3},{3,4},{4,5},{5,6},{6,7},{7,8},{8,9},{9,10},{10,1... | collective-permute-start | bytes 1966088 | tf_op jit(solution)/shard_map/ppermute | solution.py:155
  52.3 19.4 %collective-permute-start.7 = (bf16[320,1024]{1,0:T(8,128)(2,1)}, bf16[320,1024]{1,0:T(8,128)(2,1)S(1)}, u32[]{:S(2)}, u32[]{:S(2)}) collective-permute-start(bf16[320,1024]{1,0:T(8,128)(2,1)} %collective-permute-done.2), channel_id=1, source_target_pairs={{0,1},{1,2},{2,3},{3,4},{4,5},{5,6},{6,7},{7,8},{8,9},{9,10},{10,1... | collective-permute-start | bytes 1966088 | tf_op jit(solution)/shard_map/ppermute | solution.py:155
  59.3 18.5 %collective-permute-start.10 = (bf16[320,1024]{1,0:T(8,128)(2,1)}, bf16[320,1024]{1,0:T(8,128)(2,1)S(1)}, u32[]{:S(2)}, u32[]{:S(2)}) collective-permute-start(bf16[320,1024]{1,0:T(8,128)(2,1)} %collective-permute-done.9), channel_id=1, source_target_pairs={{0,1},{1,2},{2,3},{3,4},{4,5},{5,6},{6,7},{7,8},{8,9},{9,10},{10,1... | collective-permute-start | bytes 1966088 | tf_op jit(solution)/shard_map/ppermute | solution.py:155
  64.4 30.7 %all-to-all-start.3 = ((f32[32,16,640]{2,1,0:T(8,128)}), f32[32,16,640]{2,1,0:T(8,128)S(1)}, u32[]{:S(2)}, u32[]{:S(2)}) async-start(f32[32,16,640]{2,1,0:T(8,128)} %pad_maximum_fusion), calls=%async_computation.3 | async-start | bytes 2621440 | tf_op jit(solution)/shard_map/all_to_all | solution.py:172
  71.7 12.4 %collective-permute-start.8 = (bf16[320,1024]{1,0:T(8,128)(2,1)S(1)}, bf16[320,1024]{1,0:T(8,128)(2,1)}, u32[]{:S(2)}, u32[]{:S(2)}) collective-permute-start(bf16[320,1024]{1,0:T(8,128)(2,1)S(1)} %collective-permute-done.7), channel_id=1, source_target_pairs={{0,1},{1,2},{2,3},{3,4},{4,5},{5,6},{6,7},{7,8},{8,9},{9,10},{10,1... | collective-permute-start | bytes 1966088 | tf_op jit(solution)/shard_map/ppermute | solution.py:155
  77.8 12.8 %collective-permute-start.13 = (bf16[320,1024]{1,0:T(8,128)(2,1)S(1)}, bf16[320,1024]{1,0:T(8,128)(2,1)}, u32[]{:S(2)}, u32[]{:S(2)}) collective-permute-start(bf16[320,1024]{1,0:T(8,128)(2,1)S(1)} %collective-permute-done.10), channel_id=1, source_target_pairs={{0,1},{1,2},{2,3},{3,4},{4,5},{5,6},{6,7},{7,8},{8,9},{9,10},{10,1... | collective-permute-start | bytes 1966088 | tf_op jit(solution)/shard_map/ppermute | solution.py:155
  84.1 18.0 %collective-permute-start.11 = (bf16[320,1024]{1,0:T(8,128)(2,1)}, bf16[320,1024]{1,0:T(8,128)(2,1)}, u32[]{:S(2)}, u32[]{:S(2)}) collective-permute-start(bf16[320,1024]{1,0:T(8,128)(2,1)} %collective-permute-done.8), channel_id=1, source_target_pairs={{0,1},{1,2},{2,3},{3,4},{4,5},{5,6},{6,7},{7,8},{8,9},{9,10},{10,1... | collective-permute-start | bytes 1966088 | tf_op jit(solution)/shard_map/ppermute | solution.py:155
  90.6 20.0 %collective-permute-start.14 = (bf16[320,1024]{1,0:T(8,128)(2,1)}, bf16[320,1024]{1,0:T(8,128)(2,1)S(1)}, u32[]{:S(2)}, u32[]{:S(2)}) collective-permute-start(bf16[320,1024]{1,0:T(8,128)(2,1)} %collective-permute-done.13), channel_id=1, source_target_pairs={{0,1},{1,2},{2,3},{3,4},{4,5},{5,6},{6,7},{7,8},{8,9},{9,10},{10,1... | collective-permute-start | bytes 1966088 | tf_op jit(solution)/shard_map/ppermute | solution.py:155
  95.1 26.1 %all-to-all-start.2 = ((f32[32,16,640]{2,1,0:T(8,128)}), f32[32,16,640]{2,1,0:T(8,128)S(1)}, u32[]{:S(2)}, u32[]{:S(2)}) async-start(f32[32,16,640]{2,1,0:T(8,128)} %pad_maximum_fusion.1), calls=%async_computation.2 | async-start | bytes 2621440 | tf_op jit(solution)/shard_map/all_to_all | solution.py:172
  102.1 14.2 %collective-permute-start.12 = (bf16[320,1024]{1,0:T(8,128)(2,1)}, bf16[320,1024]{1,0:T(8,128)(2,1)}, u32[]{:S(2)}, u32[]{:S(2)}) collective-permute-start(bf16[320,1024]{1,0:T(8,128)(2,1)} %collective-permute-done.11), channel_id=1, source_target_pairs={{0,1},{1,2},{2,3},{3,4},{4,5},{5,6},{6,7},{7,8},{8,9},{9,10},{10,1... | collective-permute-start | bytes 1966088 | tf_op jit(solution)/shard_map/ppermute | solution.py:155
  110.6 22.6 %collective-permute-start.16 = (bf16[320,1024]{1,0:T(8,128)(2,1)S(1)}, bf16[320,1024]{1,0:T(8,128)(2,1)}, u32[]{:S(2)}, u32[]{:S(2)}) collective-permute-start(bf16[320,1024]{1,0:T(8,128)(2,1)S(1)} %collective-permute-done.14), channel_id=1, source_target_pairs={{0,1},{1,2},{2,3},{3,4},{4,5},{5,6},{6,7},{7,8},{8,9},{9,10},{10,1... | collective-permute-start | bytes 1966088 | tf_op jit(solution)/shard_map/ppermute | solution.py:155
  121.2 25.4 %all-to-all-start.1 = ((f32[32,16,640]{2,1,0:T(8,128)}), f32[32,16,640]{2,1,0:T(8,128)}, u32[]{:S(2)}, u32[]{:S(2)}) async-start(f32[32,16,640]{2,1,0:T(8,128)} %pad_maximum_fusion.2), calls=%async_computation.1 | async-start | bytes 2621440 | tf_op jit(solution)/shard_map/all_to_all | solution.py:172
  128.5 8.7 %collective-permute-start.15 = (bf16[160,1024]{1,0:T(8,128)(2,1)S(1)}, bf16[160,1024]{1,0:T(8,128)(2,1)S(1)}, u32[]{:S(2)}, u32[]{:S(2)}) collective-permute-start(bf16[160,1024]{1,0:T(8,128)(2,1)S(1)} %constant_dynamic-slice_fusion.1), channel_id=1, source_target_pairs={{0,1},{1,2},{2,3},{3,4},{4,5},{5,6},{6,7},{7,8},{8,9},{9,10},{10,1... | collective-permute-start | bytes 983048 | tf_op jit(solution)/shard_map/ppermute | solution.py:155
  134.2 8.2 %collective-permute-start.17 = (bf16[160,1024]{1,0:T(8,128)(2,1)S(1)}, bf16[160,1024]{1,0:T(8,128)(2,1)S(1)}, u32[]{:S(2)}, u32[]{:S(2)}) collective-permute-start(bf16[160,1024]{1,0:T(8,128)(2,1)S(1)} %constant_dynamic-slice_fusion), channel_id=1, source_target_pairs={{0,1},{1,2},{2,3},{3,4},{4,5},{5,6},{6,7},{7,8},{8,9},{9,10},{10,1... | collective-permute-start | bytes 983048 | tf_op jit(solution)/shard_map/ppermute | solution.py:155
  146.6 25.5 %all-to-all-start = ((f32[32,16,640]{2,1,0:T(8,128)}), f32[32,16,640]{2,1,0:T(8,128)}, u32[]{:S(2)}, u32[]{:S(2)}) async-start(f32[32,16,640]{2,1,0:T(8,128)} %pad_maximum_fusion.3), calls=%async_computation | async-start | bytes 2621440 | tf_op jit(solution)/shard_map/all_to_all | solution.py:193
  190.1 20.2 %all-to-all-start.5 = ((f32[16,8,128]{2,1,0:T(8,128)}), f32[16,8,128]{2,1,0:T(8,128)S(1)}, u32[]{:S(2)}, u32[]{:S(2)}) async-start(f32[16,8,128]{2,1,0:T(8,128)} %shard_map.32), calls=%async_computation.5 | async-start | bytes 131072 | tf_op jit(solution)/shard_map/all_to_all | solution.py:198
  (11 other events, 71.1 us)

commit v8 on v7

--- a/solution.py
+++ b/solution.py
@@ -8,7 +8,8 @@
 from jax.sharding import PartitionSpec as P
 
 epsilon = 1e-06
-GROUPS = (4, 4, 4, 4)
+GROUPS = (768, 896, 896)
+TIES = {(5, 0): 0}
 VMEM = pltpu.VMEM
 LIMIT = 48 * 1024 * 1024
 EXACT = lax.Precision.HIGHEST
@@ -104,17 +105,17 @@
         width *= 2
     part, width = out_ref.shape[1:]
     for core in range(2):
-        place = 0
+        sums = []
         for block_ref in blocks:
             total = 0.0
             for r in range(replicas):
                 row = (r + core) % 2 * part
                 total = total + block_ref[r // 2 * 2 + core, row:row + part] * down[r:r + 1]
-            for start in range(0, total.shape[1], width):
-                away, piece = order[core][place]
-                slab = lax.rem(here_ref[0] + away, slabs)
-                out_ref[slab * 2 + piece] = total[:, start:start + width]
-                place += 1
+            sums.append(total)
+        sums = jnp.concatenate(sums, axis=1)
+        for place, (away, piece) in enumerate(order[core]):
+            slab = lax.rem(here_ref[0] + away, slabs)
+            out_ref[slab * 2 + piece] = sums[:, place * width:(place + 1) * width]
 
 
 def weighted_sums(replicas, slabs, order, here, parts, blocks):
@@ -154,43 +155,56 @@
     def move(slab):
         return lax.ppermute(slab, ("dp", "tensor"), onward)
 
+    def take(pieces, count):
+        taken = []
+        while count:
+            piece = pieces[0]
+            size = min(count, piece.shape[0])
+            taken.append(piece[:size])
+            count -= size
+            pieces = [piece[size:]][: piece.shape[0] > size] + pieces[1:]
+        return jnp.concatenate(taken, axis=0), pieces
+
     mine = activations.T
     chains = [mine, lax.ppermute(mine, "dp", sibling)]
-    grads = [out_grads, lax.ppermute(out_grads, "dp", sibling)]
+    grads = [out_grads, out_grads]
     chains[1], grads[1] = lax.optimization_barrier((chains[1], grads[1]))
+    grads[1] = lax.ppermute(grads[1], "dp", sibling)
     held = [[own_half(slab)] for slab in chains]
     order = [[(0, 0)], [(0, 1)]]
     blocks = []
     gram = jnp.zeros((8, 128), jnp.float32)
     sizes = list(GROUPS)
-    ready = None
     for step in range(1, half + 1):
         if step < half:
             chains = [move(slab) for slab in chains]
-            if ready is not None:
-                chains[0], ready = lax.optimization_barrier((chains[0], ready))
-                blocks.append(lax.all_to_all(ready, "dp", 0, 0))
-                ready = None
+            if step == 1:
+                chains[1], grads[1] = lax.optimization_barrier((chains[1], grads[1]))
             for k in range(2):
-                held[k] += [chains[k][:rows], chains[k][rows:]]
+                if (step, k) in TIES:
+                    place = TIES[step, k]
+                    chains[k], blocks[place] = lax.optimization_barrier((chains[k], blocks[place]))
+                held[k].append(chains[k])
             order[0] += [(slabs - step, 0), (slabs - step, 1)]
             order[1] += [(step, 0), (step, 1)]
         else:
             for k in range(2):
                 held[k].append(move(own_half(chains[k])))
                 order[k].append((half, k))
-        if len(held[0]) >= sizes[0]:
+        if sum(piece.shape[0] for piece in held[0]) >= sizes[0]:
             count = sizes.pop(0)
             parts = []
             for k in range(2):
-                group, held[k] = held[k][:count], held[k][count:]
+                group, held[k] = take(held[k], count)
                 grad = lax.dot_general(
-                    grads[k], jnp.concatenate(group, axis=0), (((0,), (1,)), ((), ())),
+                    grads[k], group, (((0,), (1,)), ((), ())),
                     preferred_element_type=jnp.float32,
                 )
                 parts.append(grad.reshape(replicas, part, -1))
             ready = jnp.concatenate(parts, axis=1)
-    blocks.append(lax.all_to_all(ready, "dp", 0, 0))
+            if step < half:
+                chains[1], ready = lax.optimization_barrier((chains[1], ready))
+            blocks.append(lax.all_to_all(ready, "dp", 0, 0))
     for block in blocks:
         gram = gram_add(replicas, block, gram)
     peers = jnp.broadcast_to(gram, (replicas, *gram.shape))

time: 230 us -> 227 us (0.987)
  waiting for transfers between devices: 46.5 us -> 52.5 us
  Pallas kernels: 15.4 us -> 12.7 us
    ppermute x16, waiting for transfers between devices: 17.3 us -> 20.6 us  [move(): return lax.ppermute(slab, ('dp', 'tensor'), onward)]
    all_to_all x4 -> x3, waiting for transfers between devices: 17.7 us -> 20.3 us  [on_device(): blocks.append(lax.all_to_all(ready, 'dp', 0, 0))]
    pallas_call x4 -> x3, Pallas kernels: 11.2 us -> 8.68 us  [gram_add(): pl.pallas_call(functools.partial(gram_kernel, replicas), out_shape=jax.Sh...]
    dot_general x8 -> x6, matrix products: 12.7 us -> 10.5 us  [on_device(): lax.dot_general(grads[k], group, (((0,), (1,)), ((), ())), preferred_elem...]
    concatenate x4 -> x3, other arithmetic: 4.65 us -> 4.03 us  [on_device(): ready = jnp.concatenate(parts, axis=1)]
    all_to_all x4 -> x3, starting transfers between devices: 26.6 us -> 26.3 us  [on_device(): blocks.append(lax.all_to_all(ready, 'dp', 0, 0))]
  transfers between devices with their start and end apart: 23 -> 22, of which waited for: 13 -> 11; matrix products, arithmetic and copies ran while one was open for 11% -> 9% of each run, Pallas kernels for 3% -> 2%
where the time goes in v8:
time: 227 us; the launch traced here: 225 us
  starting transfers between devices  111 us (49%)
  waiting for transfers between devices  52.5 us (23%)
  blocking collectives  27.4 us (12%)
  Pallas kernels  12.7 us (6%)
  matrix products  10.5 us (5%)
  local copies, waits for them, and re-layouts  6.62 us (3%)
  other arithmetic  4.03 us (2%)
    ppermute x16, starting transfers between devices, move(): return lax.ppermute(slab, ('dp', 'tensor'), onward)  67.5 us
    all_to_all x3, starting transfers between devices, on_device(): blocks.append(lax.all_to_all(ready, 'dp', 0, 0))  26.3 us
    ppermute x16, waiting for transfers between devices, move(): return lax.ppermute(slab, ('dp', 'tensor'), onward)  20.6 us
    all_to_all x3, waiting for transfers between devices, on_device(): blocks.append(lax.all_to_all(ready, 'dp', 0, 0))  20.3 us
    all_to_all x1, blocking collectives, on_device(): home = lax.all_to_all(home, 'dp', 0, 0)  14.1 us
    all_to_all x1, blocking collectives, on_device(): parts = sum_and_spread(lax.all_to_all(peers, 'dp', 0, 0), slabs)  13.3 us
    all_to_all x1, waiting for transfers between devices, on_device(): parts = lax.all_to_all(parts, 'tensor', 0, 0)  11.6 us
    dot_general x6, matrix products, on_device(): lax.dot_general(grads[k], group, (((0,), (1,)), ((), ())), preferred_elem...  10.5 us
  transfers between devices with their start and end apart: 22, of which 11 were waited for; matrix products, arithmetic and copies ran while one was open for 9% of the time, Pallas kernels for 2%

profile of v8, /device:TPU:1, one launch (start us, length us, event | category | flops | bytes accessed | tf_op | source)
XLA Modules:
  0.0 225.5 jit_solution(10185427509515246377)
XLA Ops:
  0.0 8.8 %collective-permute-start.5 = (bf16[320,1024]{1,0:T(8,128)(2,1)}, bf16[320,1024]{1,0:T(8,128)(2,1)S(1)}, u32[]{:S(2)}, u32[]{:S(2)}) collective-permute-start(bf16[320,1024]{1,0:T(8,128)(2,1)} %bitcast.36), channel_id=1, source_target_pairs={{0,16},{16,0},{32,48},{48,32},{64,80},{80,64},{96,112},{112,96},{1... | collective-permute-start | bytes 1966088 | tf_op jit(solution)/shard_map/ppermute | solution.py:169
  8.8 5.8 %collective-permute-start = (bf16[320,1024]{1,0:T(8,128)(2,1)}, bf16[320,1024]{1,0:T(8,128)(2,1)}, u32[]{:S(2)}, u32[]{:S(2)}) collective-permute-start(bf16[320,1024]{1,0:T(8,128)(2,1)} %bitcast.37), channel_id=1, source_target_pairs={{0,1},{1,2},{2,3},{3,4},{4,5},{5,6},{6,7},{7,8},{8,9},{9,10},{10,1... | collective-permute-start | bytes 1966088 | tf_op jit(solution)/shard_map/ppermute | solution.py:156
  19.1 3.2 %collective-permute-done = bf16[320,1024]{1,0:T(8,128)(2,1)} collective-permute-done((bf16[320,1024]{1,0:T(8,128)(2,1)}, bf16[320,1024]{1,0:T(8,128)(2,1)}, u32[]{:S(2)}, u32[]{:S(2)}) %collective-permute-start) | collective-permute-done | bytes 655392 | tf_op jit(solution)/shard_map/ppermute | solution.py:156
  22.4 5.0 %collective-permute-start.1 = (bf16[320,1024]{1,0:T(8,128)(2,1)}, bf16[320,1024]{1,0:T(8,128)(2,1)S(1)}, u32[]{:S(2)}, u32[]{:S(2)}) collective-permute-start(bf16[320,1024]{1,0:T(8,128)(2,1)} %collective-permute-done), channel_id=1, source_target_pairs={{0,1},{1,2},{2,3},{3,4},{4,5},{5,6},{6,7},{7,8},{8,9},{9,10},{10,1... | collective-permute-start | bytes 1966088 | tf_op jit(solution)/shard_map/ppermute | solution.py:156
  29.3 5.0 %collective-permute-start.8 = (bf16[320,1024]{1,0:T(8,128)(2,1)S(1)}, bf16[320,1024]{1,0:T(8,128)(2,1)S(1)}, u32[]{:S(2)}, u32[]{:S(2)}) collective-permute-start(bf16[320,1024]{1,0:T(8,128)(2,1)S(1)} %collective-permute-done.6), channel_id=1, source_target_pairs={{0,1},{1,2},{2,3},{3,4},{4,5},{5,6},{6,7},{7,8},{8,9},{9,10},{10,1... | collective-permute-start | bytes 1966088 | tf_op jit(solution)/shard_map/ppermute | solution.py:156
  36.5 5.1 %collective-permute-start.2 = (bf16[320,1024]{1,0:T(8,128)(2,1)S(1)}, bf16[320,1024]{1,0:T(8,128)(2,1)}, u32[]{:S(2)}, u32[]{:S(2)}) collective-permute-start(bf16[320,1024]{1,0:T(8,128)(2,1)S(1)} %collective-permute-done.1), channel_id=1, source_target_pairs={{0,1},{1,2},{2,3},{3,4},{4,5},{5,6},{6,7},{7,8},{8,9},{9,10},{10,1... | collective-permute-start | bytes 1966088 | tf_op jit(solution)/shard_map/ppermute | solution.py:156
  45.3 5.0 %collective-permute-start.12 = (bf16[320,1024]{1,0:T(8,128)(2,1)S(1)}, bf16[320,1024]{1,0:T(8,128)(2,1)}, u32[]{:S(2)}, u32[]{:S(2)}) collective-permute-start(bf16[320,1024]{1,0:T(8,128)(2,1)S(1)} %collective-permute-done.8), channel_id=1, source_target_pairs={{0,1},{1,2},{2,3},{3,4},{4,5},{5,6},{6,7},{7,8},{8,9},{9,10},{10,1... | collective-permute-start | bytes 1966088 | tf_op jit(solution)/shard_map/ppermute | solution.py:156
  50.3 7.2 %all-to-all-start = ((f32[32,16,768]{2,1,0:T(8,128)}), f32[32,16,768]{2,1,0:T(8,128)S(1)}, u32[]{:S(2)}, u32[]{:S(2)}) async-start(f32[32,16,768]{2,1,0:T(8,128)} %pad_maximum_fusion.2), calls=%async_computation | async-start | bytes 3145728 | tf_op jit(solution)/shard_map/all_to_all | solution.py:207
  63.0 6.4 %collective-permute-done.3 = bf16[320,1024]{1,0:T(8,128)(2,1)S(1)} collective-permute-done((bf16[320,1024]{1,0:T(8,128)(2,1)}, bf16[320,1024]{1,0:T(8,128)(2,1)S(1)}, u32[]{:S(2)}, u32[]{:S(2)}) %collective-permute-start.3) | collective-permute-done | bytes 655392 | tf_op jit(solution)/shard_map/ppermute | solution.py:156
  69.4 4.2 %collective-permute-start.4 = (bf16[320,1024]{1,0:T(8,128)(2,1)S(1)}, bf16[320,1024]{1,0:T(8,128)(2,1)S(1)}, u32[]{:S(2)}, u32[]{:S(2)}) collective-permute-start(bf16[320,1024]{1,0:T(8,128)(2,1)S(1)} %collective-permute-done.3), channel_id=1, source_target_pairs={{0,1},{1,2},{2,3},{3,4},{4,5},{5,6},{6,7},{7,8},{8,9},{9,10},{10,1... | collective-permute-start | bytes 1966088 | tf_op jit(solution)/shard_map/ppermute | solution.py:156
  76.5 3.9 %collective-permute-start.14 = (bf16[320,1024]{1,0:T(8,128)(2,1)}, bf16[320,1024]{1,0:T(8,128)(2,1)}, u32[]{:S(2)}, u32[]{:S(2)}) collective-permute-start(bf16[320,1024]{1,0:T(8,128)(2,1)} %collective-permute-done.13), channel_id=1, source_target_pairs={{0,1},{1,2},{2,3},{3,4},{4,5},{5,6},{6,7},{7,8},{8,9},{9,10},{10,1... | collective-permute-start | bytes 1966088 | tf_op jit(solution)/shard_map/ppermute | solution.py:156
  83.5 4.0 %collective-permute-start.9 = (bf16[320,1024]{1,0:T(8,128)(2,1)S(1)}, bf16[320,1024]{1,0:T(8,128)(2,1)}, u32[]{:S(2)}, u32[]{:S(2)}) collective-permute-start(bf16[320,1024]{1,0:T(8,128)(2,1)S(1)} %collective-permute-done.4), channel_id=1, source_target_pairs={{0,1},{1,2},{2,3},{3,4},{4,5},{5,6},{6,7},{7,8},{8,9},{9,10},{10,1... | collective-permute-start | bytes 1966088 | tf_op jit(solution)/shard_map/ppermute | solution.py:156
  95.1 3.9 %collective-permute-start.15 = (bf16[320,1024]{1,0:T(8,128)(2,1)}, bf16[320,1024]{1,0:T(8,128)(2,1)}, u32[]{:S(2)}, u32[]{:S(2)}) collective-permute-start(bf16[320,1024]{1,0:T(8,128)(2,1)} %collective-permute-done.14), channel_id=1, source_target_pairs={{0,1},{1,2},{2,3},{3,4},{4,5},{5,6},{6,7},{7,8},{8,9},{9,10},{10,1... | collective-permute-start | bytes 1966088 | tf_op jit(solution)/shard_map/ppermute | solution.py:156
  101.5 7.5 %all-to-all-start.2 = ((f32[32,16,896]{2,1,0:T(8,128)}), f32[32,16,896]{2,1,0:T(8,128)S(1)}, u32[]{:S(2)}, u32[]{:S(2)}) async-start(f32[32,16,896]{2,1,0:T(8,128)} %pad_maximum_fusion), calls=%async_computation.2 | async-start | bytes 3670016 | tf_op jit(solution)/shard_map/all_to_all | solution.py:207
  109.0 5.0 %collective-permute-start.16 = (bf16[320,1024]{1,0:T(8,128)(2,1)}, bf16[320,1024]{1,0:T(8,128)(2,1)S(1)}, u32[]{:S(2)}, u32[]{:S(2)}) collective-permute-start(bf16[320,1024]{1,0:T(8,128)(2,1)} %collective-permute-done.15), channel_id=1, source_target_pairs={{0,1},{1,2},{2,3},{3,4},{4,5},{5,6},{6,7},{7,8},{8,9},{9,10},{10,1... | collective-permute-start | bytes 1966088 | tf_op jit(solution)/shard_map/ppermute | solution.py:156
  115.0 5.0 %collective-permute-start.11 = (bf16[160,1024]{1,0:T(8,128)(2,1)S(1)}, bf16[160,1024]{1,0:T(8,128)(2,1)S(1)}, u32[]{:S(2)}, u32[]{:S(2)}) collective-permute-start(bf16[160,1024]{1,0:T(8,128)(2,1)S(1)} %constant_dynamic-slice_fusion.1), channel_id=1, source_target_pairs={{0,1},{1,2},{2,3},{3,4},{4,5},{5,6},{6,7},{7,8},{8,9},{9,10},{10,1... | collective-permute-start | bytes 983048 | tf_op jit(solution)/shard_map/ppermute | solution.py:156
  121.8 5.2 %collective-permute-start.17 = (bf16[160,1024]{1,0:T(8,128)(2,1)S(1)}, bf16[160,1024]{1,0:T(8,128)(2,1)S(1)}, u32[]{:S(2)}, u32[]{:S(2)}) collective-permute-start(bf16[160,1024]{1,0:T(8,128)(2,1)S(1)} %constant_dynamic-slice_fusion), channel_id=1, source_target_pairs={{0,1},{1,2},{2,3},{3,4},{4,5},{5,6},{6,7},{7,8},{8,9},{9,10},{10,1... | collective-permute-start | bytes 983048 | tf_op jit(solution)/shard_map/ppermute | solution.py:156
  134.3 11.6 %all-to-all-start.1 = ((f32[32,16,896]{2,1,0:T(8,128)}), f32[32,16,896]{2,1,0:T(8,128)}, u32[]{:S(2)}, u32[]{:S(2)}) async-start(f32[32,16,896]{2,1,0:T(8,128)} %pad_maximum_fusion.1), calls=%async_computation.1 | async-start | bytes 3670016 | tf_op jit(solution)/shard_map/all_to_all | solution.py:207
  150.6 20.3 %all-to-all-done.1.refs_2_ = f32[32,16,896]{2,1,0:T(8,128)} async-done(((f32[32,16,896]{2,1,0:T(8,128)}), f32[32,16,896]{2,1,0:T(8,128)}, u32[]{:S(2)}, u32[]{:S(2)}) %all-to-all-start.1) | async-done | bytes 1835040 | tf_op jit(solution)/shard_map/all_to_all | solution.py:207
  170.9 4.0 %shard_map.30 = f32[8,128]{1,0:T(8,128)S(1)} custom-call(f32[16,32,896]{2,1,0:T(8,128)} %bitcast.12.block_ref, f32[8,128]{1,0:T(8,128)S(1)} %shard_map.29.before_ref), custom_call_target="tpu_custom_call" | custom-call | flops 1409286144 | bytes 1835008 | tf_op jit(solution)/shard_map/pallas_call | solution.py:49
  174.9 13.3 %all_to_all.30.parts_ref = f32[32,8,128]{2,1,0:T(8,128)} all-to-all(f32[32,8,128]{2,1,0:T(8,128)S(1)} %broadcast_in_dim.7), channel_id=1, replica_groups=mesh['dp'=32,'tensor'=16] {'dp'}, dimensions={0} | all-to-all | bytes 262144 | tf_op jit(solution)/shard_map/all_to_all | solution.py:211
  189.8 6.8 %all-to-all-start.4 = ((f32[16,8,128]{2,1,0:T(8,128)}), f32[16,8,128]{2,1,0:T(8,128)S(1)}, u32[]{:S(2)}, u32[]{:S(2)}) async-start(f32[16,8,128]{2,1,0:T(8,128)} %shard_map.31), calls=%async_computation.4 | async-start | bytes 131072 | tf_op jit(solution)/shard_map/all_to_all | solution.py:212
  196.6 11.6 %all-to-all-done.4.parts_ref = f32[16,8,128]{2,1,0:T(8,128)S(1)} async-done(((f32[16,8,128]{2,1,0:T(8,128)}), f32[16,8,128]{2,1,0:T(8,128)S(1)}, u32[]{:S(2)}, u32[]{:S(2)}) %all-to-all-start.4) | async-done | bytes 65568 | tf_op jit(solution)/shard_map/all_to_all | solution.py:212
  210.6 14.1 %all_to_all.31 = f32[32,8,160]{2,1,0:T(8,128)S(1)} all-to-all(f32[32,8,160]{2,1,0:T(8,128)S(1)} %shard_map.32), channel_id=1, replica_groups=mesh['dp'=32,'tensor'=16] {'dp'}, dimensions={0} | all-to-all | bytes 327680 | tf_op jit(solution)/shard_map/all_to_all | solution.py:214
  (67 shorter events, 53.3 us)
Async XLA Ops:
  0.0 14.5 %collective-permute-start.5 = (bf16[320,1024]{1,0:T(8,128)(2,1)}, bf16[320,1024]{1,0:T(8,128)(2,1)S(1)}, u32[]{:S(2)}, u32[]{:S(2)}) collective-permute-start(bf16[320,1024]{1,0:T(8,128)(2,1)} %bitcast.36), channel_id=1, source_target_pairs={{0,16},{16,0},{32,48},{48,32},{64,80},{80,64},{96,112},{112,96},{1... | collective-permute-start | bytes 1966088 | tf_op jit(solution)/shard_map/ppermute | solution.py:169
  8.8 13.6 %collective-permute-start = (bf16[320,1024]{1,0:T(8,128)(2,1)}, bf16[320,1024]{1,0:T(8,128)(2,1)}, u32[]{:S(2)}, u32[]{:S(2)}) collective-permute-start(bf16[320,1024]{1,0:T(8,128)(2,1)} %bitcast.37), channel_id=1, source_target_pairs={{0,1},{1,2},{2,3},{3,4},{4,5},{5,6},{6,7},{7,8},{8,9},{9,10},{10,1... | collective-permute-start | bytes 1966088 | tf_op jit(solution)/shard_map/ppermute | solution.py:156
  14.6 14.7 %collective-permute-start.6 = (bf16[320,1024]{1,0:T(8,128)(2,1)S(1)}, bf16[320,1024]{1,0:T(8,128)(2,1)S(1)}, u32[]{:S(2)}, u32[]{:S(2)}) collective-permute-start(bf16[320,1024]{1,0:T(8,128)(2,1)S(1)} %collective-permute-done.5), channel_id=1, source_target_pairs={{0,1},{1,2},{2,3},{3,4},{4,5},{5,6},{6,7},{7,8},{8,9},{9,10},{10,1... | collective-permute-start | bytes 1966088 | tf_op jit(solution)/shard_map/ppermute | solution.py:156
  17.2 10.2 %collective-permute-start.7 = (bf16[1024,256]{1,0:T(8,128)(2,1)}, bf16[1024,256]{1,0:T(8,128)(2,1)S(1)}, u32[]{:S(2)}, u32[]{:S(2)}) collective-permute-start(bf16[1024,256]{1,0:T(8,128)(2,1)} %param.3), channel_id=1, source_target_pairs={{0,16},{16,0},{32,48},{48,32},{64,80},{80,64},{96,112},{112,96},{1... | collective-permute-start | bytes 1572872 | tf_op jit(solution)/shard_map/ppermute | solution.py:172
  22.4 14.0 %collective-permute-start.1 = (bf16[320,1024]{1,0:T(8,128)(2,1)}, bf16[320,1024]{1,0:T(8,128)(2,1)S(1)}, u32[]{:S(2)}, u32[]{:S(2)}) collective-permute-start(bf16[320,1024]{1,0:T(8,128)(2,1)} %collective-permute-done), channel_id=1, source_target_pairs={{0,1},{1,2},{2,3},{3,4},{4,5},{5,6},{6,7},{7,8},{8,9},{9,10},{10,1... | collective-permute-start | bytes 1966088 | tf_op jit(solution)/shard_map/ppermute | solution.py:156
  29.3 14.0 %collective-permute-start.8 = (bf16[320,1024]{1,0:T(8,128)(2,1)S(1)}, bf16[320,1024]{1,0:T(8,128)(2,1)S(1)}, u32[]{:S(2)}, u32[]{:S(2)}) collective-permute-start(bf16[320,1024]{1,0:T(8,128)(2,1)S(1)} %collective-permute-done.6), channel_id=1, source_target_pairs={{0,1},{1,2},{2,3},{3,4},{4,5},{5,6},{6,7},{7,8},{8,9},{9,10},{10,1... | collective-permute-start | bytes 1966088 | tf_op jit(solution)/shard_map/ppermute | solution.py:156
  36.5 21.1 %collective-permute-start.2 = (bf16[320,1024]{1,0:T(8,128)(2,1)S(1)}, bf16[320,1024]{1,0:T(8,128)(2,1)}, u32[]{:S(2)}, u32[]{:S(2)}) collective-permute-start(bf16[320,1024]{1,0:T(8,128)(2,1)S(1)} %collective-permute-done.1), channel_id=1, source_target_pairs={{0,1},{1,2},{2,3},{3,4},{4,5},{5,6},{6,7},{7,8},{8,9},{9,10},{10,1... | collective-permute-start | bytes 1966088 | tf_op jit(solution)/shard_map/ppermute | solution.py:156
  45.3 15.2 %collective-permute-start.12 = (bf16[320,1024]{1,0:T(8,128)(2,1)S(1)}, bf16[320,1024]{1,0:T(8,128)(2,1)}, u32[]{:S(2)}, u32[]{:S(2)}) collective-permute-start(bf16[320,1024]{1,0:T(8,128)(2,1)S(1)} %collective-permute-done.8), channel_id=1, source_target_pairs={{0,1},{1,2},{2,3},{3,4},{4,5},{5,6},{6,7},{7,8},{8,9},{9,10},{10,1... | collective-permute-start | bytes 1966088 | tf_op jit(solution)/shard_map/ppermute | solution.py:156
  50.3 33.1 %all-to-all-start = ((f32[32,16,768]{2,1,0:T(8,128)}), f32[32,16,768]{2,1,0:T(8,128)S(1)}, u32[]{:S(2)}, u32[]{:S(2)}) async-start(f32[32,16,768]{2,1,0:T(8,128)} %pad_maximum_fusion.2), calls=%async_computation | async-start | bytes 3145728 | tf_op jit(solution)/shard_map/all_to_all | solution.py:207
  57.6 11.8 %collective-permute-start.3 = (bf16[320,1024]{1,0:T(8,128)(2,1)}, bf16[320,1024]{1,0:T(8,128)(2,1)S(1)}, u32[]{:S(2)}, u32[]{:S(2)}) collective-permute-start(bf16[320,1024]{1,0:T(8,128)(2,1)} %collective-permute-done.2), channel_id=1, source_target_pairs={{0,1},{1,2},{2,3},{3,4},{4,5},{5,6},{6,7},{7,8},{8,9},{9,10},{10,1... | collective-permute-start | bytes 1966088 | tf_op jit(solution)/shard_map/ppermute | solution.py:156
  60.6 16.0 %collective-permute-start.13 = (bf16[320,1024]{1,0:T(8,128)(2,1)}, bf16[320,1024]{1,0:T(8,128)(2,1)}, u32[]{:S(2)}, u32[]{:S(2)}) collective-permute-start(bf16[320,1024]{1,0:T(8,128)(2,1)} %collective-permute-done.12), channel_id=1, source_target_pairs={{0,1},{1,2},{2,3},{3,4},{4,5},{5,6},{6,7},{7,8},{8,9},{9,10},{10,1... | collective-permute-start | bytes 1966088 | tf_op jit(solution)/shard_map/ppermute | solution.py:156
  69.4 11.7 %copy-start.1 = (bf16[320,1024]{1,0:T(8,128)(2,1)}, bf16[320,1024]{1,0:T(8,128)(2,1)S(1)}, u32[]{:S(2)}) copy-start(bf16[320,1024]{1,0:T(8,128)(2,1)S(1)} %collective-permute-done.3) | copy-start | bytes 1966084
  69.4 14.0 %collective-permute-start.4 = (bf16[320,1024]{1,0:T(8,128)(2,1)S(1)}, bf16[320,1024]{1,0:T(8,128)(2,1)S(1)}, u32[]{:S(2)}, u32[]{:S(2)}) collective-permute-start(bf16[320,1024]{1,0:T(8,128)(2,1)S(1)} %collective-permute-done.3), channel_id=1, source_target_pairs={{0,1},{1,2},{2,3},{3,4},{4,5},{5,6},{6,7},{7,8},{8,9},{9,10},{10,1... | collective-permute-start | bytes 1966088 | tf_op jit(solution)/shard_map/ppermute | solution.py:156
  76.5 14.0 %collective-permute-start.14 = (bf16[320,1024]{1,0:T(8,128)(2,1)}, bf16[320,1024]{1,0:T(8,128)(2,1)}, u32[]{:S(2)}, u32[]{:S(2)}) collective-permute-start(bf16[320,1024]{1,0:T(8,128)(2,1)} %collective-permute-done.13), channel_id=1, source_target_pairs={{0,1},{1,2},{2,3},{3,4},{4,5},{5,6},{6,7},{7,8},{8,9},{9,10},{10,1... | collective-permute-start | bytes 1966088 | tf_op jit(solution)/shard_map/ppermute | solution.py:156
  83.5 15.5 %collective-permute-start.9 = (bf16[320,1024]{1,0:T(8,128)(2,1)S(1)}, bf16[320,1024]{1,0:T(8,128)(2,1)}, u32[]{:S(2)}, u32[]{:S(2)}) collective-permute-start(bf16[320,1024]{1,0:T(8,128)(2,1)S(1)} %collective-permute-done.4), channel_id=1, source_target_pairs={{0,1},{1,2},{2,3},{3,4},{4,5},{5,6},{6,7},{7,8},{8,9},{9,10},{10,1... | collective-permute-start | bytes 1966088 | tf_op jit(solution)/shard_map/ppermute | solution.py:156
  95.1 13.9 %collective-permute-start.15 = (bf16[320,1024]{1,0:T(8,128)(2,1)}, bf16[320,1024]{1,0:T(8,128)(2,1)}, u32[]{:S(2)}, u32[]{:S(2)}) collective-permute-start(bf16[320,1024]{1,0:T(8,128)(2,1)} %collective-permute-done.14), channel_id=1, source_target_pairs={{0,1},{1,2},{2,3},{3,4},{4,5},{5,6},{6,7},{7,8},{8,9},{9,10},{10,1... | collective-permute-start | bytes 1966088 | tf_op jit(solution)/shard_map/ppermute | solution.py:156
  99.0 15.1 %collective-permute-start.10 = (bf16[320,1024]{1,0:T(8,128)(2,1)}, bf16[320,1024]{1,0:T(8,128)(2,1)}, u32[]{:S(2)}, u32[]{:S(2)}) collective-permute-start(bf16[320,1024]{1,0:T(8,128)(2,1)} %collective-permute-done.9), channel_id=1, source_target_pairs={{0,1},{1,2},{2,3},{3,4},{4,5},{5,6},{6,7},{7,8},{8,9},{9,10},{10,1... | collective-permute-start | bytes 1966088 | tf_op jit(solution)/shard_map/ppermute | solution.py:156
  101.5 32.8 %all-to-all-start.2 = ((f32[32,16,896]{2,1,0:T(8,128)}), f32[32,16,896]{2,1,0:T(8,128)S(1)}, u32[]{:S(2)}, u32[]{:S(2)}) async-start(f32[32,16,896]{2,1,0:T(8,128)} %pad_maximum_fusion), calls=%async_computation.2 | async-start | bytes 3670016 | tf_op jit(solution)/shard_map/all_to_all | solution.py:207
  109.0 20.0 %copy-start.3 = (bf16[1024,256]{1,0:T(8,128)(2,1)S(1)}, bf16[1024,256]{1,0:T(8,128)(2,1)}, u32[]{:S(2)}) copy-start(bf16[1024,256]{1,0:T(8,128)(2,1)} %param.3) | copy-start | bytes 1572868
  109.0 12.8 %collective-permute-start.16 = (bf16[320,1024]{1,0:T(8,128)(2,1)}, bf16[320,1024]{1,0:T(8,128)(2,1)S(1)}, u32[]{:S(2)}, u32[]{:S(2)}) collective-permute-start(bf16[320,1024]{1,0:T(8,128)(2,1)} %collective-permute-done.15), channel_id=1, source_target_pairs={{0,1},{1,2},{2,3},{3,4},{4,5},{5,6},{6,7},{7,8},{8,9},{9,10},{10,1... | collective-permute-start | bytes 1966088 | tf_op jit(solution)/shard_map/ppermute | solution.py:156
  115.0 13.9 %collective-permute-start.11 = (bf16[160,1024]{1,0:T(8,128)(2,1)S(1)}, bf16[160,1024]{1,0:T(8,128)(2,1)S(1)}, u32[]{:S(2)}, u32[]{:S(2)}) collective-permute-start(bf16[160,1024]{1,0:T(8,128)(2,1)S(1)} %constant_dynamic-slice_fusion.1), channel_id=1, source_target_pairs={{0,1},{1,2},{2,3},{3,4},{4,5},{5,6},{6,7},{7,8},{8,9},{9,10},{10,1... | collective-permute-start | bytes 983048 | tf_op jit(solution)/shard_map/ppermute | solution.py:156
  121.8 9.2 %collective-permute-start.17 = (bf16[160,1024]{1,0:T(8,128)(2,1)S(1)}, bf16[160,1024]{1,0:T(8,128)(2,1)S(1)}, u32[]{:S(2)}, u32[]{:S(2)}) collective-permute-start(bf16[160,1024]{1,0:T(8,128)(2,1)S(1)} %constant_dynamic-slice_fusion), channel_id=1, source_target_pairs={{0,1},{1,2},{2,3},{3,4},{4,5},{5,6},{6,7},{7,8},{8,9},{9,10},{10,1... | collective-permute-start | bytes 983048 | tf_op jit(solution)/shard_map/ppermute | solution.py:156
  134.3 36.6 %all-to-all-start.1 = ((f32[32,16,896]{2,1,0:T(8,128)}), f32[32,16,896]{2,1,0:T(8,128)}, u32[]{:S(2)}, u32[]{:S(2)}) async-start(f32[32,16,896]{2,1,0:T(8,128)} %pad_maximum_fusion.1), calls=%async_computation.1 | async-start | bytes 3670016 | tf_op jit(solution)/shard_map/all_to_all | solution.py:207
  189.8 18.4 %all-to-all-start.4 = ((f32[16,8,128]{2,1,0:T(8,128)}), f32[16,8,128]{2,1,0:T(8,128)S(1)}, u32[]{:S(2)}, u32[]{:S(2)}) async-start(f32[16,8,128]{2,1,0:T(8,128)} %shard_map.31), calls=%async_computation.4 | async-start | bytes 131072 | tf_op jit(solution)/shard_map/all_to_all | solution.py:212
  (6 other events, 37.6 us)

commit v9 on v8

--- a/solution.py
+++ b/solution.py
@@ -8,8 +8,8 @@
 from jax.sharding import PartitionSpec as P
 
 epsilon = 1e-06
-GROUPS = (768, 896, 896)
-TIES = {(5, 0): 0}
+GROUPS = (768, 640, 640, 512)
+TIES = {(4, 1): 0, (6, 1): 1}
 VMEM = pltpu.VMEM
 LIMIT = 48 * 1024 * 1024
 EXACT = lax.Precision.HIGHEST

time: 227 us -> 229 us (level)
  waiting for transfers between devices: 52.5 us -> 46.2 us
  local copies, waits for them, and re-layouts: 6.62 us -> 10.2 us
  starting transfers between devices: 111 us -> 114 us
    all_to_all x3 -> x4, waiting for transfers between devices: 20.3 us -> 14 us  [on_device(): blocks.append(lax.all_to_all(ready, 'dp', 0, 0))]
    all_to_all x3 -> x4, starting transfers between devices: 26.3 us -> 28.8 us  [on_device(): blocks.append(lax.all_to_all(ready, 'dp', 0, 0))]
    pallas_call x3 -> x4, Pallas kernels: 8.68 us -> 10.6 us  [gram_add(): pl.pallas_call(functools.partial(gram_kernel, replicas), out_shape=jax.Sh...]
    dot_general x6 -> x8, matrix products: 10.5 us -> 11.9 us  [on_device(): lax.dot_general(grads[k], group, (((0,), (1,)), ((), ())), preferred_elem...]
    concatenate x3 -> x4, other arithmetic: 4.03 us -> 4.7 us  [on_device(): ready = jnp.concatenate(parts, axis=1)]
  transfers between devices with their start and end apart: 22 -> 23, of which waited for: 11 -> 13; matrix products, arithmetic and copies ran while one was open for 9% -> 11% of each run, Pallas kernels for 2% -> 3%
where the time goes in v9:
time: 229 us; the launch traced here: 227 us
  starting transfers between devices  114 us (50%)
  waiting for transfers between devices  46.2 us (20%)
  blocking collectives  25.5 us (11%)
  Pallas kernels  14.8 us (6%)
  matrix products  11.9 us (5%)
  local copies, waits for them, and re-layouts  10.2 us (4%)
  other arithmetic  4.7 us (2%)
    ppermute x16, starting transfers between devices, move(): return lax.ppermute(slab, ('dp', 'tensor'), onward)  65.6 us
    all_to_all x4, starting transfers between devices, on_device(): blocks.append(lax.all_to_all(ready, 'dp', 0, 0))  28.8 us
    ppermute x16, waiting for transfers between devices, move(): return lax.ppermute(slab, ('dp', 'tensor'), onward)  20.6 us
    all_to_all x1, blocking collectives, on_device(): home = lax.all_to_all(home, 'dp', 0, 0)  14.1 us
    all_to_all x4, waiting for transfers between devices, on_device(): blocks.append(lax.all_to_all(ready, 'dp', 0, 0))  14 us
    dot_general x8, matrix products, on_device(): lax.dot_general(grads[k], group, (((0,), (1,)), ((), ())), preferred_elem...  11.9 us
    all_to_all x1, waiting for transfers between devices, on_device(): parts = lax.all_to_all(parts, 'tensor', 0, 0)  11.6 us
    all_to_all x1, blocking collectives, on_device(): parts = sum_and_spread(lax.all_to_all(peers, 'dp', 0, 0), slabs)  11.5 us
  transfers between devices with their start and end apart: 23, of which 13 were waited for; matrix products, arithmetic and copies ran while one was open for 11% of the time, Pallas kernels for 3%

profile of v9, /device:TPU:1, one launch (start us, length us, event | category | flops | bytes accessed | tf_op | source)
XLA Modules:
  0.0 227.4 jit_solution(7945641755350744380)
XLA Ops:
  0.0 8.8 %collective-permute-start.8 = (bf16[320,1024]{1,0:T(8,128)(2,1)}, bf16[320,1024]{1,0:T(8,128)(2,1)S(1)}, u32[]{:S(2)}, u32[]{:S(2)}) collective-permute-start(bf16[320,1024]{1,0:T(8,128)(2,1)} %bitcast.45), channel_id=1, source_target_pairs={{0,16},{16,0},{32,48},{48,32},{64,80},{80,64},{96,112},{112,96},{1... | collective-permute-start | bytes 1966088 | tf_op jit(solution)/shard_map/ppermute | solution.py:169
  8.8 5.8 %collective-permute-start = (bf16[320,1024]{1,0:T(8,128)(2,1)}, bf16[320,1024]{1,0:T(8,128)(2,1)}, u32[]{:S(2)}, u32[]{:S(2)}) collective-permute-start(bf16[320,1024]{1,0:T(8,128)(2,1)} %bitcast.46), channel_id=1, source_target_pairs={{0,1},{1,2},{2,3},{3,4},{4,5},{5,6},{6,7},{7,8},{8,9},{9,10},{10,1... | collective-permute-start | bytes 1966088 | tf_op jit(solution)/shard_map/ppermute | solution.py:156
  22.4 5.0 %collective-permute-start.1 = (bf16[320,1024]{1,0:T(8,128)(2,1)}, bf16[320,1024]{1,0:T(8,128)(2,1)S(1)}, u32[]{:S(2)}, u32[]{:S(2)}) collective-permute-start(bf16[320,1024]{1,0:T(8,128)(2,1)} %collective-permute-done), channel_id=1, source_target_pairs={{0,1},{1,2},{2,3},{3,4},{4,5},{5,6},{6,7},{7,8},{8,9},{9,10},{10,1... | collective-permute-start | bytes 1966088 | tf_op jit(solution)/shard_map/ppermute | solution.py:156
  29.3 5.0 %collective-permute-start.11 = (bf16[320,1024]{1,0:T(8,128)(2,1)S(1)}, bf16[320,1024]{1,0:T(8,128)(2,1)S(1)}, u32[]{:S(2)}, u32[]{:S(2)}) collective-permute-start(bf16[320,1024]{1,0:T(8,128)(2,1)S(1)} %collective-permute-done.9), channel_id=1, source_target_pairs={{0,1},{1,2},{2,3},{3,4},{4,5},{5,6},{6,7},{7,8},{8,9},{9,10},{10,1... | collective-permute-start | bytes 1966088 | tf_op jit(solution)/shard_map/ppermute | solution.py:156
  36.5 5.1 %collective-permute-start.2 = (bf16[320,1024]{1,0:T(8,128)(2,1)S(1)}, bf16[320,1024]{1,0:T(8,128)(2,1)}, u32[]{:S(2)}, u32[]{:S(2)}) collective-permute-start(bf16[320,1024]{1,0:T(8,128)(2,1)S(1)} %collective-permute-done.1), channel_id=1, source_target_pairs={{0,1},{1,2},{2,3},{3,4},{4,5},{5,6},{6,7},{7,8},{8,9},{9,10},{10,1... | collective-permute-start | bytes 1966088 | tf_op jit(solution)/shard_map/ppermute | solution.py:156
  45.3 8.4 %all-to-all-start = ((f32[32,16,768]{2,1,0:T(8,128)}), f32[32,16,768]{2,1,0:T(8,128)S(1)}, u32[]{:S(2)}, u32[]{:S(2)}) async-start(f32[32,16,768]{2,1,0:T(8,128)} %pad_maximum_fusion), calls=%async_computation | async-start | bytes 3145728 | tf_op jit(solution)/shard_map/all_to_all | solution.py:207
  53.7 3.8 %collective-permute-start.12 = (bf16[320,1024]{1,0:T(8,128)(2,1)S(1)}, bf16[320,1024]{1,0:T(8,128)(2,1)S(1)}, u32[]{:S(2)}, u32[]{:S(2)}) collective-permute-start(bf16[320,1024]{1,0:T(8,128)(2,1)S(1)} %collective-permute-done.11), channel_id=1, source_target_pairs={{0,1},{1,2},{2,3},{3,4},{4,5},{5,6},{6,7},{7,8},{8,9},{9,10},{10,1... | collective-permute-start | bytes 1966088 | tf_op jit(solution)/shard_map/ppermute | solution.py:156
  60.0 5.3 %collective-permute-done.12 = bf16[320,1024]{1,0:T(8,128)(2,1)S(1)} collective-permute-done((bf16[320,1024]{1,0:T(8,128)(2,1)S(1)}, bf16[320,1024]{1,0:T(8,128)(2,1)S(1)}, u32[]{:S(2)}, u32[]{:S(2)}) %collective-permute-start.12) | collective-permute-done | bytes 655392 | tf_op jit(solution)/shard_map/ppermute | solution.py:156
  65.4 5.0 %collective-permute-start.13 = (bf16[320,1024]{1,0:T(8,128)(2,1)S(1)}, bf16[320,1024]{1,0:T(8,128)(2,1)}, u32[]{:S(2)}, u32[]{:S(2)}) collective-permute-start(bf16[320,1024]{1,0:T(8,128)(2,1)S(1)} %collective-permute-done.12), channel_id=1, source_target_pairs={{0,1},{1,2},{2,3},{3,4},{4,5},{5,6},{6,7},{7,8},{8,9},{9,10},{10,1... | collective-permute-start | bytes 1966088 | tf_op jit(solution)/shard_map/ppermute | solution.py:156
  72.4 4.9 %collective-permute-start.4 = (bf16[320,1024]{1,0:T(8,128)(2,1)S(1)}, bf16[320,1024]{1,0:T(8,128)(2,1)}, u32[]{:S(2)}, u32[]{:S(2)}) collective-permute-start(bf16[320,1024]{1,0:T(8,128)(2,1)S(1)} %collective-permute-done.3), channel_id=1, source_target_pairs={{0,1},{1,2},{2,3},{3,4},{4,5},{5,6},{6,7},{7,8},{8,9},{9,10},{10,1... | collective-permute-start | bytes 1966088 | tf_op jit(solution)/shard_map/ppermute | solution.py:156
  83.7 4.7 %collective-permute-start.14 = (bf16[320,1024]{1,0:T(8,128)(2,1)}, bf16[320,1024]{1,0:T(8,128)(2,1)}, u32[]{:S(2)}, u32[]{:S(2)}) collective-permute-start(bf16[320,1024]{1,0:T(8,128)(2,1)} %collective-permute-done.13), channel_id=1, source_target_pairs={{0,1},{1,2},{2,3},{3,4},{4,5},{5,6},{6,7},{7,8},{8,9},{9,10},{10,1... | collective-permute-start | bytes 1966088 | tf_op jit(solution)/shard_map/ppermute | solution.py:156
  88.4 7.1 %all-to-all-start.1 = ((f32[32,16,640]{2,1,0:T(8,128)}), f32[32,16,640]{2,1,0:T(8,128)S(1)}, u32[]{:S(2)}, u32[]{:S(2)}) async-start(f32[32,16,640]{2,1,0:T(8,128)} %pad_maximum_fusion.1), calls=%async_computation.1 | async-start | bytes 2621440 | tf_op jit(solution)/shard_map/all_to_all | solution.py:207
  95.5 4.4 %collective-permute-start.5 = (bf16[320,1024]{1,0:T(8,128)(2,1)}, bf16[320,1024]{1,0:T(8,128)(2,1)}, u32[]{:S(2)}, u32[]{:S(2)}) collective-permute-start(bf16[320,1024]{1,0:T(8,128)(2,1)} %collective-permute-done.4), channel_id=1, source_target_pairs={{0,1},{1,2},{2,3},{3,4},{4,5},{5,6},{6,7},{7,8},{8,9},{9,10},{10,1... | collective-permute-start | bytes 1966088 | tf_op jit(solution)/shard_map/ppermute | solution.py:156
  103.3 4.4 %collective-permute-done.5 = bf16[320,1024]{1,0:T(8,128)(2,1)} collective-permute-done((bf16[320,1024]{1,0:T(8,128)(2,1)}, bf16[320,1024]{1,0:T(8,128)(2,1)}, u32[]{:S(2)}, u32[]{:S(2)}) %collective-permute-start.5) | collective-permute-done | bytes 655392 | tf_op jit(solution)/shard_map/ppermute | solution.py:156
  108.8 5.2 %collective-permute-start.6 = (bf16[320,1024]{1,0:T(8,128)(2,1)}, bf16[320,1024]{1,0:T(8,128)(2,1)}, u32[]{:S(2)}, u32[]{:S(2)}) collective-permute-start(bf16[320,1024]{1,0:T(8,128)(2,1)} %collective-permute-done.5), channel_id=1, source_target_pairs={{0,1},{1,2},{2,3},{3,4},{4,5},{5,6},{6,7},{7,8},{8,9},{9,10},{10,1... | collective-permute-start | bytes 1966088 | tf_op jit(solution)/shard_map/ppermute | solution.py:156
  120.1 4.0 %collective-permute-start.16 = (bf16[320,1024]{1,0:T(8,128)(2,1)}, bf16[320,1024]{1,0:T(8,128)(2,1)S(1)}, u32[]{:S(2)}, u32[]{:S(2)}) collective-permute-start(bf16[320,1024]{1,0:T(8,128)(2,1)} %collective-permute-done.15), channel_id=1, source_target_pairs={{0,1},{1,2},{2,3},{3,4},{4,5},{5,6},{6,7},{7,8},{8,9},{9,10},{10,1... | collective-permute-start | bytes 1966088 | tf_op jit(solution)/shard_map/ppermute | solution.py:156
  124.1 7.0 %all-to-all-start.3 = ((f32[32,16,640]{2,1,0:T(8,128)}), f32[32,16,640]{2,1,0:T(8,128)}, u32[]{:S(2)}, u32[]{:S(2)}) async-start(f32[32,16,640]{2,1,0:T(8,128)} %pad_maximum_fusion.2), calls=%async_computation.3 | async-start | bytes 2621440 | tf_op jit(solution)/shard_map/all_to_all | solution.py:207
  145.9 4.4 %all-to-all-done.3.refs_2_ = f32[32,16,640]{2,1,0:T(8,128)} async-done(((f32[32,16,640]{2,1,0:T(8,128)}), f32[32,16,640]{2,1,0:T(8,128)}, u32[]{:S(2)}, u32[]{:S(2)}) %all-to-all-start.3) | async-done | bytes 1310752 | tf_op jit(solution)/shard_map/all_to_all | solution.py:207
  150.3 6.2 %all-to-all-start.2 = ((f32[32,16,512]{2,1,0:T(8,128)}), f32[32,16,512]{2,1,0:T(8,128)}, u32[]{:S(2)}, u32[]{:S(2)}) async-start(f32[32,16,512]{2,1,0:T(8,128)} %pad_maximum_fusion.3), calls=%async_computation.2 | async-start | bytes 2097152 | tf_op jit(solution)/shard_map/all_to_all | solution.py:207
  164.2 9.6 %all-to-all-done.2.refs_3_ = f32[32,16,512]{2,1,0:T(8,128)} async-done(((f32[32,16,512]{2,1,0:T(8,128)}), f32[32,16,512]{2,1,0:T(8,128)}, u32[]{:S(2)}, u32[]{:S(2)}) %all-to-all-start.2) | async-done | bytes 1048608 | tf_op jit(solution)/shard_map/all_to_all | solution.py:207
  176.8 11.5 %all_to_all.35.parts_ref = f32[32,8,128]{2,1,0:T(8,128)} all-to-all(f32[32,8,128]{2,1,0:T(8,128)S(1)} %broadcast_in_dim.7), channel_id=1, replica_groups=mesh['dp'=32,'tensor'=16] {'dp'}, dimensions={0} | all-to-all | bytes 262144 | tf_op jit(solution)/shard_map/all_to_all | solution.py:211
  189.8 8.6 %all-to-all-start.5 = ((f32[16,8,128]{2,1,0:T(8,128)}), f32[16,8,128]{2,1,0:T(8,128)S(1)}, u32[]{:S(2)}, u32[]{:S(2)}) async-start(f32[16,8,128]{2,1,0:T(8,128)} %shard_map.32), calls=%async_computation.5 | async-start | bytes 131072 | tf_op jit(solution)/shard_map/all_to_all | solution.py:212
  198.4 11.6 %all-to-all-done.5.parts_ref = f32[16,8,128]{2,1,0:T(8,128)S(1)} async-done(((f32[16,8,128]{2,1,0:T(8,128)}), f32[16,8,128]{2,1,0:T(8,128)S(1)}, u32[]{:S(2)}, u32[]{:S(2)}) %all-to-all-start.5) | async-done | bytes 65568 | tf_op jit(solution)/shard_map/all_to_all | solution.py:212
  212.6 14.1 %all_to_all.36 = f32[32,8,160]{2,1,0:T(8,128)S(1)} all-to-all(f32[32,8,160]{2,1,0:T(8,128)S(1)} %shard_map.33), channel_id=1, replica_groups=mesh['dp'=32,'tensor'=16] {'dp'}, dimensions={0} | all-to-all | bytes 327680 | tf_op jit(solution)/shard_map/all_to_all | solution.py:214
  (73 shorter events, 67.2 us)
Async XLA Ops:
  0.0 14.5 %collective-permute-start.8 = (bf16[320,1024]{1,0:T(8,128)(2,1)}, bf16[320,1024]{1,0:T(8,128)(2,1)S(1)}, u32[]{:S(2)}, u32[]{:S(2)}) collective-permute-start(bf16[320,1024]{1,0:T(8,128)(2,1)} %bitcast.45), channel_id=1, source_target_pairs={{0,16},{16,0},{32,48},{48,32},{64,80},{80,64},{96,112},{112,96},{1... | collective-permute-start | bytes 1966088 | tf_op jit(solution)/shard_map/ppermute | solution.py:169
  8.8 13.6 %collective-permute-start = (bf16[320,1024]{1,0:T(8,128)(2,1)}, bf16[320,1024]{1,0:T(8,128)(2,1)}, u32[]{:S(2)}, u32[]{:S(2)}) collective-permute-start(bf16[320,1024]{1,0:T(8,128)(2,1)} %bitcast.46), channel_id=1, source_target_pairs={{0,1},{1,2},{2,3},{3,4},{4,5},{5,6},{6,7},{7,8},{8,9},{9,10},{10,1... | collective-permute-start | bytes 1966088 | tf_op jit(solution)/shard_map/ppermute | solution.py:156
  14.6 14.7 %collective-permute-start.9 = (bf16[320,1024]{1,0:T(8,128)(2,1)S(1)}, bf16[320,1024]{1,0:T(8,128)(2,1)S(1)}, u32[]{:S(2)}, u32[]{:S(2)}) collective-permute-start(bf16[320,1024]{1,0:T(8,128)(2,1)S(1)} %collective-permute-done.8), channel_id=1, source_target_pairs={{0,1},{1,2},{2,3},{3,4},{4,5},{5,6},{6,7},{7,8},{8,9},{9,10},{10,1... | collective-permute-start | bytes 1966088 | tf_op jit(solution)/shard_map/ppermute | solution.py:156
  17.2 10.2 %collective-permute-start.10 = (bf16[1024,256]{1,0:T(8,128)(2,1)}, bf16[1024,256]{1,0:T(8,128)(2,1)S(1)}, u32[]{:S(2)}, u32[]{:S(2)}) collective-permute-start(bf16[1024,256]{1,0:T(8,128)(2,1)} %param.3), channel_id=1, source_target_pairs={{0,16},{16,0},{32,48},{48,32},{64,80},{80,64},{96,112},{112,96},{1... | collective-permute-start | bytes 1572872 | tf_op jit(solution)/shard_map/ppermute | solution.py:172
  22.4 14.0 %collective-permute-start.1 = (bf16[320,1024]{1,0:T(8,128)(2,1)}, bf16[320,1024]{1,0:T(8,128)(2,1)S(1)}, u32[]{:S(2)}, u32[]{:S(2)}) collective-permute-start(bf16[320,1024]{1,0:T(8,128)(2,1)} %collective-permute-done), channel_id=1, source_target_pairs={{0,1},{1,2},{2,3},{3,4},{4,5},{5,6},{6,7},{7,8},{8,9},{9,10},{10,1... | collective-permute-start | bytes 1966088 | tf_op jit(solution)/shard_map/ppermute | solution.py:156
  29.3 14.0 %collective-permute-start.11 = (bf16[320,1024]{1,0:T(8,128)(2,1)S(1)}, bf16[320,1024]{1,0:T(8,128)(2,1)S(1)}, u32[]{:S(2)}, u32[]{:S(2)}) collective-permute-start(bf16[320,1024]{1,0:T(8,128)(2,1)S(1)} %collective-permute-done.9), channel_id=1, source_target_pairs={{0,1},{1,2},{2,3},{3,4},{4,5},{5,6},{6,7},{7,8},{8,9},{9,10},{10,1... | collective-permute-start | bytes 1966088 | tf_op jit(solution)/shard_map/ppermute | solution.py:156
  36.5 21.1 %collective-permute-start.2 = (bf16[320,1024]{1,0:T(8,128)(2,1)S(1)}, bf16[320,1024]{1,0:T(8,128)(2,1)}, u32[]{:S(2)}, u32[]{:S(2)}) collective-permute-start(bf16[320,1024]{1,0:T(8,128)(2,1)S(1)} %collective-permute-done.1), channel_id=1, source_target_pairs={{0,1},{1,2},{2,3},{3,4},{4,5},{5,6},{6,7},{7,8},{8,9},{9,10},{10,1... | collective-permute-start | bytes 1966088 | tf_op jit(solution)/shard_map/ppermute | solution.py:156
  45.3 34.2 %all-to-all-start = ((f32[32,16,768]{2,1,0:T(8,128)}), f32[32,16,768]{2,1,0:T(8,128)S(1)}, u32[]{:S(2)}, u32[]{:S(2)}) async-start(f32[32,16,768]{2,1,0:T(8,128)} %pad_maximum_fusion), calls=%async_computation | async-start | bytes 3145728 | tf_op jit(solution)/shard_map/all_to_all | solution.py:207
  53.7 11.6 %collective-permute-start.12 = (bf16[320,1024]{1,0:T(8,128)(2,1)S(1)}, bf16[320,1024]{1,0:T(8,128)(2,1)S(1)}, u32[]{:S(2)}, u32[]{:S(2)}) collective-permute-start(bf16[320,1024]{1,0:T(8,128)(2,1)S(1)} %collective-permute-done.11), channel_id=1, source_target_pairs={{0,1},{1,2},{2,3},{3,4},{4,5},{5,6},{6,7},{7,8},{8,9},{9,10},{10,1... | collective-permute-start | bytes 1966088 | tf_op jit(solution)/shard_map/ppermute | solution.py:156
  57.6 14.8 %collective-permute-start.3 = (bf16[320,1024]{1,0:T(8,128)(2,1)}, bf16[320,1024]{1,0:T(8,128)(2,1)S(1)}, u32[]{:S(2)}, u32[]{:S(2)}) collective-permute-start(bf16[320,1024]{1,0:T(8,128)(2,1)} %collective-permute-done.2), channel_id=1, source_target_pairs={{0,1},{1,2},{2,3},{3,4},{4,5},{5,6},{6,7},{7,8},{8,9},{9,10},{10,1... | collective-permute-start | bytes 1966088 | tf_op jit(solution)/shard_map/ppermute | solution.py:156
  65.4 13.8 %copy-start = (bf16[320,1024]{1,0:T(8,128)(2,1)}, bf16[320,1024]{1,0:T(8,128)(2,1)S(1)}, u32[]{:S(2)}) copy-start(bf16[320,1024]{1,0:T(8,128)(2,1)S(1)} %collective-permute-done.12) | copy-start | bytes 1966084
  65.4 14.1 %collective-permute-start.13 = (bf16[320,1024]{1,0:T(8,128)(2,1)S(1)}, bf16[320,1024]{1,0:T(8,128)(2,1)}, u32[]{:S(2)}, u32[]{:S(2)}) collective-permute-start(bf16[320,1024]{1,0:T(8,128)(2,1)S(1)} %collective-permute-done.12), channel_id=1, source_target_pairs={{0,1},{1,2},{2,3},{3,4},{4,5},{5,6},{6,7},{7,8},{8,9},{9,10},{10,1... | collective-permute-start | bytes 1966088 | tf_op jit(solution)/shard_map/ppermute | solution.py:156
  72.4 23.1 %collective-permute-start.4 = (bf16[320,1024]{1,0:T(8,128)(2,1)S(1)}, bf16[320,1024]{1,0:T(8,128)(2,1)}, u32[]{:S(2)}, u32[]{:S(2)}) collective-permute-start(bf16[320,1024]{1,0:T(8,128)(2,1)S(1)} %collective-permute-done.3), channel_id=1, source_target_pairs={{0,1},{1,2},{2,3},{3,4},{4,5},{5,6},{6,7},{7,8},{8,9},{9,10},{10,1... | collective-permute-start | bytes 1966088 | tf_op jit(solution)/shard_map/ppermute | solution.py:156
  83.7 16.3 %collective-permute-start.14 = (bf16[320,1024]{1,0:T(8,128)(2,1)}, bf16[320,1024]{1,0:T(8,128)(2,1)}, u32[]{:S(2)}, u32[]{:S(2)}) collective-permute-start(bf16[320,1024]{1,0:T(8,128)(2,1)} %collective-permute-done.13), channel_id=1, source_target_pairs={{0,1},{1,2},{2,3},{3,4},{4,5},{5,6},{6,7},{7,8},{8,9},{9,10},{10,1... | collective-permute-start | bytes 1966088 | tf_op jit(solution)/shard_map/ppermute | solution.py:156
  88.4 27.6 %all-to-all-start.1 = ((f32[32,16,640]{2,1,0:T(8,128)}), f32[32,16,640]{2,1,0:T(8,128)S(1)}, u32[]{:S(2)}, u32[]{:S(2)}) async-start(f32[32,16,640]{2,1,0:T(8,128)} %pad_maximum_fusion.1), calls=%async_computation.1 | async-start | bytes 2621440 | tf_op jit(solution)/shard_map/all_to_all | solution.py:207
  95.5 12.2 %collective-permute-start.5 = (bf16[320,1024]{1,0:T(8,128)(2,1)}, bf16[320,1024]{1,0:T(8,128)(2,1)}, u32[]{:S(2)}, u32[]{:S(2)}) collective-permute-start(bf16[320,1024]{1,0:T(8,128)(2,1)} %collective-permute-done.4), channel_id=1, source_target_pairs={{0,1},{1,2},{2,3},{3,4},{4,5},{5,6},{6,7},{7,8},{8,9},{9,10},{10,1... | collective-permute-start | bytes 1966088 | tf_op jit(solution)/shard_map/ppermute | solution.py:156
  99.9 16.0 %collective-permute-start.15 = (bf16[320,1024]{1,0:T(8,128)(2,1)}, bf16[320,1024]{1,0:T(8,128)(2,1)}, u32[]{:S(2)}, u32[]{:S(2)}) collective-permute-start(bf16[320,1024]{1,0:T(8,128)(2,1)} %collective-permute-done.14), channel_id=1, source_target_pairs={{0,1},{1,2},{2,3},{3,4},{4,5},{5,6},{6,7},{7,8},{8,9},{9,10},{10,1... | collective-permute-start | bytes 1966088 | tf_op jit(solution)/shard_map/ppermute | solution.py:156
  108.8 22.3 %collective-permute-start.6 = (bf16[320,1024]{1,0:T(8,128)(2,1)}, bf16[320,1024]{1,0:T(8,128)(2,1)}, u32[]{:S(2)}, u32[]{:S(2)}) collective-permute-start(bf16[320,1024]{1,0:T(8,128)(2,1)} %collective-permute-done.5), channel_id=1, source_target_pairs={{0,1},{1,2},{2,3},{3,4},{4,5},{5,6},{6,7},{7,8},{8,9},{9,10},{10,1... | collective-permute-start | bytes 1966088 | tf_op jit(solution)/shard_map/ppermute | solution.py:156
  120.1 15.9 %collective-permute-start.16 = (bf16[320,1024]{1,0:T(8,128)(2,1)}, bf16[320,1024]{1,0:T(8,128)(2,1)S(1)}, u32[]{:S(2)}, u32[]{:S(2)}) collective-permute-start(bf16[320,1024]{1,0:T(8,128)(2,1)} %collective-permute-done.15), channel_id=1, source_target_pairs={{0,1},{1,2},{2,3},{3,4},{4,5},{5,6},{6,7},{7,8},{8,9},{9,10},{10,1... | collective-permute-start | bytes 1966088 | tf_op jit(solution)/shard_map/ppermute | solution.py:156
  124.1 26.2 %all-to-all-start.3 = ((f32[32,16,640]{2,1,0:T(8,128)}), f32[32,16,640]{2,1,0:T(8,128)}, u32[]{:S(2)}, u32[]{:S(2)}) async-start(f32[32,16,640]{2,1,0:T(8,128)} %pad_maximum_fusion.2), calls=%async_computation.3 | async-start | bytes 2621440 | tf_op jit(solution)/shard_map/all_to_all | solution.py:207
  132.2 8.2 %collective-permute-start.7 = (bf16[160,1024]{1,0:T(8,128)(2,1)S(1)}, bf16[160,1024]{1,0:T(8,128)(2,1)S(1)}, u32[]{:S(2)}, u32[]{:S(2)}) collective-permute-start(bf16[160,1024]{1,0:T(8,128)(2,1)S(1)} %constant_dynamic-slice_fusion.2), channel_id=1, source_target_pairs={{0,1},{1,2},{2,3},{3,4},{4,5},{5,6},{6,7},{7,8},{8,9},{9,10},{10,1... | collective-permute-start | bytes 983048 | tf_op jit(solution)/shard_map/ppermute | solution.py:156
  136.1 8.2 %collective-permute-start.17 = (bf16[160,1024]{1,0:T(8,128)(2,1)S(1)}, bf16[160,1024]{1,0:T(8,128)(2,1)S(1)}, u32[]{:S(2)}, u32[]{:S(2)}) collective-permute-start(bf16[160,1024]{1,0:T(8,128)(2,1)S(1)} %constant_dynamic-slice_fusion), channel_id=1, source_target_pairs={{0,1},{1,2},{2,3},{3,4},{4,5},{5,6},{6,7},{7,8},{8,9},{9,10},{10,1... | collective-permute-start | bytes 983048 | tf_op jit(solution)/shard_map/ppermute | solution.py:156
  150.3 23.5 %all-to-all-start.2 = ((f32[32,16,512]{2,1,0:T(8,128)}), f32[32,16,512]{2,1,0:T(8,128)}, u32[]{:S(2)}, u32[]{:S(2)}) async-start(f32[32,16,512]{2,1,0:T(8,128)} %pad_maximum_fusion.3), calls=%async_computation.2 | async-start | bytes 2097152 | tf_op jit(solution)/shard_map/all_to_all | solution.py:207
  189.8 20.2 %all-to-all-start.5 = ((f32[16,8,128]{2,1,0:T(8,128)}), f32[16,8,128]{2,1,0:T(8,128)S(1)}, u32[]{:S(2)}, u32[]{:S(2)}) async-start(f32[16,8,128]{2,1,0:T(8,128)} %shard_map.32), calls=%async_computation.5 | async-start | bytes 131072 | tf_op jit(solution)/shard_map/all_to_all | solution.py:212
  (5 other events, 34.9 us)

commit v10 on v9

--- a/solution.py
+++ b/solution.py
@@ -8,8 +8,8 @@
 from jax.sharding import PartitionSpec as P
 
 epsilon = 1e-06
-GROUPS = (768, 640, 640, 512)
-TIES = {(4, 1): 0, (6, 1): 1}
+GROUP_ENDS = (2, 4, 6, 8)
+TIES = {(5, 0): 0, (7, 0): 1}
 VMEM = pltpu.VMEM
 LIMIT = 48 * 1024 * 1024
 EXACT = lax.Precision.HIGHEST
@@ -72,7 +72,7 @@
     )(parts)
 
 
-def combine_kernel(replicas, slabs, order, here_ref, parts_ref, *refs):
+def combine_kernel(replicas, slabs, order, counts, here_ref, parts_ref, *refs):
     blocks, out_ref = refs[:-1], refs[-1]
     packed = jnp.sum(parts_ref[...], axis=0)
     gram = jnp.concatenate(
@@ -105,26 +105,25 @@
         width *= 2
     part, width = out_ref.shape[1:]
     for core in range(2):
-        sums = []
-        for block_ref in blocks:
+        place = 0
+        for block_ref, count in zip(blocks, counts):
             total = 0.0
             for r in range(replicas):
                 row = (r + core) % 2 * part
                 total = total + block_ref[r // 2 * 2 + core, row:row + part] * down[r:r + 1]
-            sums.append(total)
-        sums = jnp.concatenate(sums, axis=1)
-        for place, (away, piece) in enumerate(order[core]):
-            slab = lax.rem(here_ref[0] + away, slabs)
-            out_ref[slab * 2 + piece] = sums[:, place * width:(place + 1) * width]
-
-
-def weighted_sums(replicas, slabs, order, here, parts, blocks):
+            for i in range(count):
+                away, piece = order[core][place]
+                slab = lax.rem(here_ref[0] + away, slabs)
+                out_ref[slab * 2 + piece] = total[:, i * width:(i + 1) * width]
+                place += 1
+
+
+def weighted_sums(replicas, slabs, order, counts, width, here, parts, blocks):
     part = blocks[0].shape[1] // 2
-    total = 2 * sum(b.shape[2] for b in blocks)
-    size = replicas * part * total
+    size = sum(b.size for b in blocks)
     return pl.pallas_call(
-        functools.partial(combine_kernel, replicas, slabs, order),
-        out_shape=jax.ShapeDtypeStruct((replicas, part, total // replicas), jnp.float32),
+        functools.partial(combine_kernel, replicas, slabs, order, counts),
+        out_shape=jax.ShapeDtypeStruct((replicas, part, width), jnp.float32),
         in_specs=[pl.BlockSpec(memory_space=pltpu.SMEM)]
         + [pl.BlockSpec(memory_space=VMEM)] * (1 + len(blocks)),
         out_specs=pl.BlockSpec(memory_space=VMEM),
@@ -155,16 +154,6 @@
     def move(slab):
         return lax.ppermute(slab, ("dp", "tensor"), onward)
 
-    def take(pieces, count):
-        taken = []
-        while count:
-            piece = pieces[0]
-            size = min(count, piece.shape[0])
-            taken.append(piece[:size])
-            count -= size
-            pieces = [piece[size:]][: piece.shape[0] > size] + pieces[1:]
-        return jnp.concatenate(taken, axis=0), pieces
-
     mine = activations.T
     chains = [mine, lax.ppermute(mine, "dp", sibling)]
     grads = [out_grads, out_grads]
@@ -174,7 +163,7 @@
     order = [[(0, 0)], [(0, 1)]]
     blocks = []
     gram = jnp.zeros((8, 128), jnp.float32)
-    sizes = list(GROUPS)
+    counts = []
     for step in range(1, half + 1):
         if step < half:
             chains = [move(slab) for slab in chains]
@@ -191,16 +180,19 @@
             for k in range(2):
                 held[k].append(move(own_half(chains[k])))
                 order[k].append((half, k))
-        if sum(piece.shape[0] for piece in held[0]) >= sizes[0]:
-            count = sizes.pop(0)
+        if step in GROUP_ENDS:
+            size = sum(piece.shape[0] for piece in held[0])
+            counts.append(size // rows)
             parts = []
             for k in range(2):
-                group, held[k] = take(held[k], count)
+                if size % 128:
+                    held[k].append(jnp.zeros((-size % 128, tokens), held[k][0].dtype))
                 grad = lax.dot_general(
-                    grads[k], group, (((0,), (1,)), ((), ())),
+                    grads[k], jnp.concatenate(held[k], axis=0), (((0,), (1,)), ((), ())),
                     preferred_element_type=jnp.float32,
                 )
                 parts.append(grad.reshape(replicas, part, -1))
+                held[k] = []
             ready = jnp.concatenate(parts, axis=1)
             if step < half:
                 chains[1], ready = lax.optimization_barrier((chains[1], ready))
@@ -210,7 +202,7 @@
     peers = jnp.broadcast_to(gram, (replicas, *gram.shape))
     parts = sum_and_spread(lax.all_to_all(peers, "dp", 0, 0), slabs)
     parts = lax.all_to_all(parts, "tensor", 0, 0)
-    home = weighted_sums(replicas, slabs, order, here, parts, blocks)
+    home = weighted_sums(replicas, slabs, order, counts, rows, here, parts, blocks)
     home = lax.all_to_all(home, "dp", 0, 0)
     return home.reshape(columns, -1).T
 

time: 229 us -> 221 us (0.965)
  local copies, waits for them, and re-layouts: 10.2 us -> 4.01 us
  matrix products: 11.9 us -> 15.4 us
  waiting for transfers between devices: 46.2 us -> 42.7 us
    slice x12 -> x0, local copies, waits for them, and re-layouts: 7.24 us -> none  [the longest x6 3.81 us: take(): pieces = [piece[size:]][:piece.shape[0] > size] + pieces[1:]]
    dot_general x8, matrix products: 11.9 us -> 15.4 us  [on_device(): lax.dot_general(grads[k], jnp.concatenate(held[k], axis=0), (((0,), (1,))...]
    all_to_all x4, waiting for transfers between devices: 14 us -> 11.4 us  [on_device(): blocks.append(lax.all_to_all(ready, 'dp', 0, 0))]
  transfers between devices with their start and end apart: 23 -> 23, of which waited for: 13 -> 11; matrix products, arithmetic and copies ran while one was open for 11% -> 11% of each run, Pallas kernels for 3% -> 4%
where the time goes in v10:
time: 221 us; the launch traced here: 220 us
  starting transfers between devices  112 us (51%)
  waiting for transfers between devices  42.7 us (19%)
  blocking collectives  25.5 us (12%)
  matrix products  15.4 us (7%)
  Pallas kernels  15.2 us (7%)
  other arithmetic  4.94 us (2%)
  local copies, waits for them, and re-layouts  4.01 us (2%)
    ppermute x16, starting transfers between devices, move(): return lax.ppermute(slab, ('dp', 'tensor'), onward)  65.6 us
    all_to_all x4, starting transfers between devices, on_device(): blocks.append(lax.all_to_all(ready, 'dp', 0, 0))  28.1 us
    ppermute x16, waiting for transfers between devices, move(): return lax.ppermute(slab, ('dp', 'tensor'), onward)  19.7 us
    dot_general x8, matrix products, on_device(): lax.dot_general(grads[k], jnp.concatenate(held[k], axis=0), (((0,), (1,))...  15.4 us
    all_to_all x1, blocking collectives, on_device(): home = lax.all_to_all(home, 'dp', 0, 0)  14.1 us
    all_to_all x1, waiting for transfers between devices, on_device(): parts = lax.all_to_all(parts, 'tensor', 0, 0)  11.6 us
    all_to_all x1, blocking collectives, on_device(): parts = sum_and_spread(lax.all_to_all(peers, 'dp', 0, 0), slabs)  11.4 us
    all_to_all x4, waiting for transfers between devices, on_device(): blocks.append(lax.all_to_all(ready, 'dp', 0, 0))  11.4 us
  transfers between devices with their start and end apart: 23, of which 11 were waited for; matrix products, arithmetic and copies ran while one was open for 11% of the time, Pallas kernels for 4%

profile of v10, /device:TPU:1, one launch (start us, length us, event | category | flops | bytes accessed | tf_op | source)
XLA Modules:
  0.0 219.7 jit_solution(4398643865449736329)
XLA Ops:
  0.0 8.8 %collective-permute-start.5 = (bf16[320,1024]{1,0:T(8,128)(2,1)}, bf16[320,1024]{1,0:T(8,128)(2,1)S(1)}, u32[]{:S(2)}, u32[]{:S(2)}) collective-permute-start(bf16[320,1024]{1,0:T(8,128)(2,1)} %bitcast.45), channel_id=1, source_target_pairs={{0,16},{16,0},{32,48},{48,32},{64,80},{80,64},{96,112},{112,96},{1... | collective-permute-start | bytes 1966088 | tf_op jit(solution)/shard_map/ppermute | solution.py:158
  8.8 5.8 %collective-permute-start = (bf16[320,1024]{1,0:T(8,128)(2,1)}, bf16[320,1024]{1,0:T(8,128)(2,1)}, u32[]{:S(2)}, u32[]{:S(2)}) collective-permute-start(bf16[320,1024]{1,0:T(8,128)(2,1)} %bitcast.46), channel_id=1, source_target_pairs={{0,1},{1,2},{2,3},{3,4},{4,5},{5,6},{6,7},{7,8},{8,9},{9,10},{10,1... | collective-permute-start | bytes 1966088 | tf_op jit(solution)/shard_map/ppermute | solution.py:155
  22.4 5.0 %collective-permute-start.1 = (bf16[320,1024]{1,0:T(8,128)(2,1)}, bf16[320,1024]{1,0:T(8,128)(2,1)S(1)}, u32[]{:S(2)}, u32[]{:S(2)}) collective-permute-start(bf16[320,1024]{1,0:T(8,128)(2,1)} %collective-permute-done), channel_id=1, source_target_pairs={{0,1},{1,2},{2,3},{3,4},{4,5},{5,6},{6,7},{7,8},{8,9},{9,10},{10,1... | collective-permute-start | bytes 1966088 | tf_op jit(solution)/shard_map/ppermute | solution.py:155
  29.3 5.1 %collective-permute-start.8 = (bf16[320,1024]{1,0:T(8,128)(2,1)}, bf16[320,1024]{1,0:T(8,128)(2,1)S(1)}, u32[]{:S(2)}, u32[]{:S(2)}) collective-permute-start(bf16[320,1024]{1,0:T(8,128)(2,1)} %collective-permute-done.6), channel_id=1, source_target_pairs={{0,1},{1,2},{2,3},{3,4},{4,5},{5,6},{6,7},{7,8},{8,9},{9,10},{10,1... | collective-permute-start | bytes 1966088 | tf_op jit(solution)/shard_map/ppermute | solution.py:155
  36.4 4.9 %collective-permute-start.2 = (bf16[320,1024]{1,0:T(8,128)(2,1)S(1)}, bf16[320,1024]{1,0:T(8,128)(2,1)}, u32[]{:S(2)}, u32[]{:S(2)}) collective-permute-start(bf16[320,1024]{1,0:T(8,128)(2,1)S(1)} %collective-permute-done.1), channel_id=1, source_target_pairs={{0,1},{1,2},{2,3},{3,4},{4,5},{5,6},{6,7},{7,8},{8,9},{9,10},{10,1... | collective-permute-start | bytes 1966088 | tf_op jit(solution)/shard_map/ppermute | solution.py:155
  46.9 4.9 %collective-permute-start.11 = (bf16[320,1024]{1,0:T(8,128)(2,1)S(1)}, bf16[320,1024]{1,0:T(8,128)(2,1)}, u32[]{:S(2)}, u32[]{:S(2)}) collective-permute-start(bf16[320,1024]{1,0:T(8,128)(2,1)S(1)} %collective-permute-done.8), channel_id=1, source_target_pairs={{0,1},{1,2},{2,3},{3,4},{4,5},{5,6},{6,7},{7,8},{8,9},{9,10},{10,1... | collective-permute-start | bytes 1966088 | tf_op jit(solution)/shard_map/ppermute | solution.py:155
  51.8 7.2 %all-to-all-start = ((f32[32,16,896]{2,1,0:T(8,128)}), f32[32,16,896]{2,1,0:T(8,128)S(1)}, u32[]{:S(2)}, u32[]{:S(2)}) async-start(f32[32,16,896]{2,1,0:T(8,128)} %pad_maximum_fusion), calls=%async_computation | async-start | bytes 3670016 | tf_op jit(solution)/shard_map/all_to_all | solution.py:199
  64.6 6.4 %collective-permute-done.3 = bf16[320,1024]{1,0:T(8,128)(2,1)S(1)} collective-permute-done((bf16[320,1024]{1,0:T(8,128)(2,1)}, bf16[320,1024]{1,0:T(8,128)(2,1)S(1)}, u32[]{:S(2)}, u32[]{:S(2)}) %collective-permute-start.3) | collective-permute-done | bytes 655392 | tf_op jit(solution)/shard_map/ppermute | solution.py:155
  71.0 4.2 %collective-permute-start.4 = (bf16[320,1024]{1,0:T(8,128)(2,1)S(1)}, bf16[320,1024]{1,0:T(8,128)(2,1)}, u32[]{:S(2)}, u32[]{:S(2)}) collective-permute-start(bf16[320,1024]{1,0:T(8,128)(2,1)S(1)} %collective-permute-done.3), channel_id=1, source_target_pairs={{0,1},{1,2},{2,3},{3,4},{4,5},{5,6},{6,7},{7,8},{8,9},{9,10},{10,1... | collective-permute-start | bytes 1966088 | tf_op jit(solution)/shard_map/ppermute | solution.py:155
  81.3 4.1 %collective-permute-start.14 = (bf16[320,1024]{1,0:T(8,128)(2,1)}, bf16[320,1024]{1,0:T(8,128)(2,1)}, u32[]{:S(2)}, u32[]{:S(2)}) collective-permute-start(bf16[320,1024]{1,0:T(8,128)(2,1)} %collective-permute-done.12), channel_id=1, source_target_pairs={{0,1},{1,2},{2,3},{3,4},{4,5},{5,6},{6,7},{7,8},{8,9},{9,10},{10,1... | collective-permute-start | bytes 1966088 | tf_op jit(solution)/shard_map/ppermute | solution.py:155
  85.4 3.6 %collective-permute-start.9 = (bf16[320,1024]{1,0:T(8,128)(2,1)}, bf16[320,1024]{1,0:T(8,128)(2,1)}, u32[]{:S(2)}, u32[]{:S(2)}) collective-permute-start(bf16[320,1024]{1,0:T(8,128)(2,1)} %collective-permute-done.4), channel_id=1, source_target_pairs={{0,1},{1,2},{2,3},{3,4},{4,5},{5,6},{6,7},{7,8},{8,9},{9,10},{10,1... | collective-permute-start | bytes 1966088 | tf_op jit(solution)/shard_map/ppermute | solution.py:155
  89.0 7.5 %all-to-all-start.1 = ((f32[32,16,640]{2,1,0:T(8,128)}), f32[32,16,640]{2,1,0:T(8,128)S(1)}, u32[]{:S(2)}, u32[]{:S(2)}) async-start(f32[32,16,640]{2,1,0:T(8,128)} %pad_maximum_fusion.1), calls=%async_computation.1 | async-start | bytes 2621440 | tf_op jit(solution)/shard_map/all_to_all | solution.py:199
  96.5 5.0 %collective-permute-start.15 = (bf16[320,1024]{1,0:T(8,128)(2,1)}, bf16[320,1024]{1,0:T(8,128)(2,1)}, u32[]{:S(2)}, u32[]{:S(2)}) collective-permute-start(bf16[320,1024]{1,0:T(8,128)(2,1)} %collective-permute-done.14), channel_id=1, source_target_pairs={{0,1},{1,2},{2,3},{3,4},{4,5},{5,6},{6,7},{7,8},{8,9},{9,10},{10,1... | collective-permute-start | bytes 1966088 | tf_op jit(solution)/shard_map/ppermute | solution.py:155
  101.5 3.9 %collective-permute-start.10 = (bf16[320,1024]{1,0:T(8,128)(2,1)}, bf16[320,1024]{1,0:T(8,128)(2,1)}, u32[]{:S(2)}, u32[]{:S(2)}) collective-permute-start(bf16[320,1024]{1,0:T(8,128)(2,1)} %collective-permute-done.9), channel_id=1, source_target_pairs={{0,1},{1,2},{2,3},{3,4},{4,5},{5,6},{6,7},{7,8},{8,9},{9,10},{10,1... | collective-permute-start | bytes 1966088 | tf_op jit(solution)/shard_map/ppermute | solution.py:155
  112.5 5.2 %collective-permute-start.16 = (bf16[320,1024]{1,0:T(8,128)(2,1)}, bf16[320,1024]{1,0:T(8,128)(2,1)}, u32[]{:S(2)}, u32[]{:S(2)}) collective-permute-start(bf16[320,1024]{1,0:T(8,128)(2,1)} %collective-permute-done.15), channel_id=1, source_target_pairs={{0,1},{1,2},{2,3},{3,4},{4,5},{5,6},{6,7},{7,8},{8,9},{9,10},{10,1... | collective-permute-start | bytes 1966088 | tf_op jit(solution)/shard_map/ppermute | solution.py:155
  117.7 7.2 %all-to-all-start.3 = ((f32[32,16,640]{2,1,0:T(8,128)}), f32[32,16,640]{2,1,0:T(8,128)}, u32[]{:S(2)}, u32[]{:S(2)}) async-start(f32[32,16,640]{2,1,0:T(8,128)} %pad_maximum_fusion.2), calls=%async_computation.3 | async-start | bytes 2621440 | tf_op jit(solution)/shard_map/all_to_all | solution.py:199
  126.0 4.0 %collective-permute-start.13 = (bf16[160,1024]{1,0:T(8,128)(2,1)S(1)}, bf16[160,1024]{1,0:T(8,128)(2,1)S(1)}, u32[]{:S(2)}, u32[]{:S(2)}) collective-permute-start(bf16[160,1024]{1,0:T(8,128)(2,1)S(1)} %constant_dynamic-slice_fusion.1), channel_id=1, source_target_pairs={{0,1},{1,2},{2,3},{3,4},{4,5},{5,6},{6,7},{7,8},{8,9},{9,10},{10,1... | collective-permute-start | bytes 983048 | tf_op jit(solution)/shard_map/ppermute | solution.py:155
  144.1 6.2 %all-to-all-start.2 = ((f32[32,16,512]{2,1,0:T(8,128)}), f32[32,16,512]{2,1,0:T(8,128)}, u32[]{:S(2)}, u32[]{:S(2)}) async-start(f32[32,16,512]{2,1,0:T(8,128)} %pad_maximum_fusion.3), calls=%async_computation.2 | async-start | bytes 2097152 | tf_op jit(solution)/shard_map/all_to_all | solution.py:199
  155.0 3.5 %shard_map.30.before_ref = f32[8,128]{1,0:T(8,128)S(1)} custom-call(f32[16,32,640]{2,1,0:T(8,128)} %bitcast.16.block_ref, f32[8,128]{1,0:T(8,128)S(1)} %shard_map.29.before_ref), custom_call_target="tpu_custom_call" | custom-call | flops 1006632960 | bytes 1310720 | tf_op jit(solution)/shard_map/pallas_call | solution.py:49
  158.4 9.2 %all-to-all-done.2.refs_3_ = f32[32,16,512]{2,1,0:T(8,128)} async-done(((f32[32,16,512]{2,1,0:T(8,128)}), f32[32,16,512]{2,1,0:T(8,128)}, u32[]{:S(2)}, u32[]{:S(2)}) %all-to-all-start.2) | async-done | bytes 1048608 | tf_op jit(solution)/shard_map/all_to_all | solution.py:199
  170.6 11.4 %all_to_all.35.parts_ref = f32[32,8,128]{2,1,0:T(8,128)} all-to-all(f32[32,8,128]{2,1,0:T(8,128)S(1)} %broadcast_in_dim.7), channel_id=1, replica_groups=mesh['dp'=32,'tensor'=16] {'dp'}, dimensions={0} | all-to-all | bytes 262144 | tf_op jit(solution)/shard_map/all_to_all | solution.py:203
  183.6 7.1 %all-to-all-start.5 = ((f32[16,8,128]{2,1,0:T(8,128)}), f32[16,8,128]{2,1,0:T(8,128)S(1)}, u32[]{:S(2)}, u32[]{:S(2)}) async-start(f32[16,8,128]{2,1,0:T(8,128)} %shard_map.32), calls=%async_computation.5 | async-start | bytes 131072 | tf_op jit(solution)/shard_map/all_to_all | solution.py:204
  190.7 11.6 %all-to-all-done.5.parts_ref = f32[16,8,128]{2,1,0:T(8,128)S(1)} async-done(((f32[16,8,128]{2,1,0:T(8,128)}), f32[16,8,128]{2,1,0:T(8,128)S(1)}, u32[]{:S(2)}, u32[]{:S(2)}) %all-to-all-start.5) | async-done | bytes 65568 | tf_op jit(solution)/shard_map/all_to_all | solution.py:204
  204.9 14.1 %all_to_all.36 = f32[32,8,160]{2,1,0:T(8,128)S(1)} all-to-all(f32[32,8,160]{2,1,0:T(8,128)S(1)} %shard_map.33), channel_id=1, replica_groups=mesh['dp'=32,'tensor'=16] {'dp'}, dimensions={0} | all-to-all | bytes 327680 | tf_op jit(solution)/shard_map/all_to_all | solution.py:206
  (63 shorter events, 63.6 us)
Async XLA Ops:
  0.0 14.5 %collective-permute-start.5 = (bf16[320,1024]{1,0:T(8,128)(2,1)}, bf16[320,1024]{1,0:T(8,128)(2,1)S(1)}, u32[]{:S(2)}, u32[]{:S(2)}) collective-permute-start(bf16[320,1024]{1,0:T(8,128)(2,1)} %bitcast.45), channel_id=1, source_target_pairs={{0,16},{16,0},{32,48},{48,32},{64,80},{80,64},{96,112},{112,96},{1... | collective-permute-start | bytes 1966088 | tf_op jit(solution)/shard_map/ppermute | solution.py:158
  8.8 13.6 %collective-permute-start = (bf16[320,1024]{1,0:T(8,128)(2,1)}, bf16[320,1024]{1,0:T(8,128)(2,1)}, u32[]{:S(2)}, u32[]{:S(2)}) collective-permute-start(bf16[320,1024]{1,0:T(8,128)(2,1)} %bitcast.46), channel_id=1, source_target_pairs={{0,1},{1,2},{2,3},{3,4},{4,5},{5,6},{6,7},{7,8},{8,9},{9,10},{10,1... | collective-permute-start | bytes 1966088 | tf_op jit(solution)/shard_map/ppermute | solution.py:155
  14.6 14.7 %collective-permute-start.6 = (bf16[320,1024]{1,0:T(8,128)(2,1)S(1)}, bf16[320,1024]{1,0:T(8,128)(2,1)}, u32[]{:S(2)}, u32[]{:S(2)}) collective-permute-start(bf16[320,1024]{1,0:T(8,128)(2,1)S(1)} %collective-permute-done.5), channel_id=1, source_target_pairs={{0,1},{1,2},{2,3},{3,4},{4,5},{5,6},{6,7},{7,8},{8,9},{9,10},{10,1... | collective-permute-start | bytes 1966088 | tf_op jit(solution)/shard_map/ppermute | solution.py:155
  17.2 10.2 %collective-permute-start.7 = (bf16[1024,256]{1,0:T(8,128)(2,1)}, bf16[1024,256]{1,0:T(8,128)(2,1)S(1)}, u32[]{:S(2)}, u32[]{:S(2)}) collective-permute-start(bf16[1024,256]{1,0:T(8,128)(2,1)} %param.3), channel_id=1, source_target_pairs={{0,16},{16,0},{32,48},{48,32},{64,80},{80,64},{96,112},{112,96},{1... | collective-permute-start | bytes 1572872 | tf_op jit(solution)/shard_map/ppermute | solution.py:161
  22.4 14.0 %collective-permute-start.1 = (bf16[320,1024]{1,0:T(8,128)(2,1)}, bf16[320,1024]{1,0:T(8,128)(2,1)S(1)}, u32[]{:S(2)}, u32[]{:S(2)}) collective-permute-start(bf16[320,1024]{1,0:T(8,128)(2,1)} %collective-permute-done), channel_id=1, source_target_pairs={{0,1},{1,2},{2,3},{3,4},{4,5},{5,6},{6,7},{7,8},{8,9},{9,10},{10,1... | collective-permute-start | bytes 1966088 | tf_op jit(solution)/shard_map/ppermute | solution.py:155
  29.3 14.2 %collective-permute-start.8 = (bf16[320,1024]{1,0:T(8,128)(2,1)}, bf16[320,1024]{1,0:T(8,128)(2,1)S(1)}, u32[]{:S(2)}, u32[]{:S(2)}) collective-permute-start(bf16[320,1024]{1,0:T(8,128)(2,1)} %collective-permute-done.6), channel_id=1, source_target_pairs={{0,1},{1,2},{2,3},{3,4},{4,5},{5,6},{6,7},{7,8},{8,9},{9,10},{10,1... | collective-permute-start | bytes 1966088 | tf_op jit(solution)/shard_map/ppermute | solution.py:155
  36.4 22.6 %collective-permute-start.2 = (bf16[320,1024]{1,0:T(8,128)(2,1)S(1)}, bf16[320,1024]{1,0:T(8,128)(2,1)}, u32[]{:S(2)}, u32[]{:S(2)}) collective-permute-start(bf16[320,1024]{1,0:T(8,128)(2,1)S(1)} %collective-permute-done.1), channel_id=1, source_target_pairs={{0,1},{1,2},{2,3},{3,4},{4,5},{5,6},{6,7},{7,8},{8,9},{9,10},{10,1... | collective-permute-start | bytes 1966088 | tf_op jit(solution)/shard_map/ppermute | solution.py:155
  46.9 15.2 %collective-permute-start.11 = (bf16[320,1024]{1,0:T(8,128)(2,1)S(1)}, bf16[320,1024]{1,0:T(8,128)(2,1)}, u32[]{:S(2)}, u32[]{:S(2)}) collective-permute-start(bf16[320,1024]{1,0:T(8,128)(2,1)S(1)} %collective-permute-done.8), channel_id=1, source_target_pairs={{0,1},{1,2},{2,3},{3,4},{4,5},{5,6},{6,7},{7,8},{8,9},{9,10},{10,1... | collective-permute-start | bytes 1966088 | tf_op jit(solution)/shard_map/ppermute | solution.py:155
  51.8 33.6 %all-to-all-start = ((f32[32,16,896]{2,1,0:T(8,128)}), f32[32,16,896]{2,1,0:T(8,128)S(1)}, u32[]{:S(2)}, u32[]{:S(2)}) async-start(f32[32,16,896]{2,1,0:T(8,128)} %pad_maximum_fusion), calls=%async_computation | async-start | bytes 3670016 | tf_op jit(solution)/shard_map/all_to_all | solution.py:199
  59.0 19.1 %copy-start.2 = (bf16[1024,256]{1,0:T(8,128)(2,1)S(1)}, bf16[1024,256]{1,0:T(8,128)(2,1)}, u32[]{:S(2)}) copy-start(bf16[1024,256]{1,0:T(8,128)(2,1)} %copy-done) | copy-start | bytes 1572868
  59.0 12.0 %collective-permute-start.3 = (bf16[320,1024]{1,0:T(8,128)(2,1)}, bf16[320,1024]{1,0:T(8,128)(2,1)S(1)}, u32[]{:S(2)}, u32[]{:S(2)}) collective-permute-start(bf16[320,1024]{1,0:T(8,128)(2,1)} %collective-permute-done.2), channel_id=1, source_target_pairs={{0,1},{1,2},{2,3},{3,4},{4,5},{5,6},{6,7},{7,8},{8,9},{9,10},{10,1... | collective-permute-start | bytes 1966088 | tf_op jit(solution)/shard_map/ppermute | solution.py:155
  62.1 16.0 %collective-permute-start.12 = (bf16[320,1024]{1,0:T(8,128)(2,1)}, bf16[320,1024]{1,0:T(8,128)(2,1)}, u32[]{:S(2)}, u32[]{:S(2)}) collective-permute-start(bf16[320,1024]{1,0:T(8,128)(2,1)} %collective-permute-done.11), channel_id=1, source_target_pairs={{0,1},{1,2},{2,3},{3,4},{4,5},{5,6},{6,7},{7,8},{8,9},{9,10},{10,1... | collective-permute-start | bytes 1966088 | tf_op jit(solution)/shard_map/ppermute | solution.py:155
  71.0 14.4 %collective-permute-start.4 = (bf16[320,1024]{1,0:T(8,128)(2,1)S(1)}, bf16[320,1024]{1,0:T(8,128)(2,1)}, u32[]{:S(2)}, u32[]{:S(2)}) collective-permute-start(bf16[320,1024]{1,0:T(8,128)(2,1)S(1)} %collective-permute-done.3), channel_id=1, source_target_pairs={{0,1},{1,2},{2,3},{3,4},{4,5},{5,6},{6,7},{7,8},{8,9},{9,10},{10,1... | collective-permute-start | bytes 1966088 | tf_op jit(solution)/shard_map/ppermute | solution.py:155
  81.3 15.2 %collective-permute-start.14 = (bf16[320,1024]{1,0:T(8,128)(2,1)}, bf16[320,1024]{1,0:T(8,128)(2,1)}, u32[]{:S(2)}, u32[]{:S(2)}) collective-permute-start(bf16[320,1024]{1,0:T(8,128)(2,1)} %collective-permute-done.12), channel_id=1, source_target_pairs={{0,1},{1,2},{2,3},{3,4},{4,5},{5,6},{6,7},{7,8},{8,9},{9,10},{10,1... | collective-permute-start | bytes 1966088 | tf_op jit(solution)/shard_map/ppermute | solution.py:155
  85.4 16.2 %collective-permute-start.9 = (bf16[320,1024]{1,0:T(8,128)(2,1)}, bf16[320,1024]{1,0:T(8,128)(2,1)}, u32[]{:S(2)}, u32[]{:S(2)}) collective-permute-start(bf16[320,1024]{1,0:T(8,128)(2,1)} %collective-permute-done.4), channel_id=1, source_target_pairs={{0,1},{1,2},{2,3},{3,4},{4,5},{5,6},{6,7},{7,8},{8,9},{9,10},{10,1... | collective-permute-start | bytes 1966088 | tf_op jit(solution)/shard_map/ppermute | solution.py:155
  89.0 28.7 %all-to-all-start.1 = ((f32[32,16,640]{2,1,0:T(8,128)}), f32[32,16,640]{2,1,0:T(8,128)S(1)}, u32[]{:S(2)}, u32[]{:S(2)}) async-start(f32[32,16,640]{2,1,0:T(8,128)} %pad_maximum_fusion.1), calls=%async_computation.1 | async-start | bytes 2621440 | tf_op jit(solution)/shard_map/all_to_all | solution.py:199
  96.5 12.8 %collective-permute-start.15 = (bf16[320,1024]{1,0:T(8,128)(2,1)}, bf16[320,1024]{1,0:T(8,128)(2,1)}, u32[]{:S(2)}, u32[]{:S(2)}) collective-permute-start(bf16[320,1024]{1,0:T(8,128)(2,1)} %collective-permute-done.14), channel_id=1, source_target_pairs={{0,1},{1,2},{2,3},{3,4},{4,5},{5,6},{6,7},{7,8},{8,9},{9,10},{10,1... | collective-permute-start | bytes 1966088 | tf_op jit(solution)/shard_map/ppermute | solution.py:155
  101.5 23.4 %collective-permute-start.10 = (bf16[320,1024]{1,0:T(8,128)(2,1)}, bf16[320,1024]{1,0:T(8,128)(2,1)}, u32[]{:S(2)}, u32[]{:S(2)}) collective-permute-start(bf16[320,1024]{1,0:T(8,128)(2,1)} %collective-permute-done.9), channel_id=1, source_target_pairs={{0,1},{1,2},{2,3},{3,4},{4,5},{5,6},{6,7},{7,8},{8,9},{9,10},{10,1... | collective-permute-start | bytes 1966088 | tf_op jit(solution)/shard_map/ppermute | solution.py:155
  112.5 17.4 %collective-permute-start.16 = (bf16[320,1024]{1,0:T(8,128)(2,1)}, bf16[320,1024]{1,0:T(8,128)(2,1)}, u32[]{:S(2)}, u32[]{:S(2)}) collective-permute-start(bf16[320,1024]{1,0:T(8,128)(2,1)} %collective-permute-done.15), channel_id=1, source_target_pairs={{0,1},{1,2},{2,3},{3,4},{4,5},{5,6},{6,7},{7,8},{8,9},{9,10},{10,1... | collective-permute-start | bytes 1966088 | tf_op jit(solution)/shard_map/ppermute | solution.py:155
  117.7 26.4 %all-to-all-start.3 = ((f32[32,16,640]{2,1,0:T(8,128)}), f32[32,16,640]{2,1,0:T(8,128)}, u32[]{:S(2)}, u32[]{:S(2)}) async-start(f32[32,16,640]{2,1,0:T(8,128)} %pad_maximum_fusion.2), calls=%async_computation.3 | async-start | bytes 2621440 | tf_op jit(solution)/shard_map/all_to_all | solution.py:199
  126.0 8.4 %collective-permute-start.13 = (bf16[160,1024]{1,0:T(8,128)(2,1)S(1)}, bf16[160,1024]{1,0:T(8,128)(2,1)S(1)}, u32[]{:S(2)}, u32[]{:S(2)}) collective-permute-start(bf16[160,1024]{1,0:T(8,128)(2,1)S(1)} %constant_dynamic-slice_fusion.1), channel_id=1, source_target_pairs={{0,1},{1,2},{2,3},{3,4},{4,5},{5,6},{6,7},{7,8},{8,9},{9,10},{10,1... | collective-permute-start | bytes 983048 | tf_op jit(solution)/shard_map/ppermute | solution.py:155
  130.9 8.2 %collective-permute-start.17 = (bf16[160,1024]{1,0:T(8,128)(2,1)S(1)}, bf16[160,1024]{1,0:T(8,128)(2,1)S(1)}, u32[]{:S(2)}, u32[]{:S(2)}) collective-permute-start(bf16[160,1024]{1,0:T(8,128)(2,1)S(1)} %constant_dynamic-slice_fusion), channel_id=1, source_target_pairs={{0,1},{1,2},{2,3},{3,4},{4,5},{5,6},{6,7},{7,8},{8,9},{9,10},{10,1... | collective-permute-start | bytes 983048 | tf_op jit(solution)/shard_map/ppermute | solution.py:155
  144.1 23.5 %all-to-all-start.2 = ((f32[32,16,512]{2,1,0:T(8,128)}), f32[32,16,512]{2,1,0:T(8,128)}, u32[]{:S(2)}, u32[]{:S(2)}) async-start(f32[32,16,512]{2,1,0:T(8,128)} %pad_maximum_fusion.3), calls=%async_computation.2 | async-start | bytes 2097152 | tf_op jit(solution)/shard_map/all_to_all | solution.py:199
  183.6 18.7 %all-to-all-start.5 = ((f32[16,8,128]{2,1,0:T(8,128)}), f32[16,8,128]{2,1,0:T(8,128)S(1)}, u32[]{:S(2)}, u32[]{:S(2)}) async-start(f32[16,8,128]{2,1,0:T(8,128)} %shard_map.32), calls=%async_computation.5 | async-start | bytes 131072 | tf_op jit(solution)/shard_map/all_to_all | solution.py:204
  (4 other events, 41.0 us)

commit v11 on v10

--- a/solution.py
+++ b/solution.py
@@ -15,16 +15,19 @@
 EXACT = lax.Precision.HIGHEST
 
 
-def gram_kernel(replicas, block_ref, before_ref, out_ref):
+def gram_kernel(replicas, core_ref, block_ref, before_ref, out_ref):
     part = block_ref.shape[1] // 4
     rows = replicas * part
     i = lax.broadcasted_iota(jnp.int32, (rows, rows), 0)
     j = lax.broadcasted_iota(jnp.int32, (rows, rows), 1)
     whole = jnp.zeros((rows, rows), jnp.float32)
-    for core in range(2):
-        first = block_ref[:, (3 * core) * part:(3 * core + 1) * part]
-        second = block_ref[:, (1 + core) * part:(2 + core) * part]
-        both = jnp.concatenate([first, second], axis=1).reshape(rows, -1)
+    core = core_ref[0]
+    for k in range(2):
+        even = pl.multiple_of(core * 2 * part + k * part, part)
+        odd = pl.multiple_of((1 - core) * 2 * part + k * part, part)
+        both = jnp.concatenate(
+            [block_ref[:, pl.ds(even, part)], block_ref[:, pl.ds(odd, part)]], axis=1
+        ).reshape(rows, -1)
         whole = whole + lax.dot_general(
             both, both, (((1,), (1,)), ((), ())),
             precision=EXACT, preferred_element_type=jnp.float32,
@@ -43,19 +46,18 @@
     out_ref[...] = total
 
 
-def gram_add(replicas, block, before):
-    block = block.reshape(replicas // 2, 2 * block.shape[1], -1)
+def gram_add(replicas, core, block, before):
     size = block.size
     return pl.pallas_call(
         functools.partial(gram_kernel, replicas),
         out_shape=jax.ShapeDtypeStruct((8, 128), jnp.float32),
-        in_specs=[pl.BlockSpec(memory_space=VMEM)] * 2,
+        in_specs=[pl.BlockSpec(memory_space=pltpu.SMEM)] + [pl.BlockSpec(memory_space=VMEM)] * 2,
         out_specs=pl.BlockSpec(memory_space=VMEM),
         cost_estimate=pl.CostEstimate(
             flops=12 * size * replicas * 8, bytes_accessed=4 * size, transcendentals=0
         ),
         compiler_params=pltpu.CompilerParams(vmem_limit_bytes=LIMIT),
-    )(block, before)
+    )(core.reshape(1), block, before)
 
 
 def spread_kernel(parts_ref, out_ref):
@@ -72,7 +74,7 @@
     )(parts)
 
 
-def combine_kernel(replicas, slabs, order, counts, here_ref, parts_ref, *refs):
+def combine_kernel(replicas, slabs, order, counts, here_ref, core_ref, parts_ref, *refs):
     blocks, out_ref = refs[:-1], refs[-1]
     packed = jnp.sum(parts_ref[...], axis=0)
     gram = jnp.concatenate(
@@ -104,42 +106,46 @@
         down = new_down
         width *= 2
     part, width = out_ref.shape[1:]
-    for core in range(2):
-        place = 0
-        for block_ref, count in zip(blocks, counts):
-            total = 0.0
-            for r in range(replicas):
-                row = (r + core) % 2 * part
-                total = total + block_ref[r // 2 * 2 + core, row:row + part] * down[r:r + 1]
-            for i in range(count):
-                away, piece = order[core][place]
-                slab = lax.rem(here_ref[0] + away, slabs)
-                out_ref[slab * 2 + piece] = total[:, i * width:(i + 1) * width]
-                place += 1
-
-
-def weighted_sums(replicas, slabs, order, counts, width, here, parts, blocks):
+    here, core = here_ref[0], core_ref[0]
+    starts = [pl.multiple_of(core * part, part), pl.multiple_of((1 - core) * part, part)]
+    out_ref[...] = jnp.zeros(out_ref.shape, jnp.float32)
+    place = 0
+    for block_ref, count in zip(blocks, counts):
+        total = 0.0
+        for r in range(replicas):
+            total = total + block_ref[r // 2, pl.ds(starts[r % 2], part)] * down[r:r + 1]
+        for i in range(count):
+            step, piece = order[place]
+            away = jnp.where(core == 0, slabs - step, step)
+            slab = lax.rem(here + away, slabs)
+            piece = core if piece is None else piece
+            out_ref[slab * 2 + piece] = total[:, i * width:(i + 1) * width]
+            place += 1
+
+
+def weighted_sums(replicas, slabs, order, counts, width, here, core, parts, blocks):
     part = blocks[0].shape[1] // 2
     size = sum(b.size for b in blocks)
     return pl.pallas_call(
         functools.partial(combine_kernel, replicas, slabs, order, counts),
         out_shape=jax.ShapeDtypeStruct((replicas, part, width), jnp.float32),
-        in_specs=[pl.BlockSpec(memory_space=pltpu.SMEM)]
+        in_specs=[pl.BlockSpec(memory_space=pltpu.SMEM)] * 2
         + [pl.BlockSpec(memory_space=VMEM)] * (1 + len(blocks)),
         out_specs=pl.BlockSpec(memory_space=VMEM),
         cost_estimate=pl.CostEstimate(flops=2 * size, bytes_accessed=4 * size, transcendentals=0),
         compiler_params=pltpu.CompilerParams(vmem_limit_bytes=LIMIT),
-    )(here.reshape(1), parts, *blocks)
+    )(here.reshape(1), core.reshape(1), parts, *blocks)
 
 
 def on_device(activations, out_grads):
     replicas = lax.axis_size("dp")
     slabs = lax.axis_size("tensor")
     here = lax.axis_index("tensor").astype(jnp.int32)
-    core = lax.axis_index("dp") % 2
+    core = lax.axis_index("dp").astype(jnp.int32) % 2
     tokens, slab_rows = activations.shape
     columns = out_grads.shape[1]
-    part = columns // replicas
+    chips = replicas // 2
+    same_core = [list(range(k, replicas, 2)) for k in range(2)]
     half = slabs // 2
     rows = slab_rows // 2
     sibling = [(r, r ^ 1) for r in range(replicas)]
@@ -160,7 +166,7 @@
     chains[1], grads[1] = lax.optimization_barrier((chains[1], grads[1]))
     grads[1] = lax.ppermute(grads[1], "dp", sibling)
     held = [[own_half(slab)] for slab in chains]
-    order = [[(0, 0)], [(0, 1)]]
+    order = [(0, None)]
     blocks = []
     gram = jnp.zeros((8, 128), jnp.float32)
     counts = []
@@ -174,12 +180,11 @@
                     place = TIES[step, k]
                     chains[k], blocks[place] = lax.optimization_barrier((chains[k], blocks[place]))
                 held[k].append(chains[k])
-            order[0] += [(slabs - step, 0), (slabs - step, 1)]
-            order[1] += [(step, 0), (step, 1)]
+            order += [(step, 0), (step, 1)]
         else:
             for k in range(2):
                 held[k].append(move(own_half(chains[k])))
-                order[k].append((half, k))
+            order.append((half, None))
         if step in GROUP_ENDS:
             size = sum(piece.shape[0] for piece in held[0])
             counts.append(size // rows)
@@ -191,19 +196,20 @@
                     grads[k], jnp.concatenate(held[k], axis=0), (((0,), (1,)), ((), ())),
                     preferred_element_type=jnp.float32,
                 )
-                parts.append(grad.reshape(replicas, part, -1))
+                parts.append(grad.reshape(chips, columns // chips, -1))
                 held[k] = []
             ready = jnp.concatenate(parts, axis=1)
             if step < half:
                 chains[1], ready = lax.optimization_barrier((chains[1], ready))
-            blocks.append(lax.all_to_all(ready, "dp", 0, 0))
+            blocks.append(lax.all_to_all(ready, "dp", 0, 0, axis_index_groups=same_core))
     for block in blocks:
-        gram = gram_add(replicas, block, gram)
+        gram = gram_add(replicas, core, block, gram)
     peers = jnp.broadcast_to(gram, (replicas, *gram.shape))
     parts = sum_and_spread(lax.all_to_all(peers, "dp", 0, 0), slabs)
     parts = lax.all_to_all(parts, "tensor", 0, 0)
-    home = weighted_sums(replicas, slabs, order, counts, rows, here, parts, blocks)
+    home = weighted_sums(replicas, slabs, order, counts, rows, here, core, parts, blocks)
     home = lax.all_to_all(home, "dp", 0, 0)
+    home = jnp.sum(home.reshape(chips, 2, columns // chips, -1), axis=1)
     return home.reshape(columns, -1).T
 
 

time: 221 us -> 222 us (level)
  starting transfers between devices: 112 us -> 94.4 us
  waiting for transfers between devices: 42.7 us -> 53.1 us
  blocking collectives: 25.5 us -> 32.9 us
    ppermute x16, starting transfers between devices: 65.6 us -> 55.6 us  [move(): return lax.ppermute(slab, ('dp', 'tensor'), onward)]
    all_to_all x4, waiting for transfers between devices: 11.4 us -> 17.6 us  [on_device(): lax.all_to_all(ready, 'dp', 0, 0, axis_index_groups=same_core)]
    all_to_all x1, blocking collectives: 11.4 us -> 16.1 us  [on_device(): parts = sum_and_spread(lax.all_to_all(peers, 'dp', 0, 0), slabs)]
    all_to_all x4, starting transfers between devices: 28.1 us -> 23.8 us  [on_device(): lax.all_to_all(ready, 'dp', 0, 0, axis_index_groups=same_core)]
    ppermute x16, waiting for transfers between devices: 19.7 us -> 23.9 us  [move(): return lax.ppermute(slab, ('dp', 'tensor'), onward)]
    all_to_all x1, starting transfers between devices: 7.11 us -> 4.34 us  [on_device(): parts = lax.all_to_all(parts, 'tensor', 0, 0)]
    all_to_all x1, blocking collectives: 14.1 us -> 16.7 us  [on_device(): home = lax.all_to_all(home, 'dp', 0, 0)]
  transfers between devices with their start and end apart: 23 -> 23, of which waited for: 11 -> 14; matrix products, arithmetic and copies ran while one was open for 11% -> 11% of each run, Pallas kernels for 4% -> 4%
where the time goes in v11:
time: 222 us; the launch traced here: 220 us
  starting transfers between devices  94.4 us (43%)
  waiting for transfers between devices  53.1 us (24%)
  blocking collectives  32.9 us (15%)
  Pallas kernels  15.4 us (7%)
  matrix products  15.2 us (7%)
  other arithmetic  4.98 us (2%)
  local copies, waits for them, and re-layouts  4.01 us (2%)
    ppermute x16, starting transfers between devices, move(): return lax.ppermute(slab, ('dp', 'tensor'), onward)  55.6 us
    ppermute x16, waiting for transfers between devices, move(): return lax.ppermute(slab, ('dp', 'tensor'), onward)  23.9 us
    all_to_all x4, starting transfers between devices, on_device(): lax.all_to_all(ready, 'dp', 0, 0, axis_index_groups=same_core)  23.8 us
    all_to_all x4, waiting for transfers between devices, on_device(): lax.all_to_all(ready, 'dp', 0, 0, axis_index_groups=same_core)  17.6 us
    all_to_all x1, blocking collectives, on_device(): home = lax.all_to_all(home, 'dp', 0, 0)  16.7 us
    all_to_all x1, blocking collectives, on_device(): parts = sum_and_spread(lax.all_to_all(peers, 'dp', 0, 0), slabs)  16.1 us
    dot_general x8, matrix products, on_device(): lax.dot_general(grads[k], jnp.concatenate(held[k], axis=0), (((0,), (1,))...  15.2 us
    all_to_all x1, waiting for transfers between devices, on_device(): parts = lax.all_to_all(parts, 'tensor', 0, 0)  11.6 us
  transfers between devices with their start and end apart: 23, of which 14 were waited for; matrix products, arithmetic and copies ran while one was open for 11% of the time, Pallas kernels for 4%

profile of v11, /device:TPU:1, one launch (start us, length us, event | category | flops | bytes accessed | tf_op | source)
XLA Modules:
  0.0 220.4 jit_solution(11464010308661850605)
XLA Ops:
  0.0 8.8 %collective-permute-start.5 = (bf16[320,1024]{1,0:T(8,128)(2,1)}, bf16[320,1024]{1,0:T(8,128)(2,1)S(1)}, u32[]{:S(2)}, u32[]{:S(2)}) collective-permute-start(bf16[320,1024]{1,0:T(8,128)(2,1)} %bitcast.43), channel_id=1, source_target_pairs={{0,16},{16,0},{32,48},{48,32},{64,80},{80,64},{96,112},{112,96},{1... | collective-permute-start | bytes 1966088 | tf_op jit(solution)/shard_map/ppermute | solution.py:164
  8.8 5.8 %collective-permute-start = (bf16[320,1024]{1,0:T(8,128)(2,1)}, bf16[320,1024]{1,0:T(8,128)(2,1)}, u32[]{:S(2)}, u32[]{:S(2)}) collective-permute-start(bf16[320,1024]{1,0:T(8,128)(2,1)} %bitcast.44), channel_id=1, source_target_pairs={{0,1},{1,2},{2,3},{3,4},{4,5},{5,6},{6,7},{7,8},{8,9},{9,10},{10,1... | collective-permute-start | bytes 1966088 | tf_op jit(solution)/shard_map/ppermute | solution.py:161
  19.1 3.2 %collective-permute-done = bf16[320,1024]{1,0:T(8,128)(2,1)} collective-permute-done((bf16[320,1024]{1,0:T(8,128)(2,1)}, bf16[320,1024]{1,0:T(8,128)(2,1)}, u32[]{:S(2)}, u32[]{:S(2)}) %collective-permute-start) | collective-permute-done | bytes 655392 | tf_op jit(solution)/shard_map/ppermute | solution.py:161
  22.4 5.0 %collective-permute-start.1 = (bf16[320,1024]{1,0:T(8,128)(2,1)}, bf16[320,1024]{1,0:T(8,128)(2,1)S(1)}, u32[]{:S(2)}, u32[]{:S(2)}) collective-permute-start(bf16[320,1024]{1,0:T(8,128)(2,1)} %collective-permute-done), channel_id=1, source_target_pairs={{0,1},{1,2},{2,3},{3,4},{4,5},{5,6},{6,7},{7,8},{8,9},{9,10},{10,1... | collective-permute-start | bytes 1966088 | tf_op jit(solution)/shard_map/ppermute | solution.py:161
  29.3 5.1 %collective-permute-start.8 = (bf16[320,1024]{1,0:T(8,128)(2,1)}, bf16[320,1024]{1,0:T(8,128)(2,1)S(1)}, u32[]{:S(2)}, u32[]{:S(2)}) collective-permute-start(bf16[320,1024]{1,0:T(8,128)(2,1)} %collective-permute-done.6), channel_id=1, source_target_pairs={{0,1},{1,2},{2,3},{3,4},{4,5},{5,6},{6,7},{7,8},{8,9},{9,10},{10,1... | collective-permute-start | bytes 1966088 | tf_op jit(solution)/shard_map/ppermute | solution.py:161
  36.4 4.9 %collective-permute-start.2 = (bf16[320,1024]{1,0:T(8,128)(2,1)S(1)}, bf16[320,1024]{1,0:T(8,128)(2,1)}, u32[]{:S(2)}, u32[]{:S(2)}) collective-permute-start(bf16[320,1024]{1,0:T(8,128)(2,1)S(1)} %collective-permute-done.1), channel_id=1, source_target_pairs={{0,1},{1,2},{2,3},{3,4},{4,5},{5,6},{6,7},{7,8},{8,9},{9,10},{10,1... | collective-permute-start | bytes 1966088 | tf_op jit(solution)/shard_map/ppermute | solution.py:161
  47.0 4.9 %collective-permute-start.11 = (bf16[320,1024]{1,0:T(8,128)(2,1)S(1)}, bf16[320,1024]{1,0:T(8,128)(2,1)}, u32[]{:S(2)}, u32[]{:S(2)}) collective-permute-start(bf16[320,1024]{1,0:T(8,128)(2,1)S(1)} %collective-permute-done.8), channel_id=1, source_target_pairs={{0,1},{1,2},{2,3},{3,4},{4,5},{5,6},{6,7},{7,8},{8,9},{9,10},{10,1... | collective-permute-start | bytes 1966088 | tf_op jit(solution)/shard_map/ppermute | solution.py:161
  51.8 6.8 %all-to-all-start = ((f32[16,32,896]{2,1,0:T(8,128)}), f32[16,32,896]{2,1,0:T(8,128)S(1)}, u32[]{:S(2)}, u32[]{:S(2)}) async-start(f32[16,32,896]{2,1,0:T(8,128)} %pad_maximum_fusion), calls=%async_computation | async-start | bytes 3670016 | tf_op jit(solution)/shard_map/all_to_all | solution.py:204
  60.7 3.8 %collective-permute-start.12 = (bf16[320,1024]{1,0:T(8,128)(2,1)}, bf16[320,1024]{1,0:T(8,128)(2,1)S(1)}, u32[]{:S(2)}, u32[]{:S(2)}) collective-permute-start(bf16[320,1024]{1,0:T(8,128)(2,1)} %collective-permute-done.11), channel_id=1, source_target_pairs={{0,1},{1,2},{2,3},{3,4},{4,5},{5,6},{6,7},{7,8},{8,9},{9,10},{10,1... | collective-permute-start | bytes 1966088 | tf_op jit(solution)/shard_map/ppermute | solution.py:161
  64.5 6.1 %collective-permute-done.3 = bf16[320,1024]{1,0:T(8,128)(2,1)S(1)} collective-permute-done((bf16[320,1024]{1,0:T(8,128)(2,1)}, bf16[320,1024]{1,0:T(8,128)(2,1)S(1)}, u32[]{:S(2)}, u32[]{:S(2)}) %collective-permute-start.3) | collective-permute-done | bytes 655392 | tf_op jit(solution)/shard_map/ppermute | solution.py:161
  88.5 3.8 %collective-permute-done.14 = bf16[320,1024]{1,0:T(8,128)(2,1)} collective-permute-done((bf16[320,1024]{1,0:T(8,128)(2,1)S(1)}, bf16[320,1024]{1,0:T(8,128)(2,1)}, u32[]{:S(2)}, u32[]{:S(2)}) %collective-permute-start.14) | collective-permute-done | bytes 655392 | tf_op jit(solution)/shard_map/ppermute | solution.py:161
  92.3 4.0 %collective-permute-start.15 = (bf16[320,1024]{1,0:T(8,128)(2,1)}, bf16[320,1024]{1,0:T(8,128)(2,1)}, u32[]{:S(2)}, u32[]{:S(2)}) collective-permute-start(bf16[320,1024]{1,0:T(8,128)(2,1)} %collective-permute-done.14), channel_id=1, source_target_pairs={{0,1},{1,2},{2,3},{3,4},{4,5},{5,6},{6,7},{7,8},{8,9},{9,10},{10,1... | collective-permute-start | bytes 1966088 | tf_op jit(solution)/shard_map/ppermute | solution.py:161
  96.3 6.6 %all-to-all-start.1 = ((f32[16,32,640]{2,1,0:T(8,128)}), f32[16,32,640]{2,1,0:T(8,128)S(1)}, u32[]{:S(2)}, u32[]{:S(2)}) async-start(f32[16,32,640]{2,1,0:T(8,128)} %pad_maximum_fusion.1), calls=%async_computation.1 | async-start | bytes 2621440 | tf_op jit(solution)/shard_map/all_to_all | solution.py:204
  110.2 3.2 %collective-permute-start.16 = (bf16[320,1024]{1,0:T(8,128)(2,1)}, bf16[320,1024]{1,0:T(8,128)(2,1)}, u32[]{:S(2)}, u32[]{:S(2)}) collective-permute-start(bf16[320,1024]{1,0:T(8,128)(2,1)} %collective-permute-done.15), channel_id=1, source_target_pairs={{0,1},{1,2},{2,3},{3,4},{4,5},{5,6},{6,7},{7,8},{8,9},{9,10},{10,1... | collective-permute-start | bytes 1966088 | tf_op jit(solution)/shard_map/ppermute | solution.py:161
  113.5 8.1 %all-to-all-done.1.block_ref.refs_1_ = f32[16,32,640]{2,1,0:T(8,128)S(1)} async-done(((f32[16,32,640]{2,1,0:T(8,128)}), f32[16,32,640]{2,1,0:T(8,128)S(1)}, u32[]{:S(2)}, u32[]{:S(2)}) %all-to-all-start.1) | async-done | bytes 1310752 | tf_op jit(solution)/shard_map/all_to_all | solution.py:204
  121.6 5.6 %all-to-all-start.3 = ((f32[16,32,640]{2,1,0:T(8,128)}), f32[16,32,640]{2,1,0:T(8,128)}, u32[]{:S(2)}, u32[]{:S(2)}) async-start(f32[16,32,640]{2,1,0:T(8,128)} %pad_maximum_fusion.2), calls=%async_computation.3 | async-start | bytes 2621440 | tf_op jit(solution)/shard_map/all_to_all | solution.py:204
  133.3 3.3 %collective-permute-done.13 = bf16[160,1024]{1,0:T(8,128)(2,1)S(1)} collective-permute-done((bf16[160,1024]{1,0:T(8,128)(2,1)S(1)}, bf16[160,1024]{1,0:T(8,128)(2,1)S(1)}, u32[]{:S(2)}, u32[]{:S(2)}) %collective-permute-start.13) | collective-permute-done | bytes 327712 | tf_op jit(solution)/shard_map/ppermute | solution.py:161
  145.2 4.8 %all-to-all-start.2 = ((f32[16,32,512]{2,1,0:T(8,128)}), f32[16,32,512]{2,1,0:T(8,128)}, u32[]{:S(2)}, u32[]{:S(2)}) async-start(f32[16,32,512]{2,1,0:T(8,128)} %pad_maximum_fusion.3), calls=%async_computation.2 | async-start | bytes 2097152 | tf_op jit(solution)/shard_map/all_to_all | solution.py:204
  154.7 3.5 %shard_map.30.before_ref = f32[8,128]{1,0:T(8,128)S(1)} custom-call(s32[1]{0:T(128)} %bitcast.1.core_ref, f32[16,32,640]{2,1,0:T(8,128)} %all-to-all-done.3.block_ref.refs_2_, f32[8,128]{1,0:T(8,128)S(1)} %shard_map.29.before_ref), custom_call_target="tpu_custom_call" | custom-call | flops 1006632960 | bytes 1310720 | tf_op jit(solution)/shard_map/pallas_call | solution.py:51
  158.2 5.3 %all-to-all-done.2.block_ref.refs_3_ = f32[16,32,512]{2,1,0:T(8,128)} async-done(((f32[16,32,512]{2,1,0:T(8,128)}), f32[16,32,512]{2,1,0:T(8,128)}, u32[]{:S(2)}, u32[]{:S(2)}) %all-to-all-start.2) | async-done | bytes 1048608 | tf_op jit(solution)/shard_map/all_to_all | solution.py:204
  166.5 16.1 %all_to_all.35.parts_ref = f32[32,8,128]{2,1,0:T(8,128)} all-to-all(f32[32,8,128]{2,1,0:T(8,128)S(1)} %broadcast_in_dim.7), channel_id=1, replica_groups=mesh['dp'=32,'tensor'=16] {'dp'}, dimensions={0} | all-to-all | bytes 262144 | tf_op jit(solution)/shard_map/all_to_all | solution.py:208
  184.2 4.3 %all-to-all-start.5 = ((f32[16,8,128]{2,1,0:T(8,128)}), f32[16,8,128]{2,1,0:T(8,128)S(1)}, u32[]{:S(2)}, u32[]{:S(2)}) async-start(f32[16,8,128]{2,1,0:T(8,128)} %shard_map.32), calls=%async_computation.5 | async-start | bytes 131072 | tf_op jit(solution)/shard_map/all_to_all | solution.py:209
  188.5 11.6 %all-to-all-done.5.parts_ref = f32[16,8,128]{2,1,0:T(8,128)S(1)} async-done(((f32[16,8,128]{2,1,0:T(8,128)}), f32[16,8,128]{2,1,0:T(8,128)S(1)}, u32[]{:S(2)}, u32[]{:S(2)}) %all-to-all-start.5) | async-done | bytes 65568 | tf_op jit(solution)/shard_map/all_to_all | solution.py:209
  202.8 16.7 %all_to_all.36 = f32[32,16,160]{2,1,0:T(8,128)S(1)} all-to-all(f32[32,16,160]{2,1,0:T(8,128)S(1)} %shard_map.33), channel_id=1, replica_groups=mesh['dp'=32,'tensor'=16] {'dp'}, dimensions={0} | all-to-all | bytes 655360 | tf_op jit(solution)/shard_map/all_to_all | solution.py:211
  (64 shorter events, 68.5 us)
Async XLA Ops:
  0.0 14.5 %collective-permute-start.5 = (bf16[320,1024]{1,0:T(8,128)(2,1)}, bf16[320,1024]{1,0:T(8,128)(2,1)S(1)}, u32[]{:S(2)}, u32[]{:S(2)}) collective-permute-start(bf16[320,1024]{1,0:T(8,128)(2,1)} %bitcast.43), channel_id=1, source_target_pairs={{0,16},{16,0},{32,48},{48,32},{64,80},{80,64},{96,112},{112,96},{1... | collective-permute-start | bytes 1966088 | tf_op jit(solution)/shard_map/ppermute | solution.py:164
  8.8 13.6 %collective-permute-start = (bf16[320,1024]{1,0:T(8,128)(2,1)}, bf16[320,1024]{1,0:T(8,128)(2,1)}, u32[]{:S(2)}, u32[]{:S(2)}) collective-permute-start(bf16[320,1024]{1,0:T(8,128)(2,1)} %bitcast.44), channel_id=1, source_target_pairs={{0,1},{1,2},{2,3},{3,4},{4,5},{5,6},{6,7},{7,8},{8,9},{9,10},{10,1... | collective-permute-start | bytes 1966088 | tf_op jit(solution)/shard_map/ppermute | solution.py:161
  14.6 14.7 %collective-permute-start.6 = (bf16[320,1024]{1,0:T(8,128)(2,1)S(1)}, bf16[320,1024]{1,0:T(8,128)(2,1)}, u32[]{:S(2)}, u32[]{:S(2)}) collective-permute-start(bf16[320,1024]{1,0:T(8,128)(2,1)S(1)} %collective-permute-done.5), channel_id=1, source_target_pairs={{0,1},{1,2},{2,3},{3,4},{4,5},{5,6},{6,7},{7,8},{8,9},{9,10},{10,1... | collective-permute-start | bytes 1966088 | tf_op jit(solution)/shard_map/ppermute | solution.py:161
  17.2 10.2 %collective-permute-start.7 = (bf16[1024,256]{1,0:T(8,128)(2,1)}, bf16[1024,256]{1,0:T(8,128)(2,1)S(1)}, u32[]{:S(2)}, u32[]{:S(2)}) collective-permute-start(bf16[1024,256]{1,0:T(8,128)(2,1)} %param.3), channel_id=1, source_target_pairs={{0,16},{16,0},{32,48},{48,32},{64,80},{80,64},{96,112},{112,96},{1... | collective-permute-start | bytes 1572872 | tf_op jit(solution)/shard_map/ppermute | solution.py:167
  22.4 14.0 %collective-permute-start.1 = (bf16[320,1024]{1,0:T(8,128)(2,1)}, bf16[320,1024]{1,0:T(8,128)(2,1)S(1)}, u32[]{:S(2)}, u32[]{:S(2)}) collective-permute-start(bf16[320,1024]{1,0:T(8,128)(2,1)} %collective-permute-done), channel_id=1, source_target_pairs={{0,1},{1,2},{2,3},{3,4},{4,5},{5,6},{6,7},{7,8},{8,9},{9,10},{10,1... | collective-permute-start | bytes 1966088 | tf_op jit(solution)/shard_map/ppermute | solution.py:161
  29.3 14.2 %collective-permute-start.8 = (bf16[320,1024]{1,0:T(8,128)(2,1)}, bf16[320,1024]{1,0:T(8,128)(2,1)S(1)}, u32[]{:S(2)}, u32[]{:S(2)}) collective-permute-start(bf16[320,1024]{1,0:T(8,128)(2,1)} %collective-permute-done.6), channel_id=1, source_target_pairs={{0,1},{1,2},{2,3},{3,4},{4,5},{5,6},{6,7},{7,8},{8,9},{9,10},{10,1... | collective-permute-start | bytes 1966088 | tf_op jit(solution)/shard_map/ppermute | solution.py:161
  36.4 22.2 %collective-permute-start.2 = (bf16[320,1024]{1,0:T(8,128)(2,1)S(1)}, bf16[320,1024]{1,0:T(8,128)(2,1)}, u32[]{:S(2)}, u32[]{:S(2)}) collective-permute-start(bf16[320,1024]{1,0:T(8,128)(2,1)S(1)} %collective-permute-done.1), channel_id=1, source_target_pairs={{0,1},{1,2},{2,3},{3,4},{4,5},{5,6},{6,7},{7,8},{8,9},{9,10},{10,1... | collective-permute-start | bytes 1966088 | tf_op jit(solution)/shard_map/ppermute | solution.py:161
  47.0 13.7 %collective-permute-start.11 = (bf16[320,1024]{1,0:T(8,128)(2,1)S(1)}, bf16[320,1024]{1,0:T(8,128)(2,1)}, u32[]{:S(2)}, u32[]{:S(2)}) collective-permute-start(bf16[320,1024]{1,0:T(8,128)(2,1)S(1)} %collective-permute-done.8), channel_id=1, source_target_pairs={{0,1},{1,2},{2,3},{3,4},{4,5},{5,6},{6,7},{7,8},{8,9},{9,10},{10,1... | collective-permute-start | bytes 1966088 | tf_op jit(solution)/shard_map/ppermute | solution.py:161
  51.8 34.7 %all-to-all-start = ((f32[16,32,896]{2,1,0:T(8,128)}), f32[16,32,896]{2,1,0:T(8,128)S(1)}, u32[]{:S(2)}, u32[]{:S(2)}) async-start(f32[16,32,896]{2,1,0:T(8,128)} %pad_maximum_fusion), calls=%async_computation | async-start | bytes 3670016 | tf_op jit(solution)/shard_map/all_to_all | solution.py:204
  58.6 19.0 %copy-start.2 = (bf16[1024,256]{1,0:T(8,128)(2,1)S(1)}, bf16[1024,256]{1,0:T(8,128)(2,1)}, u32[]{:S(2)}) copy-start(bf16[1024,256]{1,0:T(8,128)(2,1)} %copy-done) | copy-start | bytes 1572868
  58.6 12.0 %collective-permute-start.3 = (bf16[320,1024]{1,0:T(8,128)(2,1)}, bf16[320,1024]{1,0:T(8,128)(2,1)S(1)}, u32[]{:S(2)}, u32[]{:S(2)}) collective-permute-start(bf16[320,1024]{1,0:T(8,128)(2,1)} %collective-permute-done.2), channel_id=1, source_target_pairs={{0,1},{1,2},{2,3},{3,4},{4,5},{5,6},{6,7},{7,8},{8,9},{9,10},{10,1... | collective-permute-start | bytes 1966088 | tf_op jit(solution)/shard_map/ppermute | solution.py:161
  60.7 16.9 %collective-permute-start.12 = (bf16[320,1024]{1,0:T(8,128)(2,1)}, bf16[320,1024]{1,0:T(8,128)(2,1)S(1)}, u32[]{:S(2)}, u32[]{:S(2)}) collective-permute-start(bf16[320,1024]{1,0:T(8,128)(2,1)} %collective-permute-done.11), channel_id=1, source_target_pairs={{0,1},{1,2},{2,3},{3,4},{4,5},{5,6},{6,7},{7,8},{8,9},{9,10},{10,1... | collective-permute-start | bytes 1966088 | tf_op jit(solution)/shard_map/ppermute | solution.py:161
  70.6 14.1 %collective-permute-start.4 = (bf16[320,1024]{1,0:T(8,128)(2,1)S(1)}, bf16[320,1024]{1,0:T(8,128)(2,1)}, u32[]{:S(2)}, u32[]{:S(2)}) collective-permute-start(bf16[320,1024]{1,0:T(8,128)(2,1)S(1)} %collective-permute-done.3), channel_id=1, source_target_pairs={{0,1},{1,2},{2,3},{3,4},{4,5},{5,6},{6,7},{7,8},{8,9},{9,10},{10,1... | collective-permute-start | bytes 1966088 | tf_op jit(solution)/shard_map/ppermute | solution.py:161
  80.6 11.7 %collective-permute-start.14 = (bf16[320,1024]{1,0:T(8,128)(2,1)S(1)}, bf16[320,1024]{1,0:T(8,128)(2,1)}, u32[]{:S(2)}, u32[]{:S(2)}) collective-permute-start(bf16[320,1024]{1,0:T(8,128)(2,1)S(1)} %collective-permute-done.12), channel_id=1, source_target_pairs={{0,1},{1,2},{2,3},{3,4},{4,5},{5,6},{6,7},{7,8},{8,9},{9,10},{10,1... | collective-permute-start | bytes 1966088 | tf_op jit(solution)/shard_map/ppermute | solution.py:161
  86.6 16.4 %collective-permute-start.9 = (bf16[320,1024]{1,0:T(8,128)(2,1)}, bf16[320,1024]{1,0:T(8,128)(2,1)}, u32[]{:S(2)}, u32[]{:S(2)}) collective-permute-start(bf16[320,1024]{1,0:T(8,128)(2,1)} %collective-permute-done.4), channel_id=1, source_target_pairs={{0,1},{1,2},{2,3},{3,4},{4,5},{5,6},{6,7},{7,8},{8,9},{9,10},{10,1... | collective-permute-start | bytes 1966088 | tf_op jit(solution)/shard_map/ppermute | solution.py:161
  92.3 14.8 %collective-permute-start.15 = (bf16[320,1024]{1,0:T(8,128)(2,1)}, bf16[320,1024]{1,0:T(8,128)(2,1)}, u32[]{:S(2)}, u32[]{:S(2)}) collective-permute-start(bf16[320,1024]{1,0:T(8,128)(2,1)} %collective-permute-done.14), channel_id=1, source_target_pairs={{0,1},{1,2},{2,3},{3,4},{4,5},{5,6},{6,7},{7,8},{8,9},{9,10},{10,1... | collective-permute-start | bytes 1966088 | tf_op jit(solution)/shard_map/ppermute | solution.py:161
  96.3 25.2 %all-to-all-start.1 = ((f32[16,32,640]{2,1,0:T(8,128)}), f32[16,32,640]{2,1,0:T(8,128)S(1)}, u32[]{:S(2)}, u32[]{:S(2)}) async-start(f32[16,32,640]{2,1,0:T(8,128)} %pad_maximum_fusion.1), calls=%async_computation.1 | async-start | bytes 2621440 | tf_op jit(solution)/shard_map/all_to_all | solution.py:204
  103.0 24.2 %collective-permute-start.10 = (bf16[320,1024]{1,0:T(8,128)(2,1)}, bf16[320,1024]{1,0:T(8,128)(2,1)}, u32[]{:S(2)}, u32[]{:S(2)}) collective-permute-start(bf16[320,1024]{1,0:T(8,128)(2,1)} %collective-permute-done.9), channel_id=1, source_target_pairs={{0,1},{1,2},{2,3},{3,4},{4,5},{5,6},{6,7},{7,8},{8,9},{9,10},{10,1... | collective-permute-start | bytes 1966088 | tf_op jit(solution)/shard_map/ppermute | solution.py:161
  110.2 20.1 %collective-permute-start.16 = (bf16[320,1024]{1,0:T(8,128)(2,1)}, bf16[320,1024]{1,0:T(8,128)(2,1)}, u32[]{:S(2)}, u32[]{:S(2)}) collective-permute-start(bf16[320,1024]{1,0:T(8,128)(2,1)} %collective-permute-done.15), channel_id=1, source_target_pairs={{0,1},{1,2},{2,3},{3,4},{4,5},{5,6},{6,7},{7,8},{8,9},{9,10},{10,1... | collective-permute-start | bytes 1966088 | tf_op jit(solution)/shard_map/ppermute | solution.py:161
  121.6 23.6 %all-to-all-start.3 = ((f32[16,32,640]{2,1,0:T(8,128)}), f32[16,32,640]{2,1,0:T(8,128)}, u32[]{:S(2)}, u32[]{:S(2)}) async-start(f32[16,32,640]{2,1,0:T(8,128)} %pad_maximum_fusion.2), calls=%async_computation.3 | async-start | bytes 2621440 | tf_op jit(solution)/shard_map/all_to_all | solution.py:204
  128.2 8.4 %collective-permute-start.13 = (bf16[160,1024]{1,0:T(8,128)(2,1)S(1)}, bf16[160,1024]{1,0:T(8,128)(2,1)S(1)}, u32[]{:S(2)}, u32[]{:S(2)}) collective-permute-start(bf16[160,1024]{1,0:T(8,128)(2,1)S(1)} %constant_dynamic-slice_fusion.1), channel_id=1, source_target_pairs={{0,1},{1,2},{2,3},{3,4},{4,5},{5,6},{6,7},{7,8},{8,9},{9,10},{10,1... | collective-permute-start | bytes 983048 | tf_op jit(solution)/shard_map/ppermute | solution.py:161
  131.3 8.8 %collective-permute-start.17 = (bf16[160,1024]{1,0:T(8,128)(2,1)S(1)}, bf16[160,1024]{1,0:T(8,128)(2,1)S(1)}, u32[]{:S(2)}, u32[]{:S(2)}) collective-permute-start(bf16[160,1024]{1,0:T(8,128)(2,1)S(1)} %constant_dynamic-slice_fusion), channel_id=1, source_target_pairs={{0,1},{1,2},{2,3},{3,4},{4,5},{5,6},{6,7},{7,8},{8,9},{9,10},{10,1... | collective-permute-start | bytes 983048 | tf_op jit(solution)/shard_map/ppermute | solution.py:161
  145.2 18.3 %all-to-all-start.2 = ((f32[16,32,512]{2,1,0:T(8,128)}), f32[16,32,512]{2,1,0:T(8,128)}, u32[]{:S(2)}, u32[]{:S(2)}) async-start(f32[16,32,512]{2,1,0:T(8,128)} %pad_maximum_fusion.3), calls=%async_computation.2 | async-start | bytes 2097152 | tf_op jit(solution)/shard_map/all_to_all | solution.py:204
  184.2 15.9 %all-to-all-start.5 = ((f32[16,8,128]{2,1,0:T(8,128)}), f32[16,8,128]{2,1,0:T(8,128)S(1)}, u32[]{:S(2)}, u32[]{:S(2)}) async-start(f32[16,8,128]{2,1,0:T(8,128)} %shard_map.32), calls=%async_computation.5 | async-start | bytes 131072 | tf_op jit(solution)/shard_map/all_to_all | solution.py:209
  (4 other events, 31.0 us)

commit v12 on v11

--- a/solution.py
+++ b/solution.py
@@ -9,7 +9,7 @@
 
 epsilon = 1e-06
 GROUP_ENDS = (2, 4, 6, 8)
-TIES = {(5, 0): 0, (7, 0): 1}
+TIES = {(5, 0): 0, (6, 1): 1}
 VMEM = pltpu.VMEM
 LIMIT = 48 * 1024 * 1024
 EXACT = lax.Precision.HIGHEST

time: 222 us -> 224 us (level)
  starting transfers between devices: 94.4 us -> 97 us
    all_to_all x1, starting transfers between devices: 4.34 us -> 9.28 us  [on_device(): parts = lax.all_to_all(parts, 'tensor', 0, 0)]
    all_to_all x4, starting transfers between devices: 23.8 us -> 20.6 us  [on_device(): lax.all_to_all(ready, 'dp', 0, 0, axis_index_groups=same_core)]
where the time goes in v12:
time: 224 us; the launch traced here: 223 us
  starting transfers between devices  97 us (43%)
  waiting for transfers between devices  52.6 us (23%)
  blocking collectives  31.6 us (14%)
  matrix products  16.6 us (7%)
  Pallas kernels  15.4 us (7%)
  other arithmetic  4.93 us (2%)
  local copies, waits for them, and re-layouts  4 us (2%)
    ppermute x16, starting transfers between devices, move(): return lax.ppermute(slab, ('dp', 'tensor'), onward)  56.4 us
    ppermute x16, waiting for transfers between devices, move(): return lax.ppermute(slab, ('dp', 'tensor'), onward)  25.5 us
    all_to_all x4, starting transfers between devices, on_device(): lax.all_to_all(ready, 'dp', 0, 0, axis_index_groups=same_core)  20.6 us
    all_to_all x1, blocking collectives, on_device(): home = lax.all_to_all(home, 'dp', 0, 0)  16.7 us
    dot_general x8, matrix products, on_device(): lax.dot_general(grads[k], jnp.concatenate(held[k], axis=0), (((0,), (1,))...  16.6 us
    all_to_all x4, waiting for transfers between devices, on_device(): lax.all_to_all(ready, 'dp', 0, 0, axis_index_groups=same_core)  15.5 us
    all_to_all x1, blocking collectives, on_device(): parts = sum_and_spread(lax.all_to_all(peers, 'dp', 0, 0), slabs)  14.9 us
    all_to_all x1, waiting for transfers between devices, on_device(): parts = lax.all_to_all(parts, 'tensor', 0, 0)  11.6 us
  transfers between devices with their start and end apart: 23, of which 14 were waited for; matrix products, arithmetic and copies ran while one was open for 11% of the time, Pallas kernels for 4%

profile of v12, /device:TPU:1, one launch (start us, length us, event | category | flops | bytes accessed | tf_op | source)
XLA Modules:
  0.0 222.6 jit_solution(502547797346748083)
XLA Ops:
  0.0 8.8 %collective-permute-start.5 = (bf16[320,1024]{1,0:T(8,128)(2,1)}, bf16[320,1024]{1,0:T(8,128)(2,1)S(1)}, u32[]{:S(2)}, u32[]{:S(2)}) collective-permute-start(bf16[320,1024]{1,0:T(8,128)(2,1)} %bitcast.43), channel_id=1, source_target_pairs={{0,16},{16,0},{32,48},{48,32},{64,80},{80,64},{96,112},{112,96},{1... | collective-permute-start | bytes 1966088 | tf_op jit(solution)/shard_map/ppermute | solution.py:164
  8.8 5.8 %collective-permute-start = (bf16[320,1024]{1,0:T(8,128)(2,1)}, bf16[320,1024]{1,0:T(8,128)(2,1)}, u32[]{:S(2)}, u32[]{:S(2)}) collective-permute-start(bf16[320,1024]{1,0:T(8,128)(2,1)} %bitcast.44), channel_id=1, source_target_pairs={{0,1},{1,2},{2,3},{3,4},{4,5},{5,6},{6,7},{7,8},{8,9},{9,10},{10,1... | collective-permute-start | bytes 1966088 | tf_op jit(solution)/shard_map/ppermute | solution.py:161
  19.1 3.2 %collective-permute-done = bf16[320,1024]{1,0:T(8,128)(2,1)} collective-permute-done((bf16[320,1024]{1,0:T(8,128)(2,1)}, bf16[320,1024]{1,0:T(8,128)(2,1)}, u32[]{:S(2)}, u32[]{:S(2)}) %collective-permute-start) | collective-permute-done | bytes 655392 | tf_op jit(solution)/shard_map/ppermute | solution.py:161
  22.4 5.0 %collective-permute-start.1 = (bf16[320,1024]{1,0:T(8,128)(2,1)}, bf16[320,1024]{1,0:T(8,128)(2,1)S(1)}, u32[]{:S(2)}, u32[]{:S(2)}) collective-permute-start(bf16[320,1024]{1,0:T(8,128)(2,1)} %collective-permute-done), channel_id=1, source_target_pairs={{0,1},{1,2},{2,3},{3,4},{4,5},{5,6},{6,7},{7,8},{8,9},{9,10},{10,1... | collective-permute-start | bytes 1966088 | tf_op jit(solution)/shard_map/ppermute | solution.py:161
  29.3 5.1 %collective-permute-start.8 = (bf16[320,1024]{1,0:T(8,128)(2,1)}, bf16[320,1024]{1,0:T(8,128)(2,1)S(1)}, u32[]{:S(2)}, u32[]{:S(2)}) collective-permute-start(bf16[320,1024]{1,0:T(8,128)(2,1)} %collective-permute-done.6), channel_id=1, source_target_pairs={{0,1},{1,2},{2,3},{3,4},{4,5},{5,6},{6,7},{7,8},{8,9},{9,10},{10,1... | collective-permute-start | bytes 1966088 | tf_op jit(solution)/shard_map/ppermute | solution.py:161
  36.4 4.9 %collective-permute-start.2 = (bf16[320,1024]{1,0:T(8,128)(2,1)S(1)}, bf16[320,1024]{1,0:T(8,128)(2,1)}, u32[]{:S(2)}, u32[]{:S(2)}) collective-permute-start(bf16[320,1024]{1,0:T(8,128)(2,1)S(1)} %collective-permute-done.1), channel_id=1, source_target_pairs={{0,1},{1,2},{2,3},{3,4},{4,5},{5,6},{6,7},{7,8},{8,9},{9,10},{10,1... | collective-permute-start | bytes 1966088 | tf_op jit(solution)/shard_map/ppermute | solution.py:161
  46.9 4.9 %collective-permute-start.12 = (bf16[320,1024]{1,0:T(8,128)(2,1)S(1)}, bf16[320,1024]{1,0:T(8,128)(2,1)}, u32[]{:S(2)}, u32[]{:S(2)}) collective-permute-start(bf16[320,1024]{1,0:T(8,128)(2,1)S(1)} %collective-permute-done.8), channel_id=1, source_target_pairs={{0,1},{1,2},{2,3},{3,4},{4,5},{5,6},{6,7},{7,8},{8,9},{9,10},{10,1... | collective-permute-start | bytes 1966088 | tf_op jit(solution)/shard_map/ppermute | solution.py:161
  51.8 6.8 %all-to-all-start = ((f32[16,32,896]{2,1,0:T(8,128)}), f32[16,32,896]{2,1,0:T(8,128)S(1)}, u32[]{:S(2)}, u32[]{:S(2)}) async-start(f32[16,32,896]{2,1,0:T(8,128)} %pad_maximum_fusion), calls=%async_computation | async-start | bytes 3670016 | tf_op jit(solution)/shard_map/all_to_all | solution.py:204
  60.7 3.8 %collective-permute-start.13 = (bf16[320,1024]{1,0:T(8,128)(2,1)}, bf16[320,1024]{1,0:T(8,128)(2,1)}, u32[]{:S(2)}, u32[]{:S(2)}) collective-permute-start(bf16[320,1024]{1,0:T(8,128)(2,1)} %collective-permute-done.12), channel_id=1, source_target_pairs={{0,1},{1,2},{2,3},{3,4},{4,5},{5,6},{6,7},{7,8},{8,9},{9,10},{10,1... | collective-permute-start | bytes 1966088 | tf_op jit(solution)/shard_map/ppermute | solution.py:161
  64.4 6.2 %collective-permute-done.3 = bf16[320,1024]{1,0:T(8,128)(2,1)} collective-permute-done((bf16[320,1024]{1,0:T(8,128)(2,1)}, bf16[320,1024]{1,0:T(8,128)(2,1)}, u32[]{:S(2)}, u32[]{:S(2)}) %collective-permute-start.3) | collective-permute-done | bytes 655392 | tf_op jit(solution)/shard_map/ppermute | solution.py:161
  80.8 3.0 %collective-permute-start.14 = (bf16[320,1024]{1,0:T(8,128)(2,1)}, bf16[320,1024]{1,0:T(8,128)(2,1)}, u32[]{:S(2)}, u32[]{:S(2)}) collective-permute-start(bf16[320,1024]{1,0:T(8,128)(2,1)} %collective-permute-done.13), channel_id=1, source_target_pairs={{0,1},{1,2},{2,3},{3,4},{4,5},{5,6},{6,7},{7,8},{8,9},{9,10},{10,1... | collective-permute-start | bytes 1966088 | tf_op jit(solution)/shard_map/ppermute | solution.py:161
  86.5 3.9 %all-to-all-start.1 = ((f32[16,32,640]{2,1,0:T(8,128)}), f32[16,32,640]{2,1,0:T(8,128)S(1)}, u32[]{:S(2)}, u32[]{:S(2)}) async-start(f32[16,32,640]{2,1,0:T(8,128)} %pad_maximum_fusion.1), calls=%async_computation.1 | async-start | bytes 2621440 | tf_op jit(solution)/shard_map/all_to_all | solution.py:204
  92.7 3.9 %collective-permute-start.15 = (bf16[320,1024]{1,0:T(8,128)(2,1)}, bf16[320,1024]{1,0:T(8,128)(2,1)}, u32[]{:S(2)}, u32[]{:S(2)}) collective-permute-start(bf16[320,1024]{1,0:T(8,128)(2,1)} %collective-permute-done.14), channel_id=1, source_target_pairs={{0,1},{1,2},{2,3},{3,4},{4,5},{5,6},{6,7},{7,8},{8,9},{9,10},{10,1... | collective-permute-start | bytes 1966088 | tf_op jit(solution)/shard_map/ppermute | solution.py:161
  96.7 5.7 %collective-permute-done.9 = bf16[320,1024]{1,0:T(8,128)(2,1)} collective-permute-done((bf16[320,1024]{1,0:T(8,128)(2,1)}, bf16[320,1024]{1,0:T(8,128)(2,1)}, u32[]{:S(2)}, u32[]{:S(2)}) %collective-permute-start.9) | collective-permute-done | bytes 655392 | tf_op jit(solution)/shard_map/ppermute | solution.py:161
  108.4 5.0 %all-to-all-done.1.block_ref.refs_1_ = f32[16,32,640]{2,1,0:T(8,128)S(1)} async-done(((f32[16,32,640]{2,1,0:T(8,128)}), f32[16,32,640]{2,1,0:T(8,128)S(1)}, u32[]{:S(2)}, u32[]{:S(2)}) %all-to-all-start.1) | async-done | bytes 1310752 | tf_op jit(solution)/shard_map/all_to_all | solution.py:204
  118.7 4.4 %all-to-all-start.3 = ((f32[16,32,640]{2,1,0:T(8,128)}), f32[16,32,640]{2,1,0:T(8,128)}, u32[]{:S(2)}, u32[]{:S(2)}) async-start(f32[16,32,640]{2,1,0:T(8,128)} %pad_maximum_fusion.2), calls=%async_computation.3 | async-start | bytes 2621440 | tf_op jit(solution)/shard_map/all_to_all | solution.py:204
  134.4 3.5 %collective-permute-done.17 = bf16[160,1024]{1,0:T(8,128)(2,1)S(1)} collective-permute-done((bf16[160,1024]{1,0:T(8,128)(2,1)S(1)}, bf16[160,1024]{1,0:T(8,128)(2,1)S(1)}, u32[]{:S(2)}, u32[]{:S(2)}) %collective-permute-start.17) | collective-permute-done | bytes 327712 | tf_op jit(solution)/shard_map/ppermute | solution.py:161
  141.8 5.5 %all-to-all-start.2 = ((f32[16,32,512]{2,1,0:T(8,128)}), f32[16,32,512]{2,1,0:T(8,128)}, u32[]{:S(2)}, u32[]{:S(2)}) async-start(f32[16,32,512]{2,1,0:T(8,128)} %pad_maximum_fusion.3), calls=%async_computation.2 | async-start | bytes 2097152 | tf_op jit(solution)/shard_map/all_to_all | solution.py:204
  152.1 3.5 %shard_map.30.before_ref = f32[8,128]{1,0:T(8,128)S(1)} custom-call(s32[1]{0:T(128)} %bitcast.1.core_ref, f32[16,32,640]{2,1,0:T(8,128)} %all-to-all-done.3.block_ref.refs_2_, f32[8,128]{1,0:T(8,128)S(1)} %shard_map.29.before_ref), custom_call_target="tpu_custom_call" | custom-call | flops 1006632960 | bytes 1310720 | tf_op jit(solution)/shard_map/pallas_call | solution.py:51
  155.5 6.5 %all-to-all-done.2.block_ref.refs_3_ = f32[16,32,512]{2,1,0:T(8,128)} async-done(((f32[16,32,512]{2,1,0:T(8,128)}), f32[16,32,512]{2,1,0:T(8,128)}, u32[]{:S(2)}, u32[]{:S(2)}) %all-to-all-start.2) | async-done | bytes 1048608 | tf_op jit(solution)/shard_map/all_to_all | solution.py:204
  165.1 14.9 %all_to_all.35.parts_ref = f32[32,8,128]{2,1,0:T(8,128)} all-to-all(f32[32,8,128]{2,1,0:T(8,128)S(1)} %broadcast_in_dim.7), channel_id=1, replica_groups=mesh['dp'=32,'tensor'=16] {'dp'}, dimensions={0} | all-to-all | bytes 262144 | tf_op jit(solution)/shard_map/all_to_all | solution.py:208
  181.5 9.3 %all-to-all-start.5 = ((f32[16,8,128]{2,1,0:T(8,128)}), f32[16,8,128]{2,1,0:T(8,128)S(1)}, u32[]{:S(2)}, u32[]{:S(2)}) async-start(f32[16,8,128]{2,1,0:T(8,128)} %shard_map.32), calls=%async_computation.5 | async-start | bytes 131072 | tf_op jit(solution)/shard_map/all_to_all | solution.py:209
  190.8 11.6 %all-to-all-done.5.parts_ref = f32[16,8,128]{2,1,0:T(8,128)S(1)} async-done(((f32[16,8,128]{2,1,0:T(8,128)}), f32[16,8,128]{2,1,0:T(8,128)S(1)}, u32[]{:S(2)}, u32[]{:S(2)}) %all-to-all-start.5) | async-done | bytes 65568 | tf_op jit(solution)/shard_map/all_to_all | solution.py:209
  205.1 16.7 %all_to_all.36 = f32[32,16,160]{2,1,0:T(8,128)S(1)} all-to-all(f32[32,16,160]{2,1,0:T(8,128)S(1)} %shard_map.33), channel_id=1, replica_groups=mesh['dp'=32,'tensor'=16] {'dp'}, dimensions={0} | all-to-all | bytes 655360 | tf_op jit(solution)/shard_map/all_to_all | solution.py:211
  (64 shorter events, 70.2 us)
Async XLA Ops:
  0.0 14.5 %collective-permute-start.5 = (bf16[320,1024]{1,0:T(8,128)(2,1)}, bf16[320,1024]{1,0:T(8,128)(2,1)S(1)}, u32[]{:S(2)}, u32[]{:S(2)}) collective-permute-start(bf16[320,1024]{1,0:T(8,128)(2,1)} %bitcast.43), channel_id=1, source_target_pairs={{0,16},{16,0},{32,48},{48,32},{64,80},{80,64},{96,112},{112,96},{1... | collective-permute-start | bytes 1966088 | tf_op jit(solution)/shard_map/ppermute | solution.py:164
  8.8 13.6 %collective-permute-start = (bf16[320,1024]{1,0:T(8,128)(2,1)}, bf16[320,1024]{1,0:T(8,128)(2,1)}, u32[]{:S(2)}, u32[]{:S(2)}) collective-permute-start(bf16[320,1024]{1,0:T(8,128)(2,1)} %bitcast.44), channel_id=1, source_target_pairs={{0,1},{1,2},{2,3},{3,4},{4,5},{5,6},{6,7},{7,8},{8,9},{9,10},{10,1... | collective-permute-start | bytes 1966088 | tf_op jit(solution)/shard_map/ppermute | solution.py:161
  14.6 14.7 %collective-permute-start.6 = (bf16[320,1024]{1,0:T(8,128)(2,1)S(1)}, bf16[320,1024]{1,0:T(8,128)(2,1)}, u32[]{:S(2)}, u32[]{:S(2)}) collective-permute-start(bf16[320,1024]{1,0:T(8,128)(2,1)S(1)} %collective-permute-done.5), channel_id=1, source_target_pairs={{0,1},{1,2},{2,3},{3,4},{4,5},{5,6},{6,7},{7,8},{8,9},{9,10},{10,1... | collective-permute-start | bytes 1966088 | tf_op jit(solution)/shard_map/ppermute | solution.py:161
  17.2 10.2 %collective-permute-start.7 = (bf16[1024,256]{1,0:T(8,128)(2,1)}, bf16[1024,256]{1,0:T(8,128)(2,1)S(1)}, u32[]{:S(2)}, u32[]{:S(2)}) collective-permute-start(bf16[1024,256]{1,0:T(8,128)(2,1)} %param.3), channel_id=1, source_target_pairs={{0,16},{16,0},{32,48},{48,32},{64,80},{80,64},{96,112},{112,96},{1... | collective-permute-start | bytes 1572872 | tf_op jit(solution)/shard_map/ppermute | solution.py:167
  22.4 14.0 %collective-permute-start.1 = (bf16[320,1024]{1,0:T(8,128)(2,1)}, bf16[320,1024]{1,0:T(8,128)(2,1)S(1)}, u32[]{:S(2)}, u32[]{:S(2)}) collective-permute-start(bf16[320,1024]{1,0:T(8,128)(2,1)} %collective-permute-done), channel_id=1, source_target_pairs={{0,1},{1,2},{2,3},{3,4},{4,5},{5,6},{6,7},{7,8},{8,9},{9,10},{10,1... | collective-permute-start | bytes 1966088 | tf_op jit(solution)/shard_map/ppermute | solution.py:161
  29.3 14.2 %collective-permute-start.8 = (bf16[320,1024]{1,0:T(8,128)(2,1)}, bf16[320,1024]{1,0:T(8,128)(2,1)S(1)}, u32[]{:S(2)}, u32[]{:S(2)}) collective-permute-start(bf16[320,1024]{1,0:T(8,128)(2,1)} %collective-permute-done.6), channel_id=1, source_target_pairs={{0,1},{1,2},{2,3},{3,4},{4,5},{5,6},{6,7},{7,8},{8,9},{9,10},{10,1... | collective-permute-start | bytes 1966088 | tf_op jit(solution)/shard_map/ppermute | solution.py:161
  36.4 22.2 %collective-permute-start.2 = (bf16[320,1024]{1,0:T(8,128)(2,1)S(1)}, bf16[320,1024]{1,0:T(8,128)(2,1)}, u32[]{:S(2)}, u32[]{:S(2)}) collective-permute-start(bf16[320,1024]{1,0:T(8,128)(2,1)S(1)} %collective-permute-done.1), channel_id=1, source_target_pairs={{0,1},{1,2},{2,3},{3,4},{4,5},{5,6},{6,7},{7,8},{8,9},{9,10},{10,1... | collective-permute-start | bytes 1966088 | tf_op jit(solution)/shard_map/ppermute | solution.py:161
  46.9 13.7 %collective-permute-start.12 = (bf16[320,1024]{1,0:T(8,128)(2,1)S(1)}, bf16[320,1024]{1,0:T(8,128)(2,1)}, u32[]{:S(2)}, u32[]{:S(2)}) collective-permute-start(bf16[320,1024]{1,0:T(8,128)(2,1)S(1)} %collective-permute-done.8), channel_id=1, source_target_pairs={{0,1},{1,2},{2,3},{3,4},{4,5},{5,6},{6,7},{7,8},{8,9},{9,10},{10,1... | collective-permute-start | bytes 1966088 | tf_op jit(solution)/shard_map/ppermute | solution.py:161
  51.8 34.7 %all-to-all-start = ((f32[16,32,896]{2,1,0:T(8,128)}), f32[16,32,896]{2,1,0:T(8,128)S(1)}, u32[]{:S(2)}, u32[]{:S(2)}) async-start(f32[16,32,896]{2,1,0:T(8,128)} %pad_maximum_fusion), calls=%async_computation | async-start | bytes 3670016 | tf_op jit(solution)/shard_map/all_to_all | solution.py:204
  58.6 19.1 %copy-start.3 = (bf16[1024,256]{1,0:T(8,128)(2,1)S(1)}, bf16[1024,256]{1,0:T(8,128)(2,1)}, u32[]{:S(2)}) copy-start(bf16[1024,256]{1,0:T(8,128)(2,1)} %copy-done.1) | copy-start | bytes 1572868
  58.6 12.1 %collective-permute-start.3 = (bf16[320,1024]{1,0:T(8,128)(2,1)}, bf16[320,1024]{1,0:T(8,128)(2,1)}, u32[]{:S(2)}, u32[]{:S(2)}) collective-permute-start(bf16[320,1024]{1,0:T(8,128)(2,1)} %collective-permute-done.2), channel_id=1, source_target_pairs={{0,1},{1,2},{2,3},{3,4},{4,5},{5,6},{6,7},{7,8},{8,9},{9,10},{10,1... | collective-permute-start | bytes 1966088 | tf_op jit(solution)/shard_map/ppermute | solution.py:161
  60.7 17.0 %collective-permute-start.13 = (bf16[320,1024]{1,0:T(8,128)(2,1)}, bf16[320,1024]{1,0:T(8,128)(2,1)}, u32[]{:S(2)}, u32[]{:S(2)}) collective-permute-start(bf16[320,1024]{1,0:T(8,128)(2,1)} %collective-permute-done.12), channel_id=1, source_target_pairs={{0,1},{1,2},{2,3},{3,4},{4,5},{5,6},{6,7},{7,8},{8,9},{9,10},{10,1... | collective-permute-start | bytes 1966088 | tf_op jit(solution)/shard_map/ppermute | solution.py:161
  70.7 19.8 %collective-permute-start.4 = (bf16[320,1024]{1,0:T(8,128)(2,1)}, bf16[320,1024]{1,0:T(8,128)(2,1)}, u32[]{:S(2)}, u32[]{:S(2)}) collective-permute-start(bf16[320,1024]{1,0:T(8,128)(2,1)} %collective-permute-done.3), channel_id=1, source_target_pairs={{0,1},{1,2},{2,3},{3,4},{4,5},{5,6},{6,7},{7,8},{8,9},{9,10},{10,1... | collective-permute-start | bytes 1966088 | tf_op jit(solution)/shard_map/ppermute | solution.py:161
  80.8 11.9 %collective-permute-start.14 = (bf16[320,1024]{1,0:T(8,128)(2,1)}, bf16[320,1024]{1,0:T(8,128)(2,1)}, u32[]{:S(2)}, u32[]{:S(2)}) collective-permute-start(bf16[320,1024]{1,0:T(8,128)(2,1)} %collective-permute-done.13), channel_id=1, source_target_pairs={{0,1},{1,2},{2,3},{3,4},{4,5},{5,6},{6,7},{7,8},{8,9},{9,10},{10,1... | collective-permute-start | bytes 1966088 | tf_op jit(solution)/shard_map/ppermute | solution.py:161
  86.5 26.9 %all-to-all-start.1 = ((f32[16,32,640]{2,1,0:T(8,128)}), f32[16,32,640]{2,1,0:T(8,128)S(1)}, u32[]{:S(2)}, u32[]{:S(2)}) async-start(f32[16,32,640]{2,1,0:T(8,128)} %pad_maximum_fusion.1), calls=%async_computation.1 | async-start | bytes 2621440 | tf_op jit(solution)/shard_map/all_to_all | solution.py:204
  90.5 11.9 %collective-permute-start.9 = (bf16[320,1024]{1,0:T(8,128)(2,1)}, bf16[320,1024]{1,0:T(8,128)(2,1)}, u32[]{:S(2)}, u32[]{:S(2)}) collective-permute-start(bf16[320,1024]{1,0:T(8,128)(2,1)} %collective-permute-done.4), channel_id=1, source_target_pairs={{0,1},{1,2},{2,3},{3,4},{4,5},{5,6},{6,7},{7,8},{8,9},{9,10},{10,1... | collective-permute-start | bytes 1966088 | tf_op jit(solution)/shard_map/ppermute | solution.py:161
  92.7 20.7 %collective-permute-start.15 = (bf16[320,1024]{1,0:T(8,128)(2,1)}, bf16[320,1024]{1,0:T(8,128)(2,1)}, u32[]{:S(2)}, u32[]{:S(2)}) collective-permute-start(bf16[320,1024]{1,0:T(8,128)(2,1)} %collective-permute-done.14), channel_id=1, source_target_pairs={{0,1},{1,2},{2,3},{3,4},{4,5},{5,6},{6,7},{7,8},{8,9},{9,10},{10,1... | collective-permute-start | bytes 1966088 | tf_op jit(solution)/shard_map/ppermute | solution.py:161
  102.4 20.7 %collective-permute-start.10 = (bf16[320,1024]{1,0:T(8,128)(2,1)}, bf16[320,1024]{1,0:T(8,128)(2,1)}, u32[]{:S(2)}, u32[]{:S(2)}) collective-permute-start(bf16[320,1024]{1,0:T(8,128)(2,1)} %collective-permute-done.9), channel_id=1, source_target_pairs={{0,1},{1,2},{2,3},{3,4},{4,5},{5,6},{6,7},{7,8},{8,9},{9,10},{10,1... | collective-permute-start | bytes 1966088 | tf_op jit(solution)/shard_map/ppermute | solution.py:161
  116.7 11.9 %collective-permute-start.16 = (bf16[320,1024]{1,0:T(8,128)(2,1)}, bf16[320,1024]{1,0:T(8,128)(2,1)}, u32[]{:S(2)}, u32[]{:S(2)}) collective-permute-start(bf16[320,1024]{1,0:T(8,128)(2,1)} %collective-permute-done.15), channel_id=1, source_target_pairs={{0,1},{1,2},{2,3},{3,4},{4,5},{5,6},{6,7},{7,8},{8,9},{9,10},{10,1... | collective-permute-start | bytes 1966088 | tf_op jit(solution)/shard_map/ppermute | solution.py:161
  118.7 23.2 %all-to-all-start.3 = ((f32[16,32,640]{2,1,0:T(8,128)}), f32[16,32,640]{2,1,0:T(8,128)}, u32[]{:S(2)}, u32[]{:S(2)}) async-start(f32[16,32,640]{2,1,0:T(8,128)} %pad_maximum_fusion.2), calls=%async_computation.3 | async-start | bytes 2621440 | tf_op jit(solution)/shard_map/all_to_all | solution.py:204
  124.1 8.5 %collective-permute-start.11 = (bf16[160,1024]{1,0:T(8,128)(2,1)S(1)}, bf16[160,1024]{1,0:T(8,128)(2,1)S(1)}, u32[]{:S(2)}, u32[]{:S(2)}) collective-permute-start(bf16[160,1024]{1,0:T(8,128)(2,1)S(1)} %constant_dynamic-slice_fusion.1), channel_id=1, source_target_pairs={{0,1},{1,2},{2,3},{3,4},{4,5},{5,6},{6,7},{7,8},{8,9},{9,10},{10,1... | collective-permute-start | bytes 983048 | tf_op jit(solution)/shard_map/ppermute | solution.py:161
  129.7 8.2 %collective-permute-start.17 = (bf16[160,1024]{1,0:T(8,128)(2,1)S(1)}, bf16[160,1024]{1,0:T(8,128)(2,1)S(1)}, u32[]{:S(2)}, u32[]{:S(2)}) collective-permute-start(bf16[160,1024]{1,0:T(8,128)(2,1)S(1)} %constant_dynamic-slice_fusion), channel_id=1, source_target_pairs={{0,1},{1,2},{2,3},{3,4},{4,5},{5,6},{6,7},{7,8},{8,9},{9,10},{10,1... | collective-permute-start | bytes 983048 | tf_op jit(solution)/shard_map/ppermute | solution.py:161
  141.8 20.3 %all-to-all-start.2 = ((f32[16,32,512]{2,1,0:T(8,128)}), f32[16,32,512]{2,1,0:T(8,128)}, u32[]{:S(2)}, u32[]{:S(2)}) async-start(f32[16,32,512]{2,1,0:T(8,128)} %pad_maximum_fusion.3), calls=%async_computation.2 | async-start | bytes 2097152 | tf_op jit(solution)/shard_map/all_to_all | solution.py:204
  181.5 20.9 %all-to-all-start.5 = ((f32[16,8,128]{2,1,0:T(8,128)}), f32[16,8,128]{2,1,0:T(8,128)S(1)}, u32[]{:S(2)}, u32[]{:S(2)}) async-start(f32[16,8,128]{2,1,0:T(8,128)} %shard_map.32), calls=%async_computation.5 | async-start | bytes 131072 | tf_op jit(solution)/shard_map/all_to_all | solution.py:209
  (4 other events, 30.9 us)

commit v13 on v12

--- a/solution.py
+++ b/solution.py
@@ -74,7 +74,7 @@
     )(parts)
 
 
-def combine_kernel(replicas, slabs, order, counts, here_ref, core_ref, parts_ref, *refs):
+def combine_kernel(replicas, slabs, layouts, here_ref, core_ref, parts_ref, *refs):
     blocks, out_ref = refs[:-1], refs[-1]
     packed = jnp.sum(parts_ref[...], axis=0)
     gram = jnp.concatenate(
@@ -109,25 +109,22 @@
     here, core = here_ref[0], core_ref[0]
     starts = [pl.multiple_of(core * part, part), pl.multiple_of((1 - core) * part, part)]
     out_ref[...] = jnp.zeros(out_ref.shape, jnp.float32)
-    place = 0
-    for block_ref, count in zip(blocks, counts):
+    for block_ref, layout in zip(blocks, layouts):
         total = 0.0
         for r in range(replicas):
             total = total + block_ref[r // 2, pl.ds(starts[r % 2], part)] * down[r:r + 1]
-        for i in range(count):
-            step, piece = order[place]
+        for step, piece, place, count, column in layout:
             away = jnp.where(core == 0, slabs - step, step)
             slab = lax.rem(here + away, slabs)
             piece = core if piece is None else piece
-            out_ref[slab * 2 + piece] = total[:, i * width:(i + 1) * width]
-            place += 1
-
-
-def weighted_sums(replicas, slabs, order, counts, width, here, core, parts, blocks):
+            out_ref[slab * 2 + piece, :, place:place + count] = total[:, column:column + count]
+
+
+def weighted_sums(replicas, slabs, layouts, width, here, core, parts, blocks):
     part = blocks[0].shape[1] // 2
     size = sum(b.size for b in blocks)
     return pl.pallas_call(
-        functools.partial(combine_kernel, replicas, slabs, order, counts),
+        functools.partial(combine_kernel, replicas, slabs, layouts),
         out_shape=jax.ShapeDtypeStruct((replicas, part, width), jnp.float32),
         in_specs=[pl.BlockSpec(memory_space=pltpu.SMEM)] * 2
         + [pl.BlockSpec(memory_space=VMEM)] * (1 + len(blocks)),
@@ -165,11 +162,23 @@
     grads = [out_grads, out_grads]
     chains[1], grads[1] = lax.optimization_barrier((chains[1], grads[1]))
     grads[1] = lax.ppermute(grads[1], "dp", sibling)
+    def layout_of(order):
+        layout, column = [], 0
+        for step, start, count in order:
+            while count:
+                piece = None if start is None else start // rows
+                place = 0 if start is None else start % rows
+                run = min(count, rows - place)
+                layout.append((step, piece, place, run, column))
+                column, count = column + run, count - run
+                start = None if start is None else start + run
+        return layout
+
     held = [[own_half(slab)] for slab in chains]
-    order = [(0, None)]
-    blocks = []
+    order = [(0, None, rows)]
+    left, left_order = [[], []], []
+    blocks, layouts = [], []
     gram = jnp.zeros((8, 128), jnp.float32)
-    counts = []
     for step in range(1, half + 1):
         if step < half:
             chains = [move(slab) for slab in chains]
@@ -180,16 +189,28 @@
                     place = TIES[step, k]
                     chains[k], blocks[place] = lax.optimization_barrier((chains[k], blocks[place]))
                 held[k].append(chains[k])
-            order += [(step, 0), (step, 1)]
+            order.append((step, 0, slab_rows))
         else:
             for k in range(2):
                 held[k].append(move(own_half(chains[k])))
-            order.append((half, None))
+            order.append((half, None, rows))
         if step in GROUP_ENDS:
-            size = sum(piece.shape[0] for piece in held[0])
-            counts.append(size // rows)
-            parts = []
+            if step < half:
+                spare = sum(piece.shape[0] for piece in held[0]) % 128
+                if spare:
+                    for k in range(2):
+                        left[k].append(held[k][-1][-spare:])
+                        held[k][-1] = held[k][-1][:-spare]
+                    last, start, count = order.pop()
+                    order.append((last, start, count - spare))
+                    left_order.append((last, start + count - spare, spare))
+            else:
+                held = [held[k] + left[k] for k in range(2)]
+                order += left_order
+            layouts.append(layout_of(order))
+            order, parts = [], []
             for k in range(2):
+                size = sum(piece.shape[0] for piece in held[k])
                 if size % 128:
                     held[k].append(jnp.zeros((-size % 128, tokens), held[k][0].dtype))
                 grad = lax.dot_general(
@@ -207,7 +228,7 @@
     peers = jnp.broadcast_to(gram, (replicas, *gram.shape))
     parts = sum_and_spread(lax.all_to_all(peers, "dp", 0, 0), slabs)
     parts = lax.all_to_all(parts, "tensor", 0, 0)
-    home = weighted_sums(replicas, slabs, order, counts, rows, here, core, parts, blocks)
+    home = weighted_sums(replicas, slabs, layouts, rows, here, core, parts, blocks)
     home = lax.all_to_all(home, "dp", 0, 0)
     home = jnp.sum(home.reshape(chips, 2, columns // chips, -1), axis=1)
     return home.reshape(columns, -1).T

time: 224 us -> 218 us (0.973)
  matrix products: 16.6 us -> 11.5 us
    dot_general x8, matrix products: 16.6 us -> 11.5 us  [on_device(): lax.dot_general(grads[k], jnp.concatenate(held[k], axis=0), (((0,), (1,))...]
    all_to_all x1, starting transfers between devices: 9.28 us -> 6.88 us  [on_device(): parts = lax.all_to_all(parts, 'tensor', 0, 0)]
  transfers between devices with their start and end apart: 23 -> 23, of which waited for: 14 -> 14; matrix products, arithmetic and copies ran while one was open for 11% -> 9% of each run, Pallas kernels for 4% -> 4%
where the time goes in v13:
time: 218 us; the launch traced here: 216 us
  starting transfers between devices  95.6 us (44%)
  waiting for transfers between devices  51.5 us (24%)
  blocking collectives  32.1 us (15%)
  Pallas kernels  14.9 us (7%)
  matrix products  11.5 us (5%)
  local copies, waits for them, and re-layouts  5.55 us (3%)
  other arithmetic  4.85 us (2%)
    ppermute x16, starting transfers between devices, move(): return lax.ppermute(slab, ('dp', 'tensor'), onward)  55.5 us
    ppermute x16, waiting for transfers between devices, move(): return lax.ppermute(slab, ('dp', 'tensor'), onward)  25.2 us
    all_to_all x4, starting transfers between devices, on_device(): lax.all_to_all(ready, 'dp', 0, 0, axis_index_groups=same_core)  22.6 us
    all_to_all x1, blocking collectives, on_device(): home = lax.all_to_all(home, 'dp', 0, 0)  16.7 us
    all_to_all x1, blocking collectives, on_device(): parts = sum_and_spread(lax.all_to_all(peers, 'dp', 0, 0), slabs)  15.4 us
    all_to_all x4, waiting for transfers between devices, on_device(): lax.all_to_all(ready, 'dp', 0, 0, axis_index_groups=same_core)  14.6 us
    all_to_all x1, waiting for transfers between devices, on_device(): parts = lax.all_to_all(parts, 'tensor', 0, 0)  11.7 us
    dot_general x8, matrix products, on_device(): lax.dot_general(grads[k], jnp.concatenate(held[k], axis=0), (((0,), (1,))...  11.5 us
  transfers between devices with their start and end apart: 23, of which 14 were waited for; matrix products, arithmetic and copies ran while one was open for 9% of the time, Pallas kernels for 4%

profile of v13, /device:TPU:1, one launch (start us, length us, event | category | flops | bytes accessed | tf_op | source)
XLA Modules:
  0.0 216.4 jit_solution(6375277420770076467)
XLA Ops:
  0.0 8.8 %collective-permute-start.5 = (bf16[320,1024]{1,0:T(8,128)(2,1)}, bf16[320,1024]{1,0:T(8,128)(2,1)S(1)}, u32[]{:S(2)}, u32[]{:S(2)}) collective-permute-start(bf16[320,1024]{1,0:T(8,128)(2,1)} %bitcast.43), channel_id=1, source_target_pairs={{0,16},{16,0},{32,48},{48,32},{64,80},{80,64},{96,112},{112,96},{1... | collective-permute-start | bytes 1966088 | tf_op jit(solution)/shard_map/ppermute | solution.py:161
  8.8 5.7 %collective-permute-start = (bf16[320,1024]{1,0:T(8,128)(2,1)}, bf16[320,1024]{1,0:T(8,128)(2,1)S(1)}, u32[]{:S(2)}, u32[]{:S(2)}) collective-permute-start(bf16[320,1024]{1,0:T(8,128)(2,1)} %bitcast.44), channel_id=1, source_target_pairs={{0,1},{1,2},{2,3},{3,4},{4,5},{5,6},{6,7},{7,8},{8,9},{9,10},{10,1... | collective-permute-start | bytes 1966088 | tf_op jit(solution)/shard_map/ppermute | solution.py:158
  19.1 3.2 %collective-permute-done = bf16[320,1024]{1,0:T(8,128)(2,1)S(1)} collective-permute-done((bf16[320,1024]{1,0:T(8,128)(2,1)}, bf16[320,1024]{1,0:T(8,128)(2,1)S(1)}, u32[]{:S(2)}, u32[]{:S(2)}) %collective-permute-start) | collective-permute-done | bytes 655392 | tf_op jit(solution)/shard_map/ppermute | solution.py:158
  22.4 4.9 %collective-permute-start.1 = (bf16[320,1024]{1,0:T(8,128)(2,1)S(1)}, bf16[320,1024]{1,0:T(8,128)(2,1)S(1)}, u32[]{:S(2)}, u32[]{:S(2)}) collective-permute-start(bf16[320,1024]{1,0:T(8,128)(2,1)S(1)} %collective-permute-done), channel_id=1, source_target_pairs={{0,1},{1,2},{2,3},{3,4},{4,5},{5,6},{6,7},{7,8},{8,9},{9,10},{10,1... | collective-permute-start | bytes 1966088 | tf_op jit(solution)/shard_map/ppermute | solution.py:158
  29.3 5.0 %collective-permute-start.8 = (bf16[320,1024]{1,0:T(8,128)(2,1)S(1)}, bf16[320,1024]{1,0:T(8,128)(2,1)S(1)}, u32[]{:S(2)}, u32[]{:S(2)}) collective-permute-start(bf16[320,1024]{1,0:T(8,128)(2,1)S(1)} %collective-permute-done.6), channel_id=1, source_target_pairs={{0,1},{1,2},{2,3},{3,4},{4,5},{5,6},{6,7},{7,8},{8,9},{9,10},{10,1... | collective-permute-start | bytes 1966088 | tf_op jit(solution)/shard_map/ppermute | solution.py:158
  36.4 5.2 %collective-permute-start.2 = (bf16[320,1024]{1,0:T(8,128)(2,1)S(1)}, bf16[320,1024]{1,0:T(8,128)(2,1)}, u32[]{:S(2)}, u32[]{:S(2)}) collective-permute-start(bf16[320,1024]{1,0:T(8,128)(2,1)S(1)} %collective-permute-done.1), channel_id=1, source_target_pairs={{0,1},{1,2},{2,3},{3,4},{4,5},{5,6},{6,7},{7,8},{8,9},{9,10},{10,1... | collective-permute-start | bytes 1966088 | tf_op jit(solution)/shard_map/ppermute | solution.py:158
  45.3 5.0 %collective-permute-start.12 = (bf16[320,1024]{1,0:T(8,128)(2,1)S(1)}, bf16[320,1024]{1,0:T(8,128)(2,1)}, u32[]{:S(2)}, u32[]{:S(2)}) collective-permute-start(bf16[320,1024]{1,0:T(8,128)(2,1)S(1)} %collective-permute-done.8), channel_id=1, source_target_pairs={{0,1},{1,2},{2,3},{3,4},{4,5},{5,6},{6,7},{7,8},{8,9},{9,10},{10,1... | collective-permute-start | bytes 1966088 | tf_op jit(solution)/shard_map/ppermute | solution.py:158
  50.4 6.8 %all-to-all-start = ((f32[16,32,768]{2,1,0:T(8,128)}), f32[16,32,768]{2,1,0:T(8,128)S(1)}, u32[]{:S(2)}, u32[]{:S(2)}) async-start(f32[16,32,768]{2,1,0:T(8,128)} %pad_maximum_fusion), calls=%async_computation | async-start | bytes 3145728 | tf_op jit(solution)/shard_map/all_to_all | solution.py:225
  59.2 3.8 %collective-permute-start.13 = (bf16[320,1024]{1,0:T(8,128)(2,1)}, bf16[320,1024]{1,0:T(8,128)(2,1)}, u32[]{:S(2)}, u32[]{:S(2)}) collective-permute-start(bf16[320,1024]{1,0:T(8,128)(2,1)} %collective-permute-done.12), channel_id=1, source_target_pairs={{0,1},{1,2},{2,3},{3,4},{4,5},{5,6},{6,7},{7,8},{8,9},{9,10},{10,1... | collective-permute-start | bytes 1966088 | tf_op jit(solution)/shard_map/ppermute | solution.py:158
  63.0 6.2 %collective-permute-done.3 = bf16[320,1024]{1,0:T(8,128)(2,1)} collective-permute-done((bf16[320,1024]{1,0:T(8,128)(2,1)}, bf16[320,1024]{1,0:T(8,128)(2,1)}, u32[]{:S(2)}, u32[]{:S(2)}) %collective-permute-start.3) | collective-permute-done | bytes 655392 | tf_op jit(solution)/shard_map/ppermute | solution.py:158
  69.2 3.0 %collective-permute-start.4 = (bf16[320,1024]{1,0:T(8,128)(2,1)}, bf16[320,1024]{1,0:T(8,128)(2,1)S(1)}, u32[]{:S(2)}, u32[]{:S(2)}) collective-permute-start(bf16[320,1024]{1,0:T(8,128)(2,1)} %collective-permute-done.3), channel_id=1, source_target_pairs={{0,1},{1,2},{2,3},{3,4},{4,5},{5,6},{6,7},{7,8},{8,9},{9,10},{10,1... | collective-permute-start | bytes 1966088 | tf_op jit(solution)/shard_map/ppermute | solution.py:158
  82.2 6.7 %all-to-all-start.1 = ((f32[16,32,640]{2,1,0:T(8,128)}), f32[16,32,640]{2,1,0:T(8,128)S(1)}, u32[]{:S(2)}, u32[]{:S(2)}) async-start(f32[16,32,640]{2,1,0:T(8,128)} %pad_maximum_fusion.1), calls=%async_computation.1 | async-start | bytes 2621440 | tf_op jit(solution)/shard_map/all_to_all | solution.py:225
  91.3 3.7 %collective-permute-start.15 = (bf16[320,1024]{1,0:T(8,128)(2,1)}, bf16[320,1024]{1,0:T(8,128)(2,1)}, u32[]{:S(2)}, u32[]{:S(2)}) collective-permute-start(bf16[320,1024]{1,0:T(8,128)(2,1)} %collective-permute-done.14), channel_id=1, source_target_pairs={{0,1},{1,2},{2,3},{3,4},{4,5},{5,6},{6,7},{7,8},{8,9},{9,10},{10,1... | collective-permute-start | bytes 1966088 | tf_op jit(solution)/shard_map/ppermute | solution.py:158
  95.0 5.6 %collective-permute-done.9 = bf16[320,1024]{1,0:T(8,128)(2,1)} collective-permute-done((bf16[320,1024]{1,0:T(8,128)(2,1)S(1)}, bf16[320,1024]{1,0:T(8,128)(2,1)}, u32[]{:S(2)}, u32[]{:S(2)}) %collective-permute-start.9) | collective-permute-done | bytes 655392 | tf_op jit(solution)/shard_map/ppermute | solution.py:158
  100.7 3.0 %collective-permute-start.10 = (bf16[320,1024]{1,0:T(8,128)(2,1)}, bf16[320,1024]{1,0:T(8,128)(2,1)}, u32[]{:S(2)}, u32[]{:S(2)}) collective-permute-start(bf16[320,1024]{1,0:T(8,128)(2,1)} %collective-permute-done.9), channel_id=1, source_target_pairs={{0,1},{1,2},{2,3},{3,4},{4,5},{5,6},{6,7},{7,8},{8,9},{9,10},{10,1... | collective-permute-start | bytes 1966088 | tf_op jit(solution)/shard_map/ppermute | solution.py:158
  105.8 5.4 %all-to-all-done.1.block_ref.refs_1_ = f32[16,32,640]{2,1,0:T(8,128)S(1)} async-done(((f32[16,32,640]{2,1,0:T(8,128)}), f32[16,32,640]{2,1,0:T(8,128)S(1)}, u32[]{:S(2)}, u32[]{:S(2)}) %all-to-all-start.1) | async-done | bytes 1310752 | tf_op jit(solution)/shard_map/all_to_all | solution.py:225
  116.3 4.4 %all-to-all-start.3 = ((f32[16,32,640]{2,1,0:T(8,128)}), f32[16,32,640]{2,1,0:T(8,128)}, u32[]{:S(2)}, u32[]{:S(2)}) async-start(f32[16,32,640]{2,1,0:T(8,128)} %pad_maximum_fusion.2), calls=%async_computation.3 | async-start | bytes 2621440 | tf_op jit(solution)/shard_map/all_to_all | solution.py:225
  138.8 4.7 %all-to-all-start.2 = ((f32[16,32,512]{2,1,0:T(8,128)}), f32[16,32,512]{2,1,0:T(8,128)}, u32[]{:S(2)}, u32[]{:S(2)}) async-start(f32[16,32,512]{2,1,0:T(8,128)} %pad_maximum_fusion.3), calls=%async_computation.2 | async-start | bytes 2097152 | tf_op jit(solution)/shard_map/all_to_all | solution.py:225
  147.8 3.5 %shard_map.30.before_ref = f32[8,128]{1,0:T(8,128)S(1)} custom-call(s32[1]{0:T(128)} %bitcast.1.core_ref, f32[16,32,640]{2,1,0:T(8,128)} %all-to-all-done.3.block_ref.refs_2_, f32[8,128]{1,0:T(8,128)S(1)} %shard_map.29.before_ref), custom_call_target="tpu_custom_call" | custom-call | flops 1006632960 | bytes 1310720 | tf_op jit(solution)/shard_map/pallas_call | solution.py:51
  151.3 6.4 %all-to-all-done.2.block_ref.refs_3_ = f32[16,32,512]{2,1,0:T(8,128)} async-done(((f32[16,32,512]{2,1,0:T(8,128)}), f32[16,32,512]{2,1,0:T(8,128)}, u32[]{:S(2)}, u32[]{:S(2)}) %all-to-all-start.2) | async-done | bytes 1048608 | tf_op jit(solution)/shard_map/all_to_all | solution.py:225
  160.6 15.4 %all_to_all.35.parts_ref = f32[32,8,128]{2,1,0:T(8,128)} all-to-all(f32[32,8,128]{2,1,0:T(8,128)S(1)} %broadcast_in_dim.7), channel_id=1, replica_groups=mesh['dp'=32,'tensor'=16] {'dp'}, dimensions={0} | all-to-all | bytes 262144 | tf_op jit(solution)/shard_map/all_to_all | solution.py:229
  177.7 6.9 %all-to-all-start.5 = ((f32[16,8,128]{2,1,0:T(8,128)}), f32[16,8,128]{2,1,0:T(8,128)S(1)}, u32[]{:S(2)}, u32[]{:S(2)}) async-start(f32[16,8,128]{2,1,0:T(8,128)} %shard_map.32), calls=%async_computation.5 | async-start | bytes 131072 | tf_op jit(solution)/shard_map/all_to_all | solution.py:230
  184.6 11.7 %all-to-all-done.5.parts_ref = f32[16,8,128]{2,1,0:T(8,128)S(1)} async-done(((f32[16,8,128]{2,1,0:T(8,128)}), f32[16,8,128]{2,1,0:T(8,128)S(1)}, u32[]{:S(2)}, u32[]{:S(2)}) %all-to-all-start.5) | async-done | bytes 65568 | tf_op jit(solution)/shard_map/all_to_all | solution.py:230
  198.9 16.7 %all_to_all.36 = f32[32,16,160]{2,1,0:T(8,128)S(1)} all-to-all(f32[32,16,160]{2,1,0:T(8,128)S(1)} %shard_map.33), channel_id=1, replica_groups=mesh['dp'=32,'tensor'=16] {'dp'}, dimensions={0} | all-to-all | bytes 655360 | tf_op jit(solution)/shard_map/all_to_all | solution.py:232
  (72 shorter events, 64.2 us)
Async XLA Ops:
  0.0 14.5 %collective-permute-start.5 = (bf16[320,1024]{1,0:T(8,128)(2,1)}, bf16[320,1024]{1,0:T(8,128)(2,1)S(1)}, u32[]{:S(2)}, u32[]{:S(2)}) collective-permute-start(bf16[320,1024]{1,0:T(8,128)(2,1)} %bitcast.43), channel_id=1, source_target_pairs={{0,16},{16,0},{32,48},{48,32},{64,80},{80,64},{96,112},{112,96},{1... | collective-permute-start | bytes 1966088 | tf_op jit(solution)/shard_map/ppermute | solution.py:161
  8.8 13.6 %collective-permute-start = (bf16[320,1024]{1,0:T(8,128)(2,1)}, bf16[320,1024]{1,0:T(8,128)(2,1)S(1)}, u32[]{:S(2)}, u32[]{:S(2)}) collective-permute-start(bf16[320,1024]{1,0:T(8,128)(2,1)} %bitcast.44), channel_id=1, source_target_pairs={{0,1},{1,2},{2,3},{3,4},{4,5},{5,6},{6,7},{7,8},{8,9},{9,10},{10,1... | collective-permute-start | bytes 1966088 | tf_op jit(solution)/shard_map/ppermute | solution.py:158
  14.5 14.7 %collective-permute-start.6 = (bf16[320,1024]{1,0:T(8,128)(2,1)S(1)}, bf16[320,1024]{1,0:T(8,128)(2,1)S(1)}, u32[]{:S(2)}, u32[]{:S(2)}) collective-permute-start(bf16[320,1024]{1,0:T(8,128)(2,1)S(1)} %collective-permute-done.5), channel_id=1, source_target_pairs={{0,1},{1,2},{2,3},{3,4},{4,5},{5,6},{6,7},{7,8},{8,9},{9,10},{10,1... | collective-permute-start | bytes 1966088 | tf_op jit(solution)/shard_map/ppermute | solution.py:158
  17.2 10.1 %collective-permute-start.7 = (bf16[1024,256]{1,0:T(8,128)(2,1)}, bf16[1024,256]{1,0:T(8,128)(2,1)S(1)}, u32[]{:S(2)}, u32[]{:S(2)}) collective-permute-start(bf16[1024,256]{1,0:T(8,128)(2,1)} %param.3), channel_id=1, source_target_pairs={{0,16},{16,0},{32,48},{48,32},{64,80},{80,64},{96,112},{112,96},{1... | collective-permute-start | bytes 1572872 | tf_op jit(solution)/shard_map/ppermute | solution.py:164
  22.4 13.9 %collective-permute-start.1 = (bf16[320,1024]{1,0:T(8,128)(2,1)S(1)}, bf16[320,1024]{1,0:T(8,128)(2,1)S(1)}, u32[]{:S(2)}, u32[]{:S(2)}) collective-permute-start(bf16[320,1024]{1,0:T(8,128)(2,1)S(1)} %collective-permute-done), channel_id=1, source_target_pairs={{0,1},{1,2},{2,3},{3,4},{4,5},{5,6},{6,7},{7,8},{8,9},{9,10},{10,1... | collective-permute-start | bytes 1966088 | tf_op jit(solution)/shard_map/ppermute | solution.py:158
  29.3 14.0 %collective-permute-start.8 = (bf16[320,1024]{1,0:T(8,128)(2,1)S(1)}, bf16[320,1024]{1,0:T(8,128)(2,1)S(1)}, u32[]{:S(2)}, u32[]{:S(2)}) collective-permute-start(bf16[320,1024]{1,0:T(8,128)(2,1)S(1)} %collective-permute-done.6), channel_id=1, source_target_pairs={{0,1},{1,2},{2,3},{3,4},{4,5},{5,6},{6,7},{7,8},{8,9},{9,10},{10,1... | collective-permute-start | bytes 1966088 | tf_op jit(solution)/shard_map/ppermute | solution.py:158
  36.4 20.8 %collective-permute-start.2 = (bf16[320,1024]{1,0:T(8,128)(2,1)S(1)}, bf16[320,1024]{1,0:T(8,128)(2,1)}, u32[]{:S(2)}, u32[]{:S(2)}) collective-permute-start(bf16[320,1024]{1,0:T(8,128)(2,1)S(1)} %collective-permute-done.1), channel_id=1, source_target_pairs={{0,1},{1,2},{2,3},{3,4},{4,5},{5,6},{6,7},{7,8},{8,9},{9,10},{10,1... | collective-permute-start | bytes 1966088 | tf_op jit(solution)/shard_map/ppermute | solution.py:158
  45.3 13.9 %collective-permute-start.12 = (bf16[320,1024]{1,0:T(8,128)(2,1)S(1)}, bf16[320,1024]{1,0:T(8,128)(2,1)}, u32[]{:S(2)}, u32[]{:S(2)}) collective-permute-start(bf16[320,1024]{1,0:T(8,128)(2,1)S(1)} %collective-permute-done.8), channel_id=1, source_target_pairs={{0,1},{1,2},{2,3},{3,4},{4,5},{5,6},{6,7},{7,8},{8,9},{9,10},{10,1... | collective-permute-start | bytes 1966088 | tf_op jit(solution)/shard_map/ppermute | solution.py:158
  50.4 31.8 %all-to-all-start = ((f32[16,32,768]{2,1,0:T(8,128)}), f32[16,32,768]{2,1,0:T(8,128)S(1)}, u32[]{:S(2)}, u32[]{:S(2)}) async-start(f32[16,32,768]{2,1,0:T(8,128)} %pad_maximum_fusion), calls=%async_computation | async-start | bytes 3145728 | tf_op jit(solution)/shard_map/all_to_all | solution.py:225
  57.1 19.1 %copy-start.7 = (bf16[1024,256]{1,0:T(8,128)(2,1)S(1)}, bf16[1024,256]{1,0:T(8,128)(2,1)}, u32[]{:S(2)}) copy-start(bf16[1024,256]{1,0:T(8,128)(2,1)} %copy-done.5) | copy-start | bytes 1572868
  57.1 12.1 %collective-permute-start.3 = (bf16[320,1024]{1,0:T(8,128)(2,1)}, bf16[320,1024]{1,0:T(8,128)(2,1)}, u32[]{:S(2)}, u32[]{:S(2)}) collective-permute-start(bf16[320,1024]{1,0:T(8,128)(2,1)} %collective-permute-done.2), channel_id=1, source_target_pairs={{0,1},{1,2},{2,3},{3,4},{4,5},{5,6},{6,7},{7,8},{8,9},{9,10},{10,1... | collective-permute-start | bytes 1966088 | tf_op jit(solution)/shard_map/ppermute | solution.py:158
  59.2 17.0 %collective-permute-start.13 = (bf16[320,1024]{1,0:T(8,128)(2,1)}, bf16[320,1024]{1,0:T(8,128)(2,1)}, u32[]{:S(2)}, u32[]{:S(2)}) collective-permute-start(bf16[320,1024]{1,0:T(8,128)(2,1)} %collective-permute-done.12), channel_id=1, source_target_pairs={{0,1},{1,2},{2,3},{3,4},{4,5},{5,6},{6,7},{7,8},{8,9},{9,10},{10,1... | collective-permute-start | bytes 1966088 | tf_op jit(solution)/shard_map/ppermute | solution.py:158
  69.2 19.7 %collective-permute-start.4 = (bf16[320,1024]{1,0:T(8,128)(2,1)}, bf16[320,1024]{1,0:T(8,128)(2,1)S(1)}, u32[]{:S(2)}, u32[]{:S(2)}) collective-permute-start(bf16[320,1024]{1,0:T(8,128)(2,1)} %collective-permute-done.3), channel_id=1, source_target_pairs={{0,1},{1,2},{2,3},{3,4},{4,5},{5,6},{6,7},{7,8},{8,9},{9,10},{10,1... | collective-permute-start | bytes 1966088 | tf_op jit(solution)/shard_map/ppermute | solution.py:158
  79.4 11.9 %collective-permute-start.14 = (bf16[320,1024]{1,0:T(8,128)(2,1)}, bf16[320,1024]{1,0:T(8,128)(2,1)}, u32[]{:S(2)}, u32[]{:S(2)}) collective-permute-start(bf16[320,1024]{1,0:T(8,128)(2,1)} %collective-permute-done.13), channel_id=1, source_target_pairs={{0,1},{1,2},{2,3},{3,4},{4,5},{5,6},{6,7},{7,8},{8,9},{9,10},{10,1... | collective-permute-start | bytes 1966088 | tf_op jit(solution)/shard_map/ppermute | solution.py:158
  82.2 28.9 %all-to-all-start.1 = ((f32[16,32,640]{2,1,0:T(8,128)}), f32[16,32,640]{2,1,0:T(8,128)S(1)}, u32[]{:S(2)}, u32[]{:S(2)}) async-start(f32[16,32,640]{2,1,0:T(8,128)} %pad_maximum_fusion.1), calls=%async_computation.1 | async-start | bytes 2621440 | tf_op jit(solution)/shard_map/all_to_all | solution.py:225
  88.9 11.7 %collective-permute-start.9 = (bf16[320,1024]{1,0:T(8,128)(2,1)S(1)}, bf16[320,1024]{1,0:T(8,128)(2,1)}, u32[]{:S(2)}, u32[]{:S(2)}) collective-permute-start(bf16[320,1024]{1,0:T(8,128)(2,1)S(1)} %collective-permute-done.4), channel_id=1, source_target_pairs={{0,1},{1,2},{2,3},{3,4},{4,5},{5,6},{6,7},{7,8},{8,9},{9,10},{10,1... | collective-permute-start | bytes 1966088 | tf_op jit(solution)/shard_map/ppermute | solution.py:158
  91.3 19.9 %collective-permute-start.15 = (bf16[320,1024]{1,0:T(8,128)(2,1)}, bf16[320,1024]{1,0:T(8,128)(2,1)}, u32[]{:S(2)}, u32[]{:S(2)}) collective-permute-start(bf16[320,1024]{1,0:T(8,128)(2,1)} %collective-permute-done.14), channel_id=1, source_target_pairs={{0,1},{1,2},{2,3},{3,4},{4,5},{5,6},{6,7},{7,8},{8,9},{9,10},{10,1... | collective-permute-start | bytes 1966088 | tf_op jit(solution)/shard_map/ppermute | solution.py:158
  100.7 20.1 %collective-permute-start.10 = (bf16[320,1024]{1,0:T(8,128)(2,1)}, bf16[320,1024]{1,0:T(8,128)(2,1)}, u32[]{:S(2)}, u32[]{:S(2)}) collective-permute-start(bf16[320,1024]{1,0:T(8,128)(2,1)} %collective-permute-done.9), channel_id=1, source_target_pairs={{0,1},{1,2},{2,3},{3,4},{4,5},{5,6},{6,7},{7,8},{8,9},{9,10},{10,1... | collective-permute-start | bytes 1966088 | tf_op jit(solution)/shard_map/ppermute | solution.py:158
  114.4 11.8 %collective-permute-start.16 = (bf16[320,1024]{1,0:T(8,128)(2,1)}, bf16[320,1024]{1,0:T(8,128)(2,1)S(1)}, u32[]{:S(2)}, u32[]{:S(2)}) collective-permute-start(bf16[320,1024]{1,0:T(8,128)(2,1)} %collective-permute-done.15), channel_id=1, source_target_pairs={{0,1},{1,2},{2,3},{3,4},{4,5},{5,6},{6,7},{7,8},{8,9},{9,10},{10,1... | collective-permute-start | bytes 1966088 | tf_op jit(solution)/shard_map/ppermute | solution.py:158
  116.3 22.5 %all-to-all-start.3 = ((f32[16,32,640]{2,1,0:T(8,128)}), f32[16,32,640]{2,1,0:T(8,128)}, u32[]{:S(2)}, u32[]{:S(2)}) async-start(f32[16,32,640]{2,1,0:T(8,128)} %pad_maximum_fusion.2), calls=%async_computation.3 | async-start | bytes 2621440 | tf_op jit(solution)/shard_map/all_to_all | solution.py:225
  121.8 9.0 %collective-permute-start.11 = (bf16[160,1024]{1,0:T(8,128)(2,1)S(1)}, bf16[160,1024]{1,0:T(8,128)(2,1)S(1)}, u32[]{:S(2)}, u32[]{:S(2)}) collective-permute-start(bf16[160,1024]{1,0:T(8,128)(2,1)S(1)} %constant_dynamic-slice_fusion.1), channel_id=1, source_target_pairs={{0,1},{1,2},{2,3},{3,4},{4,5},{5,6},{6,7},{7,8},{8,9},{9,10},{10,1... | collective-permute-start | bytes 983048 | tf_op jit(solution)/shard_map/ppermute | solution.py:158
  126.3 8.2 %collective-permute-start.17 = (bf16[160,1024]{1,0:T(8,128)(2,1)S(1)}, bf16[160,1024]{1,0:T(8,128)(2,1)S(1)}, u32[]{:S(2)}, u32[]{:S(2)}) collective-permute-start(bf16[160,1024]{1,0:T(8,128)(2,1)S(1)} %constant_dynamic-slice_fusion), channel_id=1, source_target_pairs={{0,1},{1,2},{2,3},{3,4},{4,5},{5,6},{6,7},{7,8},{8,9},{9,10},{10,1... | collective-permute-start | bytes 983048 | tf_op jit(solution)/shard_map/ppermute | solution.py:158
  138.8 18.9 %all-to-all-start.2 = ((f32[16,32,512]{2,1,0:T(8,128)}), f32[16,32,512]{2,1,0:T(8,128)}, u32[]{:S(2)}, u32[]{:S(2)}) async-start(f32[16,32,512]{2,1,0:T(8,128)} %pad_maximum_fusion.3), calls=%async_computation.2 | async-start | bytes 2097152 | tf_op jit(solution)/shard_map/all_to_all | solution.py:225
  177.7 18.6 %all-to-all-start.5 = ((f32[16,8,128]{2,1,0:T(8,128)}), f32[16,8,128]{2,1,0:T(8,128)S(1)}, u32[]{:S(2)}, u32[]{:S(2)}) async-start(f32[16,8,128]{2,1,0:T(8,128)} %shard_map.32), calls=%async_computation.5 | async-start | bytes 131072 | tf_op jit(solution)/shard_map/all_to_all | solution.py:230
  (8 other events, 48.4 us)
